TPU v7x, 32 devices: a whole 2x2x4 slice. The times are simulated.
32 devices in a mesh: row: 8 (over z, y), col: 4 (over x, core).
Axes of the slice: x: 2, y: 2, z: 4, core: 2. Of those that a mesh axis runs over, the one named last changes fastest.
Arguments:
- image: bfloat16 [32, 512, 512], P(None, 'row', 'col'), may hold values from -6 to 6
- weight: bfloat16 [3, 3, 32, 32], replicated, may hold values from -0.375 to 0.375
- bias: float32 [32], replicated, may hold values from -3 to 3
- cotangent: bfloat16 [32, 512, 512], P(None, 'row', 'col'), may hold values from -60 to 60
Outputs:
- activation: bfloat16 [32, 512, 512], P(None, 'row', 'col')
- grad_image: bfloat16 [32, 512, 512], P(None, 'row', 'col')
- grad_weight: float32 [3, 3, 32, 32], replicated
- grad_bias: float32 [32], replicated
All inputs are finite; a program needn't handle non-finite values.
Results may differ from a plain program's by a relative error of at most 0.0065.
Values may be sent and summed in bfloat16 or wider, within the bound.
No kernel may reach another device: no remote copies, remote signals or barrier semaphores. Data moves between devices by JAX's collectives and lax.ppermute only.
A program may use at most 64 MiB of HBM per device.

v0:
```python
import math

import jax
import jax.numpy as jnp
from jax import lax
from jax.sharding import PartitionSpec as P

DILATION_PIXELS = 16


def from_behind(value, axis, steps):
    count = lax.axis_size(axis)
    initial, last = (max(0, -steps), min(count, count - steps))
    return lax.ppermute(value, axis, [(source, source + steps) for source in range(initial, last)])


def gelu_pair(preact):
    coef = 0.7978845608
    cube = preact * preact * preact
    tval = jnp.tanh(coef * (preact + 0.044715 * cube))
    value = 0.5 * preact * (1.0 + tval)
    slope_val = 0.5 * (1.0 + tval) + 0.5 * preact * (1.0 - tval * tval) * coef * (
        1.0 + 3.0 * 0.044715 * preact * preact
    )
    return (value, slope_val)


def extended(local_block):
    row_count = local_block.shape[1]
    column_count = local_block.shape[2]
    upper_neighbour = from_behind(local_block[:, row_count - DILATION_PIXELS :, :], "row", 1)
    lower_neighbour = from_behind(local_block[:, :DILATION_PIXELS, :], "row", -1)
    tall_block = jnp.concatenate([upper_neighbour, local_block, lower_neighbour], axis=1)
    left_margin = from_behind(tall_block[:, :, column_count - DILATION_PIXELS :], "col", 1)
    right_margin = from_behind(tall_block[:, :, :DILATION_PIXELS], "col", -1)
    return jnp.concatenate([left_margin, tall_block, right_margin], axis=2)


def tap_view(ext, row_offset, column_offset, row_count, column_count):
    start_row = DILATION_PIXELS + row_offset * DILATION_PIXELS
    start_column = DILATION_PIXELS + column_offset * DILATION_PIXELS
    return ext[:, start_row : start_row + row_count, start_column : start_column + column_count]


def row_stack(ext, row_offset, sign_flip, row_count, column_count):
    return jnp.concatenate(
        [
            tap_view(
                ext, sign_flip * row_offset, sign_flip * column_offset, row_count, column_count
            )
            for column_offset in (-1, 0, 1)
        ],
        axis=0,
    )


def shards(image, weight, bias, cotangent):
    row_count = image.shape[1]
    column_count = image.shape[2]
    channels = image.shape[0]
    height_all = row_count * lax.axis_size("row")
    width_all = column_count * lax.axis_size("col")
    scale = 1.0 / math.sqrt(height_all * width_all)
    image_ext = extended(image)
    preact = jnp.zeros(image.shape, jnp.float32) + bias[:, None, None]
    for row_offset in (-1, 0, 1):
        weight_row = jnp.transpose(weight[row_offset + 1], (1, 0, 2)).reshape(
            channels, 3 * channels
        )
        stacked = row_stack(image_ext, row_offset, 1, row_count, column_count)
        preact = preact + jnp.einsum(
            "ok,krq->orq", weight_row, stacked, preferred_element_type=jnp.float32
        )
    value, slope_val = gelu_pair(preact)
    activation = value.astype(jnp.bfloat16)
    preact_gradient = (cotangent.astype(jnp.float32) * slope_val).astype(jnp.bfloat16)
    taps = []
    for row_offset in (-1, 0, 1):
        stacked = row_stack(image_ext, row_offset, 1, row_count, column_count)
        joined = (
            jnp.einsum("orq,krq->ok", preact_gradient, stacked, preferred_element_type=jnp.float32)
            * scale
        )
        taps.append(jnp.transpose(joined.reshape(channels, 3, channels), (1, 0, 2)))
    local_weight = jnp.stack(taps)
    local_bias = jnp.sum(preact_gradient.astype(jnp.float32), axis=(1, 2)) * scale
    grad_weight, grad_bias = lax.psum((local_weight, local_bias), ("row", "col"))
    grad_ext = extended(preact_gradient)
    total = jnp.zeros(image.shape, jnp.float32)
    for row_offset in (-1, 0, 1):
        weight_row = weight[row_offset + 1].reshape(3 * channels, channels)
        stacked = row_stack(grad_ext, row_offset, -1, row_count, column_count)
        total = total + jnp.einsum(
            "kc,krq->crq", weight_row, stacked, preferred_element_type=jnp.float32
        )
    grad_image = total.astype(jnp.bfloat16)
    return (activation, grad_image, grad_weight, grad_bias)


def solution(mesh):
    return jax.shard_map(
        shards,
        mesh=mesh,
        in_specs=(P(None, "row", "col"), P(), P(), P(None, "row", "col")),
        out_specs=(P(None, "row", "col"), P(None, "row", "col"), P(), P()),
        check_vma=False,
    )
```

profile of v0, /device:TPU:0, one launch (start us, length us, event | category | flops | bytes accessed | tf_op | source)
XLA Modules:
  0.0 106.6 jit_solution(3521222350837511770)
XLA Ops:
  0.6 1.4 %copy.42 = bf16[32,64,128]{2,0,1:T(8,128)(2,1)S(1)} copy(bf16[32,64,128]{2,1,0:T(8,128)(2,1)} %param.4) | data formatting | bytes 1048576 | tf_op args[0]
  2.1 4.9 %collective-permute-start = (bf16[32,16,128]{2,0,1:T(8,128)(2,1)S(1)}, bf16[32,16,128]{2,0,1:T(8,128)(2,1)S(1)}, u32[]{:S(2)}, u32[]{:S(2)}) collective-permute-start(bf16[32,16,128]{2,0,1:T(8,128)(2,1)S(1)} %get-tuple-element.42), channel_id=1, source_target_pairs={{0,4},{4,8},{8,12},{12,16},{16,20},{20,24},{24,28},{1,5},{5,9},{9,... | collective-permute-start | bytes 393224 | tf_op jit(solution)/shard_map/ppermute | solution.py:14
  7.0 1.3 %collective-permute-start.1 = (bf16[32,16,128]{2,0,1:T(8,128)(2,1)S(1)}, bf16[32,16,128]{2,0,1:T(8,128)(2,1)S(1)}, u32[]{:S(2)}, u32[]{:S(2)}) collective-permute-start(bf16[32,16,128]{2,0,1:T(8,128)(2,1)S(1)} %get-tuple-element.41), channel_id=1, source_target_pairs={{4,0},{8,4},{12,8},{16,12},{20,16},{24,20},{28,24},{5,1},{9,5},{13... | collective-permute-start | bytes 393224 | tf_op jit(solution)/shard_map/ppermute | solution.py:14
  8.3 1.4 %collective-permute-done = bf16[32,16,128]{2,0,1:T(8,128)(2,1)S(1)} collective-permute-done((bf16[32,16,128]{2,0,1:T(8,128)(2,1)S(1)}, bf16[32,16,128]{2,0,1:T(8,128)(2,1)S(1)}, u32[]{:S(2)}, u32[]{:S(2)}) %collective-permute-start) | collective-permute-done | bytes 131104 | tf_op jit(solution)/shard_map/ppermute | solution.py:14
  9.8 0.4 constant_dynamic-update-slice_fusion.1
  10.1 3.7 %collective-permute-done.1 = bf16[32,16,128]{2,0,1:T(8,128)(2,1)S(1)} collective-permute-done((bf16[32,16,128]{2,0,1:T(8,128)(2,1)S(1)}, bf16[32,16,128]{2,0,1:T(8,128)(2,1)S(1)}, u32[]{:S(2)}, u32[]{:S(2)}) %collective-permute-start.1) | collective-permute-done | bytes 131104 | tf_op jit(solution)/shard_map/ppermute | solution.py:14
  13.9 0.3 fusion.68
  14.2 0.8 copy.45
  15.0 0.8 copy.48
  15.9 1.3 %collective-permute-start.3 = (bf16[32,96,16]{1,2,0:T(8,128)(2,1)S(1)}, bf16[32,96,16]{1,2,0:T(8,128)(2,1)S(1)}, u32[]{:S(2)}, u32[]{:S(2)}) collective-permute-start(bf16[32,96,16]{1,2,0:T(8,128)(2,1)S(1)} %copy.48), channel_id=1, source_target_pairs={{1,0},{2,1},{3,2},{5,4},{6,5},{7,6},{9,8},{10,9},{11,10},{13,12},{... | collective-permute-start | bytes 294920 | tf_op jit(solution)/shard_map/ppermute | solution.py:14
  17.1 3.0 %collective-permute-start.2 = (bf16[32,96,16]{1,2,0:T(8,128)(2,1)S(1)}, bf16[32,96,16]{1,2,0:T(8,128)(2,1)S(1)}, u32[]{:S(2)}, u32[]{:S(2)}) collective-permute-start(bf16[32,96,16]{1,2,0:T(8,128)(2,1)S(1)} %copy.45), channel_id=1, source_target_pairs={{0,1},{1,2},{2,3},{4,5},{5,6},{6,7},{8,9},{9,10},{10,11},{12,13},{... | collective-permute-start | bytes 294920 | tf_op jit(solution)/shard_map/ppermute | solution.py:14
  20.2 1.4 %fusion.71 = (bf16[1,3,32,32]{3,2,1,0:T(8,128)(2,1)}, bf16[32,3,32]{2,0,1:T(8,128)(2,1)S(1)}, bf16[32,3,32]{2,0,1:T(8,128)(2,1)S(1)}, bf16[32,3,32]{2,0,1:T(8,12...) fusion(bf16[3,3,32,32]{3,2,1,0:T(8,128)(2,1)} %param.5), kind=kLoop, calls=%fused_computation.93 | loop fusion | bytes 55296 | tf_op jit(solution)/shard_map/slice | solution.py:67
  21.7 0.7 reshape.34
  22.5 1.1 %copy.46 = bf16[32,96,16]{2,0,1:T(8,128)(2,1)S(1)} copy(bf16[32,96,16]{1,2,0:T(8,128)(2,1)S(1)} %collective-permute-done.2) | data formatting | bytes 196608 | tf_op jit(solution)/shard_map/ppermute | solution.py:14
  23.7 1.1 %copy.49 = bf16[32,96,16]{2,0,1:T(8,128)(2,1)S(1)} copy(bf16[32,96,16]{1,2,0:T(8,128)(2,1)S(1)} %collective-permute-done.3) | data formatting | bytes 196608 | tf_op jit(solution)/shard_map/ppermute | solution.py:14
  24.8 1.1 %fusion.54 = (bf16[32,64,128]{2,0,1:T(8,128)(2,1)S(1)}, bf16[32,64,128]{2,0,1:T(8,128)(2,1)S(1)}, bf16[32,64,128]{2,0,1:T(8,128)(2,1)S(1)}, bf16[32,64,128]{2,0,1:T(8,128)(2,1)S(1)}) fusion(bf16[32,96,16]{2,0,1:T(8,128)(2,1)S(1)} %copy.46, bf16[32,96,128]{2,0,1:T(8,128)(2,1)S(1)} %constant_dynamic-update-slice_fusion, bf16[32,96,16]{2,0,1:T(8,128)(2,1)S(1)} %copy.49), kind=kLoop, calls=%fused_computation.71 | loop fusion | flops 4194304 | bytes 3080192 | tf_op jit(solution)/shard_map/concatenate | solution.py:36
  25.9 0.3 fusion.50
  26.3 0.6 fusion.10
  27.0 0.2 copy-done.5
  27.2 0.4 fusion.31
  27.6 0.7 copy-done.11
  28.2 2.1 %convert_reduce_fusion = (f32[32]{0:T(128)S(1)}, bf16[32,64,128]{2,0,1:T(8,128)(2,1)S(1)}, bf16[32,64,128]{2,0,1:T(8,128)(2,1)}) fusion(bf16[32,64,128]{2,1,0:T(8,128)(2,1)S(1)} %copy-done.11, f32[64,128,32]{1,2,0:T(8,128)S(1)} %fusion.31, bf16[32,96,1]{1,0,2:T(8,128)(2,1)S(1)} %reshape.35, bf16[96,64,128]{2,0,1:T(8,128)(2,1)S(1)} %fusion.10), kind=kOutput, calls=%fused_computation.64 | convolution fusion | flops 56885216 | bytes 4200576 | tf_op jit(solution)/shard_map/ok,krq->orq/dot_general | solution.py:71
  30.3 0.6 fusion.38
  31.0 0.6 fusion.39
  31.8 0.3 copy-done.2
  32.0 0.6 fusion.40
  32.9 1.3 %collective-permute-start.5 = (bf16[32,16,128]{2,0,1:T(8,128)(2,1)S(1)}, bf16[32,16,128]{2,0,1:T(8,128)(2,1)S(1)}, u32[]{:S(2)}, u32[]{:S(2)}) collective-permute-start(bf16[32,16,128]{2,0,1:T(8,128)(2,1)S(1)} %get-tuple-element.39), channel_id=1, source_target_pairs={{4,0},{8,4},{12,8},{16,12},{20,16},{24,20},{28,24},{5,1},{9,5},{13... | collective-permute-start | bytes 393224 | tf_op jit(solution)/shard_map/ppermute | solution.py:14
  34.2 5.0 %collective-permute-start.4 = (bf16[32,16,128]{2,0,1:T(8,128)(2,1)S(1)}, bf16[32,16,128]{2,0,1:T(8,128)(2,1)S(1)}, u32[]{:S(2)}, u32[]{:S(2)}) collective-permute-start(bf16[32,16,128]{2,0,1:T(8,128)(2,1)S(1)} %get-tuple-element.40), channel_id=1, source_target_pairs={{0,4},{4,8},{8,12},{12,16},{16,20},{20,24},{24,28},{1,5},{5,9},{9,... | collective-permute-start | bytes 393224 | tf_op jit(solution)/shard_map/ppermute | solution.py:14
  39.2 2.1 %collective-permute-done.5 = bf16[32,16,128]{2,0,1:T(8,128)(2,1)S(1)} collective-permute-done((bf16[32,16,128]{2,0,1:T(8,128)(2,1)S(1)}, bf16[32,16,128]{2,0,1:T(8,128)(2,1)S(1)}, u32[]{:S(2)}, u32[]{:S(2)}) %collective-permute-start.5) | collective-permute-done | bytes 131104 | tf_op jit(solution)/shard_map/ppermute | solution.py:14
  41.2 3.6 %collective-permute-done.4 = bf16[32,16,128]{2,0,1:T(8,128)(2,1)S(1)} collective-permute-done((bf16[32,16,128]{2,0,1:T(8,128)(2,1)S(1)}, bf16[32,16,128]{2,0,1:T(8,128)(2,1)S(1)}, u32[]{:S(2)}, u32[]{:S(2)}) %collective-permute-start.4) | collective-permute-done | bytes 131104 | tf_op jit(solution)/shard_map/ppermute | solution.py:14
  44.9 0.3 fusion.67
  45.2 0.8 copy.56
  46.0 0.8 copy.58
  46.8 2.0 %collective-permute-start.7 = (bf16[32,96,16]{1,2,0:T(8,128)(2,1)S(1)}, bf16[32,96,16]{1,2,0:T(8,128)(2,1)S(1)}, u32[]{:S(2)}, u32[]{:S(2)}) collective-permute-start(bf16[32,96,16]{1,2,0:T(8,128)(2,1)S(1)} %copy.58), channel_id=1, source_target_pairs={{0,1},{1,2},{2,3},{4,5},{5,6},{6,7},{8,9},{9,10},{10,11},{12,13},{... | collective-permute-start | bytes 294920 | tf_op jit(solution)/shard_map/ppermute | solution.py:14
  48.9 1.5 %collective-permute-start.6 = (bf16[32,96,16]{1,2,0:T(8,128)(2,1)S(1)}, bf16[32,96,16]{1,2,0:T(8,128)(2,1)S(1)}, u32[]{:S(2)}, u32[]{:S(2)}) collective-permute-start(bf16[32,96,16]{1,2,0:T(8,128)(2,1)S(1)} %copy.56), channel_id=1, source_target_pairs={{1,0},{2,1},{3,2},{5,4},{6,5},{7,6},{9,8},{10,9},{11,10},{13,12},{... | collective-permute-start | bytes 294920 | tf_op jit(solution)/shard_map/ppermute | solution.py:14
  50.4 47.1 %all-reduce = (f32[3,3,32,32]{3,1,2,0:T(4,128)S(1)}, f32[32]{0:T(128)}) all-reduce(f32[3,3,32,32]{3,1,2,0:T(4,128)S(1)} %pad_maximum_fusion.11, f32[32]{0:T(128)S(1)} %broadcast_multiply_fusion), channel_id=1, replica_groups=mesh['row'=8,'col'=4] {'row','col'}, use_global_device_ids=true, to_apply=%region_0.0 | all-reduce | flops 9248 | bytes 73984 | tf_op jit(solution)/shard_map/psum | solution.py:87
  97.5 0.7 copy.65
  98.2 1.0 copy.63
  99.2 1.1 %copy.57 = bf16[32,96,16]{2,0,1:T(8,128)(2,1)S(1)} copy(bf16[32,96,16]{1,2,0:T(8,128)(2,1)S(1)} %collective-permute-done.6) | data formatting | bytes 196608 | tf_op jit(solution)/shard_map/ppermute | solution.py:14
  100.3 1.1 %copy.59 = bf16[32,96,16]{2,0,1:T(8,128)(2,1)S(1)} copy(bf16[32,96,16]{1,2,0:T(8,128)(2,1)S(1)} %collective-permute-done.7) | data formatting | bytes 196608 | tf_op jit(solution)/shard_map/ppermute | solution.py:14
  101.5 1.5 %pad_maximum_fusion.7 = (bf16[32,96,144]{2,0,1:T(8,128)(2,1)S(1)}, bf16[32,96,144]{2,0,1:T(8,128)(2,1)S(1)}) fusion(bf16[32,96,16]{2,0,1:T(8,128)(2,1)S(1)} %copy.57, bf16[32,16,128]{2,0,1:T(8,128)(2,1)S(1)} %collective-permute-done.5, bf16[32,64,128]{2,0,1:T(8,128)(2,1)S(1)} %get-tuple-element.19, bf16[32,16,128]{2,0,1:T(8,128)(2,1)S(1)} %collective-permute-done.4, ...), kind=kLoop, calls=%fused_computation.27 | loop fusion | flops 7077888 | bytes 2752512 | tf_op jit(solution)/shard_map/concatenate | solution.py:36
  103.0 0.7 fusion.65
  103.7 0.4 fusion.16
  104.1 0.4 copy-done.8
  104.4 0.4 fusion.2
  104.8 0.4 copy-done.7
  105.2 0.4 fusion.35
  105.6 1.0 copy.64
  (40 shorter events, 0.9 us)
Async XLA Ops:
  0.6 9.1 %copy-start = (bf16[32,64,128]{2,1,0:T(8,128)(2,1)S(1)}, bf16[32,64,128]{2,1,0:T(8,128)(2,1)}, u32[]{:S(2)}) copy-start(bf16[32,64,128]{2,1,0:T(8,128)(2,1)} %param.4) | copy-start | bytes 1572868
  2.1 7.6 %collective-permute-start = (bf16[32,16,128]{2,0,1:T(8,128)(2,1)S(1)}, bf16[32,16,128]{2,0,1:T(8,128)(2,1)S(1)}, u32[]{:S(2)}, u32[]{:S(2)}) collective-permute-start(bf16[32,16,128]{2,0,1:T(8,128)(2,1)S(1)} %get-tuple-element.42), channel_id=1, source_target_pairs={{0,4},{4,8},{8,12},{12,16},{16,20},{20,24},{24,28},{1,5},{5,9},{9,... | collective-permute-start | bytes 393224 | tf_op jit(solution)/shard_map/ppermute | solution.py:14
  7.0 6.9 %collective-permute-start.1 = (bf16[32,16,128]{2,0,1:T(8,128)(2,1)S(1)}, bf16[32,16,128]{2,0,1:T(8,128)(2,1)S(1)}, u32[]{:S(2)}, u32[]{:S(2)}) collective-permute-start(bf16[32,16,128]{2,0,1:T(8,128)(2,1)S(1)} %get-tuple-element.41), channel_id=1, source_target_pairs={{4,0},{8,4},{12,8},{16,12},{20,16},{24,20},{28,24},{5,1},{9,5},{13... | collective-permute-start | bytes 393224 | tf_op jit(solution)/shard_map/ppermute | solution.py:14
  9.7 4.5 %copy-start.4 = (bf16[32,16,128]{2,0,1:T(8,128)(2,1)}, bf16[32,16,128]{2,0,1:T(8,128)(2,1)S(1)}, u32[]{:S(2)}) copy-start(bf16[32,16,128]{2,0,1:T(8,128)(2,1)S(1)} %collective-permute-done) | copy-start | bytes 393220
  15.9 7.8 %collective-permute-start.3 = (bf16[32,96,16]{1,2,0:T(8,128)(2,1)S(1)}, bf16[32,96,16]{1,2,0:T(8,128)(2,1)S(1)}, u32[]{:S(2)}, u32[]{:S(2)}) collective-permute-start(bf16[32,96,16]{1,2,0:T(8,128)(2,1)S(1)} %copy.48), channel_id=1, source_target_pairs={{1,0},{2,1},{3,2},{5,4},{6,5},{7,6},{9,8},{10,9},{11,10},{13,12},{... | collective-permute-start | bytes 294920 | tf_op jit(solution)/shard_map/ppermute | solution.py:14
  17.1 5.4 %collective-permute-start.2 = (bf16[32,96,16]{1,2,0:T(8,128)(2,1)S(1)}, bf16[32,96,16]{1,2,0:T(8,128)(2,1)S(1)}, u32[]{:S(2)}, u32[]{:S(2)}) collective-permute-start(bf16[32,96,16]{1,2,0:T(8,128)(2,1)S(1)} %copy.45), channel_id=1, source_target_pairs={{0,1},{1,2},{2,3},{4,5},{5,6},{6,7},{8,9},{9,10},{10,11},{12,13},{... | collective-permute-start | bytes 294920 | tf_op jit(solution)/shard_map/ppermute | solution.py:14
  24.8 1.2 %copy-start.10 = (bf16[32,96,1]{1,0,2:T(8,128)(2,1)S(1)}, bf16[32,96,1]{1,0,2:T(8,128)(2,1)}, u32[]{:S(2)}) copy-start(bf16[32,96,1]{1,0,2:T(8,128)(2,1)} %reshape.34) | copy-start | bytes 18436
  25.9 1.0 copy-start.1
  26.3 0.9 copy-start.5
  26.3 0.9 copy-start.12
  27.2 1.0 copy-start.11
  31.0 1.1 %copy-start.2 = (bf16[32,64,128]{2,0,1:T(8,128)(2,1)S(1)}, bf16[32,64,128]{2,0,1:T(8,128)(2,1)}, u32[]{:S(2)}) copy-start(bf16[32,64,128]{2,0,1:T(8,128)(2,1)} %copy-done.1) | copy-start | bytes 1572868
  31.0 1.1 %copy-start.6 = (bf16[32,16,128]{2,0,1:T(8,128)(2,1)S(1)}, bf16[32,16,128]{2,0,1:T(8,128)(2,1)}, u32[]{:S(2)}) copy-start(bf16[32,16,128]{2,0,1:T(8,128)(2,1)} %copy-done.4) | copy-start | bytes 393220
  32.9 8.3 %collective-permute-start.5 = (bf16[32,16,128]{2,0,1:T(8,128)(2,1)S(1)}, bf16[32,16,128]{2,0,1:T(8,128)(2,1)S(1)}, u32[]{:S(2)}, u32[]{:S(2)}) collective-permute-start(bf16[32,16,128]{2,0,1:T(8,128)(2,1)S(1)} %get-tuple-element.39), channel_id=1, source_target_pairs={{4,0},{8,4},{12,8},{16,12},{20,16},{24,20},{28,24},{5,1},{9,5},{13... | collective-permute-start | bytes 393224 | tf_op jit(solution)/shard_map/ppermute | solution.py:14
  34.2 10.6 %collective-permute-start.4 = (bf16[32,16,128]{2,0,1:T(8,128)(2,1)S(1)}, bf16[32,16,128]{2,0,1:T(8,128)(2,1)S(1)}, u32[]{:S(2)}, u32[]{:S(2)}) collective-permute-start(bf16[32,16,128]{2,0,1:T(8,128)(2,1)S(1)} %get-tuple-element.40), channel_id=1, source_target_pairs={{0,4},{4,8},{8,12},{12,16},{16,20},{20,24},{24,28},{1,5},{5,9},{9,... | collective-permute-start | bytes 393224 | tf_op jit(solution)/shard_map/ppermute | solution.py:14
  45.2 53.0 %copy-start.3 = (bf16[32,64,128]{2,0,1:T(8,128)(2,1)S(1)}, bf16[32,64,128]{2,0,1:T(8,128)(2,1)}, u32[]{:S(2)}) copy-start(bf16[32,64,128]{2,0,1:T(8,128)(2,1)} %get-tuple-element.30) | copy-start | bytes 1572868
  46.8 53.5 %collective-permute-start.7 = (bf16[32,96,16]{1,2,0:T(8,128)(2,1)S(1)}, bf16[32,96,16]{1,2,0:T(8,128)(2,1)S(1)}, u32[]{:S(2)}, u32[]{:S(2)}) collective-permute-start(bf16[32,96,16]{1,2,0:T(8,128)(2,1)S(1)} %copy.58), channel_id=1, source_target_pairs={{0,1},{1,2},{2,3},{4,5},{5,6},{6,7},{8,9},{9,10},{10,11},{12,13},{... | collective-permute-start | bytes 294920 | tf_op jit(solution)/shard_map/ppermute | solution.py:14
  48.9 50.3 %collective-permute-start.6 = (bf16[32,96,16]{1,2,0:T(8,128)(2,1)S(1)}, bf16[32,96,16]{1,2,0:T(8,128)(2,1)S(1)}, u32[]{:S(2)}, u32[]{:S(2)}) collective-permute-start(bf16[32,96,16]{1,2,0:T(8,128)(2,1)S(1)} %copy.56), channel_id=1, source_target_pairs={{1,0},{2,1},{3,2},{5,4},{6,5},{7,6},{9,8},{10,9},{11,10},{13,12},{... | collective-permute-start | bytes 294920 | tf_op jit(solution)/shard_map/ppermute | solution.py:14
  102.9 0.7 copy-start.9
  103.7 0.7 copy-start.8
  104.4 0.7 copy-start.7
where the time goes:
time: 107 us
  blocking collectives  47.1 us (44%)
  starting transfers between devices  20.3 us (19%)
  local copies, waits for them, and re-layouts  18.2 us (17%)
  waiting for transfers between devices  10.8 us (10%)
  matrix products  5.81 us (5%)
  other arithmetic  3.41 us (3%)
    psum x1, blocking collectives, shards(): lax.psum((local_weight, local_bias), ('row', 'col'))  47.1 us
    ppermute x8, starting transfers between devices, from_behind(): lax.ppermute(value, axis, [(source, source + steps) for source in range(i...  20.3 us
    ppermute x8, waiting for transfers between devices, from_behind(): lax.ppermute(value, axis, [(source, source + steps) for source in range(i...  10.8 us
    unnamed x32, local copies, waits for them, and re-layouts  6.49 us
    ppermute x4, local copies, waits for them, and re-layouts, from_behind(): lax.ppermute(value, axis, [(source, source + steps) for source in range(i...  4.41 us
    dot_general x3, matrix products, shards(): jnp.einsum('ok,krq->orq', weight_row, stacked, preferred_element_type=jnp...  2.79 us
    concatenate x2, other arithmetic, extended(): return jnp.concatenate([left_margin, tall_block, right_margin], axis=2)  2.62 us
  transfers between devices with their start and end apart: 8, of which 4 were waited for; matrix products, arithmetic and copies ran while one was open for 6% of the time, Pallas kernels for 0%

commit v1 on v0

v1 whole, which is shorter than its diff:
```python
import functools
import math

import jax
import jax.numpy as jnp
from jax import lax
from jax.experimental import pallas as pl
from jax.experimental.pallas import tpu as pltpu
from jax.sharding import PartitionSpec as P

DILATION = 16
VMEM_BYTES = 16 * 2**20


def from_behind(value, axis, steps):
    count = lax.axis_size(axis)
    initial, last = (max(0, -steps), min(count, count - steps))
    return lax.ppermute(value, axis, [(source, source + steps) for source in range(initial, last)])


def add_pairs(value, axes):
    other = None
    for axis in axes:
        count = lax.axis_size(axis)
        step = 1
        while step < count:
            value = value if other is None else value + other
            other = lax.ppermute(value, axis, [(place, place ^ step) for place in range(count)])
            step *= 2
    return value, jnp.zeros_like(value) if other is None else other


def gelu_pair(preact):
    coef = 0.7978845608
    square = preact * preact
    tval = jnp.tanh(coef * (preact + 0.044715 * (square * preact)))
    half = 0.5 * (1.0 + tval)
    slope_val = half + 0.5 * preact * (1.0 - tval * tval) * coef * (1.0 + 3.0 * 0.044715 * square)
    return (preact * half, slope_val)


def lane_of(shape):
    return lax.broadcasted_iota(jnp.int32, shape, len(shape) - 1)


def pack_group(rows):
    half = len(rows) // 2
    width = rows[0].shape[-1]
    lane = lane_of(rows[0].shape)
    pair = lane // (2 * DILATION)
    front = lane % (2 * DILATION) < DILATION

    def joined(part):
        total = pltpu.roll(part[0], DILATION, 1)
        for k in range(1, half):
            total = jnp.where(pair == k, pltpu.roll(part[k], DILATION + 2 * DILATION * k, 1), total)
        return total

    low, high = joined(rows[:half]), joined(rows[half:])
    first = jnp.where(front, pltpu.roll(low, width - DILATION, 1), high)
    last = jnp.where(front, low, pltpu.roll(high, DILATION, 1))
    return first, last


def unpack_group(from_left, from_right, count):
    half = count // 2
    width = from_left.shape[-1]
    front = lane_of(from_left.shape) % (2 * DILATION) < DILATION
    low = jnp.where(front, from_right, pltpu.roll(from_left, DILATION, 1))
    high = jnp.where(front, pltpu.roll(from_right, width - DILATION, 1), from_left)
    return [
        pltpu.roll(low if k < half else high, (width - DILATION - 2 * DILATION * (k % half)) % width, 1)
        for k in range(count)
    ]


def pack_rows(block, store, first_group):
    pieces = block.shape[-1] // DILATION
    for group in range(block.shape[0] // pieces):
        first, last = pack_group([block[group * pieces + k] for k in range(pieces)])
        store(first_group + group, first, last)


def own_kernel(image_ref, rows_ref, rims_ref):
    count = image_ref.shape[1] // DILATION
    groups = rims_ref.shape[1] // count

    def store(place, first, last):
        rims_ref[0, place] = first
        rims_ref[1, place] = last

    def body(block, carry):
        start = pl.multiple_of(block * DILATION, DILATION)
        rows = jnp.swapaxes(image_ref[:, pl.ds(start, DILATION), :], 0, 1)
        rows_ref[pl.ds(start, DILATION)] = rows
        pack_rows(rows, store, block * groups)
        return carry

    lax.fori_loop(0, count, body, 0)


def rim_kernel(swap, upper_ref, lower_ref, rims_ref, first_ref, last_ref, *rows_refs):
    own = rims_ref.shape[1]
    groups = (first_ref.shape[0] - own) // 2
    first_ref[groups : groups + own] = rims_ref[0]
    last_ref[groups : groups + own] = rims_ref[1]

    def store(place, first, last):
        first_ref[place] = first
        last_ref[place] = last

    for index, ref in enumerate((upper_ref, lower_ref)):
        rows = jnp.swapaxes(ref[...], 0, 1) if swap else ref[...]
        if swap:
            rows_refs[0][index] = rows
        pack_rows(rows, store, index * (groups + own))


def spread(rows_of, left_ref, right_ref, stack_ref, block, group_start):
    channels, width = left_ref.shape[1:]
    pieces = width // DILATION
    lane = lane_of((channels, width))
    for group in range(DILATION // pieces):
        rims = unpack_group(left_ref[group_start + group], right_ref[group_start + group], pieces)
        for k in range(pieces):
            row = group * pieces + k
            value = rows_of(row)
            columns = slice(row * width, (row + 1) * width)
            before = jnp.where(lane < DILATION, rims[k], pltpu.roll(value, DILATION, 1))
            after = jnp.where(lane >= width - DILATION, rims[k], pltpu.roll(value, width - DILATION, 1))
            stack_ref[block, 0:channels, columns] = before
            stack_ref[block, channels : 2 * channels, columns] = value
            stack_ref[block, 2 * channels : 3 * channels, columns] = after


def spread_all(own_ref, upper_of, lower_of, left_ref, right_ref, stack_ref):
    count = own_ref.shape[0] // DILATION
    groups = left_ref.shape[0] // (count + 2)
    spread(upper_of, left_ref, right_ref, stack_ref, 0, 0)

    def body(block, carry):
        spread(
            lambda row: own_ref[block * DILATION + row],
            left_ref, right_ref, stack_ref, block + 1, (block + 1) * groups,
        )
        return carry

    lax.fori_loop(0, count, body, 0)
    spread(lower_of, left_ref, right_ref, stack_ref, count + 1, (count + 1) * groups)


def forward_kernel(
    scale, own_ref, outer_ref, left_ref, right_ref, cotangent_ref, weight_ref, bias_ref,
    activation_ref, grad_ref, upper_ref, lower_ref, rims_ref, terms_ref, stack_ref, sum_ref,
):
    height, channels, width = own_ref.shape
    count = height // DILATION
    groups = rims_ref.shape[1] // count
    spread_all(
        own_ref, lambda row: outer_ref[0, row], lambda row: outer_ref[1, row], left_ref, right_ref, stack_ref
    )
    terms_ref[...] = jnp.zeros_like(terms_ref)
    sum_ref[...] = jnp.zeros_like(sum_ref)
    depth = 9 * channels

    def store(place, first, last):
        rims_ref[0, place] = first
        rims_ref[1, place] = last

    def body(block, carry):
        start = pl.multiple_of(block * DILATION, DILATION)
        stacked = stack_ref[pl.ds(block, 3)].reshape(depth, DILATION * width)
        preact = jnp.dot(weight_ref[...], stacked, preferred_element_type=jnp.float32)
        cotangent = jnp.swapaxes(cotangent_ref[:, pl.ds(start, DILATION), :], 0, 1)
        bias = jnp.broadcast_to(bias_ref[...], (channels, width))
        values, grads = [], []
        total = sum_ref[...]
        for row in range(DILATION):
            value, slope_val = gelu_pair(preact[:, row * width : (row + 1) * width] + bias)
            values.append(value.astype(jnp.bfloat16))
            grad = (cotangent[row].astype(jnp.float32) * slope_val).astype(jnp.bfloat16)
            grads.append(grad)
            total = total + grad.astype(jnp.float32)
            grad_ref[start + row] = grad
        sum_ref[...] = total
        activation_ref[:, pl.ds(start, DILATION), :] = jnp.swapaxes(jnp.stack(values), 0, 1)
        terms_ref[:, :depth] += lax.dot_general(
            jnp.concatenate(grads, axis=1), stacked, (((1,), (1,)), ((), ())),
            preferred_element_type=jnp.float32,
        )
        pack_rows(grads_stack(grads), store, block * groups)
        return carry

    lax.fori_loop(0, count, body, 0)
    upper_ref[...] = grad_ref[:DILATION]
    lower_ref[...] = grad_ref[height - DILATION :]
    terms_ref[:, :depth] = terms_ref[:, :depth] * scale
    sums = jnp.sum(sum_ref[...], axis=1, keepdims=True) * scale
    terms_ref[:, depth:] = jnp.broadcast_to(sums, (channels, terms_ref.shape[1] - depth))


def grads_stack(grads):
    return jnp.stack(grads)


def backward_kernel(
    own_ref, upper_ref, lower_ref, left_ref, right_ref, weight_ref, out_ref, stack_ref
):
    height, channels, width = own_ref.shape
    spread_all(
        own_ref, lambda row: upper_ref[row], lambda row: lower_ref[row], left_ref, right_ref, stack_ref
    )

    def body(block, carry):
        start = pl.multiple_of(block * DILATION, DILATION)
        stacked = stack_ref[pl.ds(block, 3)].reshape(9 * channels, DILATION * width)
        total = jnp.dot(weight_ref[...], stacked, preferred_element_type=jnp.float32).astype(jnp.bfloat16)
        rows = jnp.stack([total[:, row * width : (row + 1) * width] for row in range(DILATION)])
        out_ref[:, pl.ds(start, DILATION), :] = jnp.swapaxes(rows, 0, 1)
        return carry

    lax.fori_loop(0, height // DILATION, body, 0)


def finish_kernel(one_ref, other_ref, weight_ref, bias_ref):
    total = one_ref[...] + other_ref[...]
    channels = total.shape[0]
    for tap in range(9):
        weight_ref[tap // 3, tap % 3] = total[:, tap * channels : (tap + 1) * channels]
    flipped = jnp.transpose(total[:, total.shape[1] - 128 :])
    bias_ref[...] = flipped[127:128, :channels]


def call(kernel, out_shapes, operands, scratch=(), flops=0):
    size = sum(math.prod(x.shape) * jnp.dtype(x.dtype).itemsize for x in (*operands, *out_shapes))
    return pl.pallas_call(
        kernel,
        out_shape=out_shapes,
        scratch_shapes=list(scratch),
        compiler_params=pltpu.CompilerParams(vmem_limit_bytes=VMEM_BYTES),
        cost_estimate=pl.CostEstimate(flops=flops, bytes_accessed=size, transcendentals=0),
    )(*operands)


def shards(image, weight, bias, cotangent):
    channels, height, width = image.shape
    bf16, f32 = jnp.bfloat16, jnp.float32
    scale = 1.0 / math.sqrt(height * lax.axis_size("row") * width * lax.axis_size("col"))
    shape = jax.ShapeDtypeStruct
    pieces = width // DILATION
    own_groups, all_groups = height // pieces, (height + 2 * DILATION) // pieces
    depth = 9 * channels
    stack = pltpu.VMEM((height // DILATION + 2, 3 * channels, DILATION * width), bf16)
    edge = shape((DILATION, channels, width), bf16)
    packed = shape((all_groups, channels, width), bf16)
    own_rims = shape((2, own_groups, channels, width), bf16)
    rows = shape((height, channels, width), bf16)
    flops = 2 * depth * channels * height * width

    upper = from_behind(image[:, height - DILATION :, :], "row", 1)
    lower = from_behind(image[:, :DILATION, :], "row", -1)
    image_rows, rims = call(own_kernel, (rows, own_rims), (image,))
    forward_weight = jnp.transpose(weight, (2, 0, 1, 3)).reshape(channels, depth)
    backward_weight = jnp.transpose(weight[::-1, ::-1], (3, 0, 1, 2)).reshape(channels, depth)
    first, last, outer = call(
        functools.partial(rim_kernel, True),
        (packed, packed, shape((2, DILATION, channels, width), bf16)),
        (upper, lower, rims),
    )
    left = from_behind(last, "col", 1)
    right = from_behind(first, "col", -1)
    activation, grads, top, bottom, rims, terms = call(
        functools.partial(forward_kernel, scale),
        (
            shape(image.shape, bf16), rows, edge, edge, own_rims,
            shape((channels, -(-(depth + 1) // 128) * 128), f32),
        ),
        (image_rows, outer, left, right, cotangent, forward_weight, bias[:, None]),
        (stack, pltpu.VMEM((channels, width), f32)),
        2 * flops,
    )
    upper = from_behind(bottom, "row", 1)
    lower = from_behind(top, "row", -1)
    first, last = call(functools.partial(rim_kernel, False), (packed, packed), (upper, lower, rims))
    left = from_behind(last, "col", 1)
    right = from_behind(first, "col", -1)
    (grad_image,) = call(
        backward_kernel,
        (shape(image.shape, bf16),),
        (grads, upper, lower, left, right, backward_weight),
        (stack,),
        flops,
    )
    one, other = add_pairs(terms, ("col", "row"))
    grad_weight, grad_bias = call(
        finish_kernel, (shape(weight.shape, f32), shape((1, channels), f32)), (one, other)
    )
    return (activation, grad_image, grad_weight, grad_bias.reshape(channels))


def solution(mesh):
    return jax.shard_map(
        shards,
        mesh=mesh,
        in_specs=(P(None, "row", "col"), P(), P(), P(None, "row", "col")),
        out_specs=(P(None, "row", "col"), P(None, "row", "col"), P(), P()),
        check_vma=False,
    )
```

time: 107 us -> 55.5 us (0.52)
  blocking collectives: 47.1 us -> 0 us
  local copies, waits for them, and re-layouts: 18.2 us -> 2.06 us
  Pallas kernels: 0 us -> 10.3 us
  starting transfers between devices: 20.3 us -> 27.7 us
  matrix products: 5.81 us -> 0 us
  other arithmetic: 3.41 us -> 0.03 us
  waiting for transfers between devices: 10.8 us -> 14.1 us
    psum x1 -> x0, blocking collectives: 47.1 us -> none  [shards(): lax.psum((local_weight, local_bias), ('row', 'col'))]
    ppermute x0 -> x5, starting transfers between devices: none -> 10.6 us  [add_pairs(): lax.ppermute(value, axis, [(place, place ^ step) for place in range(count)])]
    pallas_call x0 -> x6, Pallas kernels: none -> 10.3 us  [call(): pl.pallas_call(kernel, out_shape=out_shapes, scratch_shapes=list(scratch)...]
    ppermute x0 -> x5, waiting for transfers between devices: none -> 6.69 us  [add_pairs(): lax.ppermute(value, axis, [(place, place ^ step) for place in range(count)])]
    unnamed x32 -> x8, local copies, waits for them, and re-layouts: 6.49 us -> 0.66 us
    dot_general x9 -> x0, matrix products: 5.81 us -> none  [the longest x3 2.79 us: shards(): jnp.einsum('ok,krq->orq', weight_row, stacked, preferred_element_type=jnp...]
    slice x10 -> x1, local copies, waits for them, and re-layouts: 6.06 us -> 1.05 us  [shards(): lower = from_behind(image[:, :DILATION, :], 'row', -1)]
    ppermute x4 -> x0, local copies, waits for them, and re-layouts: 4.41 us -> none  [from_behind(): lax.ppermute(value, axis, [(source, source + steps) for source in range(i...]
  transfers between devices with their start and end apart: 8 -> 13, of which waited for: 4 -> 5; matrix products, arithmetic and copies ran while one was open for 6% -> 1% of each run, Pallas kernels for 0% -> 8%
where the time goes in v1:
time: 55.5 us; the launch traced here: 55.1 us
  starting transfers between devices  27.7 us (50%)
  waiting for transfers between devices  14.1 us (25%)
  Pallas kernels  10.3 us (19%)
  local copies, waits for them, and re-layouts  2.06 us (4%)
  between operations  0.85 us (2%)
    ppermute x8, starting transfers between devices, from_behind(): lax.ppermute(value, axis, [(source, source + steps) for source in range(i...  17.1 us
    ppermute x5, starting transfers between devices, add_pairs(): lax.ppermute(value, axis, [(place, place ^ step) for place in range(count)])  10.6 us
    pallas_call x6, Pallas kernels, call(): pl.pallas_call(kernel, out_shape=out_shapes, scratch_shapes=list(scratch)...  10.3 us
    ppermute x8, waiting for transfers between devices, from_behind(): lax.ppermute(value, axis, [(source, source + steps) for source in range(i...  7.45 us
    ppermute x5, waiting for transfers between devices, add_pairs(): lax.ppermute(value, axis, [(place, place ^ step) for place in range(count)])  6.69 us
  transfers between devices with their start and end apart: 13, of which 5 were waited for; matrix products, arithmetic and copies ran while one was open for 1% of the time, Pallas kernels for 8%

profile of v1, /device:TPU:0, one launch (start us, length us, event | category | flops | bytes accessed | tf_op | source)
XLA Modules:
  0.0 55.1 jit_solution(7424699943932028821)
XLA Ops:
  0.6 0.0 copy-start
  0.6 1.1 %fusion = (bf16[32,16,128]{2,1,0:T(8,128)(2,1)S(1)}, bf16[32,16,128]{2,1,0:T(8,128)(2,1)S(1)}) fusion(bf16[32,64,128]{2,1,0:T(8,128)(2,1)} %image_ref.1), kind=kLoop, calls=%fused_computation | loop fusion | bytes 524288 | tf_op jit(solution)/shard_map/slice | solution.py:261
  1.7 4.9 %collective-permute-start = (bf16[32,16,128]{2,1,0:T(8,128)(2,1)S(1)}, bf16[32,16,128]{2,1,0:T(8,128)(2,1)S(1)}, u32[]{:S(2)}, u32[]{:S(2)}) collective-permute-start(bf16[32,16,128]{2,1,0:T(8,128)(2,1)S(1)} %get-tuple-element.35), channel_id=1, source_target_pairs={{0,4},{4,8},{8,12},{12,16},{16,20},{20,24},{24,28},{1,5},{5,9},{9,... | collective-permute-start | bytes 393224 | tf_op jit(solution)/shard_map/ppermute | solution.py:18
  6.6 0.0 copy-start.1
  6.6 1.4 %collective-permute-start.1 = (bf16[32,16,128]{2,1,0:T(8,128)(2,1)S(1)}, bf16[32,16,128]{2,1,0:T(8,128)(2,1)S(1)}, u32[]{:S(2)}, u32[]{:S(2)}) collective-permute-start(bf16[32,16,128]{2,1,0:T(8,128)(2,1)S(1)} %get-tuple-element.34), channel_id=1, source_target_pairs={{4,0},{8,4},{12,8},{16,12},{20,16},{24,20},{28,24},{5,1},{9,5},{13... | collective-permute-start | bytes 393224 | tf_op jit(solution)/shard_map/ppermute | solution.py:18
  8.0 0.0 copy-done
  8.0 0.8 %shard_map.75 = (bf16[64,32,128]{2,1,0:T(8,128)(2,1)S(1)}, bf16[2,8,32,128]{3,2,1,0:T(8,128)(2,1)S(1)}) custom-call(bf16[32,64,128]{2,1,0:T(8,128)(2,1)S(1)} %copy-done), custom_call_target="tpu_custom_call" | custom-call | bytes 1179648 | tf_op jit(solution)/shard_map/pallas_call | solution.py:236
  8.8 0.5 collective-permute-done.upper_ref
  9.3 4.3 %collective-permute-done.1.lower_ref = bf16[32,16,128]{2,1,0:T(8,128)(2,1)S(1)} collective-permute-done((bf16[32,16,128]{2,1,0:T(8,128)(2,1)S(1)}, bf16[32,16,128]{2,1,0:T(8,128)(2,1)S(1)}, u32[]{:S(2)}, u32[]{:S(2)}) %collective-permute-start.1) | collective-permute-done | bytes 131104 | tf_op jit(solution)/shard_map/ppermute | solution.py:18
  13.6 0.0 copy-start.2
  13.6 0.2 shard_map.76
  13.8 1.3 %collective-permute-start.2 = (bf16[12,32,128]{2,1,0:T(8,128)(2,1)S(1)}, bf16[12,32,128]{2,1,0:T(8,128)(2,1)S(1)}, u32[]{:S(2)}, u32[]{:S(2)}) collective-permute-start(bf16[12,32,128]{2,1,0:T(8,128)(2,1)S(1)} %get-tuple-element.22), channel_id=1, source_target_pairs={{0,1},{1,2},{2,3},{4,5},{5,6},{6,7},{8,9},{9,10},{10,11},{12,13},{... | collective-permute-start | bytes 294920 | tf_op jit(solution)/shard_map/ppermute | solution.py:18
  15.1 1.3 %collective-permute-start.3 = (bf16[12,32,128]{2,1,0:T(8,128)(2,1)S(1)}, bf16[12,32,128]{2,1,0:T(8,128)(2,1)S(1)}, u32[]{:S(2)}, u32[]{:S(2)}) collective-permute-start(bf16[12,32,128]{2,1,0:T(8,128)(2,1)S(1)} %get-tuple-element.23), channel_id=1, source_target_pairs={{1,0},{2,1},{3,2},{5,4},{6,5},{7,6},{9,8},{10,9},{11,10},{13,12},{... | collective-permute-start | bytes 294920 | tf_op jit(solution)/shard_map/ppermute | solution.py:18
  16.4 0.0 copy-done.2
  16.4 0.1 copy.11
  16.5 0.1 reshape.17.weight_ref
  16.6 0.0 copy-start.3
  16.6 0.6 %copy-done.3 = f32[32]{0:T(128)S(1)} copy-done((f32[32]{0:T(128)S(1)}, f32[32]{0:T(128)}, u32[]{:S(2)}) %copy-start.3) | copy-done | bytes 152
  17.3 0.1 copy.12.bias_ref
  17.3 0.0 collective-permute-done.2.left_ref
  17.3 2.7 %collective-permute-done.3.right_ref = bf16[12,32,128]{2,1,0:T(8,128)(2,1)S(1)} collective-permute-done((bf16[12,32,128]{2,1,0:T(8,128)(2,1)S(1)}, bf16[12,32,128]{2,1,0:T(8,128)(2,1)S(1)}, u32[]{:S(2)}, u32[]{:S(2)}) %collective-permute-start.3) | collective-permute-done | bytes 98336 | tf_op jit(solution)/shard_map/ppermute | solution.py:18
  20.0 0.0 copy-done.1
  20.0 4.8 %shard_map.77 = (bf16[32,64,128]{2,1,0:T(8,128)(2,1)}, bf16[64,32,128]{2,1,0:T(8,128)(2,1)S(1)}, bf16[16,32,128]{2,1,0:T(8,128)(2,1)S(1)}, bf16[16,32,128]{2,1,0...) custom-call(bf16[64,32,128]{2,1,0:T(8,128)(2,1)S(1)} %get-tuple-element.19.own_ref, ...), custom_call_target="tpu_custom_call" | custom-call | flops 301989888 | bytes 3016832 | tf_op jit(solution)/shard_map/pallas_call | solution.py:236
  24.8 3.2 %collective-permute-start.8 = (f32[32,384]{1,0:T(8,128)S(1)}, f32[32,384]{1,0:T(8,128)S(1)}, u32[]{:S(2)}, u32[]{:S(2)}) collective-permute-start(f32[32,384]{1,0:T(8,128)S(1)} %get-tuple-element.31), channel_id=1, source_target_pairs={{0,1},{1,0},{2,3},{3,2},{4,5},{5,4},{6,7},{7,6},{8,9},{9,8},{10,11... | collective-permute-start | bytes 147464 | tf_op jit(solution)/shard_map/ppermute | solution.py:28
  28.1 4.3 %collective-permute-start.4 = (bf16[16,32,128]{2,1,0:T(8,128)(2,1)S(1)}, bf16[16,32,128]{2,1,0:T(8,128)(2,1)S(1)}, u32[]{:S(2)}, u32[]{:S(2)}) collective-permute-start(bf16[16,32,128]{2,1,0:T(8,128)(2,1)S(1)} %get-tuple-element.26), channel_id=1, source_target_pairs={{0,4},{4,8},{8,12},{12,16},{16,20},{20,24},{24,28},{1,5},{5,9},{9,... | collective-permute-start | bytes 393224 | tf_op jit(solution)/shard_map/ppermute | solution.py:18
  32.4 1.3 %collective-permute-start.5 = (bf16[16,32,128]{2,1,0:T(8,128)(2,1)S(1)}, bf16[16,32,128]{2,1,0:T(8,128)(2,1)S(1)}, u32[]{:S(2)}, u32[]{:S(2)}) collective-permute-start(bf16[16,32,128]{2,1,0:T(8,128)(2,1)S(1)} %get-tuple-element.27), channel_id=1, source_target_pairs={{4,0},{8,4},{12,8},{16,12},{20,16},{24,20},{28,24},{5,1},{9,5},{13... | collective-permute-start | bytes 393224 | tf_op jit(solution)/shard_map/ppermute | solution.py:18
  33.7 0.0 collective-permute-done.8
  33.7 0.1 collective-permute-start.9
  33.8 4.1 %collective-permute-done.9 = f32[32,384]{1,0:T(8,128)S(1)} collective-permute-done((f32[32,384]{1,0:T(8,128)S(1)}, f32[32,384]{1,0:T(8,128)S(1)}, u32[]{:S(2)}, u32[]{:S(2)}) %collective-permute-start.9) | collective-permute-done | bytes 49184 | tf_op jit(solution)/shard_map/ppermute | solution.py:28
  37.9 2.7 %collective-permute-start.10 = (f32[32,384]{1,0:T(8,128)S(1)}, f32[32,384]{1,0:T(8,128)S(1)}, u32[]{:S(2)}, u32[]{:S(2)}) collective-permute-start(f32[32,384]{1,0:T(8,128)S(1)} %add.13), channel_id=1, source_target_pairs={{0,4},{4,0},{8,12},{12,8},{16,20},{20,16},{24,28},{28,24},{1,5},{5... | collective-permute-start | bytes 147464 | tf_op jit(solution)/shard_map/ppermute | solution.py:28
  40.6 0.0 collective-permute-done.4.upper_ref
  40.6 0.0 collective-permute-done.5.lower_ref
  40.6 0.2 shard_map.78
  40.8 1.3 %collective-permute-start.6 = (bf16[12,32,128]{2,1,0:T(8,128)(2,1)S(1)}, bf16[12,32,128]{2,1,0:T(8,128)(2,1)S(1)}, u32[]{:S(2)}, u32[]{:S(2)}) collective-permute-start(bf16[12,32,128]{2,1,0:T(8,128)(2,1)S(1)} %get-tuple-element.29), channel_id=1, source_target_pairs={{0,1},{1,2},{2,3},{4,5},{5,6},{6,7},{8,9},{9,10},{10,11},{12,13},{... | collective-permute-start | bytes 294920 | tf_op jit(solution)/shard_map/ppermute | solution.py:18
  42.1 1.3 %collective-permute-start.7 = (bf16[12,32,128]{2,1,0:T(8,128)(2,1)S(1)}, bf16[12,32,128]{2,1,0:T(8,128)(2,1)S(1)}, u32[]{:S(2)}, u32[]{:S(2)}) collective-permute-start(bf16[12,32,128]{2,1,0:T(8,128)(2,1)S(1)} %get-tuple-element.30), channel_id=1, source_target_pairs={{1,0},{2,1},{3,2},{5,4},{6,5},{7,6},{9,8},{10,9},{11,10},{13,12},{... | collective-permute-start | bytes 294920 | tf_op jit(solution)/shard_map/ppermute | solution.py:18
  43.4 0.0 collective-permute-done.10
  43.4 1.8 %collective-permute-start.11 = (f32[32,384]{1,0:T(8,128)S(1)}, f32[32,384]{1,0:T(8,128)S(1)}, u32[]{:S(2)}, u32[]{:S(2)}) collective-permute-start(f32[32,384]{1,0:T(8,128)S(1)} %add.14), channel_id=1, source_target_pairs={{0,8},{4,12},{8,0},{12,4},{16,24},{20,28},{24,16},{28,20},{1,9},{5... | collective-permute-start | bytes 147464 | tf_op jit(solution)/shard_map/ppermute | solution.py:28
  45.2 2.6 %collective-permute-done.11 = f32[32,384]{1,0:T(8,128)S(1)} collective-permute-done((f32[32,384]{1,0:T(8,128)S(1)}, f32[32,384]{1,0:T(8,128)S(1)}, u32[]{:S(2)}, u32[]{:S(2)}) %collective-permute-start.11) | collective-permute-done | bytes 49184 | tf_op jit(solution)/shard_map/ppermute | solution.py:28
  47.8 2.8 %collective-permute-start.12 = (f32[32,384]{1,0:T(8,128)S(1)}, f32[32,384]{1,0:T(8,128)S(1)}, u32[]{:S(2)}, u32[]{:S(2)}) collective-permute-start(f32[32,384]{1,0:T(8,128)S(1)} %add.15.one_ref), channel_id=1, source_target_pairs={{0,16},{4,20},{8,24},{12,28},{16,0},{20,4},{24,8},{28,12},{1,17},{... | collective-permute-start | bytes 147464 | tf_op jit(solution)/shard_map/ppermute | solution.py:28
  50.7 0.1 copy.14.weight_ref
  50.8 0.0 collective-permute-done.6.left_ref
  50.8 0.0 collective-permute-done.7.right_ref
  50.8 3.6 %shard_map.79 = bf16[32,64,128]{2,1,0:T(8,128)(2,1)} custom-call(bf16[64,32,128]{2,1,0:T(8,128)(2,1)S(1)} %get-tuple-element.25.own_ref, bf16[16,32,128]{2,1,0:T(8,128)(2,1)S(1)} %collective-permute-done.4.upper_ref, bf16[16,32,128]{2,1,0:T(8,128)(2,1)S(1)} %collective-permute-done.5.lower_ref, bf16[12,32,128]{2,1,0:T(8,128)(2,1)S(1)} %collective-permute-done.6.left_ref, ...), custom_call_target="tpu_custom_call" | custom-call | flops 150994944 | bytes 1525760 | tf_op jit(solution)/shard_map/pallas_call | solution.py:236
  54.4 0.0 collective-permute-done.12.other_ref
  54.4 0.8 %shard_map.80 = (f32[3,3,32,32]{3,2,1,0:T(8,128)}, f32[1,32]{1,0:T(1,128)}) custom-call(f32[32,384]{1,0:T(8,128)S(1)} %add.15.one_ref, f32[32,384]{1,0:T(8,128)S(1)} %collective-permute-done.12.other_ref), custom_call_target="tpu_custom_call" | custom-call | bytes 135296 | tf_op jit(solution)/shard_map/pallas_call | solution.py:236
  (5 shorter events, 0.0 us)
Async XLA Ops:
  0.6 7.4 %copy-start = (bf16[32,64,128]{2,1,0:T(8,128)(2,1)S(1)}, bf16[32,64,128]{2,1,0:T(8,128)(2,1)}, u32[]{:S(2)}) copy-start(bf16[32,64,128]{2,1,0:T(8,128)(2,1)} %image_ref.1) | copy-start | bytes 1572868
  1.7 7.6 %collective-permute-start = (bf16[32,16,128]{2,1,0:T(8,128)(2,1)S(1)}, bf16[32,16,128]{2,1,0:T(8,128)(2,1)S(1)}, u32[]{:S(2)}, u32[]{:S(2)}) collective-permute-start(bf16[32,16,128]{2,1,0:T(8,128)(2,1)S(1)} %get-tuple-element.35), channel_id=1, source_target_pairs={{0,4},{4,8},{8,12},{12,16},{16,20},{20,24},{24,28},{1,5},{5,9},{9,... | collective-permute-start | bytes 393224 | tf_op jit(solution)/shard_map/ppermute | solution.py:18
  6.6 13.5 %copy-start.1 = (bf16[32,64,128]{2,1,0:T(8,128)(2,1)S(1)}, bf16[32,64,128]{2,1,0:T(8,128)(2,1)}, u32[]{:S(2)}) copy-start(bf16[32,64,128]{2,1,0:T(8,128)(2,1)} %cotangent_ref.1) | copy-start | bytes 1572868
  6.6 7.0 %collective-permute-start.1 = (bf16[32,16,128]{2,1,0:T(8,128)(2,1)S(1)}, bf16[32,16,128]{2,1,0:T(8,128)(2,1)S(1)}, u32[]{:S(2)}, u32[]{:S(2)}) collective-permute-start(bf16[32,16,128]{2,1,0:T(8,128)(2,1)S(1)} %get-tuple-element.34), channel_id=1, source_target_pairs={{4,0},{8,4},{12,8},{16,12},{20,16},{24,20},{28,24},{5,1},{9,5},{13... | collective-permute-start | bytes 393224 | tf_op jit(solution)/shard_map/ppermute | solution.py:18
  13.6 2.8 %copy-start.2 = (bf16[3,3,32,32]{3,2,1,0:T(8,128)(2,1)S(1)}, bf16[3,3,32,32]{3,2,1,0:T(8,128)(2,1)}, u32[]{:S(2)}) copy-start(bf16[3,3,32,32]{3,2,1,0:T(8,128)(2,1)} %param.5) | copy-start | bytes 55300
  13.8 3.5 %collective-permute-start.2 = (bf16[12,32,128]{2,1,0:T(8,128)(2,1)S(1)}, bf16[12,32,128]{2,1,0:T(8,128)(2,1)S(1)}, u32[]{:S(2)}, u32[]{:S(2)}) collective-permute-start(bf16[12,32,128]{2,1,0:T(8,128)(2,1)S(1)} %get-tuple-element.22), channel_id=1, source_target_pairs={{0,1},{1,2},{2,3},{4,5},{5,6},{6,7},{8,9},{9,10},{10,11},{12,13},{... | collective-permute-start | bytes 294920 | tf_op jit(solution)/shard_map/ppermute | solution.py:18
  15.1 4.9 %collective-permute-start.3 = (bf16[12,32,128]{2,1,0:T(8,128)(2,1)S(1)}, bf16[12,32,128]{2,1,0:T(8,128)(2,1)S(1)}, u32[]{:S(2)}, u32[]{:S(2)}) collective-permute-start(bf16[12,32,128]{2,1,0:T(8,128)(2,1)S(1)} %get-tuple-element.23), channel_id=1, source_target_pairs={{1,0},{2,1},{3,2},{5,4},{6,5},{7,6},{9,8},{10,9},{11,10},{13,12},{... | collective-permute-start | bytes 294920 | tf_op jit(solution)/shard_map/ppermute | solution.py:18
  16.6 0.7 %copy-start.3 = (f32[32]{0:T(128)S(1)}, f32[32]{0:T(128)}, u32[]{:S(2)}) copy-start(f32[32]{0:T(128)} %param.6) | copy-start | bytes 388
  24.8 8.9 %collective-permute-start.8 = (f32[32,384]{1,0:T(8,128)S(1)}, f32[32,384]{1,0:T(8,128)S(1)}, u32[]{:S(2)}, u32[]{:S(2)}) collective-permute-start(f32[32,384]{1,0:T(8,128)S(1)} %get-tuple-element.31), channel_id=1, source_target_pairs={{0,1},{1,0},{2,3},{3,2},{4,5},{5,4},{6,7},{7,6},{8,9},{9,8},{10,11... | collective-permute-start | bytes 147464 | tf_op jit(solution)/shard_map/ppermute | solution.py:28
  28.1 12.5 %collective-permute-start.4 = (bf16[16,32,128]{2,1,0:T(8,128)(2,1)S(1)}, bf16[16,32,128]{2,1,0:T(8,128)(2,1)S(1)}, u32[]{:S(2)}, u32[]{:S(2)}) collective-permute-start(bf16[16,32,128]{2,1,0:T(8,128)(2,1)S(1)} %get-tuple-element.26), channel_id=1, source_target_pairs={{0,4},{4,8},{8,12},{12,16},{16,20},{20,24},{24,28},{1,5},{5,9},{9,... | collective-permute-start | bytes 393224 | tf_op jit(solution)/shard_map/ppermute | solution.py:18
  32.4 8.2 %collective-permute-start.5 = (bf16[16,32,128]{2,1,0:T(8,128)(2,1)S(1)}, bf16[16,32,128]{2,1,0:T(8,128)(2,1)S(1)}, u32[]{:S(2)}, u32[]{:S(2)}) collective-permute-start(bf16[16,32,128]{2,1,0:T(8,128)(2,1)S(1)} %get-tuple-element.27), channel_id=1, source_target_pairs={{4,0},{8,4},{12,8},{16,12},{20,16},{24,20},{28,24},{5,1},{9,5},{13... | collective-permute-start | bytes 393224 | tf_op jit(solution)/shard_map/ppermute | solution.py:18
  33.7 4.2 %collective-permute-start.9 = (f32[32,384]{1,0:T(8,128)S(1)}, f32[32,384]{1,0:T(8,128)S(1)}, u32[]{:S(2)}, u32[]{:S(2)}) collective-permute-start(f32[32,384]{1,0:T(8,128)S(1)} %add.12), channel_id=1, source_target_pairs={{0,2},{1,3},{2,0},{3,1},{4,6},{5,7},{6,4},{7,5},{8,10},{9,11},{10,... | collective-permute-start | bytes 147464 | tf_op jit(solution)/shard_map/ppermute | solution.py:28
  37.9 5.5 %collective-permute-start.10 = (f32[32,384]{1,0:T(8,128)S(1)}, f32[32,384]{1,0:T(8,128)S(1)}, u32[]{:S(2)}, u32[]{:S(2)}) collective-permute-start(f32[32,384]{1,0:T(8,128)S(1)} %add.13), channel_id=1, source_target_pairs={{0,4},{4,0},{8,12},{12,8},{16,20},{20,16},{24,28},{28,24},{1,5},{5... | collective-permute-start | bytes 147464 | tf_op jit(solution)/shard_map/ppermute | solution.py:28
  40.8 10.0 %collective-permute-start.6 = (bf16[12,32,128]{2,1,0:T(8,128)(2,1)S(1)}, bf16[12,32,128]{2,1,0:T(8,128)(2,1)S(1)}, u32[]{:S(2)}, u32[]{:S(2)}) collective-permute-start(bf16[12,32,128]{2,1,0:T(8,128)(2,1)S(1)} %get-tuple-element.29), channel_id=1, source_target_pairs={{0,1},{1,2},{2,3},{4,5},{5,6},{6,7},{8,9},{9,10},{10,11},{12,13},{... | collective-permute-start | bytes 294920 | tf_op jit(solution)/shard_map/ppermute | solution.py:18
  42.1 8.7 %collective-permute-start.7 = (bf16[12,32,128]{2,1,0:T(8,128)(2,1)S(1)}, bf16[12,32,128]{2,1,0:T(8,128)(2,1)S(1)}, u32[]{:S(2)}, u32[]{:S(2)}) collective-permute-start(bf16[12,32,128]{2,1,0:T(8,128)(2,1)S(1)} %get-tuple-element.30), channel_id=1, source_target_pairs={{1,0},{2,1},{3,2},{5,4},{6,5},{7,6},{9,8},{10,9},{11,10},{13,12},{... | collective-permute-start | bytes 294920 | tf_op jit(solution)/shard_map/ppermute | solution.py:18
  43.4 4.4 %collective-permute-start.11 = (f32[32,384]{1,0:T(8,128)S(1)}, f32[32,384]{1,0:T(8,128)S(1)}, u32[]{:S(2)}, u32[]{:S(2)}) collective-permute-start(f32[32,384]{1,0:T(8,128)S(1)} %add.14), channel_id=1, source_target_pairs={{0,8},{4,12},{8,0},{12,4},{16,24},{20,28},{24,16},{28,20},{1,9},{5... | collective-permute-start | bytes 147464 | tf_op jit(solution)/shard_map/ppermute | solution.py:28
  47.8 6.6 %collective-permute-start.12 = (f32[32,384]{1,0:T(8,128)S(1)}, f32[32,384]{1,0:T(8,128)S(1)}, u32[]{:S(2)}, u32[]{:S(2)}) collective-permute-start(f32[32,384]{1,0:T(8,128)S(1)} %add.15.one_ref), channel_id=1, source_target_pairs={{0,16},{4,20},{8,24},{12,28},{16,0},{20,4},{24,8},{28,12},{1,17},{... | collective-permute-start | bytes 147464 | tf_op jit(solution)/shard_map/ppermute | solution.py:28

commit v2 on v1

--- a/solution.py
+++ b/solution.py
@@ -12,10 +12,11 @@
 VMEM_BYTES = 16 * 2**20
 
 
-def from_behind(value, axis, steps):
-    count = lax.axis_size(axis)
-    initial, last = (max(0, -steps), min(count, count - steps))
-    return lax.ppermute(value, axis, [(source, source + steps) for source in range(initial, last)])
+def swap_pairs(value, axis, first):
+    pairs = []
+    for place in range(first, lax.axis_size(axis) - 1, 2):
+        pairs += [(place, place + 1), (place + 1, place)]
+    return lax.ppermute(value, axis, pairs)
 
 
 def add_pairs(value, axes):
@@ -99,29 +100,31 @@
     lax.fori_loop(0, count, body, 0)
 
 
-def rim_kernel(swap, upper_ref, lower_ref, rims_ref, first_ref, last_ref, *rows_refs):
+def rim_kernel(swap, odd_ref, one_ref, two_ref, rims_ref, send_one_ref, send_two_ref, outer_ref):
     own = rims_ref.shape[1]
-    groups = (first_ref.shape[0] - own) // 2
-    first_ref[groups : groups + own] = rims_ref[0]
-    last_ref[groups : groups + own] = rims_ref[1]
+    groups = (send_one_ref.shape[0] - own) // 2
+    odd_row, odd_column = odd_ref[0] == 1, odd_ref[1] == 1
+    send_one_ref[groups : groups + own] = rims_ref[1 - odd_ref[1]]
+    send_two_ref[groups : groups + own] = rims_ref[odd_ref[1]]
 
     def store(place, first, last):
-        first_ref[place] = first
-        last_ref[place] = last
-
-    for index, ref in enumerate((upper_ref, lower_ref)):
-        rows = jnp.swapaxes(ref[...], 0, 1) if swap else ref[...]
-        if swap:
-            rows_refs[0][index] = rows
+        send_one_ref[place] = jnp.where(odd_column, first, last)
+        send_two_ref[place] = jnp.where(odd_column, last, first)
+
+    one, two = one_ref[...], two_ref[...]
+    for index, rows in enumerate((jnp.where(odd_row, one, two), jnp.where(odd_row, two, one))):
+        rows = jnp.swapaxes(rows, 0, 1) if swap else rows
+        outer_ref[index] = rows
         pack_rows(rows, store, index * (groups + own))
 
 
-def spread(rows_of, left_ref, right_ref, stack_ref, block, group_start):
-    channels, width = left_ref.shape[1:]
+def spread(rows_of, odd, one_ref, two_ref, stack_ref, block, group_start):
+    channels, width = one_ref.shape[1:]
     pieces = width // DILATION
     lane = lane_of((channels, width))
     for group in range(DILATION // pieces):
-        rims = unpack_group(left_ref[group_start + group], right_ref[group_start + group], pieces)
+        one, two = one_ref[group_start + group], two_ref[group_start + group]
+        rims = unpack_group(jnp.where(odd, one, two), jnp.where(odd, two, one), pieces)
         for k in range(pieces):
             row = group * pieces + k
             value = rows_of(row)
@@ -133,32 +136,31 @@
             stack_ref[block, 2 * channels : 3 * channels, columns] = after
 
 
-def spread_all(own_ref, upper_of, lower_of, left_ref, right_ref, stack_ref):
+def spread_all(odd_ref, own_ref, outer_ref, one_ref, two_ref, stack_ref):
     count = own_ref.shape[0] // DILATION
-    groups = left_ref.shape[0] // (count + 2)
-    spread(upper_of, left_ref, right_ref, stack_ref, 0, 0)
+    groups = one_ref.shape[0] // (count + 2)
+    odd = odd_ref[1] == 1
+    spread(lambda row: outer_ref[0, row], odd, one_ref, two_ref, stack_ref, 0, 0)
 
     def body(block, carry):
         spread(
             lambda row: own_ref[block * DILATION + row],
-            left_ref, right_ref, stack_ref, block + 1, (block + 1) * groups,
+            odd, one_ref, two_ref, stack_ref, block + 1, (block + 1) * groups,
         )
         return carry
 
     lax.fori_loop(0, count, body, 0)
-    spread(lower_of, left_ref, right_ref, stack_ref, count + 1, (count + 1) * groups)
+    spread(lambda row: outer_ref[1, row], odd, one_ref, two_ref, stack_ref, count + 1, (count + 1) * groups)
 
 
 def forward_kernel(
-    scale, own_ref, outer_ref, left_ref, right_ref, cotangent_ref, weight_ref, bias_ref,
-    activation_ref, grad_ref, upper_ref, lower_ref, rims_ref, terms_ref, stack_ref, sum_ref,
+    scale, odd_ref, own_ref, outer_ref, one_ref, two_ref, cotangent_ref, weight_ref, bias_ref,
+    activation_ref, grad_ref, send_one_ref, send_two_ref, rims_ref, terms_ref, stack_ref, sum_ref,
 ):
     height, channels, width = own_ref.shape
     count = height // DILATION
     groups = rims_ref.shape[1] // count
-    spread_all(
-        own_ref, lambda row: outer_ref[0, row], lambda row: outer_ref[1, row], left_ref, right_ref, stack_ref
-    )
+    spread_all(odd_ref, own_ref, outer_ref, one_ref, two_ref, stack_ref)
     terms_ref[...] = jnp.zeros_like(terms_ref)
     sum_ref[...] = jnp.zeros_like(sum_ref)
     depth = 9 * channels
@@ -188,28 +190,23 @@
             jnp.concatenate(grads, axis=1), stacked, (((1,), (1,)), ((), ())),
             preferred_element_type=jnp.float32,
         )
-        pack_rows(grads_stack(grads), store, block * groups)
+        pack_rows(jnp.stack(grads), store, block * groups)
         return carry
 
     lax.fori_loop(0, count, body, 0)
-    upper_ref[...] = grad_ref[:DILATION]
-    lower_ref[...] = grad_ref[height - DILATION :]
+    end = height - DILATION
+    send_one_ref[...] = grad_ref[pl.ds((1 - odd_ref[0]) * end, DILATION)]
+    send_two_ref[...] = grad_ref[pl.ds(odd_ref[0] * end, DILATION)]
     terms_ref[:, :depth] = terms_ref[:, :depth] * scale
     sums = jnp.sum(sum_ref[...], axis=1, keepdims=True) * scale
     terms_ref[:, depth:] = jnp.broadcast_to(sums, (channels, terms_ref.shape[1] - depth))
 
 
-def grads_stack(grads):
-    return jnp.stack(grads)
-
-
 def backward_kernel(
-    own_ref, upper_ref, lower_ref, left_ref, right_ref, weight_ref, out_ref, stack_ref
+    odd_ref, own_ref, outer_ref, one_ref, two_ref, weight_ref, out_ref, stack_ref
 ):
     height, channels, width = own_ref.shape
-    spread_all(
-        own_ref, lambda row: upper_ref[row], lambda row: lower_ref[row], left_ref, right_ref, stack_ref
-    )
+    spread_all(odd_ref, own_ref, outer_ref, one_ref, two_ref, stack_ref)
 
     def body(block, carry):
         start = pl.multiple_of(block * DILATION, DILATION)
@@ -231,11 +228,14 @@
     bias_ref[...] = flipped[127:128, :channels]
 
 
-def call(kernel, out_shapes, operands, scratch=(), flops=0):
+def call(kernel, out_shapes, operands, scratch=(), flops=0, scalars=0):
+    whole = pl.BlockSpec(memory_space=pltpu.VMEM)
     size = sum(math.prod(x.shape) * jnp.dtype(x.dtype).itemsize for x in (*operands, *out_shapes))
     return pl.pallas_call(
         kernel,
         out_shape=out_shapes,
+        in_specs=[pl.BlockSpec(memory_space=pltpu.SMEM)] * scalars + [whole] * (len(operands) - scalars),
+        out_specs=[whole] * len(out_shapes),
         scratch_shapes=list(scratch),
         compiler_params=pltpu.CompilerParams(vmem_limit_bytes=VMEM_BYTES),
         cost_estimate=pl.CostEstimate(flops=flops, bytes_accessed=size, transcendentals=0),
@@ -257,39 +257,43 @@
     rows = shape((height, channels, width), bf16)
     flops = 2 * depth * channels * height * width
 
-    upper = from_behind(image[:, height - DILATION :, :], "row", 1)
-    lower = from_behind(image[:, :DILATION, :], "row", -1)
+    row, column = lax.axis_index("row"), lax.axis_index("col")
+    odd = jnp.stack([row % 2, column % 2]).astype(jnp.int32)
+    outer = shape((2, DILATION, channels, width), bf16)
+    end = height - DILATION
+
+    one = swap_pairs(lax.dynamic_slice_in_dim(image, (1 - odd[0]) * end, DILATION, 1), "row", 0)
+    two = swap_pairs(lax.dynamic_slice_in_dim(image, odd[0] * end, DILATION, 1), "row", 1)
     image_rows, rims = call(own_kernel, (rows, own_rims), (image,))
     forward_weight = jnp.transpose(weight, (2, 0, 1, 3)).reshape(channels, depth)
     backward_weight = jnp.transpose(weight[::-1, ::-1], (3, 0, 1, 2)).reshape(channels, depth)
-    first, last, outer = call(
-        functools.partial(rim_kernel, True),
-        (packed, packed, shape((2, DILATION, channels, width), bf16)),
-        (upper, lower, rims),
-    )
-    left = from_behind(last, "col", 1)
-    right = from_behind(first, "col", -1)
-    activation, grads, top, bottom, rims, terms = call(
+    one, two, image_outer = call(
+        functools.partial(rim_kernel, True), (packed, packed, outer), (odd, one, two, rims), scalars=1
+    )
+    one, two = swap_pairs(one, "col", 0), swap_pairs(two, "col", 1)
+    activation, grads, one, two, rims, terms = call(
         functools.partial(forward_kernel, scale),
         (
             shape(image.shape, bf16), rows, edge, edge, own_rims,
             shape((channels, -(-(depth + 1) // 128) * 128), f32),
         ),
-        (image_rows, outer, left, right, cotangent, forward_weight, bias[:, None]),
+        (odd, image_rows, image_outer, one, two, cotangent, forward_weight, bias[:, None]),
         (stack, pltpu.VMEM((channels, width), f32)),
         2 * flops,
-    )
-    upper = from_behind(bottom, "row", 1)
-    lower = from_behind(top, "row", -1)
-    first, last = call(functools.partial(rim_kernel, False), (packed, packed), (upper, lower, rims))
-    left = from_behind(last, "col", 1)
-    right = from_behind(first, "col", -1)
+        1,
+    )
+    one, two = swap_pairs(one, "row", 0), swap_pairs(two, "row", 1)
+    one, two, grad_outer = call(
+        functools.partial(rim_kernel, False), (packed, packed, outer), (odd, one, two, rims), scalars=1
+    )
+    one, two = swap_pairs(one, "col", 0), swap_pairs(two, "col", 1)
     (grad_image,) = call(
         backward_kernel,
         (shape(image.shape, bf16),),
-        (grads, upper, lower, left, right, backward_weight),
+        (odd, grads, grad_outer, one, two, backward_weight),
         (stack,),
         flops,
+        1,
     )
     one, other = add_pairs(terms, ("col", "row"))
     grad_weight, grad_bias = call(

time: 55.5 us -> 50.2 us (0.905)
  waiting for transfers between devices: 14.1 us -> 7.95 us
  Pallas kernels: 10.3 us -> 12.9 us
  starting transfers between devices: 27.7 us -> 26.1 us
    ppermute x8, starting transfers between devices: 17.1 us -> 10.5 us  [swap_pairs(): return lax.ppermute(value, axis, pairs)]
    ppermute x8, waiting for transfers between devices: 7.45 us -> 1.93 us  [swap_pairs(): return lax.ppermute(value, axis, pairs)]
    ppermute x5, starting transfers between devices: 10.6 us -> 15.6 us  [add_pairs(): lax.ppermute(value, axis, [(place, place ^ step) for place in range(count)])]
    pallas_call x6, Pallas kernels: 10.3 us -> 12.9 us  [call(): pl.pallas_call(kernel, out_shape=out_shapes, in_specs=[pl.BlockSpec(memor...]
    slice x1 -> x0, local copies, waits for them, and re-layouts: 1.05 us -> none  [shards(): lower = from_behind(image[:, :DILATION, :], 'row', -1)]
    dynamic_slice x0 -> x1, local copies, waits for them, and re-layouts: none -> 1.05 us  [shards(): lax.dynamic_slice_in_dim(image, odd[0] * end, DILATION, 1)]
    ppermute x5, waiting for transfers between devices: 6.69 us -> 6.02 us  [add_pairs(): lax.ppermute(value, axis, [(place, place ^ step) for place in range(count)])]
  transfers between devices with their start and end apart: 13 -> 13, of which waited for: 5 -> 4; matrix products, arithmetic and copies ran while one was open for 1% -> 1% of each run, Pallas kernels for 8% -> 11%
where the time goes in v2:
time: 50.2 us; the launch traced here: 50 us
  starting transfers between devices  26.1 us (52%)
  Pallas kernels  12.9 us (26%)
  waiting for transfers between devices  7.95 us (16%)
  local copies, waits for them, and re-layouts  2.06 us (4%)
  between operations  0.86 us (2%)
    ppermute x5, starting transfers between devices, add_pairs(): lax.ppermute(value, axis, [(place, place ^ step) for place in range(count)])  15.6 us
    pallas_call x6, Pallas kernels, call(): pl.pallas_call(kernel, out_shape=out_shapes, in_specs=[pl.BlockSpec(memor...  12.9 us
    ppermute x8, starting transfers between devices, swap_pairs(): return lax.ppermute(value, axis, pairs)  10.5 us
    ppermute x5, waiting for transfers between devices, add_pairs(): lax.ppermute(value, axis, [(place, place ^ step) for place in range(count)])  6.02 us
    ppermute x8, waiting for transfers between devices, swap_pairs(): return lax.ppermute(value, axis, pairs)  1.93 us
    dynamic_slice x1, local copies, waits for them, and re-layouts, shards(): lax.dynamic_slice_in_dim(image, odd[0] * end, DILATION, 1)  1.05 us
  transfers between devices with their start and end apart: 13, of which 4 were waited for; matrix products, arithmetic and copies ran while one was open for 1% of the time, Pallas kernels for 11%

profile of v2, /device:TPU:0, one launch (start us, length us, event | category | flops | bytes accessed | tf_op | source)
XLA Modules:
  0.0 50.0 jit_solution(8616749799259153839)
XLA Ops:
  0.6 0.0 copy-start
  0.7 1.1 %constant_dynamic-slice_fusion = (bf16[32,16,128]{2,1,0:T(8,128)(2,1)S(1)}, bf16[32,16,128]{2,1,0:T(8,128)(2,1)S(1)}) fusion(bf16[32,64,128]{2,1,0:T(8,128)(2,1)} %image_ref.1, s32[]{:T(128)S(6)} %select_n.20, s32[]{:T(128)S(6)} %select_n.19), kind=kLoop, calls=%fused_computation.1 | loop fusion | bytes 524296 | tf_op jit(solution)/shard_map/dynamic_slice | solution.py:266
  1.7 3.0 %collective-permute-start = (bf16[32,16,128]{2,1,0:T(8,128)(2,1)S(1)}, bf16[32,16,128]{2,1,0:T(8,128)(2,1)S(1)}, u32[]{:S(2)}, u32[]{:S(2)}) collective-permute-start(bf16[32,16,128]{2,1,0:T(8,128)(2,1)S(1)} %get-tuple-element.37), channel_id=1, source_target_pairs={{0,4},{4,0},{8,12},{12,8},{16,20},{20,16},{24,28},{28,24},{1,5},{5... | collective-permute-start | bytes 393224 | tf_op jit(solution)/shard_map/ppermute | solution.py:19
  4.8 0.7 %collective-permute-start.1 = (bf16[32,16,128]{2,1,0:T(8,128)(2,1)S(1)}, bf16[32,16,128]{2,1,0:T(8,128)(2,1)S(1)}, u32[]{:S(2)}, u32[]{:S(2)}) collective-permute-start(bf16[32,16,128]{2,1,0:T(8,128)(2,1)S(1)} %get-tuple-element.36), channel_id=1, source_target_pairs={{4,8},{8,4},{12,16},{16,12},{20,24},{24,20},{5,9},{9,5},{13,17},{1... | collective-permute-start | bytes 393224 | tf_op jit(solution)/shard_map/ppermute | solution.py:19
  5.4 0.0 copy-done
  5.4 0.0 copy-start.1
  5.4 0.8 %shard_map.75 = (bf16[64,32,128]{2,1,0:T(8,128)(2,1)S(1)}, bf16[2,8,32,128]{3,2,1,0:T(8,128)(2,1)S(1)}) custom-call(bf16[32,64,128]{2,1,0:T(8,128)(2,1)S(1)} %copy-done), custom_call_target="tpu_custom_call" | custom-call | bytes 1179648 | tf_op jit(solution)/shard_map/pallas_call | solution.py:234
  6.3 0.1 pad_add_fusion.odd_ref
  6.3 1.9 %collective-permute-done.one_ref = bf16[32,16,128]{2,1,0:T(8,128)(2,1)S(1)} collective-permute-done((bf16[32,16,128]{2,1,0:T(8,128)(2,1)S(1)}, bf16[32,16,128]{2,1,0:T(8,128)(2,1)S(1)}, u32[]{:S(2)}, u32[]{:S(2)}) %collective-permute-start) | collective-permute-done | bytes 131104 | tf_op jit(solution)/shard_map/ppermute | solution.py:19
  8.2 0.0 collective-permute-done.1.two_ref
  8.3 0.0 copy-start.2
  8.3 0.8 %shard_map.76 = (bf16[12,32,128]{2,1,0:T(8,128)(2,1)S(1)}, bf16[12,32,128]{2,1,0:T(8,128)(2,1)S(1)}, bf16[2,16,32,128]{3,2,1,0:T(8,128)(2,1)S(1)}) custom-call(s32[2]{0:T(128)S(1)} %pad_add_fusion.odd_ref, bf16[32,16,128]{2,1,0:T(8,128)(2,1)S(1)} %collective-permute-done.one_ref, bf16[32,16,128]{2,1,0:T(8,128)(2,1)S(1)} %collective-permute-done.1.two_ref, ...), custom_call_target="tpu_custom_call" | custom-call | bytes 851976 | tf_op jit(solution)/shard_map/pallas_call | solution.py:234
  9.1 0.1 collective-permute-start.2
  9.1 0.7 %collective-permute-start.3 = (bf16[12,32,128]{2,1,0:T(8,128)(2,1)S(1)}, bf16[12,32,128]{2,1,0:T(8,128)(2,1)S(1)}, u32[]{:S(2)}, u32[]{:S(2)}) collective-permute-start(bf16[12,32,128]{2,1,0:T(8,128)(2,1)S(1)} %get-tuple-element.24), channel_id=1, source_target_pairs={{1,2},{2,1},{5,6},{6,5},{9,10},{10,9},{13,14},{14,13},{17,18},{18,... | collective-permute-start | bytes 294920 | tf_op jit(solution)/shard_map/ppermute | solution.py:19
  9.8 0.0 copy-done.2
  9.8 0.1 copy.11
  9.9 0.1 reshape.17.weight_ref
  10.0 0.0 copy-start.3
  10.0 0.6 %copy-done.3 = f32[32]{0:T(128)S(1)} copy-done((f32[32]{0:T(128)S(1)}, f32[32]{0:T(128)}, u32[]{:S(2)}) %copy-start.3) | copy-done | bytes 152
  10.7 0.1 copy.12.bias_ref
  10.7 0.0 collective-permute-done.2.one_ref
  10.8 0.0 collective-permute-done.3.two_ref
  10.8 0.0 copy-done.1
  10.8 5.6 %shard_map.77 = (bf16[32,64,128]{2,1,0:T(8,128)(2,1)}, bf16[64,32,128]{2,1,0:T(8,128)(2,1)S(1)}, bf16[16,32,128]{2,1,0:T(8,128)(2,1)S(1)}, bf16[16,32,128]{2,1,0...) custom-call(s32[2]{0:T(128)S(1)} %pad_add_fusion.odd_ref, ...), custom_call_target="tpu_custom_call" | custom-call | flops 301989888 | bytes 3016840 | tf_op jit(solution)/shard_map/pallas_call | solution.py:234
  16.4 4.8 %collective-permute-start.8 = (f32[32,384]{1,0:T(8,128)S(1)}, f32[32,384]{1,0:T(8,128)S(1)}, u32[]{:S(2)}, u32[]{:S(2)}) collective-permute-start(f32[32,384]{1,0:T(8,128)S(1)} %get-tuple-element.33), channel_id=1, source_target_pairs={{0,1},{1,0},{2,3},{3,2},{4,5},{5,4},{6,7},{7,6},{8,9},{9,8},{10,11... | collective-permute-start | bytes 147464 | tf_op jit(solution)/shard_map/ppermute | solution.py:29
  21.2 4.6 %collective-permute-start.4 = (bf16[16,32,128]{2,1,0:T(8,128)(2,1)S(1)}, bf16[16,32,128]{2,1,0:T(8,128)(2,1)S(1)}, u32[]{:S(2)}, u32[]{:S(2)}) collective-permute-start(bf16[16,32,128]{2,1,0:T(8,128)(2,1)S(1)} %get-tuple-element.27), channel_id=1, source_target_pairs={{0,4},{4,0},{8,12},{12,8},{16,20},{20,16},{24,28},{28,24},{1,5},{5... | collective-permute-start | bytes 393224 | tf_op jit(solution)/shard_map/ppermute | solution.py:19
  25.9 0.7 %collective-permute-start.5 = (bf16[16,32,128]{2,1,0:T(8,128)(2,1)S(1)}, bf16[16,32,128]{2,1,0:T(8,128)(2,1)S(1)}, u32[]{:S(2)}, u32[]{:S(2)}) collective-permute-start(bf16[16,32,128]{2,1,0:T(8,128)(2,1)S(1)} %get-tuple-element.28), channel_id=1, source_target_pairs={{4,8},{8,4},{12,16},{16,12},{20,24},{24,20},{5,9},{9,5},{13,17},{1... | collective-permute-start | bytes 393224 | tf_op jit(solution)/shard_map/ppermute | solution.py:19
  26.5 0.0 collective-permute-done.8
  26.5 1.2 %collective-permute-start.9 = (f32[32,384]{1,0:T(8,128)S(1)}, f32[32,384]{1,0:T(8,128)S(1)}, u32[]{:S(2)}, u32[]{:S(2)}) collective-permute-start(f32[32,384]{1,0:T(8,128)S(1)} %add.29), channel_id=1, source_target_pairs={{0,2},{1,3},{2,0},{3,1},{4,6},{5,7},{6,4},{7,5},{8,10},{9,11},{10,... | collective-permute-start | bytes 147464 | tf_op jit(solution)/shard_map/ppermute | solution.py:29
  27.7 3.0 %collective-permute-done.9 = f32[32,384]{1,0:T(8,128)S(1)} collective-permute-done((f32[32,384]{1,0:T(8,128)S(1)}, f32[32,384]{1,0:T(8,128)S(1)}, u32[]{:S(2)}, u32[]{:S(2)}) %collective-permute-start.9) | collective-permute-done | bytes 49184 | tf_op jit(solution)/shard_map/ppermute | solution.py:29
  30.7 4.5 %collective-permute-start.10 = (f32[32,384]{1,0:T(8,128)S(1)}, f32[32,384]{1,0:T(8,128)S(1)}, u32[]{:S(2)}, u32[]{:S(2)}) collective-permute-start(f32[32,384]{1,0:T(8,128)S(1)} %add.30), channel_id=1, source_target_pairs={{0,4},{4,0},{8,12},{12,8},{16,20},{20,16},{24,28},{28,24},{1,5},{5... | collective-permute-start | bytes 147464 | tf_op jit(solution)/shard_map/ppermute | solution.py:29
  35.2 0.0 collective-permute-done.4.one_ref
  35.2 0.0 collective-permute-done.5.two_ref
  35.2 0.8 %shard_map.78 = (bf16[12,32,128]{2,1,0:T(8,128)(2,1)S(1)}, bf16[12,32,128]{2,1,0:T(8,128)(2,1)S(1)}, bf16[2,16,32,128]{3,2,1,0:T(8,128)(2,1)S(1)}) custom-call(s32[2]{0:T(128)S(1)} %pad_add_fusion.odd_ref, bf16[16,32,128]{2,1,0:T(8,128)(2,1)S(1)} %collective-permute-done.4.one_ref, bf16[16,32,128]{2,1,0:T(8,128)(2,1)S(1)} %collective-permute-done.5.two_ref, ...), custom_call_target="tpu_custom_call" | custom-call | bytes 851976 | tf_op jit(solution)/shard_map/pallas_call | solution.py:234
  36.0 0.1 collective-permute-start.6
  36.0 0.7 %collective-permute-start.7 = (bf16[12,32,128]{2,1,0:T(8,128)(2,1)S(1)}, bf16[12,32,128]{2,1,0:T(8,128)(2,1)S(1)}, u32[]{:S(2)}, u32[]{:S(2)}) collective-permute-start(bf16[12,32,128]{2,1,0:T(8,128)(2,1)S(1)} %get-tuple-element.32), channel_id=1, source_target_pairs={{1,2},{2,1},{5,6},{6,5},{9,10},{10,9},{13,14},{14,13},{17,18},{18,... | collective-permute-start | bytes 294920 | tf_op jit(solution)/shard_map/ppermute | solution.py:19
  36.7 0.5 %collective-permute-done.10 = f32[32,384]{1,0:T(8,128)S(1)} collective-permute-done((f32[32,384]{1,0:T(8,128)S(1)}, f32[32,384]{1,0:T(8,128)S(1)}, u32[]{:S(2)}, u32[]{:S(2)}) %collective-permute-start.10) | collective-permute-done | bytes 49184 | tf_op jit(solution)/shard_map/ppermute | solution.py:29
  37.2 1.6 %collective-permute-start.11 = (f32[32,384]{1,0:T(8,128)S(1)}, f32[32,384]{1,0:T(8,128)S(1)}, u32[]{:S(2)}, u32[]{:S(2)}) collective-permute-start(f32[32,384]{1,0:T(8,128)S(1)} %add.31), channel_id=1, source_target_pairs={{0,8},{4,12},{8,0},{12,4},{16,24},{20,28},{24,16},{28,20},{1,9},{5... | collective-permute-start | bytes 147464 | tf_op jit(solution)/shard_map/ppermute | solution.py:29
  38.9 2.5 %collective-permute-done.11 = f32[32,384]{1,0:T(8,128)S(1)} collective-permute-done((f32[32,384]{1,0:T(8,128)S(1)}, f32[32,384]{1,0:T(8,128)S(1)}, u32[]{:S(2)}, u32[]{:S(2)}) %collective-permute-start.11) | collective-permute-done | bytes 49184 | tf_op jit(solution)/shard_map/ppermute | solution.py:29
  41.4 3.6 %collective-permute-start.12 = (f32[32,384]{1,0:T(8,128)S(1)}, f32[32,384]{1,0:T(8,128)S(1)}, u32[]{:S(2)}, u32[]{:S(2)}) collective-permute-start(f32[32,384]{1,0:T(8,128)S(1)} %add.32.one_ref), channel_id=1, source_target_pairs={{0,16},{4,20},{8,24},{12,28},{16,0},{20,4},{24,8},{28,12},{1,17},{... | collective-permute-start | bytes 147464 | tf_op jit(solution)/shard_map/ppermute | solution.py:29
  45.0 0.1 copy.14.weight_ref
  45.1 0.0 collective-permute-done.6.one_ref
  45.1 0.0 collective-permute-done.7.two_ref
  45.1 4.1 %shard_map.79 = bf16[32,64,128]{2,1,0:T(8,128)(2,1)} custom-call(s32[2]{0:T(128)S(1)} %pad_add_fusion.odd_ref, bf16[64,32,128]{2,1,0:T(8,128)(2,1)S(1)} %get-tuple-element.26.own_ref, bf16[2,16,32,128]{3,2,1,0:T(8,128)(2,1)S(1)} %get-tuple-element.30.outer_ref, bf16[12,32,128]{2,1,0:T(8,128)(2,1)S(1)} %collective-permute-done.6.one_ref, ...), custom_call_target="tpu_custom_call" | custom-call | flops 150994944 | bytes 1525768 | tf_op jit(solution)/shard_map/pallas_call | solution.py:234
  49.2 0.0 collective-permute-done.12.other_ref
  49.2 0.8 %shard_map.80 = (f32[3,3,32,32]{3,2,1,0:T(8,128)}, f32[1,32]{1,0:T(1,128)}) custom-call(f32[32,384]{1,0:T(8,128)S(1)} %add.32.one_ref, f32[32,384]{1,0:T(8,128)S(1)} %collective-permute-done.12.other_ref), custom_call_target="tpu_custom_call" | custom-call | bytes 135296 | tf_op jit(solution)/shard_map/pallas_call | solution.py:234
  (5 shorter events, 0.0 us)
Async XLA Ops:
  0.6 4.8 %copy-start = (bf16[32,64,128]{2,1,0:T(8,128)(2,1)S(1)}, bf16[32,64,128]{2,1,0:T(8,128)(2,1)}, u32[]{:S(2)}) copy-start(bf16[32,64,128]{2,1,0:T(8,128)(2,1)} %image_ref.1) | copy-start | bytes 1572868
  1.7 6.5 %collective-permute-start = (bf16[32,16,128]{2,1,0:T(8,128)(2,1)S(1)}, bf16[32,16,128]{2,1,0:T(8,128)(2,1)S(1)}, u32[]{:S(2)}, u32[]{:S(2)}) collective-permute-start(bf16[32,16,128]{2,1,0:T(8,128)(2,1)S(1)} %get-tuple-element.37), channel_id=1, source_target_pairs={{0,4},{4,0},{8,12},{12,8},{16,20},{20,16},{24,28},{28,24},{1,5},{5... | collective-permute-start | bytes 393224 | tf_op jit(solution)/shard_map/ppermute | solution.py:19
  4.8 3.5 %collective-permute-start.1 = (bf16[32,16,128]{2,1,0:T(8,128)(2,1)S(1)}, bf16[32,16,128]{2,1,0:T(8,128)(2,1)S(1)}, u32[]{:S(2)}, u32[]{:S(2)}) collective-permute-start(bf16[32,16,128]{2,1,0:T(8,128)(2,1)S(1)} %get-tuple-element.36), channel_id=1, source_target_pairs={{4,8},{8,4},{12,16},{16,12},{20,24},{24,20},{5,9},{9,5},{13,17},{1... | collective-permute-start | bytes 393224 | tf_op jit(solution)/shard_map/ppermute | solution.py:19
  5.4 5.3 %copy-start.1 = (bf16[32,64,128]{2,1,0:T(8,128)(2,1)S(1)}, bf16[32,64,128]{2,1,0:T(8,128)(2,1)}, u32[]{:S(2)}) copy-start(bf16[32,64,128]{2,1,0:T(8,128)(2,1)} %cotangent_ref.1) | copy-start | bytes 1572868
  8.3 1.6 %copy-start.2 = (bf16[3,3,32,32]{3,2,1,0:T(8,128)(2,1)S(1)}, bf16[3,3,32,32]{3,2,1,0:T(8,128)(2,1)}, u32[]{:S(2)}) copy-start(bf16[3,3,32,32]{3,2,1,0:T(8,128)(2,1)} %param.5) | copy-start | bytes 55300
  9.1 1.7 %collective-permute-start.2 = (bf16[12,32,128]{2,1,0:T(8,128)(2,1)S(1)}, bf16[12,32,128]{2,1,0:T(8,128)(2,1)S(1)}, u32[]{:S(2)}, u32[]{:S(2)}) collective-permute-start(bf16[12,32,128]{2,1,0:T(8,128)(2,1)S(1)} %get-tuple-element.23), channel_id=1, source_target_pairs={{0,1},{1,0},{2,3},{3,2},{4,5},{5,4},{6,7},{7,6},{8,9},{9,8},{10,11... | collective-permute-start | bytes 294920 | tf_op jit(solution)/shard_map/ppermute | solution.py:19
  9.1 1.6 %collective-permute-start.3 = (bf16[12,32,128]{2,1,0:T(8,128)(2,1)S(1)}, bf16[12,32,128]{2,1,0:T(8,128)(2,1)S(1)}, u32[]{:S(2)}, u32[]{:S(2)}) collective-permute-start(bf16[12,32,128]{2,1,0:T(8,128)(2,1)S(1)} %get-tuple-element.24), channel_id=1, source_target_pairs={{1,2},{2,1},{5,6},{6,5},{9,10},{10,9},{13,14},{14,13},{17,18},{18,... | collective-permute-start | bytes 294920 | tf_op jit(solution)/shard_map/ppermute | solution.py:19
  10.0 0.7 %copy-start.3 = (f32[32]{0:T(128)S(1)}, f32[32]{0:T(128)}, u32[]{:S(2)}) copy-start(f32[32]{0:T(128)} %param.6) | copy-start | bytes 388
  16.4 10.1 %collective-permute-start.8 = (f32[32,384]{1,0:T(8,128)S(1)}, f32[32,384]{1,0:T(8,128)S(1)}, u32[]{:S(2)}, u32[]{:S(2)}) collective-permute-start(f32[32,384]{1,0:T(8,128)S(1)} %get-tuple-element.33), channel_id=1, source_target_pairs={{0,1},{1,0},{2,3},{3,2},{4,5},{5,4},{6,7},{7,6},{8,9},{9,8},{10,11... | collective-permute-start | bytes 147464 | tf_op jit(solution)/shard_map/ppermute | solution.py:29
  21.2 14.0 %collective-permute-start.4 = (bf16[16,32,128]{2,1,0:T(8,128)(2,1)S(1)}, bf16[16,32,128]{2,1,0:T(8,128)(2,1)S(1)}, u32[]{:S(2)}, u32[]{:S(2)}) collective-permute-start(bf16[16,32,128]{2,1,0:T(8,128)(2,1)S(1)} %get-tuple-element.27), channel_id=1, source_target_pairs={{0,4},{4,0},{8,12},{12,8},{16,20},{20,16},{24,28},{28,24},{1,5},{5... | collective-permute-start | bytes 393224 | tf_op jit(solution)/shard_map/ppermute | solution.py:19
  25.9 9.3 %collective-permute-start.5 = (bf16[16,32,128]{2,1,0:T(8,128)(2,1)S(1)}, bf16[16,32,128]{2,1,0:T(8,128)(2,1)S(1)}, u32[]{:S(2)}, u32[]{:S(2)}) collective-permute-start(bf16[16,32,128]{2,1,0:T(8,128)(2,1)S(1)} %get-tuple-element.28), channel_id=1, source_target_pairs={{4,8},{8,4},{12,16},{16,12},{20,24},{24,20},{5,9},{9,5},{13,17},{1... | collective-permute-start | bytes 393224 | tf_op jit(solution)/shard_map/ppermute | solution.py:19
  26.5 4.2 %collective-permute-start.9 = (f32[32,384]{1,0:T(8,128)S(1)}, f32[32,384]{1,0:T(8,128)S(1)}, u32[]{:S(2)}, u32[]{:S(2)}) collective-permute-start(f32[32,384]{1,0:T(8,128)S(1)} %add.29), channel_id=1, source_target_pairs={{0,2},{1,3},{2,0},{3,1},{4,6},{5,7},{6,4},{7,5},{8,10},{9,11},{10,... | collective-permute-start | bytes 147464 | tf_op jit(solution)/shard_map/ppermute | solution.py:29
  30.7 6.5 %collective-permute-start.10 = (f32[32,384]{1,0:T(8,128)S(1)}, f32[32,384]{1,0:T(8,128)S(1)}, u32[]{:S(2)}, u32[]{:S(2)}) collective-permute-start(f32[32,384]{1,0:T(8,128)S(1)} %add.30), channel_id=1, source_target_pairs={{0,4},{4,0},{8,12},{12,8},{16,20},{20,16},{24,28},{28,24},{1,5},{5... | collective-permute-start | bytes 147464 | tf_op jit(solution)/shard_map/ppermute | solution.py:29
  36.0 9.1 %collective-permute-start.6 = (bf16[12,32,128]{2,1,0:T(8,128)(2,1)S(1)}, bf16[12,32,128]{2,1,0:T(8,128)(2,1)S(1)}, u32[]{:S(2)}, u32[]{:S(2)}) collective-permute-start(bf16[12,32,128]{2,1,0:T(8,128)(2,1)S(1)} %get-tuple-element.31), channel_id=1, source_target_pairs={{0,1},{1,0},{2,3},{3,2},{4,5},{5,4},{6,7},{7,6},{8,9},{9,8},{10,11... | collective-permute-start | bytes 294920 | tf_op jit(solution)/shard_map/ppermute | solution.py:19
  36.0 9.0 %collective-permute-start.7 = (bf16[12,32,128]{2,1,0:T(8,128)(2,1)S(1)}, bf16[12,32,128]{2,1,0:T(8,128)(2,1)S(1)}, u32[]{:S(2)}, u32[]{:S(2)}) collective-permute-start(bf16[12,32,128]{2,1,0:T(8,128)(2,1)S(1)} %get-tuple-element.32), channel_id=1, source_target_pairs={{1,2},{2,1},{5,6},{6,5},{9,10},{10,9},{13,14},{14,13},{17,18},{18,... | collective-permute-start | bytes 294920 | tf_op jit(solution)/shard_map/ppermute | solution.py:19
  37.2 4.2 %collective-permute-start.11 = (f32[32,384]{1,0:T(8,128)S(1)}, f32[32,384]{1,0:T(8,128)S(1)}, u32[]{:S(2)}, u32[]{:S(2)}) collective-permute-start(f32[32,384]{1,0:T(8,128)S(1)} %add.31), channel_id=1, source_target_pairs={{0,8},{4,12},{8,0},{12,4},{16,24},{20,28},{24,16},{28,20},{1,9},{5... | collective-permute-start | bytes 147464 | tf_op jit(solution)/shard_map/ppermute | solution.py:29
  41.4 7.8 %collective-permute-start.12 = (f32[32,384]{1,0:T(8,128)S(1)}, f32[32,384]{1,0:T(8,128)S(1)}, u32[]{:S(2)}, u32[]{:S(2)}) collective-permute-start(f32[32,384]{1,0:T(8,128)S(1)} %add.32.one_ref), channel_id=1, source_target_pairs={{0,16},{4,20},{8,24},{12,28},{16,0},{20,4},{24,8},{28,12},{1,17},{... | collective-permute-start | bytes 147464 | tf_op jit(solution)/shard_map/ppermute | solution.py:29

commit v3 on v2

--- a/solution.py
+++ b/solution.py
@@ -82,9 +82,21 @@
         store(first_group + group, first, last)
 
 
-def own_kernel(image_ref, rows_ref, rims_ref):
-    count = image_ref.shape[1] // DILATION
+def either(flag, body, one, two):
+    pl.when(flag == 1)(lambda: body(one, two))
+    pl.when(flag != 1)(lambda: body(two, one))
+
+
+def own_kernel(odd_ref, image_ref, bias_ref, *refs):
+    weight_refs, (rows_ref, rims_ref, send_ref, wide_ref), ready_refs = refs[:2], refs[2:6], refs[6:]
+    height = image_ref.shape[1]
+    count = height // DILATION
     groups = rims_ref.shape[1] // count
+    start = pl.multiple_of(odd_ref[0] * (height - DILATION), DILATION)
+    send_ref[...] = image_ref[:, pl.ds(start, DILATION), :]
+    wide_ref[...] = jnp.broadcast_to(bias_ref[...], wide_ref.shape)
+    for weight_ref, ready_ref in zip(weight_refs, ready_refs):
+        ready_ref[...] = weight_ref[...]
 
     def store(place, first, last):
         rims_ref[0, place] = first
@@ -103,28 +115,31 @@
 def rim_kernel(swap, odd_ref, one_ref, two_ref, rims_ref, send_one_ref, send_two_ref, outer_ref):
     own = rims_ref.shape[1]
     groups = (send_one_ref.shape[0] - own) // 2
-    odd_row, odd_column = odd_ref[0] == 1, odd_ref[1] == 1
     send_one_ref[groups : groups + own] = rims_ref[1 - odd_ref[1]]
     send_two_ref[groups : groups + own] = rims_ref[odd_ref[1]]
 
-    def store(place, first, last):
-        send_one_ref[place] = jnp.where(odd_column, first, last)
-        send_two_ref[place] = jnp.where(odd_column, last, first)
-
-    one, two = one_ref[...], two_ref[...]
-    for index, rows in enumerate((jnp.where(odd_row, one, two), jnp.where(odd_row, two, one))):
-        rows = jnp.swapaxes(rows, 0, 1) if swap else rows
-        outer_ref[index] = rows
-        pack_rows(rows, store, index * (groups + own))
-
-
-def spread(rows_of, odd, one_ref, two_ref, stack_ref, block, group_start):
-    channels, width = one_ref.shape[1:]
+    def order(upper_ref, lower_ref):
+        for index, ref in enumerate((upper_ref, lower_ref)):
+            outer_ref[index] = jnp.swapaxes(ref[...], 0, 1) if swap else ref[...]
+
+    def pack(send_first_ref, send_last_ref):
+        def store(place, first, last):
+            send_first_ref[place] = first
+            send_last_ref[place] = last
+
+        for index in range(2):
+            pack_rows(outer_ref[index], store, index * (groups + own))
+
+    either(odd_ref[0], order, one_ref, two_ref)
+    either(odd_ref[1], pack, send_one_ref, send_two_ref)
+
+
+def spread(rows_of, left_ref, right_ref, stack_ref, block, group_start):
+    channels, width = left_ref.shape[1:]
     pieces = width // DILATION
     lane = lane_of((channels, width))
     for group in range(DILATION // pieces):
-        one, two = one_ref[group_start + group], two_ref[group_start + group]
-        rims = unpack_group(jnp.where(odd, one, two), jnp.where(odd, two, one), pieces)
+        rims = unpack_group(left_ref[group_start + group], right_ref[group_start + group], pieces)
         for k in range(pieces):
             row = group * pieces + k
             value = rows_of(row)
@@ -139,64 +154,79 @@
 def spread_all(odd_ref, own_ref, outer_ref, one_ref, two_ref, stack_ref):
     count = own_ref.shape[0] // DILATION
     groups = one_ref.shape[0] // (count + 2)
-    odd = odd_ref[1] == 1
-    spread(lambda row: outer_ref[0, row], odd, one_ref, two_ref, stack_ref, 0, 0)
-
-    def body(block, carry):
-        spread(
-            lambda row: own_ref[block * DILATION + row],
-            odd, one_ref, two_ref, stack_ref, block + 1, (block + 1) * groups,
-        )
-        return carry
-
-    lax.fori_loop(0, count, body, 0)
-    spread(lambda row: outer_ref[1, row], odd, one_ref, two_ref, stack_ref, count + 1, (count + 1) * groups)
+
+    def every(left_ref, right_ref):
+        spread(lambda row: outer_ref[0, row], left_ref, right_ref, stack_ref, 0, 0)
+
+        def body(block, carry):
+            spread(
+                lambda row: own_ref[block * DILATION + row],
+                left_ref, right_ref, stack_ref, block + 1, (block + 1) * groups,
+            )
+            return carry
+
+        lax.fori_loop(0, count, body, 0)
+        spread(lambda row: outer_ref[1, row], left_ref, right_ref, stack_ref, count + 1, (count + 1) * groups)
+
+    either(odd_ref[1], every, one_ref, two_ref)
+
+
+def stacked_at(stack_ref, block):
+    rows, columns = stack_ref.shape[1:]
+    return stack_ref[pl.ds(block, 3)].reshape(3 * rows, columns)
 
 
 def forward_kernel(
-    scale, odd_ref, own_ref, outer_ref, one_ref, two_ref, cotangent_ref, weight_ref, bias_ref,
-    activation_ref, grad_ref, send_one_ref, send_two_ref, rims_ref, terms_ref, stack_ref, sum_ref,
+    odd_ref, own_ref, outer_ref, one_ref, two_ref, cotangent_ref, weight_ref, bias_ref,
+    activation_ref, grad_ref, send_ref, stack_ref,
 ):
     height, channels, width = own_ref.shape
+    spread_all(odd_ref, own_ref, outer_ref, one_ref, two_ref, stack_ref)
+
+    def body(block, carry):
+        start = pl.multiple_of(block * DILATION, DILATION)
+        preact = jnp.dot(weight_ref[...], stacked_at(stack_ref, block), preferred_element_type=jnp.float32)
+        cotangent = jnp.swapaxes(cotangent_ref[:, pl.ds(start, DILATION), :], 0, 1)
+        values = []
+        for row in range(DILATION):
+            value, slope_val = gelu_pair(preact[:, row * width : (row + 1) * width] + bias_ref[...])
+            values.append(value.astype(jnp.bfloat16))
+            grad_ref[start + row] = (cotangent[row].astype(jnp.float32) * slope_val).astype(jnp.bfloat16)
+        activation_ref[:, pl.ds(start, DILATION), :] = jnp.swapaxes(jnp.stack(values), 0, 1)
+        return carry
+
+    lax.fori_loop(0, height // DILATION, body, 0)
+    send_ref[...] = grad_ref[pl.ds((1 - odd_ref[0]) * (height - DILATION), DILATION)]
+
+
+def terms_kernel(scale, odd_ref, grad_ref, stack_ref, send_ref, rims_ref, terms_ref, sum_ref):
+    height, channels, width = grad_ref.shape
     count = height // DILATION
     groups = rims_ref.shape[1] // count
-    spread_all(odd_ref, own_ref, outer_ref, one_ref, two_ref, stack_ref)
+    depth = 9 * channels
+    send_ref[...] = grad_ref[pl.ds(odd_ref[0] * (height - DILATION), DILATION)]
     terms_ref[...] = jnp.zeros_like(terms_ref)
     sum_ref[...] = jnp.zeros_like(sum_ref)
-    depth = 9 * channels
 
     def store(place, first, last):
         rims_ref[0, place] = first
         rims_ref[1, place] = last
 
     def body(block, carry):
-        start = pl.multiple_of(block * DILATION, DILATION)
-        stacked = stack_ref[pl.ds(block, 3)].reshape(depth, DILATION * width)
-        preact = jnp.dot(weight_ref[...], stacked, preferred_element_type=jnp.float32)
-        cotangent = jnp.swapaxes(cotangent_ref[:, pl.ds(start, DILATION), :], 0, 1)
-        bias = jnp.broadcast_to(bias_ref[...], (channels, width))
-        values, grads = [], []
+        grads = grad_ref[pl.ds(block * DILATION, DILATION)]
+        rows = [grads[row] for row in range(DILATION)]
         total = sum_ref[...]
-        for row in range(DILATION):
-            value, slope_val = gelu_pair(preact[:, row * width : (row + 1) * width] + bias)
-            values.append(value.astype(jnp.bfloat16))
-            grad = (cotangent[row].astype(jnp.float32) * slope_val).astype(jnp.bfloat16)
-            grads.append(grad)
-            total = total + grad.astype(jnp.float32)
-            grad_ref[start + row] = grad
+        for row in rows:
+            total = total + row.astype(jnp.float32)
         sum_ref[...] = total
-        activation_ref[:, pl.ds(start, DILATION), :] = jnp.swapaxes(jnp.stack(values), 0, 1)
         terms_ref[:, :depth] += lax.dot_general(
-            jnp.concatenate(grads, axis=1), stacked, (((1,), (1,)), ((), ())),
+            jnp.concatenate(rows, axis=1), stacked_at(stack_ref, block), (((1,), (1,)), ((), ())),
             preferred_element_type=jnp.float32,
         )
-        pack_rows(jnp.stack(grads), store, block * groups)
+        pack_rows(grads, store, block * groups)
         return carry
 
     lax.fori_loop(0, count, body, 0)
-    end = height - DILATION
-    send_one_ref[...] = grad_ref[pl.ds((1 - odd_ref[0]) * end, DILATION)]
-    send_two_ref[...] = grad_ref[pl.ds(odd_ref[0] * end, DILATION)]
     terms_ref[:, :depth] = terms_ref[:, :depth] * scale
     sums = jnp.sum(sum_ref[...], axis=1, keepdims=True) * scale
     terms_ref[:, depth:] = jnp.broadcast_to(sums, (channels, terms_ref.shape[1] - depth))
@@ -210,8 +240,9 @@
 
     def body(block, carry):
         start = pl.multiple_of(block * DILATION, DILATION)
-        stacked = stack_ref[pl.ds(block, 3)].reshape(9 * channels, DILATION * width)
-        total = jnp.dot(weight_ref[...], stacked, preferred_element_type=jnp.float32).astype(jnp.bfloat16)
+        total = jnp.dot(
+            weight_ref[...], stacked_at(stack_ref, block), preferred_element_type=jnp.float32
+        ).astype(jnp.bfloat16)
         rows = jnp.stack([total[:, row * width : (row + 1) * width] for row in range(DILATION)])
         out_ref[:, pl.ds(start, DILATION), :] = jnp.swapaxes(rows, 0, 1)
         return carry
@@ -250,39 +281,51 @@
     pieces = width // DILATION
     own_groups, all_groups = height // pieces, (height + 2 * DILATION) // pieces
     depth = 9 * channels
-    stack = pltpu.VMEM((height // DILATION + 2, 3 * channels, DILATION * width), bf16)
+    stack_shape = (height // DILATION + 2, 3 * channels, DILATION * width)
     edge = shape((DILATION, channels, width), bf16)
     packed = shape((all_groups, channels, width), bf16)
     own_rims = shape((2, own_groups, channels, width), bf16)
+    outer = shape((2, DILATION, channels, width), bf16)
     rows = shape((height, channels, width), bf16)
+    weights = shape((channels, depth), bf16)
+    terms = shape((channels, -(-(depth + 1) // 128) * 128), f32)
     flops = 2 * depth * channels * height * width
-
-    row, column = lax.axis_index("row"), lax.axis_index("col")
-    odd = jnp.stack([row % 2, column % 2]).astype(jnp.int32)
-    outer = shape((2, DILATION, channels, width), bf16)
-    end = height - DILATION
-
-    one = swap_pairs(lax.dynamic_slice_in_dim(image, (1 - odd[0]) * end, DILATION, 1), "row", 0)
-    two = swap_pairs(lax.dynamic_slice_in_dim(image, odd[0] * end, DILATION, 1), "row", 1)
-    image_rows, rims = call(own_kernel, (rows, own_rims), (image,))
-    forward_weight = jnp.transpose(weight, (2, 0, 1, 3)).reshape(channels, depth)
-    backward_weight = jnp.transpose(weight[::-1, ::-1], (3, 0, 1, 2)).reshape(channels, depth)
+    odd = jnp.stack([lax.axis_index("row") % 2, lax.axis_index("col") % 2]).astype(jnp.int32)
+
+    rim = lax.dynamic_slice_in_dim(image, (1 - odd[0]) * (height - DILATION), DILATION, 1)
+    one = swap_pairs(rim, "row", 0)
+    image_rows, rims, rim, wide_bias, forward_weight, backward_weight = call(
+        own_kernel,
+        (rows, own_rims, shape((channels, DILATION, width), bf16), shape((channels, width), f32), weights, weights),
+        (
+            odd, image, bias[:, None],
+            jnp.transpose(weight, (2, 0, 1, 3)).reshape(channels, depth),
+            jnp.transpose(weight[::-1, ::-1], (3, 0, 1, 2)).reshape(channels, depth),
+        ),
+        scalars=1,
+    )
+    two = swap_pairs(rim, "row", 1)
     one, two, image_outer = call(
         functools.partial(rim_kernel, True), (packed, packed, outer), (odd, one, two, rims), scalars=1
     )
     one, two = swap_pairs(one, "col", 0), swap_pairs(two, "col", 1)
-    activation, grads, one, two, rims, terms = call(
-        functools.partial(forward_kernel, scale),
-        (
-            shape(image.shape, bf16), rows, edge, edge, own_rims,
-            shape((channels, -(-(depth + 1) // 128) * 128), f32),
-        ),
-        (odd, image_rows, image_outer, one, two, cotangent, forward_weight, bias[:, None]),
-        (stack, pltpu.VMEM((channels, width), f32)),
-        2 * flops,
+    activation, grads, rim, stack = call(
+        forward_kernel,
+        (shape(image.shape, bf16), rows, edge, shape(stack_shape, bf16)),
+        (odd, image_rows, image_outer, one, two, cotangent, forward_weight, wide_bias),
+        flops=flops,
+        scalars=1,
+    )
+    one = swap_pairs(rim, "row", 0)
+    rim, rims, terms = call(
+        functools.partial(terms_kernel, scale),
+        (edge, own_rims, terms),
+        (odd, grads, stack),
+        (pltpu.VMEM((channels, width), f32),),
+        flops,
         1,
     )
-    one, two = swap_pairs(one, "row", 0), swap_pairs(two, "row", 1)
+    two = swap_pairs(rim, "row", 1)
     one, two, grad_outer = call(
         functools.partial(rim_kernel, False), (packed, packed, outer), (odd, one, two, rims), scalars=1
     )
@@ -291,7 +334,7 @@
         backward_kernel,
         (shape(image.shape, bf16),),
         (odd, grads, grad_outer, one, two, backward_weight),
-        (stack,),
+        (pltpu.VMEM(stack_shape, bf16),),
         flops,
         1,
     )

time: 50.2 us -> 57.9 us (1.15)
  local copies, waits for them, and re-layouts: 2.06 us -> 5.77 us
  starting transfers between devices: 26.1 us -> 29.2 us
  Pallas kernels: 12.9 us -> 15.1 us
  waiting for transfers between devices: 7.95 us -> 6.56 us
    ppermute x8, starting transfers between devices: 10.5 us -> 13.3 us  [swap_pairs(): return lax.ppermute(value, axis, pairs)]
    pallas_call x6 -> x7, Pallas kernels: 12.9 us -> 15.1 us  [call(): pl.pallas_call(kernel, out_shape=out_shapes, in_specs=[pl.BlockSpec(memor...]
    unnamed x8 -> x4, local copies, waits for them, and re-layouts: 0.66 us -> 2.08 us
    ppermute x8, waiting for transfers between devices: 1.93 us -> 0.63 us  [swap_pairs(): return lax.ppermute(value, axis, pairs)]
    transpose x1, local copies, waits for them, and re-layouts: 0.05 us -> 0.94 us  [shards(): jnp.transpose(weight, (2, 0, 1, 3)).reshape(channels, depth)]
    rev x1, local copies, waits for them, and re-layouts: 0.01 us -> 0.89 us  [shards(): weight[::-1, ::-1]]
    broadcast_in_dim x1, local copies, waits for them, and re-layouts: 0.09 us -> 0.74 us  [shards(): bias[:, None]]
  transfers between devices with their start and end apart: 13 -> 13, of which waited for: 4 -> 4; matrix products, arithmetic and copies ran while one was open for 1% -> 5% of each run, Pallas kernels for 11% -> 11%
where the time goes in v3:
time: 57.9 us; the launch traced here: 57.5 us
  starting transfers between devices  29.2 us (50%)
  Pallas kernels  15.1 us (26%)
  waiting for transfers between devices  6.56 us (11%)
  local copies, waits for them, and re-layouts  5.77 us (10%)
  between operations  0.79 us (1%)
    ppermute x5, starting transfers between devices, add_pairs(): lax.ppermute(value, axis, [(place, place ^ step) for place in range(count)])  16 us
    pallas_call x7, Pallas kernels, call(): pl.pallas_call(kernel, out_shape=out_shapes, in_specs=[pl.BlockSpec(memor...  15.1 us
    ppermute x8, starting transfers between devices, swap_pairs(): return lax.ppermute(value, axis, pairs)  13.3 us
    ppermute x5, waiting for transfers between devices, add_pairs(): lax.ppermute(value, axis, [(place, place ^ step) for place in range(count)])  5.93 us
    unnamed x4, local copies, waits for them, and re-layouts  2.08 us
  transfers between devices with their start and end apart: 13, of which 4 were waited for; matrix products, arithmetic and copies ran while one was open for 5% of the time, Pallas kernels for 11%

profile of v3, /device:TPU:0, one launch (start us, length us, event | category | flops | bytes accessed | tf_op | source)
XLA Modules:
  0.0 57.5 jit_solution(15515964618143921717)
XLA Ops:
  0.6 0.9 %constant_dynamic-slice_fusion = bf16[32,16,128]{2,1,0:T(8,128)(2,1)S(1)} fusion(bf16[32,64,128]{2,1,0:T(8,128)(2,1)} %image_ref.1, s32[]{:T(128)S(6)} %select_n.16), kind=kLoop, calls=%fused_computation.1 | loop fusion | bytes 262148 | tf_op jit(solution)/shard_map/dynamic_slice | solution.py:295
  1.6 3.0 %collective-permute-start = (bf16[32,16,128]{2,1,0:T(8,128)(2,1)S(1)}, bf16[32,16,128]{2,1,0:T(8,128)(2,1)S(1)}, u32[]{:S(2)}, u32[]{:S(2)}) collective-permute-start(bf16[32,16,128]{2,1,0:T(8,128)(2,1)S(1)} %constant_dynamic-slice_fusion), channel_id=1, source_target_pairs={{0,4},{4,0},{8,12},{12,8},{16,20},{20,16},{24,28},{28,24},{1,5},{5... | collective-permute-start | bytes 393224 | tf_op jit(solution)/shard_map/ppermute | solution.py:19
  4.6 0.7 %copy.13.bias_ref = f32[32,1]{1,0:T(8,128)S(1)} copy(f32[32,1]{0,1:T(1,128)} %bitcast.10) | data formatting | bytes 256 | tf_op jit(solution)/shard_map/broadcast_in_dim | solution.py:301
  5.3 0.9 %rev.3 = bf16[3,3,32,32]{3,2,1,0:T(8,128)(2,1)S(1)} reverse(bf16[3,3,32,32]{3,2,1,0:T(8,128)(2,1)} %param.5), dimensions={0,1} | reverse | bytes 36864 | tf_op jit(solution)/shard_map/rev | solution.py:303
  6.2 0.1 copy.14.refs_1_
  6.3 0.9 %copy.11 = bf16[32,3,3,32]{3,2,1,0:T(4,128)(2,1)S(1)} copy(bf16[32,3,3,32]{3,0,2,1:T(8,128)(2,1)} %bitcast.9) | data formatting | bytes 36864 | tf_op jit(solution)/shard_map/transpose | solution.py:302
  7.3 0.1 reshape.17.refs_0_
  7.4 0.1 pad_add_fusion.odd_ref
  7.5 0.0 copy-start
  7.5 1.0 %copy-done = bf16[32,64,128]{2,1,0:T(8,128)(2,1)S(1)} copy-done((bf16[32,64,128]{2,1,0:T(8,128)(2,1)S(1)}, bf16[32,64,128]{2,1,0:T(8,128)(2,1)}, u32[]{:S(2)}) %copy-start) | copy-done | bytes 524312
  8.5 1.4 %shard_map.75 = (bf16[64,32,128]{2,1,0:T(8,128)(2,1)S(1)}, bf16[2,8,32,128]{3,2,1,0:T(8,128)(2,1)S(1)}, bf16[32,16,128]{2,1,0:T(8,128)(2,1)S(1)}, f32[32,128]{1,...) custom-call(s32[2]{0:T(128)S(1)} %pad_add_fusion.odd_ref, bf16[32,64,128]{2,1,0:T(8,128)(2,1)S(1)} %copy-done, ...), custom_call_target="tpu_custom_call" | custom-call | bytes 1400968 | tf_op jit(solution)/shard_map/pallas_call | solution.py:265
  9.9 0.7 %collective-permute-start.1 = (bf16[32,16,128]{2,1,0:T(8,128)(2,1)S(1)}, bf16[32,16,128]{2,1,0:T(8,128)(2,1)S(1)}, u32[]{:S(2)}, u32[]{:S(2)}) collective-permute-start(bf16[32,16,128]{2,1,0:T(8,128)(2,1)S(1)} %get-tuple-element.26), channel_id=1, source_target_pairs={{4,8},{8,4},{12,16},{16,12},{20,24},{24,20},{5,9},{9,5},{13,17},{1... | collective-permute-start | bytes 393224 | tf_op jit(solution)/shard_map/ppermute | solution.py:19
  10.6 0.0 collective-permute-done.one_ref
  10.6 0.0 collective-permute-done.1.two_ref
  10.6 0.8 %shard_map.76 = (bf16[12,32,128]{2,1,0:T(8,128)(2,1)S(1)}, bf16[12,32,128]{2,1,0:T(8,128)(2,1)S(1)}, bf16[2,16,32,128]{3,2,1,0:T(8,128)(2,1)S(1)}) custom-call(s32[2]{0:T(128)S(1)} %pad_add_fusion.odd_ref, bf16[32,16,128]{2,1,0:T(8,128)(2,1)S(1)} %collective-permute-done.one_ref, bf16[32,16,128]{2,1,0:T(8,128)(2,1)S(1)} %collective-permute-done.1.two_ref, ...), custom_call_target="tpu_custom_call" | custom-call | bytes 851976 | tf_op jit(solution)/shard_map/pallas_call | solution.py:265
  11.5 0.1 collective-permute-start.2
  11.6 0.7 %collective-permute-start.3 = (bf16[12,32,128]{2,1,0:T(8,128)(2,1)S(1)}, bf16[12,32,128]{2,1,0:T(8,128)(2,1)S(1)}, u32[]{:S(2)}, u32[]{:S(2)}) collective-permute-start(bf16[12,32,128]{2,1,0:T(8,128)(2,1)S(1)} %get-tuple-element.30), channel_id=1, source_target_pairs={{1,2},{2,1},{5,6},{6,5},{9,10},{10,9},{13,14},{14,13},{17,18},{18,... | collective-permute-start | bytes 294920 | tf_op jit(solution)/shard_map/ppermute | solution.py:19
  12.2 0.6 %collective-permute-done.2.one_ref = bf16[12,32,128]{2,1,0:T(8,128)(2,1)S(1)} collective-permute-done((bf16[12,32,128]{2,1,0:T(8,128)(2,1)S(1)}, bf16[12,32,128]{2,1,0:T(8,128)(2,1)S(1)}, u32[]{:S(2)}, u32[]{:S(2)}) %collective-permute-start.2) | collective-permute-done | bytes 98336 | tf_op jit(solution)/shard_map/ppermute | solution.py:19
  12.8 0.0 collective-permute-done.3.two_ref
  12.8 0.0 copy-start.1
  12.8 1.0 %copy-done.1 = bf16[32,64,128]{2,1,0:T(8,128)(2,1)S(1)} copy-done((bf16[32,64,128]{2,1,0:T(8,128)(2,1)S(1)}, bf16[32,64,128]{2,1,0:T(8,128)(2,1)}, u32[]{:S(2)}) %copy-start.1) | copy-done | bytes 524312
  13.9 4.5 %shard_map.77 = (bf16[32,64,128]{2,1,0:T(8,128)(2,1)}, bf16[64,32,128]{2,1,0:T(8,128)(2,1)S(1)}, bf16[16,32,128]{2,1,0:T(8,128)(2,1)S(1)}, bf16[6,96,2048]{2,1,0:T(8,128)(2,1)S(1)}) custom-call(s32[2]{0:T(128)S(1)} %pad_add_fusion.odd_ref, bf16[64,32,128]{2,1,0:T(8,128)(2,1)S(1)} %get-tuple-element.25.own_ref, ...), custom_call_target="tpu_custom_call" | custom-call | flops 150994944 | bytes 5081096 | tf_op jit(solution)/shard_map/pallas_call | solution.py:265
  18.4 2.6 %shard_map.78 = (bf16[16,32,128]{2,1,0:T(8,128)(2,1)S(1)}, bf16[2,8,32,128]{3,2,1,0:T(8,128)(2,1)S(1)}, f32[32,384]{1,0:T(8,128)S(1)}) custom-call(s32[2]{0:T(128)S(1)} %pad_add_fusion.odd_ref, bf16[64,32,128]{2,1,0:T(8,128)(2,1)S(1)} %get-tuple-element.34.grad_ref.own_ref, bf16[6,96,2048]{2,1,0:T(8,128)(2,1)S(1)} %get-tuple-element.36.stack_ref), custom_call_target="tpu_custom_call" | custom-call | flops 150994944 | bytes 3194888 | tf_op jit(solution)/shard_map/pallas_call | solution.py:265
  21.0 5.1 %collective-permute-start.8 = (f32[32,384]{1,0:T(8,128)S(1)}, f32[32,384]{1,0:T(8,128)S(1)}, u32[]{:S(2)}, u32[]{:S(2)}) collective-permute-start(f32[32,384]{1,0:T(8,128)S(1)} %get-tuple-element.43), channel_id=1, source_target_pairs={{0,1},{1,0},{2,3},{3,2},{4,5},{5,4},{6,7},{7,6},{8,9},{9,8},{10,11... | collective-permute-start | bytes 147464 | tf_op jit(solution)/shard_map/ppermute | solution.py:29
  26.2 7.5 %collective-permute-start.4 = (bf16[16,32,128]{2,1,0:T(8,128)(2,1)S(1)}, bf16[16,32,128]{2,1,0:T(8,128)(2,1)S(1)}, u32[]{:S(2)}, u32[]{:S(2)}) collective-permute-start(bf16[16,32,128]{2,1,0:T(8,128)(2,1)S(1)} %get-tuple-element.35), channel_id=1, source_target_pairs={{0,4},{4,0},{8,12},{12,8},{16,20},{20,16},{24,28},{28,24},{1,5},{5... | collective-permute-start | bytes 393224 | tf_op jit(solution)/shard_map/ppermute | solution.py:19
  33.6 0.7 %collective-permute-start.5 = (bf16[16,32,128]{2,1,0:T(8,128)(2,1)S(1)}, bf16[16,32,128]{2,1,0:T(8,128)(2,1)S(1)}, u32[]{:S(2)}, u32[]{:S(2)}) collective-permute-start(bf16[16,32,128]{2,1,0:T(8,128)(2,1)S(1)} %get-tuple-element.37), channel_id=1, source_target_pairs={{4,8},{8,4},{12,16},{16,12},{20,24},{24,20},{5,9},{9,5},{13,17},{1... | collective-permute-start | bytes 393224 | tf_op jit(solution)/shard_map/ppermute | solution.py:19
  34.3 0.0 collective-permute-done.8
  34.3 1.3 %collective-permute-start.9 = (f32[32,384]{1,0:T(8,128)S(1)}, f32[32,384]{1,0:T(8,128)S(1)}, u32[]{:S(2)}, u32[]{:S(2)}) collective-permute-start(f32[32,384]{1,0:T(8,128)S(1)} %add.25), channel_id=1, source_target_pairs={{0,2},{1,3},{2,0},{3,1},{4,6},{5,7},{6,4},{7,5},{8,10},{9,11},{10,... | collective-permute-start | bytes 147464 | tf_op jit(solution)/shard_map/ppermute | solution.py:29
  35.6 2.9 %collective-permute-done.9 = f32[32,384]{1,0:T(8,128)S(1)} collective-permute-done((f32[32,384]{1,0:T(8,128)S(1)}, f32[32,384]{1,0:T(8,128)S(1)}, u32[]{:S(2)}, u32[]{:S(2)}) %collective-permute-start.9) | collective-permute-done | bytes 49184 | tf_op jit(solution)/shard_map/ppermute | solution.py:29
  38.5 4.5 %collective-permute-start.10 = (f32[32,384]{1,0:T(8,128)S(1)}, f32[32,384]{1,0:T(8,128)S(1)}, u32[]{:S(2)}, u32[]{:S(2)}) collective-permute-start(f32[32,384]{1,0:T(8,128)S(1)} %add.26), channel_id=1, source_target_pairs={{0,4},{4,0},{8,12},{12,8},{16,20},{20,16},{24,28},{28,24},{1,5},{5... | collective-permute-start | bytes 147464 | tf_op jit(solution)/shard_map/ppermute | solution.py:29
  42.9 0.0 collective-permute-done.4.one_ref
  42.9 0.0 collective-permute-done.5.two_ref
  42.9 0.8 %shard_map.79 = (bf16[12,32,128]{2,1,0:T(8,128)(2,1)S(1)}, bf16[12,32,128]{2,1,0:T(8,128)(2,1)S(1)}, bf16[2,16,32,128]{3,2,1,0:T(8,128)(2,1)S(1)}) custom-call(s32[2]{0:T(128)S(1)} %pad_add_fusion.odd_ref, bf16[16,32,128]{2,1,0:T(8,128)(2,1)S(1)} %collective-permute-done.4.one_ref, bf16[16,32,128]{2,1,0:T(8,128)(2,1)S(1)} %collective-permute-done.5.two_ref, ...), custom_call_target="tpu_custom_call" | custom-call | bytes 851976 | tf_op jit(solution)/shard_map/pallas_call | solution.py:265
  43.7 0.1 collective-permute-start.6
  43.8 0.7 %collective-permute-start.7 = (bf16[12,32,128]{2,1,0:T(8,128)(2,1)S(1)}, bf16[12,32,128]{2,1,0:T(8,128)(2,1)S(1)}, u32[]{:S(2)}, u32[]{:S(2)}) collective-permute-start(bf16[12,32,128]{2,1,0:T(8,128)(2,1)S(1)} %get-tuple-element.41), channel_id=1, source_target_pairs={{1,2},{2,1},{5,6},{6,5},{9,10},{10,9},{13,14},{14,13},{17,18},{18,... | collective-permute-start | bytes 294920 | tf_op jit(solution)/shard_map/ppermute | solution.py:19
  44.5 0.5 collective-permute-done.10
  45.0 1.6 %collective-permute-start.11 = (f32[32,384]{1,0:T(8,128)S(1)}, f32[32,384]{1,0:T(8,128)S(1)}, u32[]{:S(2)}, u32[]{:S(2)}) collective-permute-start(f32[32,384]{1,0:T(8,128)S(1)} %add.27), channel_id=1, source_target_pairs={{0,8},{4,12},{8,0},{12,4},{16,24},{20,28},{24,16},{28,20},{1,9},{5... | collective-permute-start | bytes 147464 | tf_op jit(solution)/shard_map/ppermute | solution.py:29
  46.6 2.5 %collective-permute-done.11 = f32[32,384]{1,0:T(8,128)S(1)} collective-permute-done((f32[32,384]{1,0:T(8,128)S(1)}, f32[32,384]{1,0:T(8,128)S(1)}, u32[]{:S(2)}, u32[]{:S(2)}) %collective-permute-start.11) | collective-permute-done | bytes 49184 | tf_op jit(solution)/shard_map/ppermute | solution.py:29
  49.2 3.5 %collective-permute-start.12 = (f32[32,384]{1,0:T(8,128)S(1)}, f32[32,384]{1,0:T(8,128)S(1)}, u32[]{:S(2)}, u32[]{:S(2)}) collective-permute-start(f32[32,384]{1,0:T(8,128)S(1)} %add.28.one_ref), channel_id=1, source_target_pairs={{0,16},{4,20},{8,24},{12,28},{16,0},{20,4},{24,8},{28,12},{1,17},{... | collective-permute-start | bytes 147464 | tf_op jit(solution)/shard_map/ppermute | solution.py:29
  52.6 0.0 collective-permute-done.6.one_ref
  52.6 0.0 collective-permute-done.7.two_ref
  52.6 4.1 %shard_map.80 = bf16[32,64,128]{2,1,0:T(8,128)(2,1)} custom-call(s32[2]{0:T(128)S(1)} %pad_add_fusion.odd_ref, bf16[64,32,128]{2,1,0:T(8,128)(2,1)S(1)} %get-tuple-element.34.grad_ref.own_ref, bf16[2,16,32,128]{3,2,1,0:T(8,128)(2,1)S(1)} %get-tuple-element.39.outer_ref, bf16[12,32,128]{2,1,0:T(8,128)(2,1)S(1)} %collective-permute-done.6.one_ref, ...), custom_call_target="tpu_custom_call" | custom-call | flops 150994944 | bytes 1525768 | tf_op jit(solution)/shard_map/pallas_call | solution.py:265
  56.8 0.0 collective-permute-done.12.other_ref
  56.8 0.8 %shard_map.81 = (f32[3,3,32,32]{3,2,1,0:T(8,128)}, f32[1,32]{1,0:T(1,128)}) custom-call(f32[32,384]{1,0:T(8,128)S(1)} %add.28.one_ref, f32[32,384]{1,0:T(8,128)S(1)} %collective-permute-done.12.other_ref), custom_call_target="tpu_custom_call" | custom-call | bytes 135296 | tf_op jit(solution)/shard_map/pallas_call | solution.py:265
  (4 shorter events, 0.0 us)
Async XLA Ops:
  1.6 9.0 %collective-permute-start = (bf16[32,16,128]{2,1,0:T(8,128)(2,1)S(1)}, bf16[32,16,128]{2,1,0:T(8,128)(2,1)S(1)}, u32[]{:S(2)}, u32[]{:S(2)}) collective-permute-start(bf16[32,16,128]{2,1,0:T(8,128)(2,1)S(1)} %constant_dynamic-slice_fusion), channel_id=1, source_target_pairs={{0,4},{4,0},{8,12},{12,8},{16,20},{20,16},{24,28},{28,24},{1,5},{5... | collective-permute-start | bytes 393224 | tf_op jit(solution)/shard_map/ppermute | solution.py:19
  7.5 1.0 %copy-start = (bf16[32,64,128]{2,1,0:T(8,128)(2,1)S(1)}, bf16[32,64,128]{2,1,0:T(8,128)(2,1)}, u32[]{:S(2)}) copy-start(bf16[32,64,128]{2,1,0:T(8,128)(2,1)} %image_ref.1) | copy-start | bytes 1572868
  9.9 0.7 %collective-permute-start.1 = (bf16[32,16,128]{2,1,0:T(8,128)(2,1)S(1)}, bf16[32,16,128]{2,1,0:T(8,128)(2,1)S(1)}, u32[]{:S(2)}, u32[]{:S(2)}) collective-permute-start(bf16[32,16,128]{2,1,0:T(8,128)(2,1)S(1)} %get-tuple-element.26), channel_id=1, source_target_pairs={{4,8},{8,4},{12,16},{16,12},{20,24},{24,20},{5,9},{9,5},{13,17},{1... | collective-permute-start | bytes 393224 | tf_op jit(solution)/shard_map/ppermute | solution.py:19
  11.5 1.4 %collective-permute-start.2 = (bf16[12,32,128]{2,1,0:T(8,128)(2,1)S(1)}, bf16[12,32,128]{2,1,0:T(8,128)(2,1)S(1)}, u32[]{:S(2)}, u32[]{:S(2)}) collective-permute-start(bf16[12,32,128]{2,1,0:T(8,128)(2,1)S(1)} %get-tuple-element.29), channel_id=1, source_target_pairs={{0,1},{1,0},{2,3},{3,2},{4,5},{5,4},{6,7},{7,6},{8,9},{9,8},{10,11... | collective-permute-start | bytes 294920 | tf_op jit(solution)/shard_map/ppermute | solution.py:19
  11.6 1.3 %collective-permute-start.3 = (bf16[12,32,128]{2,1,0:T(8,128)(2,1)S(1)}, bf16[12,32,128]{2,1,0:T(8,128)(2,1)S(1)}, u32[]{:S(2)}, u32[]{:S(2)}) collective-permute-start(bf16[12,32,128]{2,1,0:T(8,128)(2,1)S(1)} %get-tuple-element.30), channel_id=1, source_target_pairs={{1,2},{2,1},{5,6},{6,5},{9,10},{10,9},{13,14},{14,13},{17,18},{18,... | collective-permute-start | bytes 294920 | tf_op jit(solution)/shard_map/ppermute | solution.py:19
  12.8 1.0 %copy-start.1 = (bf16[32,64,128]{2,1,0:T(8,128)(2,1)S(1)}, bf16[32,64,128]{2,1,0:T(8,128)(2,1)}, u32[]{:S(2)}) copy-start(bf16[32,64,128]{2,1,0:T(8,128)(2,1)} %cotangent_ref.1) | copy-start | bytes 1572868
  21.0 13.3 %collective-permute-start.8 = (f32[32,384]{1,0:T(8,128)S(1)}, f32[32,384]{1,0:T(8,128)S(1)}, u32[]{:S(2)}, u32[]{:S(2)}) collective-permute-start(f32[32,384]{1,0:T(8,128)S(1)} %get-tuple-element.43), channel_id=1, source_target_pairs={{0,1},{1,0},{2,3},{3,2},{4,5},{5,4},{6,7},{7,6},{8,9},{9,8},{10,11... | collective-permute-start | bytes 147464 | tf_op jit(solution)/shard_map/ppermute | solution.py:29
  26.2 16.8 %collective-permute-start.4 = (bf16[16,32,128]{2,1,0:T(8,128)(2,1)S(1)}, bf16[16,32,128]{2,1,0:T(8,128)(2,1)S(1)}, u32[]{:S(2)}, u32[]{:S(2)}) collective-permute-start(bf16[16,32,128]{2,1,0:T(8,128)(2,1)S(1)} %get-tuple-element.35), channel_id=1, source_target_pairs={{0,4},{4,0},{8,12},{12,8},{16,20},{20,16},{24,28},{28,24},{1,5},{5... | collective-permute-start | bytes 393224 | tf_op jit(solution)/shard_map/ppermute | solution.py:19
  33.6 9.3 %collective-permute-start.5 = (bf16[16,32,128]{2,1,0:T(8,128)(2,1)S(1)}, bf16[16,32,128]{2,1,0:T(8,128)(2,1)S(1)}, u32[]{:S(2)}, u32[]{:S(2)}) collective-permute-start(bf16[16,32,128]{2,1,0:T(8,128)(2,1)S(1)} %get-tuple-element.37), channel_id=1, source_target_pairs={{4,8},{8,4},{12,16},{16,12},{20,24},{24,20},{5,9},{9,5},{13,17},{1... | collective-permute-start | bytes 393224 | tf_op jit(solution)/shard_map/ppermute | solution.py:19
  34.3 4.2 %collective-permute-start.9 = (f32[32,384]{1,0:T(8,128)S(1)}, f32[32,384]{1,0:T(8,128)S(1)}, u32[]{:S(2)}, u32[]{:S(2)}) collective-permute-start(f32[32,384]{1,0:T(8,128)S(1)} %add.25), channel_id=1, source_target_pairs={{0,2},{1,3},{2,0},{3,1},{4,6},{5,7},{6,4},{7,5},{8,10},{9,11},{10,... | collective-permute-start | bytes 147464 | tf_op jit(solution)/shard_map/ppermute | solution.py:29
  38.5 6.5 %collective-permute-start.10 = (f32[32,384]{1,0:T(8,128)S(1)}, f32[32,384]{1,0:T(8,128)S(1)}, u32[]{:S(2)}, u32[]{:S(2)}) collective-permute-start(f32[32,384]{1,0:T(8,128)S(1)} %add.26), channel_id=1, source_target_pairs={{0,4},{4,0},{8,12},{12,8},{16,20},{20,16},{24,28},{28,24},{1,5},{5... | collective-permute-start | bytes 147464 | tf_op jit(solution)/shard_map/ppermute | solution.py:29
  43.7 8.9 %collective-permute-start.6 = (bf16[12,32,128]{2,1,0:T(8,128)(2,1)S(1)}, bf16[12,32,128]{2,1,0:T(8,128)(2,1)S(1)}, u32[]{:S(2)}, u32[]{:S(2)}) collective-permute-start(bf16[12,32,128]{2,1,0:T(8,128)(2,1)S(1)} %get-tuple-element.40), channel_id=1, source_target_pairs={{0,1},{1,0},{2,3},{3,2},{4,5},{5,4},{6,7},{7,6},{8,9},{9,8},{10,11... | collective-permute-start | bytes 294920 | tf_op jit(solution)/shard_map/ppermute | solution.py:19
  43.8 8.8 %collective-permute-start.7 = (bf16[12,32,128]{2,1,0:T(8,128)(2,1)S(1)}, bf16[12,32,128]{2,1,0:T(8,128)(2,1)S(1)}, u32[]{:S(2)}, u32[]{:S(2)}) collective-permute-start(bf16[12,32,128]{2,1,0:T(8,128)(2,1)S(1)} %get-tuple-element.41), channel_id=1, source_target_pairs={{1,2},{2,1},{5,6},{6,5},{9,10},{10,9},{13,14},{14,13},{17,18},{18,... | collective-permute-start | bytes 294920 | tf_op jit(solution)/shard_map/ppermute | solution.py:19
  45.0 4.2 %collective-permute-start.11 = (f32[32,384]{1,0:T(8,128)S(1)}, f32[32,384]{1,0:T(8,128)S(1)}, u32[]{:S(2)}, u32[]{:S(2)}) collective-permute-start(f32[32,384]{1,0:T(8,128)S(1)} %add.27), channel_id=1, source_target_pairs={{0,8},{4,12},{8,0},{12,4},{16,24},{20,28},{24,16},{28,20},{1,9},{5... | collective-permute-start | bytes 147464 | tf_op jit(solution)/shard_map/ppermute | solution.py:29
  49.2 7.6 %collective-permute-start.12 = (f32[32,384]{1,0:T(8,128)S(1)}, f32[32,384]{1,0:T(8,128)S(1)}, u32[]{:S(2)}, u32[]{:S(2)}) collective-permute-start(f32[32,384]{1,0:T(8,128)S(1)} %add.28.one_ref), channel_id=1, source_target_pairs={{0,16},{4,20},{8,24},{12,28},{16,0},{20,4},{24,8},{28,12},{1,17},{... | collective-permute-start | bytes 147464 | tf_op jit(solution)/shard_map/ppermute | solution.py:29

commit v4 on v2

--- a/solution.py
+++ b/solution.py
@@ -23,11 +23,11 @@
     other = None
     for axis in axes:
         count = lax.axis_size(axis)
-        step = 1
-        while step < count:
+        step = count // 2
+        while step:
             value = value if other is None else value + other
             other = lax.ppermute(value, axis, [(place, place ^ step) for place in range(count)])
-            step *= 2
+            step //= 2
     return value, jnp.zeros_like(value) if other is None else other
 
 
@@ -100,31 +100,40 @@
     lax.fori_loop(0, count, body, 0)
 
 
-def rim_kernel(swap, odd_ref, one_ref, two_ref, rims_ref, send_one_ref, send_two_ref, outer_ref):
+def either(axis, body, one, two):
+    odd = lax.axis_index(axis) % 2 == 1
+    pl.when(odd)(lambda: body(one, two))
+    pl.when(jnp.logical_not(odd))(lambda: body(two, one))
+
+
+def rim_kernel(swap, one_ref, two_ref, rims_ref, send_one_ref, send_two_ref, outer_ref):
     own = rims_ref.shape[1]
     groups = (send_one_ref.shape[0] - own) // 2
-    odd_row, odd_column = odd_ref[0] == 1, odd_ref[1] == 1
-    send_one_ref[groups : groups + own] = rims_ref[1 - odd_ref[1]]
-    send_two_ref[groups : groups + own] = rims_ref[odd_ref[1]]
-
-    def store(place, first, last):
-        send_one_ref[place] = jnp.where(odd_column, first, last)
-        send_two_ref[place] = jnp.where(odd_column, last, first)
-
-    one, two = one_ref[...], two_ref[...]
-    for index, rows in enumerate((jnp.where(odd_row, one, two), jnp.where(odd_row, two, one))):
-        rows = jnp.swapaxes(rows, 0, 1) if swap else rows
-        outer_ref[index] = rows
-        pack_rows(rows, store, index * (groups + own))
-
-
-def spread(rows_of, odd, one_ref, two_ref, stack_ref, block, group_start):
-    channels, width = one_ref.shape[1:]
+
+    def order(upper_ref, lower_ref):
+        for index, ref in enumerate((upper_ref, lower_ref)):
+            outer_ref[index] = jnp.swapaxes(ref[...], 0, 1) if swap else ref[...]
+
+    def pack(send_first_ref, send_last_ref):
+        def store(place, first, last):
+            send_first_ref[place] = first
+            send_last_ref[place] = last
+
+        send_first_ref[groups : groups + own] = rims_ref[0]
+        send_last_ref[groups : groups + own] = rims_ref[1]
+        for index in range(2):
+            pack_rows(outer_ref[index], store, index * (groups + own))
+
+    either("row", order, one_ref, two_ref)
+    either("col", pack, send_one_ref, send_two_ref)
+
+
+def spread(rows_of, left_ref, right_ref, stack_ref, block, group_start):
+    channels, width = left_ref.shape[1:]
     pieces = width // DILATION
     lane = lane_of((channels, width))
     for group in range(DILATION // pieces):
-        one, two = one_ref[group_start + group], two_ref[group_start + group]
-        rims = unpack_group(jnp.where(odd, one, two), jnp.where(odd, two, one), pieces)
+        rims = unpack_group(left_ref[group_start + group], right_ref[group_start + group], pieces)
         for k in range(pieces):
             row = group * pieces + k
             value = rows_of(row)
@@ -136,31 +145,34 @@
             stack_ref[block, 2 * channels : 3 * channels, columns] = after
 
 
-def spread_all(odd_ref, own_ref, outer_ref, one_ref, two_ref, stack_ref):
+def spread_all(own_ref, outer_ref, one_ref, two_ref, stack_ref):
     count = own_ref.shape[0] // DILATION
     groups = one_ref.shape[0] // (count + 2)
-    odd = odd_ref[1] == 1
-    spread(lambda row: outer_ref[0, row], odd, one_ref, two_ref, stack_ref, 0, 0)
-
-    def body(block, carry):
-        spread(
-            lambda row: own_ref[block * DILATION + row],
-            odd, one_ref, two_ref, stack_ref, block + 1, (block + 1) * groups,
-        )
-        return carry
-
-    lax.fori_loop(0, count, body, 0)
-    spread(lambda row: outer_ref[1, row], odd, one_ref, two_ref, stack_ref, count + 1, (count + 1) * groups)
+
+    def every(left_ref, right_ref):
+        spread(lambda row: outer_ref[0, row], left_ref, right_ref, stack_ref, 0, 0)
+
+        def body(block, carry):
+            spread(
+                lambda row: own_ref[block * DILATION + row],
+                left_ref, right_ref, stack_ref, block + 1, (block + 1) * groups,
+            )
+            return carry
+
+        lax.fori_loop(0, count, body, 0)
+        spread(lambda row: outer_ref[1, row], left_ref, right_ref, stack_ref, count + 1, (count + 1) * groups)
+
+    either("col", every, one_ref, two_ref)
 
 
 def forward_kernel(
-    scale, odd_ref, own_ref, outer_ref, one_ref, two_ref, cotangent_ref, weight_ref, bias_ref,
+    scale, own_ref, outer_ref, one_ref, two_ref, cotangent_ref, weight_ref, bias_ref,
     activation_ref, grad_ref, send_one_ref, send_two_ref, rims_ref, terms_ref, stack_ref, sum_ref,
 ):
     height, channels, width = own_ref.shape
     count = height // DILATION
     groups = rims_ref.shape[1] // count
-    spread_all(odd_ref, own_ref, outer_ref, one_ref, two_ref, stack_ref)
+    spread_all(own_ref, outer_ref, one_ref, two_ref, stack_ref)
     terms_ref[...] = jnp.zeros_like(terms_ref)
     sum_ref[...] = jnp.zeros_like(sum_ref)
     depth = 9 * channels
@@ -195,18 +207,19 @@
 
     lax.fori_loop(0, count, body, 0)
     end = height - DILATION
-    send_one_ref[...] = grad_ref[pl.ds((1 - odd_ref[0]) * end, DILATION)]
-    send_two_ref[...] = grad_ref[pl.ds(odd_ref[0] * end, DILATION)]
+    odd = lax.axis_index("row") % 2
+    send_one_ref[...] = grad_ref[pl.ds((1 - odd) * end, DILATION)]
+    send_two_ref[...] = grad_ref[pl.ds(odd * end, DILATION)]
     terms_ref[:, :depth] = terms_ref[:, :depth] * scale
     sums = jnp.sum(sum_ref[...], axis=1, keepdims=True) * scale
     terms_ref[:, depth:] = jnp.broadcast_to(sums, (channels, terms_ref.shape[1] - depth))
 
 
 def backward_kernel(
-    odd_ref, own_ref, outer_ref, one_ref, two_ref, weight_ref, out_ref, stack_ref
+    own_ref, outer_ref, one_ref, two_ref, weight_ref, out_ref, stack_ref
 ):
     height, channels, width = own_ref.shape
-    spread_all(odd_ref, own_ref, outer_ref, one_ref, two_ref, stack_ref)
+    spread_all(own_ref, outer_ref, one_ref, two_ref, stack_ref)
 
     def body(block, carry):
         start = pl.multiple_of(block * DILATION, DILATION)
@@ -228,13 +241,13 @@
     bias_ref[...] = flipped[127:128, :channels]
 
 
-def call(kernel, out_shapes, operands, scratch=(), flops=0, scalars=0):
+def call(kernel, out_shapes, operands, scratch=(), flops=0):
     whole = pl.BlockSpec(memory_space=pltpu.VMEM)
     size = sum(math.prod(x.shape) * jnp.dtype(x.dtype).itemsize for x in (*operands, *out_shapes))
     return pl.pallas_call(
         kernel,
         out_shape=out_shapes,
-        in_specs=[pl.BlockSpec(memory_space=pltpu.SMEM)] * scalars + [whole] * (len(operands) - scalars),
+        in_specs=[whole] * len(operands),
         out_specs=[whole] * len(out_shapes),
         scratch_shapes=list(scratch),
         compiler_params=pltpu.CompilerParams(vmem_limit_bytes=VMEM_BYTES),
@@ -257,18 +270,17 @@
     rows = shape((height, channels, width), bf16)
     flops = 2 * depth * channels * height * width
 
-    row, column = lax.axis_index("row"), lax.axis_index("col")
-    odd = jnp.stack([row % 2, column % 2]).astype(jnp.int32)
+    odd = lax.axis_index("row") % 2
     outer = shape((2, DILATION, channels, width), bf16)
     end = height - DILATION
 
-    one = swap_pairs(lax.dynamic_slice_in_dim(image, (1 - odd[0]) * end, DILATION, 1), "row", 0)
-    two = swap_pairs(lax.dynamic_slice_in_dim(image, odd[0] * end, DILATION, 1), "row", 1)
+    one = swap_pairs(lax.dynamic_slice_in_dim(image, (1 - odd) * end, DILATION, 1), "row", 0)
+    two = swap_pairs(lax.dynamic_slice_in_dim(image, odd * end, DILATION, 1), "row", 1)
     image_rows, rims = call(own_kernel, (rows, own_rims), (image,))
     forward_weight = jnp.transpose(weight, (2, 0, 1, 3)).reshape(channels, depth)
     backward_weight = jnp.transpose(weight[::-1, ::-1], (3, 0, 1, 2)).reshape(channels, depth)
     one, two, image_outer = call(
-        functools.partial(rim_kernel, True), (packed, packed, outer), (odd, one, two, rims), scalars=1
+        functools.partial(rim_kernel, True), (packed, packed, outer), (one, two, rims)
     )
     one, two = swap_pairs(one, "col", 0), swap_pairs(two, "col", 1)
     activation, grads, one, two, rims, terms = call(
@@ -277,25 +289,23 @@
             shape(image.shape, bf16), rows, edge, edge, own_rims,
             shape((channels, -(-(depth + 1) // 128) * 128), f32),
         ),
-        (odd, image_rows, image_outer, one, two, cotangent, forward_weight, bias[:, None]),
+        (image_rows, image_outer, one, two, cotangent, forward_weight, bias[:, None]),
         (stack, pltpu.VMEM((channels, width), f32)),
         2 * flops,
-        1,
     )
     one, two = swap_pairs(one, "row", 0), swap_pairs(two, "row", 1)
     one, two, grad_outer = call(
-        functools.partial(rim_kernel, False), (packed, packed, outer), (odd, one, two, rims), scalars=1
+        functools.partial(rim_kernel, False), (packed, packed, outer), (one, two, rims)
     )
     one, two = swap_pairs(one, "col", 0), swap_pairs(two, "col", 1)
     (grad_image,) = call(
         backward_kernel,
         (shape(image.shape, bf16),),
-        (odd, grads, grad_outer, one, two, backward_weight),
+        (grads, grad_outer, one, two, backward_weight),
         (stack,),
         flops,
-        1,
-    )
-    one, other = add_pairs(terms, ("col", "row"))
+    )
+    one, other = add_pairs(terms, ("row", "col"))
     grad_weight, grad_bias = call(
         finish_kernel, (shape(weight.shape, f32), shape((1, channels), f32)), (one, other)
     )

time: 50.2 us -> 48.3 us (0.962)
  Pallas kernels: 12.9 us -> 10.8 us
    pallas_call x6, Pallas kernels: 12.9 us -> 10.8 us  [call(): pl.pallas_call(kernel, out_shape=out_shapes, in_specs=[whole] * len(opera...]
    ppermute x8, starting transfers between devices: 10.5 us -> 9.28 us  [swap_pairs(): return lax.ppermute(value, axis, pairs)]
    ppermute x5, starting transfers between devices: 15.6 us -> 16.6 us  [add_pairs(): lax.ppermute(value, axis, [(place, place ^ step) for place in range(count)])]
    ppermute x5, waiting for transfers between devices: 6.02 us -> 6.55 us  [add_pairs(): lax.ppermute(value, axis, [(place, place ^ step) for place in range(count)])]
  transfers between devices with their start and end apart: 13 -> 13, of which waited for: 4 -> 4; matrix products, arithmetic and copies ran while one was open for 1% -> 1% of each run, Pallas kernels for 11% -> 10%
where the time goes in v4:
time: 48.3 us; the launch traced here: 48 us
  starting transfers between devices  25.8 us (53%)
  Pallas kernels  10.8 us (22%)
  waiting for transfers between devices  8.45 us (17%)
  local copies, waits for them, and re-layouts  2.06 us (4%)
  between operations  0.82 us (2%)
    ppermute x5, starting transfers between devices, add_pairs(): lax.ppermute(value, axis, [(place, place ^ step) for place in range(count)])  16.6 us
    pallas_call x6, Pallas kernels, call(): pl.pallas_call(kernel, out_shape=out_shapes, in_specs=[whole] * len(opera...  10.8 us
    ppermute x8, starting transfers between devices, swap_pairs(): return lax.ppermute(value, axis, pairs)  9.28 us
    ppermute x5, waiting for transfers between devices, add_pairs(): lax.ppermute(value, axis, [(place, place ^ step) for place in range(count)])  6.55 us
    ppermute x8, waiting for transfers between devices, swap_pairs(): return lax.ppermute(value, axis, pairs)  1.9 us
    dynamic_slice x1, local copies, waits for them, and re-layouts, shards(): lax.dynamic_slice_in_dim(image, odd * end, DILATION, 1)  1.05 us
  transfers between devices with their start and end apart: 13, of which 4 were waited for; matrix products, arithmetic and copies ran while one was open for 1% of the time, Pallas kernels for 10%

profile of v4, /device:TPU:0, one launch (start us, length us, event | category | flops | bytes accessed | tf_op | source)
XLA Modules:
  0.0 48.0 jit_solution(5706495581745171995)
XLA Ops:
  0.6 0.0 copy-start
  0.7 1.1 %constant_dynamic-slice_fusion = (bf16[32,16,128]{2,1,0:T(8,128)(2,1)S(1)}, bf16[32,16,128]{2,1,0:T(8,128)(2,1)S(1)}) fusion(bf16[32,64,128]{2,1,0:T(8,128)(2,1)} %image_ref.1, s32[]{:T(128)S(6)} %select_n.15, s32[]{:T(128)S(6)} %select_n.14), kind=kLoop, calls=%fused_computation | loop fusion | bytes 524296 | tf_op jit(solution)/shard_map/dynamic_slice | solution.py:278
  1.7 3.0 %collective-permute-start = (bf16[32,16,128]{2,1,0:T(8,128)(2,1)S(1)}, bf16[32,16,128]{2,1,0:T(8,128)(2,1)S(1)}, u32[]{:S(2)}, u32[]{:S(2)}) collective-permute-start(bf16[32,16,128]{2,1,0:T(8,128)(2,1)S(1)} %get-tuple-element.37), channel_id=1, source_target_pairs={{0,4},{4,0},{8,12},{12,8},{16,20},{20,16},{24,28},{28,24},{1,5},{5... | collective-permute-start | bytes 393224 | tf_op jit(solution)/shard_map/ppermute | solution.py:19
  4.7 0.0 copy-start.1
  4.8 0.8 %collective-permute-start.1 = (bf16[32,16,128]{2,1,0:T(8,128)(2,1)S(1)}, bf16[32,16,128]{2,1,0:T(8,128)(2,1)S(1)}, u32[]{:S(2)}, u32[]{:S(2)}) collective-permute-start(bf16[32,16,128]{2,1,0:T(8,128)(2,1)S(1)} %get-tuple-element.36), channel_id=1, source_target_pairs={{4,8},{8,4},{12,16},{16,12},{20,24},{24,20},{5,9},{9,5},{13,17},{1... | collective-permute-start | bytes 393224 | tf_op jit(solution)/shard_map/ppermute | solution.py:19
  5.5 0.0 copy-done
  5.6 0.8 %shard_map.75 = (bf16[64,32,128]{2,1,0:T(8,128)(2,1)S(1)}, bf16[2,8,32,128]{3,2,1,0:T(8,128)(2,1)S(1)}) custom-call(bf16[32,64,128]{2,1,0:T(8,128)(2,1)S(1)} %copy-done), custom_call_target="tpu_custom_call" | custom-call | bytes 1179648 | tf_op jit(solution)/shard_map/pallas_call | solution.py:247
  6.4 1.9 %collective-permute-done.one_ref = bf16[32,16,128]{2,1,0:T(8,128)(2,1)S(1)} collective-permute-done((bf16[32,16,128]{2,1,0:T(8,128)(2,1)S(1)}, bf16[32,16,128]{2,1,0:T(8,128)(2,1)S(1)}, u32[]{:S(2)}, u32[]{:S(2)}) %collective-permute-start) | collective-permute-done | bytes 131104 | tf_op jit(solution)/shard_map/ppermute | solution.py:19
  8.2 0.0 collective-permute-done.1.two_ref
  8.2 0.0 copy-start.2
  8.3 0.3 shard_map.76
  8.5 0.1 collective-permute-start.2
  8.6 0.7 %collective-permute-start.3 = (bf16[12,32,128]{2,1,0:T(8,128)(2,1)S(1)}, bf16[12,32,128]{2,1,0:T(8,128)(2,1)S(1)}, u32[]{:S(2)}, u32[]{:S(2)}) collective-permute-start(bf16[12,32,128]{2,1,0:T(8,128)(2,1)S(1)} %get-tuple-element.24), channel_id=1, source_target_pairs={{1,2},{2,1},{5,6},{6,5},{9,10},{10,9},{13,14},{14,13},{17,18},{18,... | collective-permute-start | bytes 294920 | tf_op jit(solution)/shard_map/ppermute | solution.py:19
  9.3 0.0 copy-done.2
  9.3 0.1 copy.11
  9.4 0.1 reshape.17.weight_ref
  9.5 0.0 copy-start.3
  9.5 0.6 %copy-done.3 = f32[32]{0:T(128)S(1)} copy-done((f32[32]{0:T(128)S(1)}, f32[32]{0:T(128)}, u32[]{:S(2)}) %copy-start.3) | copy-done | bytes 152
  10.1 0.1 copy.12.bias_ref
  10.2 0.0 collective-permute-done.2.one_ref
  10.2 0.0 collective-permute-done.3.two_ref
  10.2 0.0 copy-done.1
  10.2 5.1 %shard_map.77 = (bf16[32,64,128]{2,1,0:T(8,128)(2,1)}, bf16[64,32,128]{2,1,0:T(8,128)(2,1)S(1)}, bf16[16,32,128]{2,1,0:T(8,128)(2,1)S(1)}, bf16[16,32,128]{2,1,0...) custom-call(bf16[64,32,128]{2,1,0:T(8,128)(2,1)S(1)} %get-tuple-element.20.own_ref, ...), custom_call_target="tpu_custom_call" | custom-call | flops 301989888 | bytes 3016832 | tf_op jit(solution)/shard_map/pallas_call | solution.py:247
  15.4 7.0 %collective-permute-start.8 = (f32[32,384]{1,0:T(8,128)S(1)}, f32[32,384]{1,0:T(8,128)S(1)}, u32[]{:S(2)}, u32[]{:S(2)}) collective-permute-start(f32[32,384]{1,0:T(8,128)S(1)} %get-tuple-element.33), channel_id=1, source_target_pairs={{0,16},{4,20},{8,24},{12,28},{16,0},{20,4},{24,8},{28,12},{1,17},{... | collective-permute-start | bytes 147464 | tf_op jit(solution)/shard_map/ppermute | solution.py:29
  22.3 0.5 %collective-permute-start.4 = (bf16[16,32,128]{2,1,0:T(8,128)(2,1)S(1)}, bf16[16,32,128]{2,1,0:T(8,128)(2,1)S(1)}, u32[]{:S(2)}, u32[]{:S(2)}) collective-permute-start(bf16[16,32,128]{2,1,0:T(8,128)(2,1)S(1)} %get-tuple-element.27), channel_id=1, source_target_pairs={{0,4},{4,0},{8,12},{12,8},{16,20},{20,16},{24,28},{28,24},{1,5},{5... | collective-permute-start | bytes 393224 | tf_op jit(solution)/shard_map/ppermute | solution.py:19
  22.9 0.7 %collective-permute-start.5 = (bf16[16,32,128]{2,1,0:T(8,128)(2,1)S(1)}, bf16[16,32,128]{2,1,0:T(8,128)(2,1)S(1)}, u32[]{:S(2)}, u32[]{:S(2)}) collective-permute-start(bf16[16,32,128]{2,1,0:T(8,128)(2,1)S(1)} %get-tuple-element.28), channel_id=1, source_target_pairs={{4,8},{8,4},{12,16},{16,12},{20,24},{24,20},{5,9},{9,5},{13,17},{1... | collective-permute-start | bytes 393224 | tf_op jit(solution)/shard_map/ppermute | solution.py:19
  23.5 0.9 %collective-permute-done.8 = f32[32,384]{1,0:T(8,128)S(1)} collective-permute-done((f32[32,384]{1,0:T(8,128)S(1)}, f32[32,384]{1,0:T(8,128)S(1)}, u32[]{:S(2)}, u32[]{:S(2)}) %collective-permute-start.8) | collective-permute-done | bytes 49184 | tf_op jit(solution)/shard_map/ppermute | solution.py:29
  24.4 3.4 %collective-permute-start.9 = (f32[32,384]{1,0:T(8,128)S(1)}, f32[32,384]{1,0:T(8,128)S(1)}, u32[]{:S(2)}, u32[]{:S(2)}) collective-permute-start(f32[32,384]{1,0:T(8,128)S(1)} %add.25), channel_id=1, source_target_pairs={{0,8},{4,12},{8,0},{12,4},{16,24},{20,28},{24,16},{28,20},{1,9},{5... | collective-permute-start | bytes 147464 | tf_op jit(solution)/shard_map/ppermute | solution.py:29
  27.8 3.4 %collective-permute-done.9 = f32[32,384]{1,0:T(8,128)S(1)} collective-permute-done((f32[32,384]{1,0:T(8,128)S(1)}, f32[32,384]{1,0:T(8,128)S(1)}, u32[]{:S(2)}, u32[]{:S(2)}) %collective-permute-start.9) | collective-permute-done | bytes 49184 | tf_op jit(solution)/shard_map/ppermute | solution.py:29
  31.2 0.3 collective-permute-start.10
  31.6 0.0 collective-permute-done.4.one_ref
  31.6 0.0 collective-permute-done.5.two_ref
  31.6 0.2 shard_map.78
  31.8 2.9 %collective-permute-start.6 = (bf16[12,32,128]{2,1,0:T(8,128)(2,1)S(1)}, bf16[12,32,128]{2,1,0:T(8,128)(2,1)S(1)}, u32[]{:S(2)}, u32[]{:S(2)}) collective-permute-start(bf16[12,32,128]{2,1,0:T(8,128)(2,1)S(1)} %get-tuple-element.31), channel_id=1, source_target_pairs={{0,1},{1,0},{2,3},{3,2},{4,5},{5,4},{6,7},{7,6},{8,9},{9,8},{10,11... | collective-permute-start | bytes 294920 | tf_op jit(solution)/shard_map/ppermute | solution.py:19
  34.7 0.7 %collective-permute-start.7 = (bf16[12,32,128]{2,1,0:T(8,128)(2,1)S(1)}, bf16[12,32,128]{2,1,0:T(8,128)(2,1)S(1)}, u32[]{:S(2)}, u32[]{:S(2)}) collective-permute-start(bf16[12,32,128]{2,1,0:T(8,128)(2,1)S(1)} %get-tuple-element.32), channel_id=1, source_target_pairs={{1,2},{2,1},{5,6},{6,5},{9,10},{10,9},{13,14},{14,13},{17,18},{18,... | collective-permute-start | bytes 294920 | tf_op jit(solution)/shard_map/ppermute | solution.py:19
  35.4 0.0 collective-permute-done.10
  35.4 5.8 %collective-permute-start.11 = (f32[32,384]{1,0:T(8,128)S(1)}, f32[32,384]{1,0:T(8,128)S(1)}, u32[]{:S(2)}, u32[]{:S(2)}) collective-permute-start(f32[32,384]{1,0:T(8,128)S(1)} %add.27), channel_id=1, source_target_pairs={{0,2},{1,3},{2,0},{3,1},{4,6},{5,7},{6,4},{7,5},{8,10},{9,11},{10,... | collective-permute-start | bytes 147464 | tf_op jit(solution)/shard_map/ppermute | solution.py:29
  41.2 2.2 %collective-permute-done.11 = f32[32,384]{1,0:T(8,128)S(1)} collective-permute-done((f32[32,384]{1,0:T(8,128)S(1)}, f32[32,384]{1,0:T(8,128)S(1)}, u32[]{:S(2)}, u32[]{:S(2)}) %collective-permute-start.11) | collective-permute-done | bytes 49184 | tf_op jit(solution)/shard_map/ppermute | solution.py:29
  43.4 0.1 collective-permute-start.12
  43.5 0.1 copy.14.weight_ref
  43.6 0.0 collective-permute-done.6.one_ref
  43.6 0.0 collective-permute-done.7.two_ref
  43.6 3.6 %shard_map.79 = bf16[32,64,128]{2,1,0:T(8,128)(2,1)} custom-call(bf16[64,32,128]{2,1,0:T(8,128)(2,1)S(1)} %get-tuple-element.26.own_ref, bf16[2,16,32,128]{3,2,1,0:T(8,128)(2,1)S(1)} %get-tuple-element.30.outer_ref, bf16[12,32,128]{2,1,0:T(8,128)(2,1)S(1)} %collective-permute-done.6.one_ref, bf16[12,32,128]{2,1,0:T(8,128)(2,1)S(1)} %collective-permute-done.7.two_ref, ...), custom_call_target="tpu_custom_call" | custom-call | flops 150994944 | bytes 1525760 | tf_op jit(solution)/shard_map/pallas_call | solution.py:247
  47.2 0.0 collective-permute-done.12.other_ref
  47.3 0.8 %shard_map.80 = (f32[3,3,32,32]{3,2,1,0:T(8,128)}, f32[1,32]{1,0:T(1,128)}) custom-call(f32[32,384]{1,0:T(8,128)S(1)} %add.28.one_ref, f32[32,384]{1,0:T(8,128)S(1)} %collective-permute-done.12.other_ref), custom_call_target="tpu_custom_call" | custom-call | bytes 135296 | tf_op jit(solution)/shard_map/pallas_call | solution.py:247
  (5 shorter events, 0.0 us)
Async XLA Ops:
  0.6 4.9 %copy-start = (bf16[32,64,128]{2,1,0:T(8,128)(2,1)S(1)}, bf16[32,64,128]{2,1,0:T(8,128)(2,1)}, u32[]{:S(2)}) copy-start(bf16[32,64,128]{2,1,0:T(8,128)(2,1)} %image_ref.1) | copy-start | bytes 1572868
  1.7 6.5 %collective-permute-start = (bf16[32,16,128]{2,1,0:T(8,128)(2,1)S(1)}, bf16[32,16,128]{2,1,0:T(8,128)(2,1)S(1)}, u32[]{:S(2)}, u32[]{:S(2)}) collective-permute-start(bf16[32,16,128]{2,1,0:T(8,128)(2,1)S(1)} %get-tuple-element.37), channel_id=1, source_target_pairs={{0,4},{4,0},{8,12},{12,8},{16,20},{20,16},{24,28},{28,24},{1,5},{5... | collective-permute-start | bytes 393224 | tf_op jit(solution)/shard_map/ppermute | solution.py:19
  4.7 5.5 %copy-start.1 = (bf16[32,64,128]{2,1,0:T(8,128)(2,1)S(1)}, bf16[32,64,128]{2,1,0:T(8,128)(2,1)}, u32[]{:S(2)}) copy-start(bf16[32,64,128]{2,1,0:T(8,128)(2,1)} %cotangent_ref.1) | copy-start | bytes 1572868
  4.8 3.5 %collective-permute-start.1 = (bf16[32,16,128]{2,1,0:T(8,128)(2,1)S(1)}, bf16[32,16,128]{2,1,0:T(8,128)(2,1)S(1)}, u32[]{:S(2)}, u32[]{:S(2)}) collective-permute-start(bf16[32,16,128]{2,1,0:T(8,128)(2,1)S(1)} %get-tuple-element.36), channel_id=1, source_target_pairs={{4,8},{8,4},{12,16},{16,12},{20,24},{24,20},{5,9},{9,5},{13,17},{1... | collective-permute-start | bytes 393224 | tf_op jit(solution)/shard_map/ppermute | solution.py:19
  8.2 1.1 %copy-start.2 = (bf16[3,3,32,32]{3,2,1,0:T(8,128)(2,1)S(1)}, bf16[3,3,32,32]{3,2,1,0:T(8,128)(2,1)}, u32[]{:S(2)}) copy-start(bf16[3,3,32,32]{3,2,1,0:T(8,128)(2,1)} %param.5) | copy-start | bytes 55300
  8.5 1.7 %collective-permute-start.2 = (bf16[12,32,128]{2,1,0:T(8,128)(2,1)S(1)}, bf16[12,32,128]{2,1,0:T(8,128)(2,1)S(1)}, u32[]{:S(2)}, u32[]{:S(2)}) collective-permute-start(bf16[12,32,128]{2,1,0:T(8,128)(2,1)S(1)} %get-tuple-element.23), channel_id=1, source_target_pairs={{0,1},{1,0},{2,3},{3,2},{4,5},{5,4},{6,7},{7,6},{8,9},{9,8},{10,11... | collective-permute-start | bytes 294920 | tf_op jit(solution)/shard_map/ppermute | solution.py:19
  8.6 1.6 %collective-permute-start.3 = (bf16[12,32,128]{2,1,0:T(8,128)(2,1)S(1)}, bf16[12,32,128]{2,1,0:T(8,128)(2,1)S(1)}, u32[]{:S(2)}, u32[]{:S(2)}) collective-permute-start(bf16[12,32,128]{2,1,0:T(8,128)(2,1)S(1)} %get-tuple-element.24), channel_id=1, source_target_pairs={{1,2},{2,1},{5,6},{6,5},{9,10},{10,9},{13,14},{14,13},{17,18},{18,... | collective-permute-start | bytes 294920 | tf_op jit(solution)/shard_map/ppermute | solution.py:19
  9.5 0.7 %copy-start.3 = (f32[32]{0:T(128)S(1)}, f32[32]{0:T(128)}, u32[]{:S(2)}) copy-start(f32[32]{0:T(128)} %param.6) | copy-start | bytes 388
  15.4 9.0 %collective-permute-start.8 = (f32[32,384]{1,0:T(8,128)S(1)}, f32[32,384]{1,0:T(8,128)S(1)}, u32[]{:S(2)}, u32[]{:S(2)}) collective-permute-start(f32[32,384]{1,0:T(8,128)S(1)} %get-tuple-element.33), channel_id=1, source_target_pairs={{0,16},{4,20},{8,24},{12,28},{16,0},{20,4},{24,8},{28,12},{1,17},{... | collective-permute-start | bytes 147464 | tf_op jit(solution)/shard_map/ppermute | solution.py:29
  22.3 9.2 %collective-permute-start.4 = (bf16[16,32,128]{2,1,0:T(8,128)(2,1)S(1)}, bf16[16,32,128]{2,1,0:T(8,128)(2,1)S(1)}, u32[]{:S(2)}, u32[]{:S(2)}) collective-permute-start(bf16[16,32,128]{2,1,0:T(8,128)(2,1)S(1)} %get-tuple-element.27), channel_id=1, source_target_pairs={{0,4},{4,0},{8,12},{12,8},{16,20},{20,16},{24,28},{28,24},{1,5},{5... | collective-permute-start | bytes 393224 | tf_op jit(solution)/shard_map/ppermute | solution.py:19
  22.9 8.7 %collective-permute-start.5 = (bf16[16,32,128]{2,1,0:T(8,128)(2,1)S(1)}, bf16[16,32,128]{2,1,0:T(8,128)(2,1)S(1)}, u32[]{:S(2)}, u32[]{:S(2)}) collective-permute-start(bf16[16,32,128]{2,1,0:T(8,128)(2,1)S(1)} %get-tuple-element.28), channel_id=1, source_target_pairs={{4,8},{8,4},{12,16},{16,12},{20,24},{24,20},{5,9},{9,5},{13,17},{1... | collective-permute-start | bytes 393224 | tf_op jit(solution)/shard_map/ppermute | solution.py:19
  24.4 6.8 %collective-permute-start.9 = (f32[32,384]{1,0:T(8,128)S(1)}, f32[32,384]{1,0:T(8,128)S(1)}, u32[]{:S(2)}, u32[]{:S(2)}) collective-permute-start(f32[32,384]{1,0:T(8,128)S(1)} %add.25), channel_id=1, source_target_pairs={{0,8},{4,12},{8,0},{12,4},{16,24},{20,28},{24,16},{28,20},{1,9},{5... | collective-permute-start | bytes 147464 | tf_op jit(solution)/shard_map/ppermute | solution.py:29
  31.2 4.2 %collective-permute-start.10 = (f32[32,384]{1,0:T(8,128)S(1)}, f32[32,384]{1,0:T(8,128)S(1)}, u32[]{:S(2)}, u32[]{:S(2)}) collective-permute-start(f32[32,384]{1,0:T(8,128)S(1)} %add.26), channel_id=1, source_target_pairs={{0,4},{4,0},{8,12},{12,8},{16,20},{20,16},{24,28},{28,24},{1,5},{5... | collective-permute-start | bytes 147464 | tf_op jit(solution)/shard_map/ppermute | solution.py:29
  31.8 11.8 %collective-permute-start.6 = (bf16[12,32,128]{2,1,0:T(8,128)(2,1)S(1)}, bf16[12,32,128]{2,1,0:T(8,128)(2,1)S(1)}, u32[]{:S(2)}, u32[]{:S(2)}) collective-permute-start(bf16[12,32,128]{2,1,0:T(8,128)(2,1)S(1)} %get-tuple-element.31), channel_id=1, source_target_pairs={{0,1},{1,0},{2,3},{3,2},{4,5},{5,4},{6,7},{7,6},{8,9},{9,8},{10,11... | collective-permute-start | bytes 294920 | tf_op jit(solution)/shard_map/ppermute | solution.py:19
  34.7 8.9 %collective-permute-start.7 = (bf16[12,32,128]{2,1,0:T(8,128)(2,1)S(1)}, bf16[12,32,128]{2,1,0:T(8,128)(2,1)S(1)}, u32[]{:S(2)}, u32[]{:S(2)}) collective-permute-start(bf16[12,32,128]{2,1,0:T(8,128)(2,1)S(1)} %get-tuple-element.32), channel_id=1, source_target_pairs={{1,2},{2,1},{5,6},{6,5},{9,10},{10,9},{13,14},{14,13},{17,18},{18,... | collective-permute-start | bytes 294920 | tf_op jit(solution)/shard_map/ppermute | solution.py:19
  35.4 8.0 %collective-permute-start.11 = (f32[32,384]{1,0:T(8,128)S(1)}, f32[32,384]{1,0:T(8,128)S(1)}, u32[]{:S(2)}, u32[]{:S(2)}) collective-permute-start(f32[32,384]{1,0:T(8,128)S(1)} %add.27), channel_id=1, source_target_pairs={{0,2},{1,3},{2,0},{3,1},{4,6},{5,7},{6,4},{7,5},{8,10},{9,11},{10,... | collective-permute-start | bytes 147464 | tf_op jit(solution)/shard_map/ppermute | solution.py:29
  43.4 3.8 %collective-permute-start.12 = (f32[32,384]{1,0:T(8,128)S(1)}, f32[32,384]{1,0:T(8,128)S(1)}, u32[]{:S(2)}, u32[]{:S(2)}) collective-permute-start(f32[32,384]{1,0:T(8,128)S(1)} %add.28.one_ref), channel_id=1, source_target_pairs={{0,1},{1,0},{2,3},{3,2},{4,5},{5,4},{6,7},{7,6},{8,9},{9,8},{10,11... | collective-permute-start | bytes 147464 | tf_op jit(solution)/shard_map/ppermute | solution.py:29

commit v5 on v4

--- a/solution.py
+++ b/solution.py
@@ -19,16 +19,15 @@
     return lax.ppermute(value, axis, pairs)
 
 
-def add_pairs(value, axes):
-    other = None
-    for axis in axes:
-        count = lax.axis_size(axis)
-        step = count // 2
-        while step:
-            value = value if other is None else value + other
-            other = lax.ppermute(value, axis, [(place, place ^ step) for place in range(count)])
-            step //= 2
-    return value, jnp.zeros_like(value) if other is None else other
+def add_pairs(value, near_axis, far_axis):
+    near, far = lax.axis_size(near_axis), lax.axis_size(far_axis)
+    steps = [(near_axis, 2**k) for k in range(near.bit_length() - 1)]
+    steps += [(far_axis, 2**k) for k in reversed(range(far.bit_length() - 1))]
+    other = jnp.zeros_like(value)
+    for place, (axis, step) in enumerate(steps):
+        value = value + other if place else value
+        other = lax.ppermute(value, axis, [(at, at ^ step) for at in range(lax.axis_size(axis))])
+    return value, other
 
 
 def gelu_pair(preact):
@@ -282,7 +281,7 @@
     one, two, image_outer = call(
         functools.partial(rim_kernel, True), (packed, packed, outer), (one, two, rims)
     )
-    one, two = swap_pairs(one, "col", 0), swap_pairs(two, "col", 1)
+    two, one = swap_pairs(two, "col", 1), swap_pairs(one, "col", 0)
     activation, grads, one, two, rims, terms = call(
         functools.partial(forward_kernel, scale),
         (
@@ -297,7 +296,7 @@
     one, two, grad_outer = call(
         functools.partial(rim_kernel, False), (packed, packed, outer), (one, two, rims)
     )
-    one, two = swap_pairs(one, "col", 0), swap_pairs(two, "col", 1)
+    two, one = swap_pairs(two, "col", 1), swap_pairs(one, "col", 0)
     (grad_image,) = call(
         backward_kernel,
         (shape(image.shape, bf16),),
@@ -305,7 +304,7 @@
         (stack,),
         flops,
     )
-    one, other = add_pairs(terms, ("row", "col"))
+    one, other = add_pairs(terms, "col", "row")
     grad_weight, grad_bias = call(
         finish_kernel, (shape(weight.shape, f32), shape((1, channels), f32)), (one, other)
     )

time: 48.3 us -> 48.2 us (level)
    ppermute x5, starting transfers between devices: 16.6 us -> 14.9 us  [add_pairs(): lax.ppermute(value, axis, [(at, at ^ step) for at in range(lax.axis_size(...]
    ppermute x8, starting transfers between devices: 9.28 us -> 10.7 us  [swap_pairs(): return lax.ppermute(value, axis, pairs)]
where the time goes in v5:
time: 48.2 us; the launch traced here: 48 us
  starting transfers between devices  25.6 us (53%)
  Pallas kernels  10.8 us (22%)
  waiting for transfers between devices  8.66 us (18%)
  local copies, waits for them, and re-layouts  2.06 us (4%)
  between operations  0.83 us (2%)
    ppermute x5, starting transfers between devices, add_pairs(): lax.ppermute(value, axis, [(at, at ^ step) for at in range(lax.axis_size(...  14.9 us
    pallas_call x6, Pallas kernels, call(): pl.pallas_call(kernel, out_shape=out_shapes, in_specs=[whole] * len(opera...  10.8 us
    ppermute x8, starting transfers between devices, swap_pairs(): return lax.ppermute(value, axis, pairs)  10.7 us
    ppermute x5, waiting for transfers between devices, add_pairs(): lax.ppermute(value, axis, [(at, at ^ step) for at in range(lax.axis_size(...  6.75 us
    ppermute x8, waiting for transfers between devices, swap_pairs(): return lax.ppermute(value, axis, pairs)  1.9 us
    dynamic_slice x1, local copies, waits for them, and re-layouts, shards(): lax.dynamic_slice_in_dim(image, odd * end, DILATION, 1)  1.05 us
  transfers between devices with their start and end apart: 13, of which 4 were waited for; matrix products, arithmetic and copies ran while one was open for 1% of the time, Pallas kernels for 10%

profile of v5, /device:TPU:0, one launch (start us, length us, event | category | flops | bytes accessed | tf_op | source)
XLA Modules:
  0.0 48.0 jit_solution(881039402102947075)
XLA Ops:
  0.6 0.0 copy-start
  0.7 1.1 %constant_dynamic-slice_fusion = (bf16[32,16,128]{2,1,0:T(8,128)(2,1)S(1)}, bf16[32,16,128]{2,1,0:T(8,128)(2,1)S(1)}) fusion(bf16[32,64,128]{2,1,0:T(8,128)(2,1)} %image_ref.1, s32[]{:T(128)S(6)} %select_n.15, s32[]{:T(128)S(6)} %select_n.14), kind=kLoop, calls=%fused_computation | loop fusion | bytes 524296 | tf_op jit(solution)/shard_map/dynamic_slice | solution.py:277
  1.7 3.0 %collective-permute-start = (bf16[32,16,128]{2,1,0:T(8,128)(2,1)S(1)}, bf16[32,16,128]{2,1,0:T(8,128)(2,1)S(1)}, u32[]{:S(2)}, u32[]{:S(2)}) collective-permute-start(bf16[32,16,128]{2,1,0:T(8,128)(2,1)S(1)} %get-tuple-element.37), channel_id=1, source_target_pairs={{0,4},{4,0},{8,12},{12,8},{16,20},{20,16},{24,28},{28,24},{1,5},{5... | collective-permute-start | bytes 393224 | tf_op jit(solution)/shard_map/ppermute | solution.py:19
  4.7 0.0 copy-start.1
  4.8 0.8 %collective-permute-start.1 = (bf16[32,16,128]{2,1,0:T(8,128)(2,1)S(1)}, bf16[32,16,128]{2,1,0:T(8,128)(2,1)S(1)}, u32[]{:S(2)}, u32[]{:S(2)}) collective-permute-start(bf16[32,16,128]{2,1,0:T(8,128)(2,1)S(1)} %get-tuple-element.36), channel_id=1, source_target_pairs={{4,8},{8,4},{12,16},{16,12},{20,24},{24,20},{5,9},{9,5},{13,17},{1... | collective-permute-start | bytes 393224 | tf_op jit(solution)/shard_map/ppermute | solution.py:19
  5.5 0.0 copy-done
  5.6 0.8 %shard_map.75 = (bf16[64,32,128]{2,1,0:T(8,128)(2,1)S(1)}, bf16[2,8,32,128]{3,2,1,0:T(8,128)(2,1)S(1)}) custom-call(bf16[32,64,128]{2,1,0:T(8,128)(2,1)S(1)} %copy-done), custom_call_target="tpu_custom_call" | custom-call | bytes 1179648 | tf_op jit(solution)/shard_map/pallas_call | solution.py:246
  6.4 1.9 %collective-permute-done.one_ref = bf16[32,16,128]{2,1,0:T(8,128)(2,1)S(1)} collective-permute-done((bf16[32,16,128]{2,1,0:T(8,128)(2,1)S(1)}, bf16[32,16,128]{2,1,0:T(8,128)(2,1)S(1)}, u32[]{:S(2)}, u32[]{:S(2)}) %collective-permute-start) | collective-permute-done | bytes 131104 | tf_op jit(solution)/shard_map/ppermute | solution.py:19
  8.2 0.0 collective-permute-done.1.two_ref
  8.2 0.0 copy-start.2
  8.3 0.3 shard_map.76
  8.5 0.1 collective-permute-start.2
  8.6 0.7 %collective-permute-start.3 = (bf16[12,32,128]{2,1,0:T(8,128)(2,1)S(1)}, bf16[12,32,128]{2,1,0:T(8,128)(2,1)S(1)}, u32[]{:S(2)}, u32[]{:S(2)}) collective-permute-start(bf16[12,32,128]{2,1,0:T(8,128)(2,1)S(1)} %get-tuple-element.24), channel_id=1, source_target_pairs={{1,2},{2,1},{5,6},{6,5},{9,10},{10,9},{13,14},{14,13},{17,18},{18,... | collective-permute-start | bytes 294920 | tf_op jit(solution)/shard_map/ppermute | solution.py:19
  9.3 0.0 copy-done.2
  9.3 0.1 copy.11
  9.4 0.1 reshape.17.weight_ref
  9.5 0.0 copy-start.3
  9.5 0.6 %copy-done.3 = f32[32]{0:T(128)S(1)} copy-done((f32[32]{0:T(128)S(1)}, f32[32]{0:T(128)}, u32[]{:S(2)}) %copy-start.3) | copy-done | bytes 152
  10.1 0.1 copy.12.bias_ref
  10.2 0.0 collective-permute-done.2.one_ref
  10.2 0.0 collective-permute-done.3.two_ref
  10.2 0.0 copy-done.1
  10.2 5.1 %shard_map.77 = (bf16[32,64,128]{2,1,0:T(8,128)(2,1)}, bf16[64,32,128]{2,1,0:T(8,128)(2,1)S(1)}, bf16[16,32,128]{2,1,0:T(8,128)(2,1)S(1)}, bf16[16,32,128]{2,1,0...) custom-call(bf16[64,32,128]{2,1,0:T(8,128)(2,1)S(1)} %get-tuple-element.20.own_ref, ...), custom_call_target="tpu_custom_call" | custom-call | flops 301989888 | bytes 3016832 | tf_op jit(solution)/shard_map/pallas_call | solution.py:246
  15.4 4.8 %collective-permute-start.8 = (f32[32,384]{1,0:T(8,128)S(1)}, f32[32,384]{1,0:T(8,128)S(1)}, u32[]{:S(2)}, u32[]{:S(2)}) collective-permute-start(f32[32,384]{1,0:T(8,128)S(1)} %get-tuple-element.33), channel_id=1, source_target_pairs={{0,1},{1,0},{2,3},{3,2},{4,5},{5,4},{6,7},{7,6},{8,9},{9,8},{10,11... | collective-permute-start | bytes 147464 | tf_op jit(solution)/shard_map/ppermute | solution.py:29
  20.2 4.8 %collective-permute-start.4 = (bf16[16,32,128]{2,1,0:T(8,128)(2,1)S(1)}, bf16[16,32,128]{2,1,0:T(8,128)(2,1)S(1)}, u32[]{:S(2)}, u32[]{:S(2)}) collective-permute-start(bf16[16,32,128]{2,1,0:T(8,128)(2,1)S(1)} %get-tuple-element.27), channel_id=1, source_target_pairs={{0,4},{4,0},{8,12},{12,8},{16,20},{20,16},{24,28},{28,24},{1,5},{5... | collective-permute-start | bytes 393224 | tf_op jit(solution)/shard_map/ppermute | solution.py:19
  24.9 0.7 %collective-permute-start.5 = (bf16[16,32,128]{2,1,0:T(8,128)(2,1)S(1)}, bf16[16,32,128]{2,1,0:T(8,128)(2,1)S(1)}, u32[]{:S(2)}, u32[]{:S(2)}) collective-permute-start(bf16[16,32,128]{2,1,0:T(8,128)(2,1)S(1)} %get-tuple-element.28), channel_id=1, source_target_pairs={{4,8},{8,4},{12,16},{16,12},{20,24},{24,20},{5,9},{9,5},{13,17},{1... | collective-permute-start | bytes 393224 | tf_op jit(solution)/shard_map/ppermute | solution.py:19
  25.6 0.0 collective-permute-done.8
  25.6 1.2 %collective-permute-start.9 = (f32[32,384]{1,0:T(8,128)S(1)}, f32[32,384]{1,0:T(8,128)S(1)}, u32[]{:S(2)}, u32[]{:S(2)}) collective-permute-start(f32[32,384]{1,0:T(8,128)S(1)} %add.25), channel_id=1, source_target_pairs={{0,2},{1,3},{2,0},{3,1},{4,6},{5,7},{6,4},{7,5},{8,10},{9,11},{10,... | collective-permute-start | bytes 147464 | tf_op jit(solution)/shard_map/ppermute | solution.py:29
  26.8 3.0 %collective-permute-done.9 = f32[32,384]{1,0:T(8,128)S(1)} collective-permute-done((f32[32,384]{1,0:T(8,128)S(1)}, f32[32,384]{1,0:T(8,128)S(1)}, u32[]{:S(2)}, u32[]{:S(2)}) %collective-permute-start.9) | collective-permute-done | bytes 49184 | tf_op jit(solution)/shard_map/ppermute | solution.py:29
  29.8 5.4 %collective-permute-start.10 = (f32[32,384]{1,0:T(8,128)S(1)}, f32[32,384]{1,0:T(8,128)S(1)}, u32[]{:S(2)}, u32[]{:S(2)}) collective-permute-start(f32[32,384]{1,0:T(8,128)S(1)} %add.26), channel_id=1, source_target_pairs={{0,16},{4,20},{8,24},{12,28},{16,0},{20,4},{24,8},{28,12},{1,17},{... | collective-permute-start | bytes 147464 | tf_op jit(solution)/shard_map/ppermute | solution.py:29
  35.2 0.0 collective-permute-done.4.one_ref
  35.2 0.0 collective-permute-done.5.two_ref
  35.2 0.2 shard_map.78
  35.4 0.1 collective-permute-start.6
  35.5 0.7 %collective-permute-start.7 = (bf16[12,32,128]{2,1,0:T(8,128)(2,1)S(1)}, bf16[12,32,128]{2,1,0:T(8,128)(2,1)S(1)}, u32[]{:S(2)}, u32[]{:S(2)}) collective-permute-start(bf16[12,32,128]{2,1,0:T(8,128)(2,1)S(1)} %get-tuple-element.32), channel_id=1, source_target_pairs={{1,2},{2,1},{5,6},{6,5},{9,10},{10,9},{13,14},{14,13},{17,18},{18,... | collective-permute-start | bytes 294920 | tf_op jit(solution)/shard_map/ppermute | solution.py:19
  36.2 1.1 %collective-permute-done.10 = f32[32,384]{1,0:T(8,128)S(1)} collective-permute-done((f32[32,384]{1,0:T(8,128)S(1)}, f32[32,384]{1,0:T(8,128)S(1)}, u32[]{:S(2)}, u32[]{:S(2)}) %collective-permute-start.10) | collective-permute-done | bytes 49184 | tf_op jit(solution)/shard_map/ppermute | solution.py:29
  37.3 1.6 %collective-permute-start.11 = (f32[32,384]{1,0:T(8,128)S(1)}, f32[32,384]{1,0:T(8,128)S(1)}, u32[]{:S(2)}, u32[]{:S(2)}) collective-permute-start(f32[32,384]{1,0:T(8,128)S(1)} %add.27), channel_id=1, source_target_pairs={{0,8},{4,12},{8,0},{12,4},{16,24},{20,28},{24,16},{28,20},{1,9},{5... | collective-permute-start | bytes 147464 | tf_op jit(solution)/shard_map/ppermute | solution.py:29
  38.9 2.7 %collective-permute-done.11 = f32[32,384]{1,0:T(8,128)S(1)} collective-permute-done((f32[32,384]{1,0:T(8,128)S(1)}, f32[32,384]{1,0:T(8,128)S(1)}, u32[]{:S(2)}, u32[]{:S(2)}) %collective-permute-start.11) | collective-permute-done | bytes 49184 | tf_op jit(solution)/shard_map/ppermute | solution.py:29
  41.6 1.9 %collective-permute-start.12 = (f32[32,384]{1,0:T(8,128)S(1)}, f32[32,384]{1,0:T(8,128)S(1)}, u32[]{:S(2)}, u32[]{:S(2)}) collective-permute-start(f32[32,384]{1,0:T(8,128)S(1)} %add.28.one_ref), channel_id=1, source_target_pairs={{0,4},{4,0},{8,12},{12,8},{16,20},{20,16},{24,28},{28,24},{1,5},{5... | collective-permute-start | bytes 147464 | tf_op jit(solution)/shard_map/ppermute | solution.py:29
  43.5 0.1 copy.14.weight_ref
  43.6 0.0 collective-permute-done.6.one_ref
  43.6 0.0 collective-permute-done.7.two_ref
  43.6 3.6 %shard_map.79 = bf16[32,64,128]{2,1,0:T(8,128)(2,1)} custom-call(bf16[64,32,128]{2,1,0:T(8,128)(2,1)S(1)} %get-tuple-element.26.own_ref, bf16[2,16,32,128]{3,2,1,0:T(8,128)(2,1)S(1)} %get-tuple-element.30.outer_ref, bf16[12,32,128]{2,1,0:T(8,128)(2,1)S(1)} %collective-permute-done.6.one_ref, bf16[12,32,128]{2,1,0:T(8,128)(2,1)S(1)} %collective-permute-done.7.two_ref, ...), custom_call_target="tpu_custom_call" | custom-call | flops 150994944 | bytes 1525760 | tf_op jit(solution)/shard_map/pallas_call | solution.py:246
  47.2 0.0 collective-permute-done.12.other_ref
  47.2 0.8 %shard_map.80 = (f32[3,3,32,32]{3,2,1,0:T(8,128)}, f32[1,32]{1,0:T(1,128)}) custom-call(f32[32,384]{1,0:T(8,128)S(1)} %add.28.one_ref, f32[32,384]{1,0:T(8,128)S(1)} %collective-permute-done.12.other_ref), custom_call_target="tpu_custom_call" | custom-call | bytes 135296 | tf_op jit(solution)/shard_map/pallas_call | solution.py:246
  (5 shorter events, 0.0 us)
Async XLA Ops:
  0.6 4.9 %copy-start = (bf16[32,64,128]{2,1,0:T(8,128)(2,1)S(1)}, bf16[32,64,128]{2,1,0:T(8,128)(2,1)}, u32[]{:S(2)}) copy-start(bf16[32,64,128]{2,1,0:T(8,128)(2,1)} %image_ref.1) | copy-start | bytes 1572868
  1.7 6.5 %collective-permute-start = (bf16[32,16,128]{2,1,0:T(8,128)(2,1)S(1)}, bf16[32,16,128]{2,1,0:T(8,128)(2,1)S(1)}, u32[]{:S(2)}, u32[]{:S(2)}) collective-permute-start(bf16[32,16,128]{2,1,0:T(8,128)(2,1)S(1)} %get-tuple-element.37), channel_id=1, source_target_pairs={{0,4},{4,0},{8,12},{12,8},{16,20},{20,16},{24,28},{28,24},{1,5},{5... | collective-permute-start | bytes 393224 | tf_op jit(solution)/shard_map/ppermute | solution.py:19
  4.7 5.5 %copy-start.1 = (bf16[32,64,128]{2,1,0:T(8,128)(2,1)S(1)}, bf16[32,64,128]{2,1,0:T(8,128)(2,1)}, u32[]{:S(2)}) copy-start(bf16[32,64,128]{2,1,0:T(8,128)(2,1)} %cotangent_ref.1) | copy-start | bytes 1572868
  4.8 3.5 %collective-permute-start.1 = (bf16[32,16,128]{2,1,0:T(8,128)(2,1)S(1)}, bf16[32,16,128]{2,1,0:T(8,128)(2,1)S(1)}, u32[]{:S(2)}, u32[]{:S(2)}) collective-permute-start(bf16[32,16,128]{2,1,0:T(8,128)(2,1)S(1)} %get-tuple-element.36), channel_id=1, source_target_pairs={{4,8},{8,4},{12,16},{16,12},{20,24},{24,20},{5,9},{9,5},{13,17},{1... | collective-permute-start | bytes 393224 | tf_op jit(solution)/shard_map/ppermute | solution.py:19
  8.2 1.1 %copy-start.2 = (bf16[3,3,32,32]{3,2,1,0:T(8,128)(2,1)S(1)}, bf16[3,3,32,32]{3,2,1,0:T(8,128)(2,1)}, u32[]{:S(2)}) copy-start(bf16[3,3,32,32]{3,2,1,0:T(8,128)(2,1)} %param.5) | copy-start | bytes 55300
  8.5 1.7 %collective-permute-start.2 = (bf16[12,32,128]{2,1,0:T(8,128)(2,1)S(1)}, bf16[12,32,128]{2,1,0:T(8,128)(2,1)S(1)}, u32[]{:S(2)}, u32[]{:S(2)}) collective-permute-start(bf16[12,32,128]{2,1,0:T(8,128)(2,1)S(1)} %get-tuple-element.23), channel_id=1, source_target_pairs={{0,1},{1,0},{2,3},{3,2},{4,5},{5,4},{6,7},{7,6},{8,9},{9,8},{10,11... | collective-permute-start | bytes 294920 | tf_op jit(solution)/shard_map/ppermute | solution.py:19
  8.6 1.6 %collective-permute-start.3 = (bf16[12,32,128]{2,1,0:T(8,128)(2,1)S(1)}, bf16[12,32,128]{2,1,0:T(8,128)(2,1)S(1)}, u32[]{:S(2)}, u32[]{:S(2)}) collective-permute-start(bf16[12,32,128]{2,1,0:T(8,128)(2,1)S(1)} %get-tuple-element.24), channel_id=1, source_target_pairs={{1,2},{2,1},{5,6},{6,5},{9,10},{10,9},{13,14},{14,13},{17,18},{18,... | collective-permute-start | bytes 294920 | tf_op jit(solution)/shard_map/ppermute | solution.py:19
  9.5 0.7 %copy-start.3 = (f32[32]{0:T(128)S(1)}, f32[32]{0:T(128)}, u32[]{:S(2)}) copy-start(f32[32]{0:T(128)} %param.6) | copy-start | bytes 388
  15.4 10.2 %collective-permute-start.8 = (f32[32,384]{1,0:T(8,128)S(1)}, f32[32,384]{1,0:T(8,128)S(1)}, u32[]{:S(2)}, u32[]{:S(2)}) collective-permute-start(f32[32,384]{1,0:T(8,128)S(1)} %get-tuple-element.33), channel_id=1, source_target_pairs={{0,1},{1,0},{2,3},{3,2},{4,5},{5,4},{6,7},{7,6},{8,9},{9,8},{10,11... | collective-permute-start | bytes 147464 | tf_op jit(solution)/shard_map/ppermute | solution.py:29
  20.2 15.0 %collective-permute-start.4 = (bf16[16,32,128]{2,1,0:T(8,128)(2,1)S(1)}, bf16[16,32,128]{2,1,0:T(8,128)(2,1)S(1)}, u32[]{:S(2)}, u32[]{:S(2)}) collective-permute-start(bf16[16,32,128]{2,1,0:T(8,128)(2,1)S(1)} %get-tuple-element.27), channel_id=1, source_target_pairs={{0,4},{4,0},{8,12},{12,8},{16,20},{20,16},{24,28},{28,24},{1,5},{5... | collective-permute-start | bytes 393224 | tf_op jit(solution)/shard_map/ppermute | solution.py:19
  24.9 10.3 %collective-permute-start.5 = (bf16[16,32,128]{2,1,0:T(8,128)(2,1)S(1)}, bf16[16,32,128]{2,1,0:T(8,128)(2,1)S(1)}, u32[]{:S(2)}, u32[]{:S(2)}) collective-permute-start(bf16[16,32,128]{2,1,0:T(8,128)(2,1)S(1)} %get-tuple-element.28), channel_id=1, source_target_pairs={{4,8},{8,4},{12,16},{16,12},{20,24},{24,20},{5,9},{9,5},{13,17},{1... | collective-permute-start | bytes 393224 | tf_op jit(solution)/shard_map/ppermute | solution.py:19
  25.6 4.2 %collective-permute-start.9 = (f32[32,384]{1,0:T(8,128)S(1)}, f32[32,384]{1,0:T(8,128)S(1)}, u32[]{:S(2)}, u32[]{:S(2)}) collective-permute-start(f32[32,384]{1,0:T(8,128)S(1)} %add.25), channel_id=1, source_target_pairs={{0,2},{1,3},{2,0},{3,1},{4,6},{5,7},{6,4},{7,5},{8,10},{9,11},{10,... | collective-permute-start | bytes 147464 | tf_op jit(solution)/shard_map/ppermute | solution.py:29
  29.8 7.5 %collective-permute-start.10 = (f32[32,384]{1,0:T(8,128)S(1)}, f32[32,384]{1,0:T(8,128)S(1)}, u32[]{:S(2)}, u32[]{:S(2)}) collective-permute-start(f32[32,384]{1,0:T(8,128)S(1)} %add.26), channel_id=1, source_target_pairs={{0,16},{4,20},{8,24},{12,28},{16,0},{20,4},{24,8},{28,12},{1,17},{... | collective-permute-start | bytes 147464 | tf_op jit(solution)/shard_map/ppermute | solution.py:29
  35.4 8.2 %collective-permute-start.6 = (bf16[12,32,128]{2,1,0:T(8,128)(2,1)S(1)}, bf16[12,32,128]{2,1,0:T(8,128)(2,1)S(1)}, u32[]{:S(2)}, u32[]{:S(2)}) collective-permute-start(bf16[12,32,128]{2,1,0:T(8,128)(2,1)S(1)} %get-tuple-element.31), channel_id=1, source_target_pairs={{0,1},{1,0},{2,3},{3,2},{4,5},{5,4},{6,7},{7,6},{8,9},{9,8},{10,11... | collective-permute-start | bytes 294920 | tf_op jit(solution)/shard_map/ppermute | solution.py:19
  35.5 8.1 %collective-permute-start.7 = (bf16[12,32,128]{2,1,0:T(8,128)(2,1)S(1)}, bf16[12,32,128]{2,1,0:T(8,128)(2,1)S(1)}, u32[]{:S(2)}, u32[]{:S(2)}) collective-permute-start(bf16[12,32,128]{2,1,0:T(8,128)(2,1)S(1)} %get-tuple-element.32), channel_id=1, source_target_pairs={{1,2},{2,1},{5,6},{6,5},{9,10},{10,9},{13,14},{14,13},{17,18},{18,... | collective-permute-start | bytes 294920 | tf_op jit(solution)/shard_map/ppermute | solution.py:19
  37.3 4.3 %collective-permute-start.11 = (f32[32,384]{1,0:T(8,128)S(1)}, f32[32,384]{1,0:T(8,128)S(1)}, u32[]{:S(2)}, u32[]{:S(2)}) collective-permute-start(f32[32,384]{1,0:T(8,128)S(1)} %add.27), channel_id=1, source_target_pairs={{0,8},{4,12},{8,0},{12,4},{16,24},{20,28},{24,16},{28,20},{1,9},{5... | collective-permute-start | bytes 147464 | tf_op jit(solution)/shard_map/ppermute | solution.py:29
  41.6 5.6 %collective-permute-start.12 = (f32[32,384]{1,0:T(8,128)S(1)}, f32[32,384]{1,0:T(8,128)S(1)}, u32[]{:S(2)}, u32[]{:S(2)}) collective-permute-start(f32[32,384]{1,0:T(8,128)S(1)} %add.28.one_ref), channel_id=1, source_target_pairs={{0,4},{4,0},{8,12},{12,8},{16,20},{20,16},{24,28},{28,24},{1,5},{5... | collective-permute-start | bytes 147464 | tf_op jit(solution)/shard_map/ppermute | solution.py:29

commit v6 on v5

--- a/solution.py
+++ b/solution.py
@@ -12,11 +12,29 @@
 VMEM_BYTES = 16 * 2**20
 
 
+def partners(axis, first):
+    count = lax.axis_size(axis)
+    to = list(range(count))
+    for at in range(first, count - 1, 2):
+        to[at], to[at + 1] = at + 1, at
+    return list(enumerate(to))
+
+
+def alone(axis, first):
+    places = [at for at, other in partners(axis, first) if at == other]
+    at = lax.axis_index(axis)
+    return functools.reduce(jnp.logical_or, [at == place for place in places]) if places else None
+
+
+def clear_if(flag, ref):
+    if flag is not None:
+        @pl.when(flag)
+        def _():
+            ref[...] = jnp.zeros_like(ref)
+
+
 def swap_pairs(value, axis, first):
-    pairs = []
-    for place in range(first, lax.axis_size(axis) - 1, 2):
-        pairs += [(place, place + 1), (place + 1, place)]
-    return lax.ppermute(value, axis, pairs)
+    return lax.ppermute(value, axis, partners(axis, first))
 
 
 def add_pairs(value, near_axis, far_axis):
@@ -125,6 +143,8 @@
 
     either("row", order, one_ref, two_ref)
     either("col", pack, send_one_ref, send_two_ref)
+    clear_if(alone("col", 0), send_one_ref)
+    clear_if(alone("col", 1), send_two_ref)
 
 
 def spread(rows_of, left_ref, right_ref, stack_ref, block, group_start):
@@ -209,6 +229,8 @@
     odd = lax.axis_index("row") % 2
     send_one_ref[...] = grad_ref[pl.ds((1 - odd) * end, DILATION)]
     send_two_ref[...] = grad_ref[pl.ds(odd * end, DILATION)]
+    clear_if(alone("row", 0), send_one_ref)
+    clear_if(alone("row", 1), send_two_ref)
     terms_ref[:, :depth] = terms_ref[:, :depth] * scale
     sums = jnp.sum(sum_ref[...], axis=1, keepdims=True) * scale
     terms_ref[:, depth:] = jnp.broadcast_to(sums, (channels, terms_ref.shape[1] - depth))
@@ -273,8 +295,14 @@
     outer = shape((2, DILATION, channels, width), bf16)
     end = height - DILATION
 
-    one = swap_pairs(lax.dynamic_slice_in_dim(image, (1 - odd) * end, DILATION, 1), "row", 0)
-    two = swap_pairs(lax.dynamic_slice_in_dim(image, odd * end, DILATION, 1), "row", 1)
+
+    def image_rim(start, first):
+        rim = lax.dynamic_slice_in_dim(image, start, DILATION, 1)
+        flag = alone("row", first)
+        return rim if flag is None else jnp.where(flag, jnp.zeros_like(rim), rim)
+
+    one = swap_pairs(image_rim((1 - odd) * end, 0), "row", 0)
+    two = swap_pairs(image_rim(odd * end, 1), "row", 1)
     image_rows, rims = call(own_kernel, (rows, own_rims), (image,))
     forward_weight = jnp.transpose(weight, (2, 0, 1, 3)).reshape(channels, depth)
     backward_weight = jnp.transpose(weight[::-1, ::-1], (3, 0, 1, 2)).reshape(channels, depth)

time: 48.2 us -> 48.3 us (level)
  other arithmetic: 0.03 us -> 1.09 us
  local copies, waits for them, and re-layouts: 2.06 us -> 1.01 us
    select_n x0 -> x1, other arithmetic: none -> 1.06 us  [image_rim(): return rim if flag is None else jnp.where(flag, jnp.zeros_like(rim), rim)]
    dynamic_slice x1 -> x0, local copies, waits for them, and re-layouts: 1.05 us -> none  [shards(): lax.dynamic_slice_in_dim(image, odd * end, DILATION, 1)]
where the time goes in v6:
time: 48.3 us; the launch traced here: 48 us
  starting transfers between devices  25.6 us (53%)
  Pallas kernels  10.9 us (23%)
  waiting for transfers between devices  8.65 us (18%)
  other arithmetic  1.09 us (2%)
  local copies, waits for them, and re-layouts  1.01 us (2%)
  between operations  0.84 us (2%)
    ppermute x5, starting transfers between devices, add_pairs(): lax.ppermute(value, axis, [(at, at ^ step) for at in range(lax.axis_size(...  14.9 us
    pallas_call x6, Pallas kernels, call(): pl.pallas_call(kernel, out_shape=out_shapes, in_specs=[whole] * len(opera...  10.9 us
    ppermute x8, starting transfers between devices, swap_pairs(): return lax.ppermute(value, axis, partners(axis, first))  10.7 us
    ppermute x5, waiting for transfers between devices, add_pairs(): lax.ppermute(value, axis, [(at, at ^ step) for at in range(lax.axis_size(...  6.75 us
    ppermute x8, waiting for transfers between devices, swap_pairs(): return lax.ppermute(value, axis, partners(axis, first))  1.9 us
    select_n x1, other arithmetic, image_rim(): return rim if flag is None else jnp.where(flag, jnp.zeros_like(rim), rim)  1.06 us
  transfers between devices with their start and end apart: 13, of which 4 were waited for; matrix products, arithmetic and copies ran while one was open for 1% of the time, Pallas kernels for 10%

profile of v6, /device:TPU:0, one launch (start us, length us, event | category | flops | bytes accessed | tf_op | source)
XLA Modules:
  0.0 48.0 jit_solution(2672498875951157162)
XLA Ops:
  0.6 0.0 copy-start
  0.7 1.1 %dynamic-slice_select_fusion = (bf16[32,16,128]{2,1,0:T(8,128)(2,1)S(1)}, bf16[32,16,128]{2,1,0:T(8,128)(2,1)S(1)}) fusion(bf16[32,64,128]{2,1,0:T(8,128)(2,1)} %image_ref.1, s32[]{:T(128)S(6)} %select_n.24, pred[]{:T(512)S(6)} %or.3, s32[]{:T(128)S(6)} %select_n.22), kind=kLoop, calls=%fused_computation | loop fusion | flops 65536 | bytes 524297 | tf_op jit(solution)/shard_map/jit(_where)/select_n | solution.py:302
  1.7 3.0 %collective-permute-start = (bf16[32,16,128]{2,1,0:T(8,128)(2,1)S(1)}, bf16[32,16,128]{2,1,0:T(8,128)(2,1)S(1)}, u32[]{:S(2)}, u32[]{:S(2)}) collective-permute-start(bf16[32,16,128]{2,1,0:T(8,128)(2,1)S(1)} %get-tuple-element.37), channel_id=1, source_target_pairs={{0,4},{4,0},{8,12},{12,8},{16,20},{20,16},{24,28},{28,24},{1,5},{5... | collective-permute-start | bytes 393224 | tf_op jit(solution)/shard_map/ppermute | solution.py:37
  4.8 0.0 copy-start.1
  4.8 0.8 %collective-permute-start.1 = (bf16[32,16,128]{2,1,0:T(8,128)(2,1)S(1)}, bf16[32,16,128]{2,1,0:T(8,128)(2,1)S(1)}, u32[]{:S(2)}, u32[]{:S(2)}) collective-permute-start(bf16[32,16,128]{2,1,0:T(8,128)(2,1)S(1)} %get-tuple-element.36), channel_id=1, source_target_pairs={{0,0},{4,8},{8,4},{12,16},{16,12},{20,24},{24,20},{28,28},{1,1},{5... | collective-permute-start | bytes 393224 | tf_op jit(solution)/shard_map/ppermute | solution.py:37
  5.6 0.0 copy-done
  5.6 0.8 %shard_map.75 = (bf16[64,32,128]{2,1,0:T(8,128)(2,1)S(1)}, bf16[2,8,32,128]{3,2,1,0:T(8,128)(2,1)S(1)}) custom-call(bf16[32,64,128]{2,1,0:T(8,128)(2,1)S(1)} %copy-done), custom_call_target="tpu_custom_call" | custom-call | bytes 1179648 | tf_op jit(solution)/shard_map/pallas_call | solution.py:268
  6.4 1.9 %collective-permute-done.one_ref = bf16[32,16,128]{2,1,0:T(8,128)(2,1)S(1)} collective-permute-done((bf16[32,16,128]{2,1,0:T(8,128)(2,1)S(1)}, bf16[32,16,128]{2,1,0:T(8,128)(2,1)S(1)}, u32[]{:S(2)}, u32[]{:S(2)}) %collective-permute-start) | collective-permute-done | bytes 131104 | tf_op jit(solution)/shard_map/ppermute | solution.py:37
  8.3 0.0 collective-permute-done.1.two_ref
  8.3 0.0 copy-start.2
  8.3 0.3 shard_map.76
  8.6 0.1 collective-permute-start.2
  8.7 0.7 %collective-permute-start.3 = (bf16[12,32,128]{2,1,0:T(8,128)(2,1)S(1)}, bf16[12,32,128]{2,1,0:T(8,128)(2,1)S(1)}, u32[]{:S(2)}, u32[]{:S(2)}) collective-permute-start(bf16[12,32,128]{2,1,0:T(8,128)(2,1)S(1)} %get-tuple-element.24), channel_id=1, source_target_pairs={{0,0},{1,2},{2,1},{3,3},{4,4},{5,6},{6,5},{7,7},{8,8},{9,10},{10,9... | collective-permute-start | bytes 294920 | tf_op jit(solution)/shard_map/ppermute | solution.py:37
  9.3 0.0 copy-done.2
  9.3 0.1 copy.11
  9.4 0.1 reshape.17.weight_ref
  9.5 0.0 copy-start.3
  9.5 0.6 %copy-done.3 = f32[32]{0:T(128)S(1)} copy-done((f32[32]{0:T(128)S(1)}, f32[32]{0:T(128)}, u32[]{:S(2)}) %copy-start.3) | copy-done | bytes 152
  10.2 0.1 copy.12.bias_ref
  10.3 0.0 collective-permute-done.2.one_ref
  10.3 0.0 collective-permute-done.3.two_ref
  10.3 0.0 copy-done.1
  10.3 5.2 %shard_map.77 = (bf16[32,64,128]{2,1,0:T(8,128)(2,1)}, bf16[64,32,128]{2,1,0:T(8,128)(2,1)S(1)}, bf16[16,32,128]{2,1,0:T(8,128)(2,1)S(1)}, bf16[16,32,128]{2,1,0...) custom-call(bf16[64,32,128]{2,1,0:T(8,128)(2,1)S(1)} %get-tuple-element.20.own_ref, ...), custom_call_target="tpu_custom_call" | custom-call | flops 301989888 | bytes 3016832 | tf_op jit(solution)/shard_map/pallas_call | solution.py:268
  15.4 4.8 %collective-permute-start.8 = (f32[32,384]{1,0:T(8,128)S(1)}, f32[32,384]{1,0:T(8,128)S(1)}, u32[]{:S(2)}, u32[]{:S(2)}) collective-permute-start(f32[32,384]{1,0:T(8,128)S(1)} %get-tuple-element.33), channel_id=1, source_target_pairs={{0,1},{1,0},{2,3},{3,2},{4,5},{5,4},{6,7},{7,6},{8,9},{9,8},{10,11... | collective-permute-start | bytes 147464 | tf_op jit(solution)/shard_map/ppermute | solution.py:47
  20.2 4.8 %collective-permute-start.4 = (bf16[16,32,128]{2,1,0:T(8,128)(2,1)S(1)}, bf16[16,32,128]{2,1,0:T(8,128)(2,1)S(1)}, u32[]{:S(2)}, u32[]{:S(2)}) collective-permute-start(bf16[16,32,128]{2,1,0:T(8,128)(2,1)S(1)} %get-tuple-element.27), channel_id=1, source_target_pairs={{0,4},{4,0},{8,12},{12,8},{16,20},{20,16},{24,28},{28,24},{1,5},{5... | collective-permute-start | bytes 393224 | tf_op jit(solution)/shard_map/ppermute | solution.py:37
  25.0 0.7 %collective-permute-start.5 = (bf16[16,32,128]{2,1,0:T(8,128)(2,1)S(1)}, bf16[16,32,128]{2,1,0:T(8,128)(2,1)S(1)}, u32[]{:S(2)}, u32[]{:S(2)}) collective-permute-start(bf16[16,32,128]{2,1,0:T(8,128)(2,1)S(1)} %get-tuple-element.28), channel_id=1, source_target_pairs={{0,0},{4,8},{8,4},{12,16},{16,12},{20,24},{24,20},{28,28},{1,1},{5... | collective-permute-start | bytes 393224 | tf_op jit(solution)/shard_map/ppermute | solution.py:37
  25.6 0.0 collective-permute-done.8
  25.7 1.2 %collective-permute-start.9 = (f32[32,384]{1,0:T(8,128)S(1)}, f32[32,384]{1,0:T(8,128)S(1)}, u32[]{:S(2)}, u32[]{:S(2)}) collective-permute-start(f32[32,384]{1,0:T(8,128)S(1)} %add.25), channel_id=1, source_target_pairs={{0,2},{1,3},{2,0},{3,1},{4,6},{5,7},{6,4},{7,5},{8,10},{9,11},{10,... | collective-permute-start | bytes 147464 | tf_op jit(solution)/shard_map/ppermute | solution.py:47
  26.9 3.0 %collective-permute-done.9 = f32[32,384]{1,0:T(8,128)S(1)} collective-permute-done((f32[32,384]{1,0:T(8,128)S(1)}, f32[32,384]{1,0:T(8,128)S(1)}, u32[]{:S(2)}, u32[]{:S(2)}) %collective-permute-start.9) | collective-permute-done | bytes 49184 | tf_op jit(solution)/shard_map/ppermute | solution.py:47
  29.8 5.4 %collective-permute-start.10 = (f32[32,384]{1,0:T(8,128)S(1)}, f32[32,384]{1,0:T(8,128)S(1)}, u32[]{:S(2)}, u32[]{:S(2)}) collective-permute-start(f32[32,384]{1,0:T(8,128)S(1)} %add.26), channel_id=1, source_target_pairs={{0,16},{4,20},{8,24},{12,28},{16,0},{20,4},{24,8},{28,12},{1,17},{... | collective-permute-start | bytes 147464 | tf_op jit(solution)/shard_map/ppermute | solution.py:47
  35.3 0.0 collective-permute-done.4.one_ref
  35.3 0.0 collective-permute-done.5.two_ref
  35.3 0.2 shard_map.78
  35.5 0.1 collective-permute-start.6
  35.6 0.7 %collective-permute-start.7 = (bf16[12,32,128]{2,1,0:T(8,128)(2,1)S(1)}, bf16[12,32,128]{2,1,0:T(8,128)(2,1)S(1)}, u32[]{:S(2)}, u32[]{:S(2)}) collective-permute-start(bf16[12,32,128]{2,1,0:T(8,128)(2,1)S(1)} %get-tuple-element.32), channel_id=1, source_target_pairs={{0,0},{1,2},{2,1},{3,3},{4,4},{5,6},{6,5},{7,7},{8,8},{9,10},{10,9... | collective-permute-start | bytes 294920 | tf_op jit(solution)/shard_map/ppermute | solution.py:37
  36.3 1.1 %collective-permute-done.10 = f32[32,384]{1,0:T(8,128)S(1)} collective-permute-done((f32[32,384]{1,0:T(8,128)S(1)}, f32[32,384]{1,0:T(8,128)S(1)}, u32[]{:S(2)}, u32[]{:S(2)}) %collective-permute-start.10) | collective-permute-done | bytes 49184 | tf_op jit(solution)/shard_map/ppermute | solution.py:47
  37.3 1.6 %collective-permute-start.11 = (f32[32,384]{1,0:T(8,128)S(1)}, f32[32,384]{1,0:T(8,128)S(1)}, u32[]{:S(2)}, u32[]{:S(2)}) collective-permute-start(f32[32,384]{1,0:T(8,128)S(1)} %add.27), channel_id=1, source_target_pairs={{0,8},{4,12},{8,0},{12,4},{16,24},{20,28},{24,16},{28,20},{1,9},{5... | collective-permute-start | bytes 147464 | tf_op jit(solution)/shard_map/ppermute | solution.py:47
  39.0 2.7 %collective-permute-done.11 = f32[32,384]{1,0:T(8,128)S(1)} collective-permute-done((f32[32,384]{1,0:T(8,128)S(1)}, f32[32,384]{1,0:T(8,128)S(1)}, u32[]{:S(2)}, u32[]{:S(2)}) %collective-permute-start.11) | collective-permute-done | bytes 49184 | tf_op jit(solution)/shard_map/ppermute | solution.py:47
  41.7 1.9 %collective-permute-start.12 = (f32[32,384]{1,0:T(8,128)S(1)}, f32[32,384]{1,0:T(8,128)S(1)}, u32[]{:S(2)}, u32[]{:S(2)}) collective-permute-start(f32[32,384]{1,0:T(8,128)S(1)} %add.28.one_ref), channel_id=1, source_target_pairs={{0,4},{4,0},{8,12},{12,8},{16,20},{20,16},{24,28},{28,24},{1,5},{5... | collective-permute-start | bytes 147464 | tf_op jit(solution)/shard_map/ppermute | solution.py:47
  43.6 0.1 copy.14.weight_ref
  43.7 0.0 collective-permute-done.6.one_ref
  43.7 0.0 collective-permute-done.7.two_ref
  43.7 3.6 %shard_map.79 = bf16[32,64,128]{2,1,0:T(8,128)(2,1)} custom-call(bf16[64,32,128]{2,1,0:T(8,128)(2,1)S(1)} %get-tuple-element.26.own_ref, bf16[2,16,32,128]{3,2,1,0:T(8,128)(2,1)S(1)} %get-tuple-element.30.outer_ref, bf16[12,32,128]{2,1,0:T(8,128)(2,1)S(1)} %collective-permute-done.6.one_ref, bf16[12,32,128]{2,1,0:T(8,128)(2,1)S(1)} %collective-permute-done.7.two_ref, ...), custom_call_target="tpu_custom_call" | custom-call | flops 150994944 | bytes 1525760 | tf_op jit(solution)/shard_map/pallas_call | solution.py:268
  47.3 0.0 collective-permute-done.12.other_ref
  47.3 0.8 %shard_map.80 = (f32[3,3,32,32]{3,2,1,0:T(8,128)}, f32[1,32]{1,0:T(1,128)}) custom-call(f32[32,384]{1,0:T(8,128)S(1)} %add.28.one_ref, f32[32,384]{1,0:T(8,128)S(1)} %collective-permute-done.12.other_ref), custom_call_target="tpu_custom_call" | custom-call | bytes 135296 | tf_op jit(solution)/shard_map/pallas_call | solution.py:268
  (5 shorter events, 0.0 us)
Async XLA Ops:
  0.6 4.9 %copy-start = (bf16[32,64,128]{2,1,0:T(8,128)(2,1)S(1)}, bf16[32,64,128]{2,1,0:T(8,128)(2,1)}, u32[]{:S(2)}) copy-start(bf16[32,64,128]{2,1,0:T(8,128)(2,1)} %image_ref.1) | copy-start | bytes 1572868
  1.7 6.5 %collective-permute-start = (bf16[32,16,128]{2,1,0:T(8,128)(2,1)S(1)}, bf16[32,16,128]{2,1,0:T(8,128)(2,1)S(1)}, u32[]{:S(2)}, u32[]{:S(2)}) collective-permute-start(bf16[32,16,128]{2,1,0:T(8,128)(2,1)S(1)} %get-tuple-element.37), channel_id=1, source_target_pairs={{0,4},{4,0},{8,12},{12,8},{16,20},{20,16},{24,28},{28,24},{1,5},{5... | collective-permute-start | bytes 393224 | tf_op jit(solution)/shard_map/ppermute | solution.py:37
  4.8 5.5 %copy-start.1 = (bf16[32,64,128]{2,1,0:T(8,128)(2,1)S(1)}, bf16[32,64,128]{2,1,0:T(8,128)(2,1)}, u32[]{:S(2)}) copy-start(bf16[32,64,128]{2,1,0:T(8,128)(2,1)} %cotangent_ref.1) | copy-start | bytes 1572868
  4.8 3.5 %collective-permute-start.1 = (bf16[32,16,128]{2,1,0:T(8,128)(2,1)S(1)}, bf16[32,16,128]{2,1,0:T(8,128)(2,1)S(1)}, u32[]{:S(2)}, u32[]{:S(2)}) collective-permute-start(bf16[32,16,128]{2,1,0:T(8,128)(2,1)S(1)} %get-tuple-element.36), channel_id=1, source_target_pairs={{0,0},{4,8},{8,4},{12,16},{16,12},{20,24},{24,20},{28,28},{1,1},{5... | collective-permute-start | bytes 393224 | tf_op jit(solution)/shard_map/ppermute | solution.py:37
  8.3 1.1 %copy-start.2 = (bf16[3,3,32,32]{3,2,1,0:T(8,128)(2,1)S(1)}, bf16[3,3,32,32]{3,2,1,0:T(8,128)(2,1)}, u32[]{:S(2)}) copy-start(bf16[3,3,32,32]{3,2,1,0:T(8,128)(2,1)} %param.5) | copy-start | bytes 55300
  8.6 1.7 %collective-permute-start.2 = (bf16[12,32,128]{2,1,0:T(8,128)(2,1)S(1)}, bf16[12,32,128]{2,1,0:T(8,128)(2,1)S(1)}, u32[]{:S(2)}, u32[]{:S(2)}) collective-permute-start(bf16[12,32,128]{2,1,0:T(8,128)(2,1)S(1)} %get-tuple-element.23), channel_id=1, source_target_pairs={{0,1},{1,0},{2,3},{3,2},{4,5},{5,4},{6,7},{7,6},{8,9},{9,8},{10,11... | collective-permute-start | bytes 294920 | tf_op jit(solution)/shard_map/ppermute | solution.py:37
  8.7 1.6 %collective-permute-start.3 = (bf16[12,32,128]{2,1,0:T(8,128)(2,1)S(1)}, bf16[12,32,128]{2,1,0:T(8,128)(2,1)S(1)}, u32[]{:S(2)}, u32[]{:S(2)}) collective-permute-start(bf16[12,32,128]{2,1,0:T(8,128)(2,1)S(1)} %get-tuple-element.24), channel_id=1, source_target_pairs={{0,0},{1,2},{2,1},{3,3},{4,4},{5,6},{6,5},{7,7},{8,8},{9,10},{10,9... | collective-permute-start | bytes 294920 | tf_op jit(solution)/shard_map/ppermute | solution.py:37
  9.5 0.7 %copy-start.3 = (f32[32]{0:T(128)S(1)}, f32[32]{0:T(128)}, u32[]{:S(2)}) copy-start(f32[32]{0:T(128)} %param.6) | copy-start | bytes 388
  15.4 10.2 %collective-permute-start.8 = (f32[32,384]{1,0:T(8,128)S(1)}, f32[32,384]{1,0:T(8,128)S(1)}, u32[]{:S(2)}, u32[]{:S(2)}) collective-permute-start(f32[32,384]{1,0:T(8,128)S(1)} %get-tuple-element.33), channel_id=1, source_target_pairs={{0,1},{1,0},{2,3},{3,2},{4,5},{5,4},{6,7},{7,6},{8,9},{9,8},{10,11... | collective-permute-start | bytes 147464 | tf_op jit(solution)/shard_map/ppermute | solution.py:47
  20.2 15.0 %collective-permute-start.4 = (bf16[16,32,128]{2,1,0:T(8,128)(2,1)S(1)}, bf16[16,32,128]{2,1,0:T(8,128)(2,1)S(1)}, u32[]{:S(2)}, u32[]{:S(2)}) collective-permute-start(bf16[16,32,128]{2,1,0:T(8,128)(2,1)S(1)} %get-tuple-element.27), channel_id=1, source_target_pairs={{0,4},{4,0},{8,12},{12,8},{16,20},{20,16},{24,28},{28,24},{1,5},{5... | collective-permute-start | bytes 393224 | tf_op jit(solution)/shard_map/ppermute | solution.py:37
  25.0 10.3 %collective-permute-start.5 = (bf16[16,32,128]{2,1,0:T(8,128)(2,1)S(1)}, bf16[16,32,128]{2,1,0:T(8,128)(2,1)S(1)}, u32[]{:S(2)}, u32[]{:S(2)}) collective-permute-start(bf16[16,32,128]{2,1,0:T(8,128)(2,1)S(1)} %get-tuple-element.28), channel_id=1, source_target_pairs={{0,0},{4,8},{8,4},{12,16},{16,12},{20,24},{24,20},{28,28},{1,1},{5... | collective-permute-start | bytes 393224 | tf_op jit(solution)/shard_map/ppermute | solution.py:37
  25.7 4.2 %collective-permute-start.9 = (f32[32,384]{1,0:T(8,128)S(1)}, f32[32,384]{1,0:T(8,128)S(1)}, u32[]{:S(2)}, u32[]{:S(2)}) collective-permute-start(f32[32,384]{1,0:T(8,128)S(1)} %add.25), channel_id=1, source_target_pairs={{0,2},{1,3},{2,0},{3,1},{4,6},{5,7},{6,4},{7,5},{8,10},{9,11},{10,... | collective-permute-start | bytes 147464 | tf_op jit(solution)/shard_map/ppermute | solution.py:47
  29.8 7.5 %collective-permute-start.10 = (f32[32,384]{1,0:T(8,128)S(1)}, f32[32,384]{1,0:T(8,128)S(1)}, u32[]{:S(2)}, u32[]{:S(2)}) collective-permute-start(f32[32,384]{1,0:T(8,128)S(1)} %add.26), channel_id=1, source_target_pairs={{0,16},{4,20},{8,24},{12,28},{16,0},{20,4},{24,8},{28,12},{1,17},{... | collective-permute-start | bytes 147464 | tf_op jit(solution)/shard_map/ppermute | solution.py:47
  35.5 8.2 %collective-permute-start.6 = (bf16[12,32,128]{2,1,0:T(8,128)(2,1)S(1)}, bf16[12,32,128]{2,1,0:T(8,128)(2,1)S(1)}, u32[]{:S(2)}, u32[]{:S(2)}) collective-permute-start(bf16[12,32,128]{2,1,0:T(8,128)(2,1)S(1)} %get-tuple-element.31), channel_id=1, source_target_pairs={{0,1},{1,0},{2,3},{3,2},{4,5},{5,4},{6,7},{7,6},{8,9},{9,8},{10,11... | collective-permute-start | bytes 294920 | tf_op jit(solution)/shard_map/ppermute | solution.py:37
  35.6 8.1 %collective-permute-start.7 = (bf16[12,32,128]{2,1,0:T(8,128)(2,1)S(1)}, bf16[12,32,128]{2,1,0:T(8,128)(2,1)S(1)}, u32[]{:S(2)}, u32[]{:S(2)}) collective-permute-start(bf16[12,32,128]{2,1,0:T(8,128)(2,1)S(1)} %get-tuple-element.32), channel_id=1, source_target_pairs={{0,0},{1,2},{2,1},{3,3},{4,4},{5,6},{6,5},{7,7},{8,8},{9,10},{10,9... | collective-permute-start | bytes 294920 | tf_op jit(solution)/shard_map/ppermute | solution.py:37
  37.3 4.3 %collective-permute-start.11 = (f32[32,384]{1,0:T(8,128)S(1)}, f32[32,384]{1,0:T(8,128)S(1)}, u32[]{:S(2)}, u32[]{:S(2)}) collective-permute-start(f32[32,384]{1,0:T(8,128)S(1)} %add.27), channel_id=1, source_target_pairs={{0,8},{4,12},{8,0},{12,4},{16,24},{20,28},{24,16},{28,20},{1,9},{5... | collective-permute-start | bytes 147464 | tf_op jit(solution)/shard_map/ppermute | solution.py:47
  41.7 5.6 %collective-permute-start.12 = (f32[32,384]{1,0:T(8,128)S(1)}, f32[32,384]{1,0:T(8,128)S(1)}, u32[]{:S(2)}, u32[]{:S(2)}) collective-permute-start(f32[32,384]{1,0:T(8,128)S(1)} %add.28.one_ref), channel_id=1, source_target_pairs={{0,4},{4,0},{8,12},{12,8},{16,20},{20,16},{24,28},{28,24},{1,5},{5... | collective-permute-start | bytes 147464 | tf_op jit(solution)/shard_map/ppermute | solution.py:47

commit v7 on v6

--- a/solution.py
+++ b/solution.py
@@ -34,7 +34,18 @@
 
 
 def swap_pairs(value, axis, first):
-    return lax.ppermute(value, axis, partners(axis, first))
+    other_axis = "col" if axis == "row" else "row"
+    columns = lax.axis_size("col")
+
+    def place(at, other):
+        row, column = (at, other) if axis == "row" else (other, at)
+        return row * columns + column
+
+    pairs = []
+    for at, to in partners(axis, first):
+        for other, other_to in partners(other_axis, 0):
+            pairs.append((place(at, other), place(to, other if to != at else other_to)))
+    return lax.ppermute(value, ("row", "col"), pairs)
 
 
 def add_pairs(value, near_axis, far_axis):

time: 48.3 us -> 44.3 us (0.917)
  starting transfers between devices: 25.6 us -> 17.8 us
  waiting for transfers between devices: 8.65 us -> 12.6 us
    ppermute x5, starting transfers between devices: 14.9 us -> 8.38 us  [add_pairs(): lax.ppermute(value, axis, [(at, at ^ step) for at in range(lax.axis_size(...]
    ppermute x8, waiting for transfers between devices: 1.9 us -> 6.45 us  [swap_pairs(): return lax.ppermute(value, ('row', 'col'), pairs)]
    ppermute x8, starting transfers between devices: 10.7 us -> 9.44 us  [swap_pairs(): return lax.ppermute(value, ('row', 'col'), pairs)]
    ppermute x5, waiting for transfers between devices: 6.75 us -> 6.16 us  [add_pairs(): lax.ppermute(value, axis, [(at, at ^ step) for at in range(lax.axis_size(...]
  transfers between devices with their start and end apart: 13 -> 13, of which waited for: 4 -> 5; matrix products, arithmetic and copies ran while one was open for 1% -> 1% of each run, Pallas kernels for 10% -> 11%
where the time goes in v7:
time: 44.3 us; the launch traced here: 44.1 us
  starting transfers between devices  17.8 us (40%)
  waiting for transfers between devices  12.6 us (28%)
  Pallas kernels  10.8 us (24%)
  other arithmetic  1.09 us (2%)
  local copies, waits for them, and re-layouts  1.01 us (2%)
  between operations  0.77 us (2%)
    pallas_call x6, Pallas kernels, call(): pl.pallas_call(kernel, out_shape=out_shapes, in_specs=[whole] * len(opera...  10.8 us
    ppermute x8, starting transfers between devices, swap_pairs(): return lax.ppermute(value, ('row', 'col'), pairs)  9.44 us
    ppermute x5, starting transfers between devices, add_pairs(): lax.ppermute(value, axis, [(at, at ^ step) for at in range(lax.axis_size(...  8.38 us
    ppermute x8, waiting for transfers between devices, swap_pairs(): return lax.ppermute(value, ('row', 'col'), pairs)  6.45 us
    ppermute x5, waiting for transfers between devices, add_pairs(): lax.ppermute(value, axis, [(at, at ^ step) for at in range(lax.axis_size(...  6.16 us
    select_n x1, other arithmetic, image_rim(): return rim if flag is None else jnp.where(flag, jnp.zeros_like(rim), rim)  1.06 us
  transfers between devices with their start and end apart: 13, of which 5 were waited for; matrix products, arithmetic and copies ran while one was open for 1% of the time, Pallas kernels for 11%

profile of v7, /device:TPU:0, one launch (start us, length us, event | category | flops | bytes accessed | tf_op | source)
XLA Modules:
  0.0 44.1 jit_solution(314746635279083240)
XLA Ops:
  0.6 0.0 copy-start
  0.7 1.1 %dynamic-slice_select_fusion = (bf16[32,16,128]{2,1,0:T(8,128)(2,1)S(1)}, bf16[32,16,128]{2,1,0:T(8,128)(2,1)S(1)}) fusion(bf16[32,64,128]{2,1,0:T(8,128)(2,1)} %image_ref.1, s32[]{:T(128)S(6)} %select_n.24, pred[]{:T(512)S(6)} %or.3, s32[]{:T(128)S(6)} %select_n.22), kind=kLoop, calls=%fused_computation | loop fusion | flops 65536 | bytes 524297 | tf_op jit(solution)/shard_map/jit(_where)/select_n | solution.py:313
  1.7 3.0 %collective-permute-start = (bf16[32,16,128]{2,1,0:T(8,128)(2,1)S(1)}, bf16[32,16,128]{2,1,0:T(8,128)(2,1)S(1)}, u32[]{:S(2)}, u32[]{:S(2)}) collective-permute-start(bf16[32,16,128]{2,1,0:T(8,128)(2,1)S(1)} %get-tuple-element.37), channel_id=1, source_target_pairs={{0,4},{1,5},{2,6},{3,7},{4,0},{5,1},{6,2},{7,3},{8,12},{9,13},{10,... | collective-permute-start | bytes 393224 | tf_op jit(solution)/shard_map/ppermute | solution.py:48
  4.8 0.0 copy-start.1
  4.8 0.0 collective-permute-start.1
  4.8 0.0 copy-done
  4.8 0.8 %shard_map.75 = (bf16[64,32,128]{2,1,0:T(8,128)(2,1)S(1)}, bf16[2,8,32,128]{3,2,1,0:T(8,128)(2,1)S(1)}) custom-call(bf16[32,64,128]{2,1,0:T(8,128)(2,1)S(1)} %copy-done), custom_call_target="tpu_custom_call" | custom-call | bytes 1179648 | tf_op jit(solution)/shard_map/pallas_call | solution.py:279
  5.6 4.8 %collective-permute-done.one_ref = bf16[32,16,128]{2,1,0:T(8,128)(2,1)S(1)} collective-permute-done((bf16[32,16,128]{2,1,0:T(8,128)(2,1)S(1)}, bf16[32,16,128]{2,1,0:T(8,128)(2,1)S(1)}, u32[]{:S(2)}, u32[]{:S(2)}) %collective-permute-start) | collective-permute-done | bytes 131104 | tf_op jit(solution)/shard_map/ppermute | solution.py:48
  10.3 0.0 collective-permute-done.1.two_ref
  10.3 0.0 copy-start.2
  10.3 0.3 shard_map.76
  10.6 0.1 collective-permute-start.2
  10.7 2.6 %collective-permute-start.3 = (bf16[12,32,128]{2,1,0:T(8,128)(2,1)S(1)}, bf16[12,32,128]{2,1,0:T(8,128)(2,1)S(1)}, u32[]{:S(2)}, u32[]{:S(2)}) collective-permute-start(bf16[12,32,128]{2,1,0:T(8,128)(2,1)S(1)} %get-tuple-element.24), channel_id=1, source_target_pairs={{0,4},{4,0},{8,12},{12,8},{16,20},{20,16},{24,28},{28,24},{1,2},{5... | collective-permute-start | bytes 294920 | tf_op jit(solution)/shard_map/ppermute | solution.py:48
  13.3 0.0 copy-done.2
  13.3 0.1 copy.11
  13.3 0.1 reshape.17.weight_ref
  13.4 0.0 copy-start.3
  13.5 0.6 %copy-done.3 = f32[32]{0:T(128)S(1)} copy-done((f32[32]{0:T(128)S(1)}, f32[32]{0:T(128)}, u32[]{:S(2)}) %copy-start.3) | copy-done | bytes 152
  14.1 0.1 copy.12.bias_ref
  14.2 0.0 collective-permute-done.2.one_ref
  14.2 1.7 %collective-permute-done.3.two_ref = bf16[12,32,128]{2,1,0:T(8,128)(2,1)S(1)} collective-permute-done((bf16[12,32,128]{2,1,0:T(8,128)(2,1)S(1)}, bf16[12,32,128]{2,1,0:T(8,128)(2,1)S(1)}, u32[]{:S(2)}, u32[]{:S(2)}) %collective-permute-start.3) | collective-permute-done | bytes 98336 | tf_op jit(solution)/shard_map/ppermute | solution.py:48
  15.9 0.0 copy-done.1
  15.9 5.1 %shard_map.77 = (bf16[32,64,128]{2,1,0:T(8,128)(2,1)}, bf16[64,32,128]{2,1,0:T(8,128)(2,1)S(1)}, bf16[16,32,128]{2,1,0:T(8,128)(2,1)S(1)}, bf16[16,32,128]{2,1,0...) custom-call(bf16[64,32,128]{2,1,0:T(8,128)(2,1)S(1)} %get-tuple-element.20.own_ref, ...), custom_call_target="tpu_custom_call" | custom-call | flops 301989888 | bytes 3016832 | tf_op jit(solution)/shard_map/pallas_call | solution.py:279
  21.0 0.0 collective-permute-start.8
  21.0 2.1 %collective-permute-start.4 = (bf16[16,32,128]{2,1,0:T(8,128)(2,1)S(1)}, bf16[16,32,128]{2,1,0:T(8,128)(2,1)S(1)}, u32[]{:S(2)}, u32[]{:S(2)}) collective-permute-start(bf16[16,32,128]{2,1,0:T(8,128)(2,1)S(1)} %get-tuple-element.27), channel_id=1, source_target_pairs={{0,4},{1,5},{2,6},{3,7},{4,0},{5,1},{6,2},{7,3},{8,12},{9,13},{10,... | collective-permute-start | bytes 393224 | tf_op jit(solution)/shard_map/ppermute | solution.py:48
  23.1 0.1 collective-permute-start.5
  23.3 0.0 collective-permute-done.8
  23.3 1.0 %collective-permute-start.9 = (f32[32,384]{1,0:T(8,128)S(1)}, f32[32,384]{1,0:T(8,128)S(1)}, u32[]{:S(2)}, u32[]{:S(2)}) collective-permute-start(f32[32,384]{1,0:T(8,128)S(1)} %add.25), channel_id=1, source_target_pairs={{0,2},{1,3},{2,0},{3,1},{4,6},{5,7},{6,4},{7,5},{8,10},{9,11},{10,... | collective-permute-start | bytes 147464 | tf_op jit(solution)/shard_map/ppermute | solution.py:58
  24.3 3.2 %collective-permute-done.9 = f32[32,384]{1,0:T(8,128)S(1)} collective-permute-done((f32[32,384]{1,0:T(8,128)S(1)}, f32[32,384]{1,0:T(8,128)S(1)}, u32[]{:S(2)}, u32[]{:S(2)}) %collective-permute-start.9) | collective-permute-done | bytes 49184 | tf_op jit(solution)/shard_map/ppermute | solution.py:58
  27.5 2.9 %collective-permute-start.10 = (f32[32,384]{1,0:T(8,128)S(1)}, f32[32,384]{1,0:T(8,128)S(1)}, u32[]{:S(2)}, u32[]{:S(2)}) collective-permute-start(f32[32,384]{1,0:T(8,128)S(1)} %add.26), channel_id=1, source_target_pairs={{0,16},{4,20},{8,24},{12,28},{16,0},{20,4},{24,8},{28,12},{1,17},{... | collective-permute-start | bytes 147464 | tf_op jit(solution)/shard_map/ppermute | solution.py:58
  30.4 0.0 collective-permute-done.4.one_ref
  30.4 0.0 collective-permute-done.5.two_ref
  30.4 0.2 shard_map.78
  30.6 0.1 collective-permute-start.6
  30.7 1.5 %collective-permute-start.7 = (bf16[12,32,128]{2,1,0:T(8,128)(2,1)S(1)}, bf16[12,32,128]{2,1,0:T(8,128)(2,1)S(1)}, u32[]{:S(2)}, u32[]{:S(2)}) collective-permute-start(bf16[12,32,128]{2,1,0:T(8,128)(2,1)S(1)} %get-tuple-element.32), channel_id=1, source_target_pairs={{0,4},{4,0},{8,12},{12,8},{16,20},{20,16},{24,28},{28,24},{1,2},{5... | collective-permute-start | bytes 294920 | tf_op jit(solution)/shard_map/ppermute | solution.py:48
  32.2 0.4 collective-permute-done.10
  32.5 1.5 %collective-permute-start.11 = (f32[32,384]{1,0:T(8,128)S(1)}, f32[32,384]{1,0:T(8,128)S(1)}, u32[]{:S(2)}, u32[]{:S(2)}) collective-permute-start(f32[32,384]{1,0:T(8,128)S(1)} %add.27), channel_id=1, source_target_pairs={{0,8},{4,12},{8,0},{12,4},{16,24},{20,28},{24,16},{28,20},{1,9},{5... | collective-permute-start | bytes 147464 | tf_op jit(solution)/shard_map/ppermute | solution.py:58
  34.1 2.6 %collective-permute-done.11 = f32[32,384]{1,0:T(8,128)S(1)} collective-permute-done((f32[32,384]{1,0:T(8,128)S(1)}, f32[32,384]{1,0:T(8,128)S(1)}, u32[]{:S(2)}, u32[]{:S(2)}) %collective-permute-start.11) | collective-permute-done | bytes 49184 | tf_op jit(solution)/shard_map/ppermute | solution.py:58
  36.7 2.9 %collective-permute-start.12 = (f32[32,384]{1,0:T(8,128)S(1)}, f32[32,384]{1,0:T(8,128)S(1)}, u32[]{:S(2)}, u32[]{:S(2)}) collective-permute-start(f32[32,384]{1,0:T(8,128)S(1)} %add.28.one_ref), channel_id=1, source_target_pairs={{0,4},{4,0},{8,12},{12,8},{16,20},{20,16},{24,28},{28,24},{1,5},{5... | collective-permute-start | bytes 147464 | tf_op jit(solution)/shard_map/ppermute | solution.py:58
  39.7 0.1 copy.14.weight_ref
  39.8 0.0 collective-permute-done.6.one_ref
  39.8 0.0 collective-permute-done.7.two_ref
  39.8 3.6 %shard_map.79 = bf16[32,64,128]{2,1,0:T(8,128)(2,1)} custom-call(bf16[64,32,128]{2,1,0:T(8,128)(2,1)S(1)} %get-tuple-element.26.own_ref, bf16[2,16,32,128]{3,2,1,0:T(8,128)(2,1)S(1)} %get-tuple-element.30.outer_ref, bf16[12,32,128]{2,1,0:T(8,128)(2,1)S(1)} %collective-permute-done.6.one_ref, bf16[12,32,128]{2,1,0:T(8,128)(2,1)S(1)} %collective-permute-done.7.two_ref, ...), custom_call_target="tpu_custom_call" | custom-call | flops 150994944 | bytes 1525760 | tf_op jit(solution)/shard_map/pallas_call | solution.py:279
  43.4 0.0 collective-permute-done.12.other_ref
  43.4 0.8 %shard_map.80 = (f32[3,3,32,32]{3,2,1,0:T(8,128)}, f32[1,32]{1,0:T(1,128)}) custom-call(f32[32,384]{1,0:T(8,128)S(1)} %add.28.one_ref, f32[32,384]{1,0:T(8,128)S(1)} %collective-permute-done.12.other_ref), custom_call_target="tpu_custom_call" | custom-call | bytes 135296 | tf_op jit(solution)/shard_map/pallas_call | solution.py:279
  (5 shorter events, 0.0 us)
Async XLA Ops:
  0.6 4.1 %copy-start = (bf16[32,64,128]{2,1,0:T(8,128)(2,1)S(1)}, bf16[32,64,128]{2,1,0:T(8,128)(2,1)}, u32[]{:S(2)}) copy-start(bf16[32,64,128]{2,1,0:T(8,128)(2,1)} %image_ref.1) | copy-start | bytes 1572868
  1.7 8.6 %collective-permute-start = (bf16[32,16,128]{2,1,0:T(8,128)(2,1)S(1)}, bf16[32,16,128]{2,1,0:T(8,128)(2,1)S(1)}, u32[]{:S(2)}, u32[]{:S(2)}) collective-permute-start(bf16[32,16,128]{2,1,0:T(8,128)(2,1)S(1)} %get-tuple-element.37), channel_id=1, source_target_pairs={{0,4},{1,5},{2,6},{3,7},{4,0},{5,1},{6,2},{7,3},{8,12},{9,13},{10,... | collective-permute-start | bytes 393224 | tf_op jit(solution)/shard_map/ppermute | solution.py:48
  4.8 11.1 %copy-start.1 = (bf16[32,64,128]{2,1,0:T(8,128)(2,1)S(1)}, bf16[32,64,128]{2,1,0:T(8,128)(2,1)}, u32[]{:S(2)}) copy-start(bf16[32,64,128]{2,1,0:T(8,128)(2,1)} %cotangent_ref.1) | copy-start | bytes 1572868
  4.8 5.6 %collective-permute-start.1 = (bf16[32,16,128]{2,1,0:T(8,128)(2,1)S(1)}, bf16[32,16,128]{2,1,0:T(8,128)(2,1)S(1)}, u32[]{:S(2)}, u32[]{:S(2)}) collective-permute-start(bf16[32,16,128]{2,1,0:T(8,128)(2,1)S(1)} %get-tuple-element.36), channel_id=1, source_target_pairs={{0,1},{1,0},{2,3},{3,2},{4,8},{5,9},{6,10},{7,11},{8,4},{9,5},{10,... | collective-permute-start | bytes 393224 | tf_op jit(solution)/shard_map/ppermute | solution.py:48
  10.3 2.9 %copy-start.2 = (bf16[3,3,32,32]{3,2,1,0:T(8,128)(2,1)S(1)}, bf16[3,3,32,32]{3,2,1,0:T(8,128)(2,1)}, u32[]{:S(2)}) copy-start(bf16[3,3,32,32]{3,2,1,0:T(8,128)(2,1)} %param.5) | copy-start | bytes 55300
  10.6 3.6 %collective-permute-start.2 = (bf16[12,32,128]{2,1,0:T(8,128)(2,1)S(1)}, bf16[12,32,128]{2,1,0:T(8,128)(2,1)S(1)}, u32[]{:S(2)}, u32[]{:S(2)}) collective-permute-start(bf16[12,32,128]{2,1,0:T(8,128)(2,1)S(1)} %get-tuple-element.23), channel_id=1, source_target_pairs={{0,1},{4,5},{8,9},{12,13},{16,17},{20,21},{24,25},{28,29},{1,0},{5... | collective-permute-start | bytes 294920 | tf_op jit(solution)/shard_map/ppermute | solution.py:48
  10.7 5.1 %collective-permute-start.3 = (bf16[12,32,128]{2,1,0:T(8,128)(2,1)S(1)}, bf16[12,32,128]{2,1,0:T(8,128)(2,1)S(1)}, u32[]{:S(2)}, u32[]{:S(2)}) collective-permute-start(bf16[12,32,128]{2,1,0:T(8,128)(2,1)S(1)} %get-tuple-element.24), channel_id=1, source_target_pairs={{0,4},{4,0},{8,12},{12,8},{16,20},{20,16},{24,28},{28,24},{1,2},{5... | collective-permute-start | bytes 294920 | tf_op jit(solution)/shard_map/ppermute | solution.py:48
  13.4 0.7 %copy-start.3 = (f32[32]{0:T(128)S(1)}, f32[32]{0:T(128)}, u32[]{:S(2)}) copy-start(f32[32]{0:T(128)} %param.6) | copy-start | bytes 388
  21.0 2.3 %collective-permute-start.8 = (f32[32,384]{1,0:T(8,128)S(1)}, f32[32,384]{1,0:T(8,128)S(1)}, u32[]{:S(2)}, u32[]{:S(2)}) collective-permute-start(f32[32,384]{1,0:T(8,128)S(1)} %get-tuple-element.33), channel_id=1, source_target_pairs={{0,1},{1,0},{2,3},{3,2},{4,5},{5,4},{6,7},{7,6},{8,9},{9,8},{10,11... | collective-permute-start | bytes 147464 | tf_op jit(solution)/shard_map/ppermute | solution.py:58
  21.0 9.4 %collective-permute-start.4 = (bf16[16,32,128]{2,1,0:T(8,128)(2,1)S(1)}, bf16[16,32,128]{2,1,0:T(8,128)(2,1)S(1)}, u32[]{:S(2)}, u32[]{:S(2)}) collective-permute-start(bf16[16,32,128]{2,1,0:T(8,128)(2,1)S(1)} %get-tuple-element.27), channel_id=1, source_target_pairs={{0,4},{1,5},{2,6},{3,7},{4,0},{5,1},{6,2},{7,3},{8,12},{9,13},{10,... | collective-permute-start | bytes 393224 | tf_op jit(solution)/shard_map/ppermute | solution.py:48
  23.1 7.3 %collective-permute-start.5 = (bf16[16,32,128]{2,1,0:T(8,128)(2,1)S(1)}, bf16[16,32,128]{2,1,0:T(8,128)(2,1)S(1)}, u32[]{:S(2)}, u32[]{:S(2)}) collective-permute-start(bf16[16,32,128]{2,1,0:T(8,128)(2,1)S(1)} %get-tuple-element.28), channel_id=1, source_target_pairs={{0,1},{1,0},{2,3},{3,2},{4,8},{5,9},{6,10},{7,11},{8,4},{9,5},{10,... | collective-permute-start | bytes 393224 | tf_op jit(solution)/shard_map/ppermute | solution.py:48
  23.3 4.2 %collective-permute-start.9 = (f32[32,384]{1,0:T(8,128)S(1)}, f32[32,384]{1,0:T(8,128)S(1)}, u32[]{:S(2)}, u32[]{:S(2)}) collective-permute-start(f32[32,384]{1,0:T(8,128)S(1)} %add.25), channel_id=1, source_target_pairs={{0,2},{1,3},{2,0},{3,1},{4,6},{5,7},{6,4},{7,5},{8,10},{9,11},{10,... | collective-permute-start | bytes 147464 | tf_op jit(solution)/shard_map/ppermute | solution.py:58
  27.5 5.1 %collective-permute-start.10 = (f32[32,384]{1,0:T(8,128)S(1)}, f32[32,384]{1,0:T(8,128)S(1)}, u32[]{:S(2)}, u32[]{:S(2)}) collective-permute-start(f32[32,384]{1,0:T(8,128)S(1)} %add.26), channel_id=1, source_target_pairs={{0,16},{4,20},{8,24},{12,28},{16,0},{20,4},{24,8},{28,12},{1,17},{... | collective-permute-start | bytes 147464 | tf_op jit(solution)/shard_map/ppermute | solution.py:58
  30.6 9.1 %collective-permute-start.6 = (bf16[12,32,128]{2,1,0:T(8,128)(2,1)S(1)}, bf16[12,32,128]{2,1,0:T(8,128)(2,1)S(1)}, u32[]{:S(2)}, u32[]{:S(2)}) collective-permute-start(bf16[12,32,128]{2,1,0:T(8,128)(2,1)S(1)} %get-tuple-element.31), channel_id=1, source_target_pairs={{0,1},{4,5},{8,9},{12,13},{16,17},{20,21},{24,25},{28,29},{1,0},{5... | collective-permute-start | bytes 294920 | tf_op jit(solution)/shard_map/ppermute | solution.py:48
  30.7 9.0 %collective-permute-start.7 = (bf16[12,32,128]{2,1,0:T(8,128)(2,1)S(1)}, bf16[12,32,128]{2,1,0:T(8,128)(2,1)S(1)}, u32[]{:S(2)}, u32[]{:S(2)}) collective-permute-start(bf16[12,32,128]{2,1,0:T(8,128)(2,1)S(1)} %get-tuple-element.32), channel_id=1, source_target_pairs={{0,4},{4,0},{8,12},{12,8},{16,20},{20,16},{24,28},{28,24},{1,2},{5... | collective-permute-start | bytes 294920 | tf_op jit(solution)/shard_map/ppermute | solution.py:48
  32.5 4.2 %collective-permute-start.11 = (f32[32,384]{1,0:T(8,128)S(1)}, f32[32,384]{1,0:T(8,128)S(1)}, u32[]{:S(2)}, u32[]{:S(2)}) collective-permute-start(f32[32,384]{1,0:T(8,128)S(1)} %add.27), channel_id=1, source_target_pairs={{0,8},{4,12},{8,0},{12,4},{16,24},{20,28},{24,16},{28,20},{1,9},{5... | collective-permute-start | bytes 147464 | tf_op jit(solution)/shard_map/ppermute | solution.py:58
  36.7 6.7 %collective-permute-start.12 = (f32[32,384]{1,0:T(8,128)S(1)}, f32[32,384]{1,0:T(8,128)S(1)}, u32[]{:S(2)}, u32[]{:S(2)}) collective-permute-start(f32[32,384]{1,0:T(8,128)S(1)} %add.28.one_ref), channel_id=1, source_target_pairs={{0,4},{4,0},{8,12},{12,8},{16,20},{20,16},{24,28},{28,24},{1,5},{5... | collective-permute-start | bytes 147464 | tf_op jit(solution)/shard_map/ppermute | solution.py:58

commit v8 on v7

--- a/solution.py
+++ b/solution.py
@@ -48,14 +48,23 @@
     return lax.ppermute(value, ("row", "col"), pairs)
 
 
+def rounds_of(axis):
+    bits = [2**k for k in reversed(range(lax.axis_size(axis).bit_length() - 1))]
+    return [(axis, bits[at : at + 2]) for at in range(0, len(bits), 2)]
+
+
 def add_pairs(value, near_axis, far_axis):
-    near, far = lax.axis_size(near_axis), lax.axis_size(far_axis)
-    steps = [(near_axis, 2**k) for k in range(near.bit_length() - 1)]
-    steps += [(far_axis, 2**k) for k in reversed(range(far.bit_length() - 1))]
     other = jnp.zeros_like(value)
-    for place, (axis, step) in enumerate(steps):
+    for place, (axis, bits) in enumerate(rounds_of(near_axis) + rounds_of(far_axis)):
         value = value + other if place else value
-        other = lax.ppermute(value, axis, [(at, at ^ step) for at in range(lax.axis_size(axis))])
+        masks = bits[::-1] + [sum(bits)] if len(bits) == 2 else bits
+        came = [
+            lax.ppermute(value, axis, [(at, at ^ mask) for at in range(lax.axis_size(axis))]) for mask in masks
+        ]
+        if len(came) == 3:
+            value, other = value + came[0], came[1] + came[2]
+        else:
+            other = came[0]
     return value, other
 
 

time: 44.3 us -> 45.4 us (1.025)
  waiting for transfers between devices: 12.6 us -> 14.2 us
  starting transfers between devices: 17.8 us -> 17.3 us
    ppermute x5 -> x7, waiting for transfers between devices: 6.16 us -> 7.8 us  [add_pairs(): lax.ppermute(value, axis, [(at, at ^ mask) for at in range(lax.axis_size(...]
    ppermute x5 -> x7, starting transfers between devices: 8.38 us -> 7.2 us  [add_pairs(): lax.ppermute(value, axis, [(at, at ^ mask) for at in range(lax.axis_size(...]
    ppermute x8, starting transfers between devices: 9.44 us -> 10.1 us  [swap_pairs(): return lax.ppermute(value, ('row', 'col'), pairs)]
  transfers between devices with their start and end apart: 13 -> 15, of which waited for: 5 -> 5; matrix products, arithmetic and copies ran while one was open for 1% -> 1% of each run, Pallas kernels for 11% -> 4%
where the time goes in v8:
time: 45.4 us; the launch traced here: 45.3 us
  starting transfers between devices  17.3 us (38%)
  waiting for transfers between devices  14.2 us (31%)
  Pallas kernels  10.9 us (24%)
  other arithmetic  1.09 us (2%)
  local copies, waits for them, and re-layouts  1.01 us (2%)
  between operations  0.76 us (2%)
    pallas_call x6, Pallas kernels, call(): pl.pallas_call(kernel, out_shape=out_shapes, in_specs=[whole] * len(opera...  10.9 us
    ppermute x8, starting transfers between devices, swap_pairs(): return lax.ppermute(value, ('row', 'col'), pairs)  10.1 us
    ppermute x7, waiting for transfers between devices, add_pairs(): lax.ppermute(value, axis, [(at, at ^ mask) for at in range(lax.axis_size(...  7.8 us
    ppermute x7, starting transfers between devices, add_pairs(): lax.ppermute(value, axis, [(at, at ^ mask) for at in range(lax.axis_size(...  7.2 us
    ppermute x8, waiting for transfers between devices, swap_pairs(): return lax.ppermute(value, ('row', 'col'), pairs)  6.45 us
    select_n x1, other arithmetic, image_rim(): return rim if flag is None else jnp.where(flag, jnp.zeros_like(rim), rim)  1.06 us
  transfers between devices with their start and end apart: 15, of which 5 were waited for; matrix products, arithmetic and copies ran while one was open for 1% of the time, Pallas kernels for 4%

profile of v8, /device:TPU:0, one launch (start us, length us, event | category | flops | bytes accessed | tf_op | source)
XLA Modules:
  0.0 45.3 jit_solution(6573137794626523280)
XLA Ops:
  0.6 0.0 copy-start
  0.7 1.1 %dynamic-slice_select_fusion = (bf16[32,16,128]{2,1,0:T(8,128)(2,1)S(1)}, bf16[32,16,128]{2,1,0:T(8,128)(2,1)S(1)}) fusion(bf16[32,64,128]{2,1,0:T(8,128)(2,1)} %image_ref.1, s32[]{:T(128)S(6)} %select_n.24, pred[]{:T(512)S(6)} %or.3, s32[]{:T(128)S(6)} %select_n.22), kind=kLoop, calls=%fused_computation | loop fusion | flops 65536 | bytes 524297 | tf_op jit(solution)/shard_map/jit(_where)/select_n | solution.py:322
  1.7 3.0 %collective-permute-start = (bf16[32,16,128]{2,1,0:T(8,128)(2,1)S(1)}, bf16[32,16,128]{2,1,0:T(8,128)(2,1)S(1)}, u32[]{:S(2)}, u32[]{:S(2)}) collective-permute-start(bf16[32,16,128]{2,1,0:T(8,128)(2,1)S(1)} %get-tuple-element.37), channel_id=1, source_target_pairs={{0,4},{1,5},{2,6},{3,7},{4,0},{5,1},{6,2},{7,3},{8,12},{9,13},{10,... | collective-permute-start | bytes 393224 | tf_op jit(solution)/shard_map/ppermute | solution.py:48
  4.8 0.0 copy-start.1
  4.8 0.0 collective-permute-start.1
  4.8 0.0 copy-done
  4.8 0.8 %shard_map.75 = (bf16[64,32,128]{2,1,0:T(8,128)(2,1)S(1)}, bf16[2,8,32,128]{3,2,1,0:T(8,128)(2,1)S(1)}) custom-call(bf16[32,64,128]{2,1,0:T(8,128)(2,1)S(1)} %copy-done), custom_call_target="tpu_custom_call" | custom-call | bytes 1179648 | tf_op jit(solution)/shard_map/pallas_call | solution.py:288
  5.6 4.8 %collective-permute-done.one_ref = bf16[32,16,128]{2,1,0:T(8,128)(2,1)S(1)} collective-permute-done((bf16[32,16,128]{2,1,0:T(8,128)(2,1)S(1)}, bf16[32,16,128]{2,1,0:T(8,128)(2,1)S(1)}, u32[]{:S(2)}, u32[]{:S(2)}) %collective-permute-start) | collective-permute-done | bytes 131104 | tf_op jit(solution)/shard_map/ppermute | solution.py:48
  10.3 0.0 collective-permute-done.1.two_ref
  10.3 0.3 shard_map.76
  10.6 0.1 collective-permute-start.2
  10.7 2.6 %collective-permute-start.3 = (bf16[12,32,128]{2,1,0:T(8,128)(2,1)S(1)}, bf16[12,32,128]{2,1,0:T(8,128)(2,1)S(1)}, u32[]{:S(2)}, u32[]{:S(2)}) collective-permute-start(bf16[12,32,128]{2,1,0:T(8,128)(2,1)S(1)} %get-tuple-element.24), channel_id=1, source_target_pairs={{0,4},{4,0},{8,12},{12,8},{16,20},{20,16},{24,28},{28,24},{1,2},{5... | collective-permute-start | bytes 294920 | tf_op jit(solution)/shard_map/ppermute | solution.py:48
  13.3 0.0 copy-done.2
  13.3 0.1 copy.11
  13.3 0.1 reshape.17.weight_ref
  13.4 0.0 copy-start.3
  13.5 0.6 %copy-done.3 = f32[32]{0:T(128)S(1)} copy-done((f32[32]{0:T(128)S(1)}, f32[32]{0:T(128)}, u32[]{:S(2)}) %copy-start.3) | copy-done | bytes 152
  14.1 0.1 copy.12.bias_ref
  14.2 0.0 collective-permute-done.2.one_ref
  14.2 1.7 %collective-permute-done.3.two_ref = bf16[12,32,128]{2,1,0:T(8,128)(2,1)S(1)} collective-permute-done((bf16[12,32,128]{2,1,0:T(8,128)(2,1)S(1)}, bf16[12,32,128]{2,1,0:T(8,128)(2,1)S(1)}, u32[]{:S(2)}, u32[]{:S(2)}) %collective-permute-start.3) | collective-permute-done | bytes 98336 | tf_op jit(solution)/shard_map/ppermute | solution.py:48
  15.9 0.0 copy-done.1
  15.9 5.1 %shard_map.77 = (bf16[32,64,128]{2,1,0:T(8,128)(2,1)}, bf16[64,32,128]{2,1,0:T(8,128)(2,1)S(1)}, bf16[16,32,128]{2,1,0:T(8,128)(2,1)S(1)}, bf16[16,32,128]{2,1,0...) custom-call(bf16[64,32,128]{2,1,0:T(8,128)(2,1)S(1)} %get-tuple-element.20.own_ref, ...), custom_call_target="tpu_custom_call" | custom-call | flops 301989888 | bytes 3016832 | tf_op jit(solution)/shard_map/pallas_call | solution.py:288
  21.0 0.6 %collective-permute-start.10 = (f32[32,384]{1,0:T(8,128)S(1)}, f32[32,384]{1,0:T(8,128)S(1)}, u32[]{:S(2)}, u32[]{:S(2)}) collective-permute-start(f32[32,384]{1,0:T(8,128)S(1)} %get-tuple-element.33), channel_id=1, source_target_pairs={{0,3},{1,2},{2,1},{3,0},{4,7},{5,6},{6,5},{7,4},{8,11},{9,10},{10,... | collective-permute-start | bytes 147464 | tf_op jit(solution)/shard_map/ppermute | solution.py:62
  21.7 0.0 collective-permute-start.8
  21.7 1.5 %collective-permute-start.9 = (f32[32,384]{1,0:T(8,128)S(1)}, f32[32,384]{1,0:T(8,128)S(1)}, u32[]{:S(2)}, u32[]{:S(2)}) collective-permute-start(f32[32,384]{1,0:T(8,128)S(1)} %get-tuple-element.33), channel_id=1, source_target_pairs={{0,2},{1,3},{2,0},{3,1},{4,6},{5,7},{6,4},{7,5},{8,10},{9,11},{10,... | collective-permute-start | bytes 147464 | tf_op jit(solution)/shard_map/ppermute | solution.py:62
  23.2 2.0 %collective-permute-start.4 = (bf16[16,32,128]{2,1,0:T(8,128)(2,1)S(1)}, bf16[16,32,128]{2,1,0:T(8,128)(2,1)S(1)}, u32[]{:S(2)}, u32[]{:S(2)}) collective-permute-start(bf16[16,32,128]{2,1,0:T(8,128)(2,1)S(1)} %get-tuple-element.27), channel_id=1, source_target_pairs={{0,4},{1,5},{2,6},{3,7},{4,0},{5,1},{6,2},{7,3},{8,12},{9,13},{10,... | collective-permute-start | bytes 393224 | tf_op jit(solution)/shard_map/ppermute | solution.py:48
  25.2 0.0 collective-permute-start.5
  25.2 0.0 collective-permute-done.10
  25.2 0.0 collective-permute-done.8
  25.2 0.8 %collective-permute-done.9 = f32[32,384]{1,0:T(8,128)S(1)} collective-permute-done((f32[32,384]{1,0:T(8,128)S(1)}, f32[32,384]{1,0:T(8,128)S(1)}, u32[]{:S(2)}, u32[]{:S(2)}) %collective-permute-start.9) | collective-permute-done | bytes 49184 | tf_op jit(solution)/shard_map/ppermute | solution.py:62
  26.0 2.3 %collective-permute-start.11 = (f32[32,384]{1,0:T(8,128)S(1)}, f32[32,384]{1,0:T(8,128)S(1)}, u32[]{:S(2)}, u32[]{:S(2)}) collective-permute-start(f32[32,384]{1,0:T(8,128)S(1)} %add_add_fusion.1), channel_id=1, source_target_pairs={{0,8},{4,12},{8,0},{12,4},{16,24},{20,28},{24,16},{28,20},{1,9},{5... | collective-permute-start | bytes 147464 | tf_op jit(solution)/shard_map/ppermute | solution.py:62
  28.3 2.6 %collective-permute-start.12 = (f32[32,384]{1,0:T(8,128)S(1)}, f32[32,384]{1,0:T(8,128)S(1)}, u32[]{:S(2)}, u32[]{:S(2)}) collective-permute-start(f32[32,384]{1,0:T(8,128)S(1)} %add_add_fusion.1), channel_id=1, source_target_pairs={{0,16},{4,20},{8,24},{12,28},{16,0},{20,4},{24,8},{28,12},{1,17},{... | collective-permute-start | bytes 147464 | tf_op jit(solution)/shard_map/ppermute | solution.py:62
  30.9 0.0 collective-permute-start.13
  30.9 0.0 collective-permute-done.4.one_ref
  30.9 0.0 collective-permute-done.5.two_ref
  30.9 0.3 shard_map.78
  31.1 0.1 collective-permute-start.6
  31.2 2.4 %collective-permute-start.7 = (bf16[12,32,128]{2,1,0:T(8,128)(2,1)S(1)}, bf16[12,32,128]{2,1,0:T(8,128)(2,1)S(1)}, u32[]{:S(2)}, u32[]{:S(2)}) collective-permute-start(bf16[12,32,128]{2,1,0:T(8,128)(2,1)S(1)} %get-tuple-element.32), channel_id=1, source_target_pairs={{0,4},{4,0},{8,12},{12,8},{16,20},{20,16},{24,28},{28,24},{1,2},{5... | collective-permute-start | bytes 294920 | tf_op jit(solution)/shard_map/ppermute | solution.py:48
  33.6 0.0 collective-permute-done.11
  33.6 0.0 collective-permute-done.12
  33.6 3.1 %collective-permute-done.13 = f32[32,384]{1,0:T(8,128)S(1)} collective-permute-done((f32[32,384]{1,0:T(8,128)S(1)}, f32[32,384]{1,0:T(8,128)S(1)}, u32[]{:S(2)}, u32[]{:S(2)}) %collective-permute-start.13) | collective-permute-done | bytes 49184 | tf_op jit(solution)/shard_map/ppermute | solution.py:62
  36.8 0.2 collective-permute-start.14
  37.0 0.1 copy.14.weight_ref
  37.1 3.9 %collective-permute-done.14.other_ref = f32[32,384]{1,0:T(8,128)S(1)} collective-permute-done((f32[32,384]{1,0:T(8,128)S(1)}, f32[32,384]{1,0:T(8,128)S(1)}, u32[]{:S(2)}, u32[]{:S(2)}) %collective-permute-start.14) | collective-permute-done | bytes 49184 | tf_op jit(solution)/shard_map/ppermute | solution.py:62
  40.9 0.8 %shard_map.80 = (f32[3,3,32,32]{3,2,1,0:T(8,128)}, f32[1,32]{1,0:T(1,128)}) custom-call(f32[32,384]{1,0:T(8,128)S(1)} %add_add_fusion.one_ref, f32[32,384]{1,0:T(8,128)S(1)} %collective-permute-done.14.other_ref), custom_call_target="tpu_custom_call" | custom-call | bytes 135296 | tf_op jit(solution)/shard_map/pallas_call | solution.py:288
  41.7 0.0 collective-permute-done.6.one_ref
  41.7 0.0 collective-permute-done.7.two_ref
  41.7 3.6 %shard_map.79 = bf16[32,64,128]{2,1,0:T(8,128)(2,1)} custom-call(bf16[64,32,128]{2,1,0:T(8,128)(2,1)S(1)} %get-tuple-element.26.own_ref, bf16[2,16,32,128]{3,2,1,0:T(8,128)(2,1)S(1)} %get-tuple-element.30.outer_ref, bf16[12,32,128]{2,1,0:T(8,128)(2,1)S(1)} %collective-permute-done.6.one_ref, bf16[12,32,128]{2,1,0:T(8,128)(2,1)S(1)} %collective-permute-done.7.two_ref, ...), custom_call_target="tpu_custom_call" | custom-call | flops 150994944 | bytes 1525760 | tf_op jit(solution)/shard_map/pallas_call | solution.py:288
  (4 shorter events, 0.0 us)
Async XLA Ops:
  0.6 4.1 %copy-start = (bf16[32,64,128]{2,1,0:T(8,128)(2,1)S(1)}, bf16[32,64,128]{2,1,0:T(8,128)(2,1)}, u32[]{:S(2)}) copy-start(bf16[32,64,128]{2,1,0:T(8,128)(2,1)} %image_ref.1) | copy-start | bytes 1572868
  1.7 8.6 %collective-permute-start = (bf16[32,16,128]{2,1,0:T(8,128)(2,1)S(1)}, bf16[32,16,128]{2,1,0:T(8,128)(2,1)S(1)}, u32[]{:S(2)}, u32[]{:S(2)}) collective-permute-start(bf16[32,16,128]{2,1,0:T(8,128)(2,1)S(1)} %get-tuple-element.37), channel_id=1, source_target_pairs={{0,4},{1,5},{2,6},{3,7},{4,0},{5,1},{6,2},{7,3},{8,12},{9,13},{10,... | collective-permute-start | bytes 393224 | tf_op jit(solution)/shard_map/ppermute | solution.py:48
  4.8 11.1 %copy-start.1 = (bf16[32,64,128]{2,1,0:T(8,128)(2,1)S(1)}, bf16[32,64,128]{2,1,0:T(8,128)(2,1)}, u32[]{:S(2)}) copy-start(bf16[32,64,128]{2,1,0:T(8,128)(2,1)} %cotangent_ref.1) | copy-start | bytes 1572868
  4.8 5.6 %collective-permute-start.1 = (bf16[32,16,128]{2,1,0:T(8,128)(2,1)S(1)}, bf16[32,16,128]{2,1,0:T(8,128)(2,1)S(1)}, u32[]{:S(2)}, u32[]{:S(2)}) collective-permute-start(bf16[32,16,128]{2,1,0:T(8,128)(2,1)S(1)} %get-tuple-element.36), channel_id=1, source_target_pairs={{0,1},{1,0},{2,3},{3,2},{4,8},{5,9},{6,10},{7,11},{8,4},{9,5},{10,... | collective-permute-start | bytes 393224 | tf_op jit(solution)/shard_map/ppermute | solution.py:48
  10.3 2.9 %copy-start.2 = (bf16[3,3,32,32]{3,2,1,0:T(8,128)(2,1)S(1)}, bf16[3,3,32,32]{3,2,1,0:T(8,128)(2,1)}, u32[]{:S(2)}) copy-start(bf16[3,3,32,32]{3,2,1,0:T(8,128)(2,1)} %param.5) | copy-start | bytes 55300
  10.6 3.6 %collective-permute-start.2 = (bf16[12,32,128]{2,1,0:T(8,128)(2,1)S(1)}, bf16[12,32,128]{2,1,0:T(8,128)(2,1)S(1)}, u32[]{:S(2)}, u32[]{:S(2)}) collective-permute-start(bf16[12,32,128]{2,1,0:T(8,128)(2,1)S(1)} %get-tuple-element.23), channel_id=1, source_target_pairs={{0,1},{4,5},{8,9},{12,13},{16,17},{20,21},{24,25},{28,29},{1,0},{5... | collective-permute-start | bytes 294920 | tf_op jit(solution)/shard_map/ppermute | solution.py:48
  10.7 5.1 %collective-permute-start.3 = (bf16[12,32,128]{2,1,0:T(8,128)(2,1)S(1)}, bf16[12,32,128]{2,1,0:T(8,128)(2,1)S(1)}, u32[]{:S(2)}, u32[]{:S(2)}) collective-permute-start(bf16[12,32,128]{2,1,0:T(8,128)(2,1)S(1)} %get-tuple-element.24), channel_id=1, source_target_pairs={{0,4},{4,0},{8,12},{12,8},{16,20},{20,16},{24,28},{28,24},{1,2},{5... | collective-permute-start | bytes 294920 | tf_op jit(solution)/shard_map/ppermute | solution.py:48
  13.4 0.7 %copy-start.3 = (f32[32]{0:T(128)S(1)}, f32[32]{0:T(128)}, u32[]{:S(2)}) copy-start(f32[32]{0:T(128)} %param.6) | copy-start | bytes 388
  21.0 4.1 %collective-permute-start.10 = (f32[32,384]{1,0:T(8,128)S(1)}, f32[32,384]{1,0:T(8,128)S(1)}, u32[]{:S(2)}, u32[]{:S(2)}) collective-permute-start(f32[32,384]{1,0:T(8,128)S(1)} %get-tuple-element.33), channel_id=1, source_target_pairs={{0,3},{1,2},{2,1},{3,0},{4,7},{5,6},{6,5},{7,4},{8,11},{9,10},{10,... | collective-permute-start | bytes 147464 | tf_op jit(solution)/shard_map/ppermute | solution.py:62
  21.7 3.5 %collective-permute-start.8 = (f32[32,384]{1,0:T(8,128)S(1)}, f32[32,384]{1,0:T(8,128)S(1)}, u32[]{:S(2)}, u32[]{:S(2)}) collective-permute-start(f32[32,384]{1,0:T(8,128)S(1)} %get-tuple-element.33), channel_id=1, source_target_pairs={{0,1},{1,0},{2,3},{3,2},{4,5},{5,4},{6,7},{7,6},{8,9},{9,8},{10,11... | collective-permute-start | bytes 147464 | tf_op jit(solution)/shard_map/ppermute | solution.py:62
  21.7 4.3 %collective-permute-start.9 = (f32[32,384]{1,0:T(8,128)S(1)}, f32[32,384]{1,0:T(8,128)S(1)}, u32[]{:S(2)}, u32[]{:S(2)}) collective-permute-start(f32[32,384]{1,0:T(8,128)S(1)} %get-tuple-element.33), channel_id=1, source_target_pairs={{0,2},{1,3},{2,0},{3,1},{4,6},{5,7},{6,4},{7,5},{8,10},{9,11},{10,... | collective-permute-start | bytes 147464 | tf_op jit(solution)/shard_map/ppermute | solution.py:62
  23.2 7.7 %collective-permute-start.4 = (bf16[16,32,128]{2,1,0:T(8,128)(2,1)S(1)}, bf16[16,32,128]{2,1,0:T(8,128)(2,1)S(1)}, u32[]{:S(2)}, u32[]{:S(2)}) collective-permute-start(bf16[16,32,128]{2,1,0:T(8,128)(2,1)S(1)} %get-tuple-element.27), channel_id=1, source_target_pairs={{0,4},{1,5},{2,6},{3,7},{4,0},{5,1},{6,2},{7,3},{8,12},{9,13},{10,... | collective-permute-start | bytes 393224 | tf_op jit(solution)/shard_map/ppermute | solution.py:48
  25.2 5.7 %collective-permute-start.5 = (bf16[16,32,128]{2,1,0:T(8,128)(2,1)S(1)}, bf16[16,32,128]{2,1,0:T(8,128)(2,1)S(1)}, u32[]{:S(2)}, u32[]{:S(2)}) collective-permute-start(bf16[16,32,128]{2,1,0:T(8,128)(2,1)S(1)} %get-tuple-element.28), channel_id=1, source_target_pairs={{0,1},{1,0},{2,3},{3,2},{4,8},{5,9},{6,10},{7,11},{8,4},{9,5},{10,... | collective-permute-start | bytes 393224 | tf_op jit(solution)/shard_map/ppermute | solution.py:48
  26.0 7.6 %collective-permute-start.11 = (f32[32,384]{1,0:T(8,128)S(1)}, f32[32,384]{1,0:T(8,128)S(1)}, u32[]{:S(2)}, u32[]{:S(2)}) collective-permute-start(f32[32,384]{1,0:T(8,128)S(1)} %add_add_fusion.1), channel_id=1, source_target_pairs={{0,8},{4,12},{8,0},{12,4},{16,24},{20,28},{24,16},{28,20},{1,9},{5... | collective-permute-start | bytes 147464 | tf_op jit(solution)/shard_map/ppermute | solution.py:62
  28.3 5.3 %collective-permute-start.12 = (f32[32,384]{1,0:T(8,128)S(1)}, f32[32,384]{1,0:T(8,128)S(1)}, u32[]{:S(2)}, u32[]{:S(2)}) collective-permute-start(f32[32,384]{1,0:T(8,128)S(1)} %add_add_fusion.1), channel_id=1, source_target_pairs={{0,16},{4,20},{8,24},{12,28},{16,0},{20,4},{24,8},{28,12},{1,17},{... | collective-permute-start | bytes 147464 | tf_op jit(solution)/shard_map/ppermute | solution.py:62
  30.9 5.9 %collective-permute-start.13 = (f32[32,384]{1,0:T(8,128)S(1)}, f32[32,384]{1,0:T(8,128)S(1)}, u32[]{:S(2)}, u32[]{:S(2)}) collective-permute-start(f32[32,384]{1,0:T(8,128)S(1)} %add_add_fusion.1), channel_id=1, source_target_pairs={{0,24},{4,28},{8,16},{12,20},{16,8},{20,12},{24,0},{28,4},{1,25},{... | collective-permute-start | bytes 147464 | tf_op jit(solution)/shard_map/ppermute | solution.py:62
  31.1 10.5 %collective-permute-start.6 = (bf16[12,32,128]{2,1,0:T(8,128)(2,1)S(1)}, bf16[12,32,128]{2,1,0:T(8,128)(2,1)S(1)}, u32[]{:S(2)}, u32[]{:S(2)}) collective-permute-start(bf16[12,32,128]{2,1,0:T(8,128)(2,1)S(1)} %get-tuple-element.31), channel_id=1, source_target_pairs={{0,1},{4,5},{8,9},{12,13},{16,17},{20,21},{24,25},{28,29},{1,0},{5... | collective-permute-start | bytes 294920 | tf_op jit(solution)/shard_map/ppermute | solution.py:48
  31.2 10.5 %collective-permute-start.7 = (bf16[12,32,128]{2,1,0:T(8,128)(2,1)S(1)}, bf16[12,32,128]{2,1,0:T(8,128)(2,1)S(1)}, u32[]{:S(2)}, u32[]{:S(2)}) collective-permute-start(bf16[12,32,128]{2,1,0:T(8,128)(2,1)S(1)} %get-tuple-element.32), channel_id=1, source_target_pairs={{0,4},{4,0},{8,12},{12,8},{16,20},{20,16},{24,28},{28,24},{1,2},{5... | collective-permute-start | bytes 294920 | tf_op jit(solution)/shard_map/ppermute | solution.py:48
  36.8 4.2 %collective-permute-start.14 = (f32[32,384]{1,0:T(8,128)S(1)}, f32[32,384]{1,0:T(8,128)S(1)}, u32[]{:S(2)}, u32[]{:S(2)}) collective-permute-start(f32[32,384]{1,0:T(8,128)S(1)} %add_add_fusion.one_ref), channel_id=1, source_target_pairs={{0,4},{4,0},{8,12},{12,8},{16,20},{20,16},{24,28},{28,24},{1,5},{5... | collective-permute-start | bytes 147464 | tf_op jit(solution)/shard_map/ppermute | solution.py:62

commit v9 on v8

--- a/solution.py
+++ b/solution.py
@@ -273,7 +273,7 @@
     lax.fori_loop(0, height // DILATION, body, 0)
 
 
-def finish_kernel(one_ref, other_ref, weight_ref, bias_ref):
+def finish_kernel(one_ref, other_ref, after_ref, weight_ref, bias_ref):
     total = one_ref[...] + other_ref[...]
     channels = total.shape[0]
     for tap in range(9):
@@ -282,18 +282,18 @@
     bias_ref[...] = flipped[127:128, :channels]
 
 
-def call(kernel, out_shapes, operands, scratch=(), flops=0):
+def call(kernel, out_shapes, operands, scratch=(), flops=0, after=()):
     whole = pl.BlockSpec(memory_space=pltpu.VMEM)
     size = sum(math.prod(x.shape) * jnp.dtype(x.dtype).itemsize for x in (*operands, *out_shapes))
     return pl.pallas_call(
         kernel,
         out_shape=out_shapes,
-        in_specs=[whole] * len(operands),
+        in_specs=[whole] * len(operands) + [pl.BlockSpec(memory_space=pl.ANY)] * len(after),
         out_specs=[whole] * len(out_shapes),
         scratch_shapes=list(scratch),
         compiler_params=pltpu.CompilerParams(vmem_limit_bytes=VMEM_BYTES),
         cost_estimate=pl.CostEstimate(flops=flops, bytes_accessed=size, transcendentals=0),
-    )(*operands)
+    )(*operands, *after)
 
 
 def shards(image, weight, bias, cotangent):
@@ -354,7 +354,8 @@
     )
     one, other = add_pairs(terms, "col", "row")
     grad_weight, grad_bias = call(
-        finish_kernel, (shape(weight.shape, f32), shape((1, channels), f32)), (one, other)
+        finish_kernel, (shape(weight.shape, f32), shape((1, channels), f32)), (one, other),
+        after=(grad_image,),
     )
     return (activation, grad_image, grad_weight, grad_bias.reshape(channels))
 

time: 45.4 us -> 42.9 us (0.945)
  waiting for transfers between devices: 14.2 us -> 10.6 us
  local copies, waits for them, and re-layouts: 1.01 us -> 2.05 us
    ppermute x7, waiting for transfers between devices: 7.8 us -> 4.18 us  [add_pairs(): lax.ppermute(value, axis, [(at, at ^ mask) for at in range(lax.axis_size(...]
    unnamed x8 -> x10, local copies, waits for them, and re-layouts: 0.66 us -> 1.7 us
  transfers between devices with their start and end apart: 15 -> 15, of which waited for: 5 -> 5; matrix products, arithmetic and copies ran while one was open for 1% -> 1% of each run, Pallas kernels for 4% -> 11%
where the time goes in v9:
time: 42.9 us; the launch traced here: 42.7 us
  starting transfers between devices  17.3 us (40%)
  Pallas kernels  10.9 us (25%)
  waiting for transfers between devices  10.6 us (25%)
  local copies, waits for them, and re-layouts  2.05 us (5%)
  other arithmetic  1.09 us (3%)
  between operations  0.77 us (2%)
    pallas_call x6, Pallas kernels, call(): pl.pallas_call(kernel, out_shape=out_shapes, in_specs=[whole] * len(opera...  10.9 us
    ppermute x8, starting transfers between devices, swap_pairs(): return lax.ppermute(value, ('row', 'col'), pairs)  10.1 us
    ppermute x7, starting transfers between devices, add_pairs(): lax.ppermute(value, axis, [(at, at ^ mask) for at in range(lax.axis_size(...  7.2 us
    ppermute x8, waiting for transfers between devices, swap_pairs(): return lax.ppermute(value, ('row', 'col'), pairs)  6.45 us
    ppermute x7, waiting for transfers between devices, add_pairs(): lax.ppermute(value, axis, [(at, at ^ mask) for at in range(lax.axis_size(...  4.18 us
    unnamed x10, local copies, waits for them, and re-layouts  1.7 us
    select_n x1, other arithmetic, image_rim(): return rim if flag is None else jnp.where(flag, jnp.zeros_like(rim), rim)  1.06 us
  transfers between devices with their start and end apart: 15, of which 5 were waited for; matrix products, arithmetic and copies ran while one was open for 1% of the time, Pallas kernels for 11%

profile of v9, /device:TPU:0, one launch (start us, length us, event | category | flops | bytes accessed | tf_op | source)
XLA Modules:
  0.0 42.7 jit_solution(11147269858531166087)
XLA Ops:
  0.6 0.0 copy-start.1
  0.7 1.1 %dynamic-slice_select_fusion = (bf16[32,16,128]{2,1,0:T(8,128)(2,1)S(1)}, bf16[32,16,128]{2,1,0:T(8,128)(2,1)S(1)}) fusion(bf16[32,64,128]{2,1,0:T(8,128)(2,1)} %image_ref.1, s32[]{:T(128)S(6)} %select_n.24, pred[]{:T(512)S(6)} %or.3, s32[]{:T(128)S(6)} %select_n.22), kind=kLoop, calls=%fused_computation | loop fusion | flops 65536 | bytes 524297 | tf_op jit(solution)/shard_map/jit(_where)/select_n | solution.py:322
  1.7 3.0 %collective-permute-start = (bf16[32,16,128]{2,1,0:T(8,128)(2,1)S(1)}, bf16[32,16,128]{2,1,0:T(8,128)(2,1)S(1)}, u32[]{:S(2)}, u32[]{:S(2)}) collective-permute-start(bf16[32,16,128]{2,1,0:T(8,128)(2,1)S(1)} %get-tuple-element.37), channel_id=1, source_target_pairs={{0,4},{1,5},{2,6},{3,7},{4,0},{5,1},{6,2},{7,3},{8,12},{9,13},{10,... | collective-permute-start | bytes 393224 | tf_op jit(solution)/shard_map/ppermute | solution.py:48
  4.8 0.0 collective-permute-start.1
  4.8 0.0 copy-done.1
  4.8 0.8 %shard_map.75 = (bf16[64,32,128]{2,1,0:T(8,128)(2,1)S(1)}, bf16[2,8,32,128]{3,2,1,0:T(8,128)(2,1)S(1)}) custom-call(bf16[32,64,128]{2,1,0:T(8,128)(2,1)S(1)} %copy-done.1), custom_call_target="tpu_custom_call" | custom-call | bytes 1179648 | tf_op jit(solution)/shard_map/pallas_call | solution.py:288
  5.6 4.8 %collective-permute-done.one_ref = bf16[32,16,128]{2,1,0:T(8,128)(2,1)S(1)} collective-permute-done((bf16[32,16,128]{2,1,0:T(8,128)(2,1)S(1)}, bf16[32,16,128]{2,1,0:T(8,128)(2,1)S(1)}, u32[]{:S(2)}, u32[]{:S(2)}) %collective-permute-start) | collective-permute-done | bytes 131104 | tf_op jit(solution)/shard_map/ppermute | solution.py:48
  10.3 0.0 collective-permute-done.1.two_ref
  10.3 0.3 shard_map.76
  10.6 0.1 collective-permute-start.2
  10.7 2.6 %collective-permute-start.3 = (bf16[12,32,128]{2,1,0:T(8,128)(2,1)S(1)}, bf16[12,32,128]{2,1,0:T(8,128)(2,1)S(1)}, u32[]{:S(2)}, u32[]{:S(2)}) collective-permute-start(bf16[12,32,128]{2,1,0:T(8,128)(2,1)S(1)} %get-tuple-element.24), channel_id=1, source_target_pairs={{0,4},{4,0},{8,12},{12,8},{16,20},{20,16},{24,28},{28,24},{1,2},{5... | collective-permute-start | bytes 294920 | tf_op jit(solution)/shard_map/ppermute | solution.py:48
  13.3 0.0 copy-done.3
  13.3 0.1 copy.11
  13.3 0.1 reshape.17.weight_ref
  13.4 0.0 copy-start.4
  13.5 0.6 %copy-done.4 = f32[32]{0:T(128)S(1)} copy-done((f32[32]{0:T(128)S(1)}, f32[32]{0:T(128)}, u32[]{:S(2)}) %copy-start.4) | copy-done | bytes 152
  14.1 0.1 copy.12.bias_ref
  14.2 0.0 collective-permute-done.2.one_ref
  14.2 1.7 %collective-permute-done.3.two_ref = bf16[12,32,128]{2,1,0:T(8,128)(2,1)S(1)} collective-permute-done((bf16[12,32,128]{2,1,0:T(8,128)(2,1)S(1)}, bf16[12,32,128]{2,1,0:T(8,128)(2,1)S(1)}, u32[]{:S(2)}, u32[]{:S(2)}) %collective-permute-start.3) | collective-permute-done | bytes 98336 | tf_op jit(solution)/shard_map/ppermute | solution.py:48
  15.9 0.0 copy-done.2
  15.9 5.1 %shard_map.77 = (bf16[32,64,128]{2,1,0:T(8,128)(2,1)}, bf16[64,32,128]{2,1,0:T(8,128)(2,1)S(1)}, bf16[16,32,128]{2,1,0:T(8,128)(2,1)S(1)}, bf16[16,32,128]{2,1,0...) custom-call(bf16[64,32,128]{2,1,0:T(8,128)(2,1)S(1)} %get-tuple-element.20.own_ref, ...), custom_call_target="tpu_custom_call" | custom-call | flops 301989888 | bytes 3016832 | tf_op jit(solution)/shard_map/pallas_call | solution.py:288
  21.0 0.6 %collective-permute-start.10 = (f32[32,384]{1,0:T(8,128)S(1)}, f32[32,384]{1,0:T(8,128)S(1)}, u32[]{:S(2)}, u32[]{:S(2)}) collective-permute-start(f32[32,384]{1,0:T(8,128)S(1)} %get-tuple-element.33), channel_id=1, source_target_pairs={{0,3},{1,2},{2,1},{3,0},{4,7},{5,6},{6,5},{7,4},{8,11},{9,10},{10,... | collective-permute-start | bytes 147464 | tf_op jit(solution)/shard_map/ppermute | solution.py:62
  21.7 0.0 collective-permute-start.8
  21.7 1.5 %collective-permute-start.9 = (f32[32,384]{1,0:T(8,128)S(1)}, f32[32,384]{1,0:T(8,128)S(1)}, u32[]{:S(2)}, u32[]{:S(2)}) collective-permute-start(f32[32,384]{1,0:T(8,128)S(1)} %get-tuple-element.33), channel_id=1, source_target_pairs={{0,2},{1,3},{2,0},{3,1},{4,6},{5,7},{6,4},{7,5},{8,10},{9,11},{10,... | collective-permute-start | bytes 147464 | tf_op jit(solution)/shard_map/ppermute | solution.py:62
  23.2 2.0 %collective-permute-start.4 = (bf16[16,32,128]{2,1,0:T(8,128)(2,1)S(1)}, bf16[16,32,128]{2,1,0:T(8,128)(2,1)S(1)}, u32[]{:S(2)}, u32[]{:S(2)}) collective-permute-start(bf16[16,32,128]{2,1,0:T(8,128)(2,1)S(1)} %get-tuple-element.27), channel_id=1, source_target_pairs={{0,4},{1,5},{2,6},{3,7},{4,0},{5,1},{6,2},{7,3},{8,12},{9,13},{10,... | collective-permute-start | bytes 393224 | tf_op jit(solution)/shard_map/ppermute | solution.py:48
  25.2 0.0 collective-permute-start.5
  25.2 0.0 collective-permute-done.10
  25.2 0.0 collective-permute-done.8
  25.2 0.8 %collective-permute-done.9 = f32[32,384]{1,0:T(8,128)S(1)} collective-permute-done((f32[32,384]{1,0:T(8,128)S(1)}, f32[32,384]{1,0:T(8,128)S(1)}, u32[]{:S(2)}, u32[]{:S(2)}) %collective-permute-start.9) | collective-permute-done | bytes 49184 | tf_op jit(solution)/shard_map/ppermute | solution.py:62
  26.0 2.3 %collective-permute-start.11 = (f32[32,384]{1,0:T(8,128)S(1)}, f32[32,384]{1,0:T(8,128)S(1)}, u32[]{:S(2)}, u32[]{:S(2)}) collective-permute-start(f32[32,384]{1,0:T(8,128)S(1)} %add_add_fusion.1), channel_id=1, source_target_pairs={{0,8},{4,12},{8,0},{12,4},{16,24},{20,28},{24,16},{28,20},{1,9},{5... | collective-permute-start | bytes 147464 | tf_op jit(solution)/shard_map/ppermute | solution.py:62
  28.3 2.6 %collective-permute-start.12 = (f32[32,384]{1,0:T(8,128)S(1)}, f32[32,384]{1,0:T(8,128)S(1)}, u32[]{:S(2)}, u32[]{:S(2)}) collective-permute-start(f32[32,384]{1,0:T(8,128)S(1)} %add_add_fusion.1), channel_id=1, source_target_pairs={{0,16},{4,20},{8,24},{12,28},{16,0},{20,4},{24,8},{28,12},{1,17},{... | collective-permute-start | bytes 147464 | tf_op jit(solution)/shard_map/ppermute | solution.py:62
  30.9 0.0 collective-permute-start.13
  30.9 0.0 collective-permute-done.4.one_ref
  30.9 0.0 collective-permute-done.5.two_ref
  30.9 0.3 shard_map.78
  31.1 0.1 collective-permute-start.6
  31.2 2.4 %collective-permute-start.7 = (bf16[12,32,128]{2,1,0:T(8,128)(2,1)S(1)}, bf16[12,32,128]{2,1,0:T(8,128)(2,1)S(1)}, u32[]{:S(2)}, u32[]{:S(2)}) collective-permute-start(bf16[12,32,128]{2,1,0:T(8,128)(2,1)S(1)} %get-tuple-element.32), channel_id=1, source_target_pairs={{0,4},{4,0},{8,12},{12,8},{16,20},{20,16},{24,28},{28,24},{1,2},{5... | collective-permute-start | bytes 294920 | tf_op jit(solution)/shard_map/ppermute | solution.py:48
  33.6 0.0 collective-permute-done.11
  33.6 0.0 collective-permute-done.12
  33.6 3.1 %collective-permute-done.13 = f32[32,384]{1,0:T(8,128)S(1)} collective-permute-done((f32[32,384]{1,0:T(8,128)S(1)}, f32[32,384]{1,0:T(8,128)S(1)}, u32[]{:S(2)}, u32[]{:S(2)}) %collective-permute-start.13) | collective-permute-done | bytes 49184 | tf_op jit(solution)/shard_map/ppermute | solution.py:62
  36.8 0.2 collective-permute-start.14
  37.0 0.1 copy.14.weight_ref
  37.1 0.0 collective-permute-done.6.one_ref
  37.1 0.0 collective-permute-done.7.two_ref
  37.1 3.6 %shard_map.79.after_ref = bf16[32,64,128]{2,1,0:T(8,128)(2,1)} custom-call(bf16[64,32,128]{2,1,0:T(8,128)(2,1)S(1)} %get-tuple-element.26.own_ref, bf16[2,16,32,128]{3,2,1,0:T(8,128)(2,1)S(1)} %get-tuple-element.30.outer_ref, bf16[12,32,128]{2,1,0:T(8,128)(2,1)S(1)} %collective-permute-done.6.one_ref, ...), custom_call_target="tpu_custom_call" | custom-call | flops 150994944 | bytes 1525760 | tf_op jit(solution)/shard_map/pallas_call | solution.py:288
  40.7 0.2 collective-permute-done.14.other_ref
  40.9 1.0 %copy-done = bf16[32,64,128]{2,1,0:T(8,128)(2,1)S(1)} copy-done((bf16[32,64,128]{2,1,0:T(8,128)(2,1)S(1)}, bf16[32,64,128]{2,1,0:T(8,128)(2,1)}, u32[]{:S(2)}) %copy-start) | copy-done | bytes 524312
  42.0 0.8 %shard_map.80 = (f32[3,3,32,32]{3,2,1,0:T(8,128)}, f32[1,32]{1,0:T(1,128)}) custom-call(f32[32,384]{1,0:T(8,128)S(1)} %add_add_fusion.one_ref, f32[32,384]{1,0:T(8,128)S(1)} %collective-permute-done.14.other_ref, bf16[32,64,128]{2,1,0:T(8,128)(2,1)S(1)} %copy-done), custom_call_target="tpu_custom_call" | custom-call | bytes 135296 | tf_op jit(solution)/shard_map/pallas_call | solution.py:288
  (6 shorter events, 0.0 us)
Async XLA Ops:
  0.6 4.1 %copy-start.1 = (bf16[32,64,128]{2,1,0:T(8,128)(2,1)S(1)}, bf16[32,64,128]{2,1,0:T(8,128)(2,1)}, u32[]{:S(2)}) copy-start(bf16[32,64,128]{2,1,0:T(8,128)(2,1)} %image_ref.1) | copy-start | bytes 1572868
  1.7 8.6 %collective-permute-start = (bf16[32,16,128]{2,1,0:T(8,128)(2,1)S(1)}, bf16[32,16,128]{2,1,0:T(8,128)(2,1)S(1)}, u32[]{:S(2)}, u32[]{:S(2)}) collective-permute-start(bf16[32,16,128]{2,1,0:T(8,128)(2,1)S(1)} %get-tuple-element.37), channel_id=1, source_target_pairs={{0,4},{1,5},{2,6},{3,7},{4,0},{5,1},{6,2},{7,3},{8,12},{9,13},{10,... | collective-permute-start | bytes 393224 | tf_op jit(solution)/shard_map/ppermute | solution.py:48
  4.8 11.1 %copy-start.2 = (bf16[32,64,128]{2,1,0:T(8,128)(2,1)S(1)}, bf16[32,64,128]{2,1,0:T(8,128)(2,1)}, u32[]{:S(2)}) copy-start(bf16[32,64,128]{2,1,0:T(8,128)(2,1)} %cotangent_ref.1) | copy-start | bytes 1572868
  4.8 5.6 %collective-permute-start.1 = (bf16[32,16,128]{2,1,0:T(8,128)(2,1)S(1)}, bf16[32,16,128]{2,1,0:T(8,128)(2,1)S(1)}, u32[]{:S(2)}, u32[]{:S(2)}) collective-permute-start(bf16[32,16,128]{2,1,0:T(8,128)(2,1)S(1)} %get-tuple-element.36), channel_id=1, source_target_pairs={{0,1},{1,0},{2,3},{3,2},{4,8},{5,9},{6,10},{7,11},{8,4},{9,5},{10,... | collective-permute-start | bytes 393224 | tf_op jit(solution)/shard_map/ppermute | solution.py:48
  10.3 2.9 %copy-start.3 = (bf16[3,3,32,32]{3,2,1,0:T(8,128)(2,1)S(1)}, bf16[3,3,32,32]{3,2,1,0:T(8,128)(2,1)}, u32[]{:S(2)}) copy-start(bf16[3,3,32,32]{3,2,1,0:T(8,128)(2,1)} %param.5) | copy-start | bytes 55300
  10.6 3.6 %collective-permute-start.2 = (bf16[12,32,128]{2,1,0:T(8,128)(2,1)S(1)}, bf16[12,32,128]{2,1,0:T(8,128)(2,1)S(1)}, u32[]{:S(2)}, u32[]{:S(2)}) collective-permute-start(bf16[12,32,128]{2,1,0:T(8,128)(2,1)S(1)} %get-tuple-element.23), channel_id=1, source_target_pairs={{0,1},{4,5},{8,9},{12,13},{16,17},{20,21},{24,25},{28,29},{1,0},{5... | collective-permute-start | bytes 294920 | tf_op jit(solution)/shard_map/ppermute | solution.py:48
  10.7 5.1 %collective-permute-start.3 = (bf16[12,32,128]{2,1,0:T(8,128)(2,1)S(1)}, bf16[12,32,128]{2,1,0:T(8,128)(2,1)S(1)}, u32[]{:S(2)}, u32[]{:S(2)}) collective-permute-start(bf16[12,32,128]{2,1,0:T(8,128)(2,1)S(1)} %get-tuple-element.24), channel_id=1, source_target_pairs={{0,4},{4,0},{8,12},{12,8},{16,20},{20,16},{24,28},{28,24},{1,2},{5... | collective-permute-start | bytes 294920 | tf_op jit(solution)/shard_map/ppermute | solution.py:48
  13.4 0.7 %copy-start.4 = (f32[32]{0:T(128)S(1)}, f32[32]{0:T(128)}, u32[]{:S(2)}) copy-start(f32[32]{0:T(128)} %param.6) | copy-start | bytes 388
  21.0 4.1 %collective-permute-start.10 = (f32[32,384]{1,0:T(8,128)S(1)}, f32[32,384]{1,0:T(8,128)S(1)}, u32[]{:S(2)}, u32[]{:S(2)}) collective-permute-start(f32[32,384]{1,0:T(8,128)S(1)} %get-tuple-element.33), channel_id=1, source_target_pairs={{0,3},{1,2},{2,1},{3,0},{4,7},{5,6},{6,5},{7,4},{8,11},{9,10},{10,... | collective-permute-start | bytes 147464 | tf_op jit(solution)/shard_map/ppermute | solution.py:62
  21.7 3.5 %collective-permute-start.8 = (f32[32,384]{1,0:T(8,128)S(1)}, f32[32,384]{1,0:T(8,128)S(1)}, u32[]{:S(2)}, u32[]{:S(2)}) collective-permute-start(f32[32,384]{1,0:T(8,128)S(1)} %get-tuple-element.33), channel_id=1, source_target_pairs={{0,1},{1,0},{2,3},{3,2},{4,5},{5,4},{6,7},{7,6},{8,9},{9,8},{10,11... | collective-permute-start | bytes 147464 | tf_op jit(solution)/shard_map/ppermute | solution.py:62
  21.7 4.3 %collective-permute-start.9 = (f32[32,384]{1,0:T(8,128)S(1)}, f32[32,384]{1,0:T(8,128)S(1)}, u32[]{:S(2)}, u32[]{:S(2)}) collective-permute-start(f32[32,384]{1,0:T(8,128)S(1)} %get-tuple-element.33), channel_id=1, source_target_pairs={{0,2},{1,3},{2,0},{3,1},{4,6},{5,7},{6,4},{7,5},{8,10},{9,11},{10,... | collective-permute-start | bytes 147464 | tf_op jit(solution)/shard_map/ppermute | solution.py:62
  23.2 7.7 %collective-permute-start.4 = (bf16[16,32,128]{2,1,0:T(8,128)(2,1)S(1)}, bf16[16,32,128]{2,1,0:T(8,128)(2,1)S(1)}, u32[]{:S(2)}, u32[]{:S(2)}) collective-permute-start(bf16[16,32,128]{2,1,0:T(8,128)(2,1)S(1)} %get-tuple-element.27), channel_id=1, source_target_pairs={{0,4},{1,5},{2,6},{3,7},{4,0},{5,1},{6,2},{7,3},{8,12},{9,13},{10,... | collective-permute-start | bytes 393224 | tf_op jit(solution)/shard_map/ppermute | solution.py:48
  25.2 5.7 %collective-permute-start.5 = (bf16[16,32,128]{2,1,0:T(8,128)(2,1)S(1)}, bf16[16,32,128]{2,1,0:T(8,128)(2,1)S(1)}, u32[]{:S(2)}, u32[]{:S(2)}) collective-permute-start(bf16[16,32,128]{2,1,0:T(8,128)(2,1)S(1)} %get-tuple-element.28), channel_id=1, source_target_pairs={{0,1},{1,0},{2,3},{3,2},{4,8},{5,9},{6,10},{7,11},{8,4},{9,5},{10,... | collective-permute-start | bytes 393224 | tf_op jit(solution)/shard_map/ppermute | solution.py:48
  26.0 7.6 %collective-permute-start.11 = (f32[32,384]{1,0:T(8,128)S(1)}, f32[32,384]{1,0:T(8,128)S(1)}, u32[]{:S(2)}, u32[]{:S(2)}) collective-permute-start(f32[32,384]{1,0:T(8,128)S(1)} %add_add_fusion.1), channel_id=1, source_target_pairs={{0,8},{4,12},{8,0},{12,4},{16,24},{20,28},{24,16},{28,20},{1,9},{5... | collective-permute-start | bytes 147464 | tf_op jit(solution)/shard_map/ppermute | solution.py:62
  28.3 5.3 %collective-permute-start.12 = (f32[32,384]{1,0:T(8,128)S(1)}, f32[32,384]{1,0:T(8,128)S(1)}, u32[]{:S(2)}, u32[]{:S(2)}) collective-permute-start(f32[32,384]{1,0:T(8,128)S(1)} %add_add_fusion.1), channel_id=1, source_target_pairs={{0,16},{4,20},{8,24},{12,28},{16,0},{20,4},{24,8},{28,12},{1,17},{... | collective-permute-start | bytes 147464 | tf_op jit(solution)/shard_map/ppermute | solution.py:62
  30.9 5.9 %collective-permute-start.13 = (f32[32,384]{1,0:T(8,128)S(1)}, f32[32,384]{1,0:T(8,128)S(1)}, u32[]{:S(2)}, u32[]{:S(2)}) collective-permute-start(f32[32,384]{1,0:T(8,128)S(1)} %add_add_fusion.1), channel_id=1, source_target_pairs={{0,24},{4,28},{8,16},{12,20},{16,8},{20,12},{24,0},{28,4},{1,25},{... | collective-permute-start | bytes 147464 | tf_op jit(solution)/shard_map/ppermute | solution.py:62
  31.1 5.9 %collective-permute-start.6 = (bf16[12,32,128]{2,1,0:T(8,128)(2,1)S(1)}, bf16[12,32,128]{2,1,0:T(8,128)(2,1)S(1)}, u32[]{:S(2)}, u32[]{:S(2)}) collective-permute-start(bf16[12,32,128]{2,1,0:T(8,128)(2,1)S(1)} %get-tuple-element.31), channel_id=1, source_target_pairs={{0,1},{4,5},{8,9},{12,13},{16,17},{20,21},{24,25},{28,29},{1,0},{5... | collective-permute-start | bytes 294920 | tf_op jit(solution)/shard_map/ppermute | solution.py:48
  31.2 5.9 %collective-permute-start.7 = (bf16[12,32,128]{2,1,0:T(8,128)(2,1)S(1)}, bf16[12,32,128]{2,1,0:T(8,128)(2,1)S(1)}, u32[]{:S(2)}, u32[]{:S(2)}) collective-permute-start(bf16[12,32,128]{2,1,0:T(8,128)(2,1)S(1)} %get-tuple-element.32), channel_id=1, source_target_pairs={{0,4},{4,0},{8,12},{12,8},{16,20},{20,16},{24,28},{28,24},{1,2},{5... | collective-permute-start | bytes 294920 | tf_op jit(solution)/shard_map/ppermute | solution.py:48
  36.8 4.2 %collective-permute-start.14 = (f32[32,384]{1,0:T(8,128)S(1)}, f32[32,384]{1,0:T(8,128)S(1)}, u32[]{:S(2)}, u32[]{:S(2)}) collective-permute-start(f32[32,384]{1,0:T(8,128)S(1)} %add_add_fusion.one_ref), channel_id=1, source_target_pairs={{0,4},{4,0},{8,12},{12,8},{16,20},{20,16},{24,28},{28,24},{1,5},{5... | collective-permute-start | bytes 147464 | tf_op jit(solution)/shard_map/ppermute | solution.py:62
  40.9 1.0 %copy-start = (bf16[32,64,128]{2,1,0:T(8,128)(2,1)S(1)}, bf16[32,64,128]{2,1,0:T(8,128)(2,1)}, u32[]{:S(2)}) copy-start(bf16[32,64,128]{2,1,0:T(8,128)(2,1)} %shard_map.79.after_ref) | copy-start | bytes 1572868

commit v10 on v8

--- a/solution.py
+++ b/solution.py
@@ -51,6 +51,16 @@
 def rounds_of(axis):
     bits = [2**k for k in reversed(range(lax.axis_size(axis).bit_length() - 1))]
     return [(axis, bits[at : at + 2]) for at in range(0, len(bits), 2)]
+
+
+def swap_corners(value, first_row, first_column):
+    columns = lax.axis_size("col")
+    pairs = [
+        (row * columns + column, row_to * columns + column_to)
+        for row, row_to in partners("row", first_row)
+        for column, column_to in partners("col", first_column)
+    ]
+    return lax.ppermute(value, ("row", "col"), pairs)
 
 
 def add_pairs(value, near_axis, far_axis):
@@ -119,7 +129,7 @@
         store(first_group + group, first, last)
 
 
-def own_kernel(image_ref, rows_ref, rims_ref):
+def own_kernel(image_ref, rows_ref, one_ref, two_ref, corner_one_ref, corner_two_ref, rims_ref):
     count = image_ref.shape[1] // DILATION
     groups = rims_ref.shape[1] // count
 
@@ -135,6 +145,29 @@
         return carry
 
     lax.fori_loop(0, count, body, 0)
+    odd_row, odd_column = lax.axis_index("row") % 2, lax.axis_index("col") % 2
+    start = (1 - odd_row) * (rims_ref.shape[1] - groups)
+    one_ref[...] = rims_ref[1 - odd_column]
+    two_ref[...] = rims_ref[odd_column]
+    corner_one_ref[...] = rims_ref[1 - odd_column, pl.ds(start, groups)]
+    corner_two_ref[...] = rims_ref[odd_column, pl.ds(start, groups)]
+    for first, rim_ref, corner_ref in ((0, one_ref, corner_one_ref), (1, two_ref, corner_two_ref)):
+        clear_if(alone("col", first), rim_ref)
+        clear_if(alone("col", first), corner_ref)
+        clear_if(alone("row", 0), corner_ref)
+
+
+def join_kernel(rows_ref, edge_ref, one_ref, two_ref, corner_one_ref, corner_two_ref, out_ref, near_ref):
+    odd = lax.axis_index("row") % 2
+    groups = (out_ref.shape[0] - DILATION) // 2
+    start = odd * (one_ref.shape[0] - groups)
+    out_ref[:DILATION] = rows_ref[pl.ds(odd * (rows_ref.shape[0] - DILATION), DILATION)]
+    out_ref[DILATION : DILATION + groups] = one_ref[pl.ds(start, groups)]
+    out_ref[DILATION + groups :] = two_ref[pl.ds(start, groups)]
+    clear_if(alone("row", 1), out_ref)
+    near_ref[:DILATION] = jnp.swapaxes(edge_ref[...], 0, 1)
+    near_ref[DILATION : DILATION + groups] = corner_one_ref[...]
+    near_ref[DILATION + groups :] = corner_two_ref[...]
 
 
 def either(axis, body, one, two):
@@ -143,13 +176,13 @@
     pl.when(jnp.logical_not(odd))(lambda: body(two, one))
 
 
-def rim_kernel(swap, one_ref, two_ref, rims_ref, send_one_ref, send_two_ref, outer_ref):
+def rim_kernel(one_ref, two_ref, rims_ref, send_one_ref, send_two_ref, outer_ref):
     own = rims_ref.shape[1]
     groups = (send_one_ref.shape[0] - own) // 2
 
     def order(upper_ref, lower_ref):
         for index, ref in enumerate((upper_ref, lower_ref)):
-            outer_ref[index] = jnp.swapaxes(ref[...], 0, 1) if swap else ref[...]
+            outer_ref[index] = ref[...]
 
     def pack(send_first_ref, send_last_ref):
         def store(place, first, last):
@@ -167,12 +200,12 @@
     clear_if(alone("col", 1), send_two_ref)
 
 
-def spread(rows_of, left_ref, right_ref, stack_ref, block, group_start):
-    channels, width = left_ref.shape[1:]
+def spread(rows_of, left_of, right_of, stack_ref, block):
+    channels, width = stack_ref.shape[1] // 3, stack_ref.shape[2] // DILATION
     pieces = width // DILATION
     lane = lane_of((channels, width))
     for group in range(DILATION // pieces):
-        rims = unpack_group(left_ref[group_start + group], right_ref[group_start + group], pieces)
+        rims = unpack_group(left_of(group), right_of(group), pieces)
         for k in range(pieces):
             row = group * pieces + k
             value = rows_of(row)
@@ -184,34 +217,69 @@
             stack_ref[block, 2 * channels : 3 * channels, columns] = after
 
 
-def spread_all(own_ref, outer_ref, one_ref, two_ref, stack_ref):
+def spread_blocks(blocks, left_ref, right_ref, stack_ref):
+    for rows_of, left_start, right_start, place in blocks:
+        spread(
+            rows_of,
+            lambda group, start=left_start: left_ref[start + group],
+            lambda group, start=right_start: right_ref[start + group],
+            stack_ref,
+            place,
+        )
+
+
+def spread_own(own_ref, left_ref, right_ref, stack_ref, start):
+    count = own_ref.shape[0] // DILATION
+    groups = DILATION * DILATION // own_ref.shape[2]
+
+    def body(block, carry):
+        at = start + block * groups
+        spread_blocks(
+            [(lambda row: own_ref[block * DILATION + row], at, at, block + 1)], left_ref, right_ref, stack_ref
+        )
+        return carry
+
+    lax.fori_loop(0, count, body, 0)
+
+
+def spread_joined(own_ref, near_ref, far_ref, one_ref, two_ref, stack_ref):
+    last = own_ref.shape[0] // DILATION + 1
+    groups = (near_ref.shape[0] - DILATION) // 2
+    near = jnp.where(lax.axis_index("row") % 2 == 1, 0, last)
+
+    def every(left, right):
+        (left_ref, left_start), (right_ref, right_start) = left, right
+        spread_own(own_ref, left_ref, right_ref, stack_ref, 0)
+        for ref, place in ((near_ref, near), (far_ref, last - near)):
+            block = (lambda row, ref=ref: ref[row], left_start, right_start, place)
+            spread_blocks([block], ref, ref, stack_ref)
+
+    either("col", every, (one_ref, DILATION), (two_ref, DILATION + groups))
+
+
+def spread_outer(own_ref, outer_ref, one_ref, two_ref, stack_ref):
     count = own_ref.shape[0] // DILATION
     groups = one_ref.shape[0] // (count + 2)
+    end = (count + 1) * groups
 
     def every(left_ref, right_ref):
-        spread(lambda row: outer_ref[0, row], left_ref, right_ref, stack_ref, 0, 0)
-
-        def body(block, carry):
-            spread(
-                lambda row: own_ref[block * DILATION + row],
-                left_ref, right_ref, stack_ref, block + 1, (block + 1) * groups,
-            )
-            return carry
-
-        lax.fori_loop(0, count, body, 0)
-        spread(lambda row: outer_ref[1, row], left_ref, right_ref, stack_ref, count + 1, (count + 1) * groups)
+        blocks = [
+            (lambda row: outer_ref[0, row], 0, 0, 0), (lambda row: outer_ref[1, row], end, end, count + 1)
+        ]
+        spread_blocks(blocks, left_ref, right_ref, stack_ref)
+        spread_own(own_ref, left_ref, right_ref, stack_ref, groups)
 
     either("col", every, one_ref, two_ref)
 
 
 def forward_kernel(
-    scale, own_ref, outer_ref, one_ref, two_ref, cotangent_ref, weight_ref, bias_ref,
+    scale, own_ref, near_ref, far_ref, one_ref, two_ref, cotangent_ref, weight_ref, bias_ref,
     activation_ref, grad_ref, send_one_ref, send_two_ref, rims_ref, terms_ref, stack_ref, sum_ref,
 ):
     height, channels, width = own_ref.shape
     count = height // DILATION
     groups = rims_ref.shape[1] // count
-    spread_all(own_ref, outer_ref, one_ref, two_ref, stack_ref)
+    spread_joined(own_ref, near_ref, far_ref, one_ref, two_ref, stack_ref)
     terms_ref[...] = jnp.zeros_like(terms_ref)
     sum_ref[...] = jnp.zeros_like(sum_ref)
     depth = 9 * channels
@@ -257,10 +325,11 @@
 
 
 def backward_kernel(
-    own_ref, outer_ref, one_ref, two_ref, weight_ref, out_ref, stack_ref
+    own_ref, outer_ref, one_ref, two_ref, weight_ref, out_ref, token_ref, stack_ref
 ):
     height, channels, width = own_ref.shape
-    spread_all(own_ref, outer_ref, one_ref, two_ref, stack_ref)
+    token_ref[...] = jnp.zeros_like(token_ref)
+    spread_outer(own_ref, outer_ref, one_ref, two_ref, stack_ref)
 
     def body(block, carry):
         start = pl.multiple_of(block * DILATION, DILATION)
@@ -273,7 +342,7 @@
     lax.fori_loop(0, height // DILATION, body, 0)
 
 
-def finish_kernel(one_ref, other_ref, weight_ref, bias_ref):
+def finish_kernel(one_ref, other_ref, after_ref, weight_ref, bias_ref):
     total = one_ref[...] + other_ref[...]
     channels = total.shape[0]
     for tap in range(9):
@@ -302,59 +371,55 @@
     scale = 1.0 / math.sqrt(height * lax.axis_size("row") * width * lax.axis_size("col"))
     shape = jax.ShapeDtypeStruct
     pieces = width // DILATION
-    own_groups, all_groups = height // pieces, (height + 2 * DILATION) // pieces
+    groups, own_groups = DILATION // pieces, height // pieces
     depth = 9 * channels
     stack = pltpu.VMEM((height // DILATION + 2, 3 * channels, DILATION * width), bf16)
     edge = shape((DILATION, channels, width), bf16)
-    packed = shape((all_groups, channels, width), bf16)
+    corner = shape((groups, channels, width), bf16)
+    own_packed = shape((own_groups, channels, width), bf16)
+    packed = shape((own_groups + 2 * groups, channels, width), bf16)
+    joint = shape((DILATION + 2 * groups, channels, width), bf16)
     own_rims = shape((2, own_groups, channels, width), bf16)
+    outer = shape((2, DILATION, channels, width), bf16)
     rows = shape((height, channels, width), bf16)
     flops = 2 * depth * channels * height * width
 
-    odd = lax.axis_index("row") % 2
-    outer = shape((2, DILATION, channels, width), bf16)
-    end = height - DILATION
-
-
-    def image_rim(start, first):
-        rim = lax.dynamic_slice_in_dim(image, start, DILATION, 1)
-        flag = alone("row", first)
-        return rim if flag is None else jnp.where(flag, jnp.zeros_like(rim), rim)
-
-    one = swap_pairs(image_rim((1 - odd) * end, 0), "row", 0)
-    two = swap_pairs(image_rim(odd * end, 1), "row", 1)
-    image_rows, rims = call(own_kernel, (rows, own_rims), (image,))
+    even = 1 - lax.axis_index("row") % 2
+    rim = lax.dynamic_slice_in_dim(image, even * (height - DILATION), DILATION, 1)
+    flag = alone("row", 0)
+    rim = swap_pairs(rim if flag is None else jnp.where(flag, jnp.zeros_like(rim), rim), "row", 0)
+    image_rows, one, two, corner_one, corner_two = call(
+        own_kernel, (rows, own_packed, own_packed, corner, corner), (image,), (pltpu.VMEM(own_rims.shape, bf16),)
+    )
     forward_weight = jnp.transpose(weight, (2, 0, 1, 3)).reshape(channels, depth)
     backward_weight = jnp.transpose(weight[::-1, ::-1], (3, 0, 1, 2)).reshape(channels, depth)
-    one, two, image_outer = call(
-        functools.partial(rim_kernel, True), (packed, packed, outer), (one, two, rims)
-    )
-    two, one = swap_pairs(two, "col", 1), swap_pairs(one, "col", 0)
+    one, two = swap_pairs(one, "col", 0), swap_pairs(two, "col", 1)
+    corner_one, corner_two = swap_corners(corner_one, 0, 0), swap_corners(corner_two, 0, 1)
+    far, near = call(join_kernel, (joint, joint), (image_rows, rim, one, two, corner_one, corner_two))
+    far = swap_pairs(far, "row", 1)
     activation, grads, one, two, rims, terms = call(
         functools.partial(forward_kernel, scale),
         (
             shape(image.shape, bf16), rows, edge, edge, own_rims,
             shape((channels, -(-(depth + 1) // 128) * 128), f32),
         ),
-        (image_rows, image_outer, one, two, cotangent, forward_weight, bias[:, None]),
+        (image_rows, near, far, one, two, cotangent, forward_weight, bias[:, None]),
         (stack, pltpu.VMEM((channels, width), f32)),
         2 * flops,
     )
     one, two = swap_pairs(one, "row", 0), swap_pairs(two, "row", 1)
-    one, two, grad_outer = call(
-        functools.partial(rim_kernel, False), (packed, packed, outer), (one, two, rims)
-    )
+    one, two, grad_outer = call(rim_kernel, (packed, packed, outer), (one, two, rims))
     two, one = swap_pairs(two, "col", 1), swap_pairs(one, "col", 0)
-    (grad_image,) = call(
+    grad_image, token = call(
         backward_kernel,
-        (shape(image.shape, bf16),),
+        (shape(image.shape, bf16), shape((8, 128), f32)),
         (grads, grad_outer, one, two, backward_weight),
         (stack,),
         flops,
     )
     one, other = add_pairs(terms, "col", "row")
     grad_weight, grad_bias = call(
-        finish_kernel, (shape(weight.shape, f32), shape((1, channels), f32)), (one, other)
+        finish_kernel, (shape(weight.shape, f32), shape((1, channels), f32)), (one, other, token)
     )
     return (activation, grad_image, grad_weight, grad_bias.reshape(channels))
 

time: 45.4 us -> 45.2 us (level)
  waiting for transfers between devices: 14.2 us -> 6.47 us
  starting transfers between devices: 17.3 us -> 24.1 us
  local copies, waits for them, and re-layouts: 1.01 us -> 2.97 us
  other arithmetic: 1.09 us -> 0.03 us
    ppermute x8, waiting for transfers between devices: 6.45 us -> 0.13 us  [swap_pairs(): return lax.ppermute(value, ('row', 'col'), pairs)]
    ppermute x7, waiting for transfers between devices: 7.8 us -> 4.12 us  [add_pairs(): lax.ppermute(value, axis, [(at, at ^ mask) for at in range(lax.axis_size(...]
    ppermute x0 -> x2, starting transfers between devices: none -> 3.21 us  [swap_corners(): return lax.ppermute(value, ('row', 'col'), pairs)]
    ppermute x0 -> x2, waiting for transfers between devices: none -> 2.22 us  [swap_corners(): return lax.ppermute(value, ('row', 'col'), pairs)]
    ppermute x8, starting transfers between devices: 10.1 us -> 12 us  [swap_pairs(): return lax.ppermute(value, ('row', 'col'), pairs)]
    ppermute x7, starting transfers between devices: 7.2 us -> 8.8 us  [add_pairs(): lax.ppermute(value, axis, [(at, at ^ mask) for at in range(lax.axis_size(...]
    select_n x1 -> x0, other arithmetic: 1.06 us -> none  [image_rim(): return rim if flag is None else jnp.where(flag, jnp.zeros_like(rim), rim)]
    unnamed x8, local copies, waits for them, and re-layouts: 0.66 us -> 1.7 us
  transfers between devices with their start and end apart: 15 -> 17, of which waited for: 5 -> 5; matrix products, arithmetic and copies ran while one was open for 1% -> 1% of each run, Pallas kernels for 4% -> 10%
where the time goes in v10:
time: 45.2 us; the launch traced here: 45 us
  starting transfers between devices  24.1 us (53%)
  Pallas kernels  10.7 us (24%)
  waiting for transfers between devices  6.47 us (14%)
  local copies, waits for them, and re-layouts  2.97 us (7%)
  between operations  0.8 us (2%)
    ppermute x8, starting transfers between devices, swap_pairs(): return lax.ppermute(value, ('row', 'col'), pairs)  12 us
    pallas_call x6, Pallas kernels, call(): pl.pallas_call(kernel, out_shape=out_shapes, in_specs=[whole] * len(opera...  10.7 us
    ppermute x7, starting transfers between devices, add_pairs(): lax.ppermute(value, axis, [(at, at ^ mask) for at in range(lax.axis_size(...  8.8 us
    ppermute x7, waiting for transfers between devices, add_pairs(): lax.ppermute(value, axis, [(at, at ^ mask) for at in range(lax.axis_size(...  4.12 us
    ppermute x2, starting transfers between devices, swap_corners(): return lax.ppermute(value, ('row', 'col'), pairs)  3.21 us
    ppermute x2, waiting for transfers between devices, swap_corners(): return lax.ppermute(value, ('row', 'col'), pairs)  2.22 us
    unnamed x8, local copies, waits for them, and re-layouts  1.7 us
    dynamic_slice x1, local copies, waits for them, and re-layouts, shards(): lax.dynamic_slice_in_dim(image, even * (height - DILATION), DILATION, 1)  0.93 us
  transfers between devices with their start and end apart: 17, of which 5 were waited for; matrix products, arithmetic and copies ran while one was open for 1% of the time, Pallas kernels for 10%

profile of v10, /device:TPU:0, one launch (start us, length us, event | category | flops | bytes accessed | tf_op | source)
XLA Modules:
  0.0 45.0 jit_solution(5606428483387676793)
XLA Ops:
  0.6 0.9 %constant_dynamic-slice_fusion = bf16[32,16,128]{2,1,0:T(8,128)(2,1)S(1)} fusion(bf16[32,64,128]{2,1,0:T(8,128)(2,1)} %image_ref.1, s32[]{:T(128)S(6)} %select_n.11), kind=kLoop, calls=%fused_computation.2 | loop fusion | bytes 262148 | tf_op jit(solution)/shard_map/dynamic_slice | solution.py:388
  1.6 3.0 %collective-permute-start = (bf16[32,16,128]{2,1,0:T(8,128)(2,1)S(1)}, bf16[32,16,128]{2,1,0:T(8,128)(2,1)S(1)}, u32[]{:S(2)}, u32[]{:S(2)}) collective-permute-start(bf16[32,16,128]{2,1,0:T(8,128)(2,1)S(1)} %constant_dynamic-slice_fusion), channel_id=1, source_target_pairs={{0,4},{1,5},{2,6},{3,7},{4,0},{5,1},{6,2},{7,3},{8,12},{9,13},{10,... | collective-permute-start | bytes 393224 | tf_op jit(solution)/shard_map/ppermute | solution.py:48
  4.6 1.0 %copy-done = bf16[32,64,128]{2,1,0:T(8,128)(2,1)S(1)} copy-done((bf16[32,64,128]{2,1,0:T(8,128)(2,1)S(1)}, bf16[32,64,128]{2,1,0:T(8,128)(2,1)}, u32[]{:S(2)}) %copy-start) | copy-done | bytes 524312
  5.7 0.8 %shard_map.75 = (bf16[64,32,128]{2,1,0:T(8,128)(2,1)S(1)}, bf16[8,32,128]{2,1,0:T(8,128)(2,1)S(1)}, bf16[8,32,128]{2,1,0:T(8,128)(2,1)S(1)}, bf16[2,32,128]{2,1,0:T(8,128)(2,1)S(1)}, bf16[2,32,128]{2,1,0:T(8,128)(2,1)S(1)}) custom-call(bf16[32,64,128]{2,1,0:T(8,128)(2,1)S(1)} %copy-done), custom_call_target="tpu_custom_call" | custom-call | bytes 1212416 | tf_op jit(solution)/shard_map/pallas_call | solution.py:357
  6.5 0.1 collective-permute-start.1
  6.6 0.1 collective-permute-start.2
  6.6 1.7 %collective-permute-start.3 = (bf16[2,32,128]{2,1,0:T(8,128)(2,1)S(1)}, bf16[2,32,128]{2,1,0:T(8,128)(2,1)S(1)}, u32[]{:S(2)}, u32[]{:S(2)}) collective-permute-start(bf16[2,32,128]{2,1,0:T(8,128)(2,1)S(1)} %get-tuple-element.27), channel_id=1, source_target_pairs={{0,5},{1,4},{2,7},{3,6},{4,1},{5,0},{6,3},{7,2},{8,13},{9,12},{10,... | collective-permute-start | bytes 49160 | tf_op jit(solution)/shard_map/ppermute | solution.py:63
  8.3 1.5 %collective-permute-start.4 = (bf16[2,32,128]{2,1,0:T(8,128)(2,1)S(1)}, bf16[2,32,128]{2,1,0:T(8,128)(2,1)S(1)}, u32[]{:S(2)}, u32[]{:S(2)}) collective-permute-start(bf16[2,32,128]{2,1,0:T(8,128)(2,1)S(1)} %get-tuple-element.28), channel_id=1, source_target_pairs={{0,4},{1,6},{2,5},{3,7},{4,0},{5,2},{6,1},{7,3},{8,12},{9,14},{10,... | collective-permute-start | bytes 49160 | tf_op jit(solution)/shard_map/ppermute | solution.py:63
  9.9 0.0 collective-permute-done.3.corner_one_ref
  9.9 2.2 %collective-permute-done.4.corner_two_ref = bf16[2,32,128]{2,1,0:T(8,128)(2,1)S(1)} collective-permute-done((bf16[2,32,128]{2,1,0:T(8,128)(2,1)S(1)}, bf16[2,32,128]{2,1,0:T(8,128)(2,1)S(1)}, u32[]{:S(2)}, u32[]{:S(2)}) %collective-permute-start.4) | collective-permute-done | bytes 16416 | tf_op jit(solution)/shard_map/ppermute | solution.py:63
  12.1 0.0 collective-permute-done.1.one_ref
  12.1 0.0 collective-permute-done.2.two_ref
  12.1 0.0 collective-permute-done.edge_ref
  12.1 0.0 copy-start.2
  12.1 0.0 copy-start.1
  12.1 0.1 shard_map.76
  12.2 0.8 %collective-permute-start.5 = (bf16[20,32,128]{2,1,0:T(8,128)(2,1)S(1)}, bf16[20,32,128]{2,1,0:T(8,128)(2,1)S(1)}, u32[]{:S(2)}, u32[]{:S(2)}) collective-permute-start(bf16[20,32,128]{2,1,0:T(8,128)(2,1)S(1)} %get-tuple-element.30), channel_id=1, source_target_pairs={{0,1},{1,0},{2,3},{3,2},{4,8},{5,9},{6,10},{7,11},{8,4},{9,5},{10,... | collective-permute-start | bytes 491528 | tf_op jit(solution)/shard_map/ppermute | solution.py:48
  13.0 0.1 copy.11
  13.1 0.1 reshape.17.weight_ref
  13.2 0.0 copy-start.3
  13.2 0.6 %copy-done.3 = f32[32]{0:T(128)S(1)} copy-done((f32[32]{0:T(128)S(1)}, f32[32]{0:T(128)}, u32[]{:S(2)}) %copy-start.3) | copy-done | bytes 152
  13.9 0.1 copy.12.bias_ref
  13.9 0.1 collective-permute-done.5.far_ref
  14.1 5.2 %shard_map.77 = (bf16[32,64,128]{2,1,0:T(8,128)(2,1)}, bf16[64,32,128]{2,1,0:T(8,128)(2,1)S(1)}, bf16[16,32,128]{2,1,0:T(8,128)(2,1)S(1)}, bf16[16,32,128]{2,1,0...) custom-call(bf16[64,32,128]{2,1,0:T(8,128)(2,1)S(1)} %get-tuple-element.24.rows_ref.own_ref, ...), custom_call_target="tpu_custom_call" | custom-call | flops 301989888 | bytes 3016832 | tf_op jit(solution)/shard_map/pallas_call | solution.py:357
  19.2 0.6 %collective-permute-start.10 = (f32[32,384]{1,0:T(8,128)S(1)}, f32[32,384]{1,0:T(8,128)S(1)}, u32[]{:S(2)}, u32[]{:S(2)}) collective-permute-start(f32[32,384]{1,0:T(8,128)S(1)} %get-tuple-element.40), channel_id=1, source_target_pairs={{0,1},{1,0},{2,3},{3,2},{4,5},{5,4},{6,7},{7,6},{8,9},{9,8},{10,11... | collective-permute-start | bytes 147464 | tf_op jit(solution)/shard_map/ppermute | solution.py:72
  19.8 1.1 %collective-permute-start.11 = (f32[32,384]{1,0:T(8,128)S(1)}, f32[32,384]{1,0:T(8,128)S(1)}, u32[]{:S(2)}, u32[]{:S(2)}) collective-permute-start(f32[32,384]{1,0:T(8,128)S(1)} %get-tuple-element.40), channel_id=1, source_target_pairs={{0,2},{1,3},{2,0},{3,1},{4,6},{5,7},{6,4},{7,5},{8,10},{9,11},{10,... | collective-permute-start | bytes 147464 | tf_op jit(solution)/shard_map/ppermute | solution.py:72
  21.0 0.2 collective-permute-start.12
  21.2 6.2 %collective-permute-start.6 = (bf16[16,32,128]{2,1,0:T(8,128)(2,1)S(1)}, bf16[16,32,128]{2,1,0:T(8,128)(2,1)S(1)}, u32[]{:S(2)}, u32[]{:S(2)}) collective-permute-start(bf16[16,32,128]{2,1,0:T(8,128)(2,1)S(1)} %get-tuple-element.33), channel_id=1, source_target_pairs={{0,4},{1,5},{2,6},{3,7},{4,0},{5,1},{6,2},{7,3},{8,12},{9,13},{10,... | collective-permute-start | bytes 393224 | tf_op jit(solution)/shard_map/ppermute | solution.py:48
  27.4 0.0 collective-permute-start.7
  27.4 0.0 collective-permute-done.10
  27.4 0.0 collective-permute-done.11
  27.4 0.0 collective-permute-done.12
  27.5 4.2 %collective-permute-start.13 = (f32[32,384]{1,0:T(8,128)S(1)}, f32[32,384]{1,0:T(8,128)S(1)}, u32[]{:S(2)}, u32[]{:S(2)}) collective-permute-start(f32[32,384]{1,0:T(8,128)S(1)} %add_add_fusion.1), channel_id=1, source_target_pairs={{0,8},{4,12},{8,0},{12,4},{16,24},{20,28},{24,16},{28,20},{1,9},{5... | collective-permute-start | bytes 147464 | tf_op jit(solution)/shard_map/ppermute | solution.py:72
  31.6 2.6 %collective-permute-start.14 = (f32[32,384]{1,0:T(8,128)S(1)}, f32[32,384]{1,0:T(8,128)S(1)}, u32[]{:S(2)}, u32[]{:S(2)}) collective-permute-start(f32[32,384]{1,0:T(8,128)S(1)} %add_add_fusion.1), channel_id=1, source_target_pairs={{0,16},{4,20},{8,24},{12,28},{16,0},{20,4},{24,8},{28,12},{1,17},{... | collective-permute-start | bytes 147464 | tf_op jit(solution)/shard_map/ppermute | solution.py:72
  34.2 0.0 collective-permute-start.15
  34.2 0.0 collective-permute-done.6.one_ref
  34.2 0.0 collective-permute-done.7.two_ref
  34.2 0.3 shard_map.78
  34.5 0.1 collective-permute-start.8
  34.6 1.7 %collective-permute-start.9 = (bf16[12,32,128]{2,1,0:T(8,128)(2,1)S(1)}, bf16[12,32,128]{2,1,0:T(8,128)(2,1)S(1)}, u32[]{:S(2)}, u32[]{:S(2)}) collective-permute-start(bf16[12,32,128]{2,1,0:T(8,128)(2,1)S(1)} %get-tuple-element.38), channel_id=1, source_target_pairs={{0,4},{4,0},{8,12},{12,8},{16,20},{20,16},{24,28},{28,24},{1,2},{5... | collective-permute-start | bytes 294920 | tf_op jit(solution)/shard_map/ppermute | solution.py:48
  36.3 1.2 %collective-permute-done.14 = f32[32,384]{1,0:T(8,128)S(1)} collective-permute-done((f32[32,384]{1,0:T(8,128)S(1)}, f32[32,384]{1,0:T(8,128)S(1)}, u32[]{:S(2)}, u32[]{:S(2)}) %collective-permute-start.14) | collective-permute-done | bytes 49184 | tf_op jit(solution)/shard_map/ppermute | solution.py:72
  37.5 2.6 %collective-permute-done.15 = f32[32,384]{1,0:T(8,128)S(1)} collective-permute-done((f32[32,384]{1,0:T(8,128)S(1)}, f32[32,384]{1,0:T(8,128)S(1)}, u32[]{:S(2)}, u32[]{:S(2)}) %collective-permute-start.15) | collective-permute-done | bytes 49184 | tf_op jit(solution)/shard_map/ppermute | solution.py:72
  40.1 0.1 collective-permute-start.16
  40.2 0.1 copy.14.weight_ref
  40.3 0.0 collective-permute-done.9.two_ref
  40.3 3.6 %shard_map.79 = (bf16[32,64,128]{2,1,0:T(8,128)(2,1)}, f32[8,128]{1,0:T(8,128)S(1)}) custom-call(bf16[64,32,128]{2,1,0:T(8,128)(2,1)S(1)} %get-tuple-element.32.own_ref, bf16[2,16,32,128]{3,2,1,0:T(8,128)(2,1)S(1)} %get-tuple-element.36.outer_ref, bf16[12,32,128]{2,1,0:T(8,128)(2,1)S(1)} %collective-permute-done.8.one_ref, ...), custom_call_target="tpu_custom_call" | custom-call | flops 150994944 | bytes 1529856 | tf_op jit(solution)/shard_map/pallas_call | solution.py:357
  44.0 0.3 collective-permute-done.16.other_ref
  44.3 0.8 %shard_map.80 = (f32[3,3,32,32]{3,2,1,0:T(8,128)}, f32[1,32]{1,0:T(1,128)}) custom-call(f32[32,384]{1,0:T(8,128)S(1)} %add_add_fusion.one_ref, f32[32,384]{1,0:T(8,128)S(1)} %collective-permute-done.16.other_ref, f32[8,128]{1,0:T(8,128)S(1)} %get-tuple-element.41.after_ref), custom_call_target="tpu_custom_call" | custom-call | bytes 139392 | tf_op jit(solution)/shard_map/pallas_call | solution.py:357
  (8 shorter events, 0.0 us)
Async XLA Ops:
  1.6 10.5 %collective-permute-start = (bf16[32,16,128]{2,1,0:T(8,128)(2,1)S(1)}, bf16[32,16,128]{2,1,0:T(8,128)(2,1)S(1)}, u32[]{:S(2)}, u32[]{:S(2)}) collective-permute-start(bf16[32,16,128]{2,1,0:T(8,128)(2,1)S(1)} %constant_dynamic-slice_fusion), channel_id=1, source_target_pairs={{0,4},{1,5},{2,6},{3,7},{4,0},{5,1},{6,2},{7,3},{8,12},{9,13},{10,... | collective-permute-start | bytes 393224 | tf_op jit(solution)/shard_map/ppermute | solution.py:48
  4.6 1.0 %copy-start = (bf16[32,64,128]{2,1,0:T(8,128)(2,1)S(1)}, bf16[32,64,128]{2,1,0:T(8,128)(2,1)}, u32[]{:S(2)}) copy-start(bf16[32,64,128]{2,1,0:T(8,128)(2,1)} %image_ref.1) | copy-start | bytes 1572868
  6.5 5.6 %collective-permute-start.1 = (bf16[8,32,128]{2,1,0:T(8,128)(2,1)S(1)}, bf16[8,32,128]{2,1,0:T(8,128)(2,1)S(1)}, u32[]{:S(2)}, u32[]{:S(2)}) collective-permute-start(bf16[8,32,128]{2,1,0:T(8,128)(2,1)S(1)} %get-tuple-element.25), channel_id=1, source_target_pairs={{0,1},{4,5},{8,9},{12,13},{16,17},{20,21},{24,25},{28,29},{1,0},{5... | collective-permute-start | bytes 196616 | tf_op jit(solution)/shard_map/ppermute | solution.py:48
  6.6 5.5 %collective-permute-start.2 = (bf16[8,32,128]{2,1,0:T(8,128)(2,1)S(1)}, bf16[8,32,128]{2,1,0:T(8,128)(2,1)S(1)}, u32[]{:S(2)}, u32[]{:S(2)}) collective-permute-start(bf16[8,32,128]{2,1,0:T(8,128)(2,1)S(1)} %get-tuple-element.26), channel_id=1, source_target_pairs={{0,4},{4,0},{8,12},{12,8},{16,20},{20,16},{24,28},{28,24},{1,2},{5... | collective-permute-start | bytes 196616 | tf_op jit(solution)/shard_map/ppermute | solution.py:48
  6.6 3.2 %collective-permute-start.3 = (bf16[2,32,128]{2,1,0:T(8,128)(2,1)S(1)}, bf16[2,32,128]{2,1,0:T(8,128)(2,1)S(1)}, u32[]{:S(2)}, u32[]{:S(2)}) collective-permute-start(bf16[2,32,128]{2,1,0:T(8,128)(2,1)S(1)} %get-tuple-element.27), channel_id=1, source_target_pairs={{0,5},{1,4},{2,7},{3,6},{4,1},{5,0},{6,3},{7,2},{8,13},{9,12},{10,... | collective-permute-start | bytes 49160 | tf_op jit(solution)/shard_map/ppermute | solution.py:63
  8.3 3.7 %collective-permute-start.4 = (bf16[2,32,128]{2,1,0:T(8,128)(2,1)S(1)}, bf16[2,32,128]{2,1,0:T(8,128)(2,1)S(1)}, u32[]{:S(2)}, u32[]{:S(2)}) collective-permute-start(bf16[2,32,128]{2,1,0:T(8,128)(2,1)S(1)} %get-tuple-element.28), channel_id=1, source_target_pairs={{0,4},{1,6},{2,5},{3,7},{4,0},{5,2},{6,1},{7,3},{8,12},{9,14},{10,... | collective-permute-start | bytes 49160 | tf_op jit(solution)/shard_map/ppermute | solution.py:63
  12.1 0.9 %copy-start.2 = (bf16[3,3,32,32]{3,2,1,0:T(8,128)(2,1)S(1)}, bf16[3,3,32,32]{3,2,1,0:T(8,128)(2,1)}, u32[]{:S(2)}) copy-start(bf16[3,3,32,32]{3,2,1,0:T(8,128)(2,1)} %param.5) | copy-start | bytes 55300
  12.1 2.0 %copy-start.1 = (bf16[32,64,128]{2,1,0:T(8,128)(2,1)S(1)}, bf16[32,64,128]{2,1,0:T(8,128)(2,1)}, u32[]{:S(2)}) copy-start(bf16[32,64,128]{2,1,0:T(8,128)(2,1)} %cotangent_ref.1) | copy-start | bytes 1572868
  12.2 1.9 %collective-permute-start.5 = (bf16[20,32,128]{2,1,0:T(8,128)(2,1)S(1)}, bf16[20,32,128]{2,1,0:T(8,128)(2,1)S(1)}, u32[]{:S(2)}, u32[]{:S(2)}) collective-permute-start(bf16[20,32,128]{2,1,0:T(8,128)(2,1)S(1)} %get-tuple-element.30), channel_id=1, source_target_pairs={{0,1},{1,0},{2,3},{3,2},{4,8},{5,9},{6,10},{7,11},{8,4},{9,5},{10,... | collective-permute-start | bytes 491528 | tf_op jit(solution)/shard_map/ppermute | solution.py:48
  13.2 0.7 %copy-start.3 = (f32[32]{0:T(128)S(1)}, f32[32]{0:T(128)}, u32[]{:S(2)}) copy-start(f32[32]{0:T(128)} %param.6) | copy-start | bytes 388
  19.2 8.2 %collective-permute-start.10 = (f32[32,384]{1,0:T(8,128)S(1)}, f32[32,384]{1,0:T(8,128)S(1)}, u32[]{:S(2)}, u32[]{:S(2)}) collective-permute-start(f32[32,384]{1,0:T(8,128)S(1)} %get-tuple-element.40), channel_id=1, source_target_pairs={{0,1},{1,0},{2,3},{3,2},{4,5},{5,4},{6,7},{7,6},{8,9},{9,8},{10,11... | collective-permute-start | bytes 147464 | tf_op jit(solution)/shard_map/ppermute | solution.py:72
  19.8 7.6 %collective-permute-start.11 = (f32[32,384]{1,0:T(8,128)S(1)}, f32[32,384]{1,0:T(8,128)S(1)}, u32[]{:S(2)}, u32[]{:S(2)}) collective-permute-start(f32[32,384]{1,0:T(8,128)S(1)} %get-tuple-element.40), channel_id=1, source_target_pairs={{0,2},{1,3},{2,0},{3,1},{4,6},{5,7},{6,4},{7,5},{8,10},{9,11},{10,... | collective-permute-start | bytes 147464 | tf_op jit(solution)/shard_map/ppermute | solution.py:72
  21.0 6.5 %collective-permute-start.12 = (f32[32,384]{1,0:T(8,128)S(1)}, f32[32,384]{1,0:T(8,128)S(1)}, u32[]{:S(2)}, u32[]{:S(2)}) collective-permute-start(f32[32,384]{1,0:T(8,128)S(1)} %get-tuple-element.40), channel_id=1, source_target_pairs={{0,3},{1,2},{2,1},{3,0},{4,7},{5,6},{6,5},{7,4},{8,11},{9,10},{10,... | collective-permute-start | bytes 147464 | tf_op jit(solution)/shard_map/ppermute | solution.py:72
  21.2 13.0 %collective-permute-start.6 = (bf16[16,32,128]{2,1,0:T(8,128)(2,1)S(1)}, bf16[16,32,128]{2,1,0:T(8,128)(2,1)S(1)}, u32[]{:S(2)}, u32[]{:S(2)}) collective-permute-start(bf16[16,32,128]{2,1,0:T(8,128)(2,1)S(1)} %get-tuple-element.33), channel_id=1, source_target_pairs={{0,4},{1,5},{2,6},{3,7},{4,0},{5,1},{6,2},{7,3},{8,12},{9,13},{10,... | collective-permute-start | bytes 393224 | tf_op jit(solution)/shard_map/ppermute | solution.py:48
  27.4 6.8 %collective-permute-start.7 = (bf16[16,32,128]{2,1,0:T(8,128)(2,1)S(1)}, bf16[16,32,128]{2,1,0:T(8,128)(2,1)S(1)}, u32[]{:S(2)}, u32[]{:S(2)}) collective-permute-start(bf16[16,32,128]{2,1,0:T(8,128)(2,1)S(1)} %get-tuple-element.34), channel_id=1, source_target_pairs={{0,1},{1,0},{2,3},{3,2},{4,8},{5,9},{6,10},{7,11},{8,4},{9,5},{10,... | collective-permute-start | bytes 393224 | tf_op jit(solution)/shard_map/ppermute | solution.py:48
  27.5 8.9 %collective-permute-start.13 = (f32[32,384]{1,0:T(8,128)S(1)}, f32[32,384]{1,0:T(8,128)S(1)}, u32[]{:S(2)}, u32[]{:S(2)}) collective-permute-start(f32[32,384]{1,0:T(8,128)S(1)} %add_add_fusion.1), channel_id=1, source_target_pairs={{0,8},{4,12},{8,0},{12,4},{16,24},{20,28},{24,16},{28,20},{1,9},{5... | collective-permute-start | bytes 147464 | tf_op jit(solution)/shard_map/ppermute | solution.py:72
  31.6 5.9 %collective-permute-start.14 = (f32[32,384]{1,0:T(8,128)S(1)}, f32[32,384]{1,0:T(8,128)S(1)}, u32[]{:S(2)}, u32[]{:S(2)}) collective-permute-start(f32[32,384]{1,0:T(8,128)S(1)} %add_add_fusion.1), channel_id=1, source_target_pairs={{0,16},{4,20},{8,24},{12,28},{16,0},{20,4},{24,8},{28,12},{1,17},{... | collective-permute-start | bytes 147464 | tf_op jit(solution)/shard_map/ppermute | solution.py:72
  34.2 5.9 %collective-permute-start.15 = (f32[32,384]{1,0:T(8,128)S(1)}, f32[32,384]{1,0:T(8,128)S(1)}, u32[]{:S(2)}, u32[]{:S(2)}) collective-permute-start(f32[32,384]{1,0:T(8,128)S(1)} %add_add_fusion.1), channel_id=1, source_target_pairs={{0,24},{4,28},{8,16},{12,20},{16,8},{20,12},{24,0},{28,4},{1,25},{... | collective-permute-start | bytes 147464 | tf_op jit(solution)/shard_map/ppermute | solution.py:72
  34.5 5.8 %collective-permute-start.8 = (bf16[12,32,128]{2,1,0:T(8,128)(2,1)S(1)}, bf16[12,32,128]{2,1,0:T(8,128)(2,1)S(1)}, u32[]{:S(2)}, u32[]{:S(2)}) collective-permute-start(bf16[12,32,128]{2,1,0:T(8,128)(2,1)S(1)} %get-tuple-element.37), channel_id=1, source_target_pairs={{0,1},{4,5},{8,9},{12,13},{16,17},{20,21},{24,25},{28,29},{1,0},{5... | collective-permute-start | bytes 294920 | tf_op jit(solution)/shard_map/ppermute | solution.py:48
  34.6 5.7 %collective-permute-start.9 = (bf16[12,32,128]{2,1,0:T(8,128)(2,1)S(1)}, bf16[12,32,128]{2,1,0:T(8,128)(2,1)S(1)}, u32[]{:S(2)}, u32[]{:S(2)}) collective-permute-start(bf16[12,32,128]{2,1,0:T(8,128)(2,1)S(1)} %get-tuple-element.38), channel_id=1, source_target_pairs={{0,4},{4,0},{8,12},{12,8},{16,20},{20,16},{24,28},{28,24},{1,2},{5... | collective-permute-start | bytes 294920 | tf_op jit(solution)/shard_map/ppermute | solution.py:48
  40.1 4.2 %collective-permute-start.16 = (f32[32,384]{1,0:T(8,128)S(1)}, f32[32,384]{1,0:T(8,128)S(1)}, u32[]{:S(2)}, u32[]{:S(2)}) collective-permute-start(f32[32,384]{1,0:T(8,128)S(1)} %add_add_fusion.one_ref), channel_id=1, source_target_pairs={{0,4},{4,0},{8,12},{12,8},{16,20},{20,16},{24,28},{28,24},{1,5},{5... | collective-permute-start | bytes 147464 | tf_op jit(solution)/shard_map/ppermute | solution.py:72

commit v11 on v8

--- a/solution.py
+++ b/solution.py
@@ -206,13 +206,13 @@
 
 def forward_kernel(
     scale, own_ref, outer_ref, one_ref, two_ref, cotangent_ref, weight_ref, bias_ref,
-    activation_ref, grad_ref, send_one_ref, send_two_ref, rims_ref, terms_ref, stack_ref, sum_ref,
+    activation_ref, grad_ref, send_one_ref, send_two_ref, rims_ref, terms_ref, stack_ref, sum_ref, taps_ref,
 ):
     height, channels, width = own_ref.shape
     count = height // DILATION
     groups = rims_ref.shape[1] // count
     spread_all(own_ref, outer_ref, one_ref, two_ref, stack_ref)
-    terms_ref[...] = jnp.zeros_like(terms_ref)
+    taps_ref[...] = jnp.zeros_like(taps_ref)
     sum_ref[...] = jnp.zeros_like(sum_ref)
     depth = 9 * channels
 
@@ -237,8 +237,8 @@
             grad_ref[start + row] = grad
         sum_ref[...] = total
         activation_ref[:, pl.ds(start, DILATION), :] = jnp.swapaxes(jnp.stack(values), 0, 1)
-        terms_ref[:, :depth] += lax.dot_general(
-            jnp.concatenate(grads, axis=1), stacked, (((1,), (1,)), ((), ())),
+        taps_ref[...] += lax.dot_general(
+            stacked, jnp.concatenate(grads, axis=1), (((1,), (1,)), ((), ())),
             preferred_element_type=jnp.float32,
         )
         pack_rows(jnp.stack(grads), store, block * groups)
@@ -251,15 +251,16 @@
     send_two_ref[...] = grad_ref[pl.ds(odd * end, DILATION)]
     clear_if(alone("row", 0), send_one_ref)
     clear_if(alone("row", 1), send_two_ref)
-    terms_ref[:, :depth] = terms_ref[:, :depth] * scale
+    terms_ref[:, :depth] = jnp.transpose(taps_ref[...]) * scale
     sums = jnp.sum(sum_ref[...], axis=1, keepdims=True) * scale
     terms_ref[:, depth:] = jnp.broadcast_to(sums, (channels, terms_ref.shape[1] - depth))
 
 
 def backward_kernel(
-    own_ref, outer_ref, one_ref, two_ref, weight_ref, out_ref, stack_ref
+    own_ref, outer_ref, one_ref, two_ref, weight_ref, out_ref, token_ref, stack_ref
 ):
     height, channels, width = own_ref.shape
+    token_ref[...] = jnp.zeros_like(token_ref)
     spread_all(own_ref, outer_ref, one_ref, two_ref, stack_ref)
 
     def body(block, carry):
@@ -273,7 +274,7 @@
     lax.fori_loop(0, height // DILATION, body, 0)
 
 
-def finish_kernel(one_ref, other_ref, weight_ref, bias_ref):
+def finish_kernel(one_ref, other_ref, after_ref, weight_ref, bias_ref):
     total = one_ref[...] + other_ref[...]
     channels = total.shape[0]
     for tap in range(9):
@@ -337,7 +338,7 @@
             shape((channels, -(-(depth + 1) // 128) * 128), f32),
         ),
         (image_rows, image_outer, one, two, cotangent, forward_weight, bias[:, None]),
-        (stack, pltpu.VMEM((channels, width), f32)),
+        (stack, pltpu.VMEM((channels, width), f32), pltpu.VMEM((depth, channels), f32)),
         2 * flops,
     )
     one, two = swap_pairs(one, "row", 0), swap_pairs(two, "row", 1)
@@ -345,16 +346,16 @@
         functools.partial(rim_kernel, False), (packed, packed, outer), (one, two, rims)
     )
     two, one = swap_pairs(two, "col", 1), swap_pairs(one, "col", 0)
-    (grad_image,) = call(
+    grad_image, token = call(
         backward_kernel,
-        (shape(image.shape, bf16),),
+        (shape(image.shape, bf16), shape((8, 128), f32)),
         (grads, grad_outer, one, two, backward_weight),
         (stack,),
         flops,
     )
     one, other = add_pairs(terms, "col", "row")
     grad_weight, grad_bias = call(
-        finish_kernel, (shape(weight.shape, f32), shape((1, channels), f32)), (one, other)
+        finish_kernel, (shape(weight.shape, f32), shape((1, channels), f32)), (one, other, token)
     )
     return (activation, grad_image, grad_weight, grad_bias.reshape(channels))
 

time: 45.4 us -> 41.8 us (0.921)
  waiting for transfers between devices: 14.2 us -> 10.6 us
    ppermute x7, waiting for transfers between devices: 7.8 us -> 4.16 us  [add_pairs(): lax.ppermute(value, axis, [(at, at ^ mask) for at in range(lax.axis_size(...]
  transfers between devices with their start and end apart: 15 -> 15, of which waited for: 5 -> 5; matrix products, arithmetic and copies ran while one was open for 1% -> 1% of each run, Pallas kernels for 4% -> 11%
where the time goes in v11:
time: 41.8 us; the launch traced here: 41.6 us
  starting transfers between devices  17.3 us (41%)
  Pallas kernels  10.8 us (26%)
  waiting for transfers between devices  10.6 us (25%)
  other arithmetic  1.09 us (3%)
  local copies, waits for them, and re-layouts  1.01 us (2%)
  between operations  0.77 us (2%)
    pallas_call x6, Pallas kernels, call(): pl.pallas_call(kernel, out_shape=out_shapes, in_specs=[whole] * len(opera...  10.8 us
    ppermute x8, starting transfers between devices, swap_pairs(): return lax.ppermute(value, ('row', 'col'), pairs)  10.1 us
    ppermute x7, starting transfers between devices, add_pairs(): lax.ppermute(value, axis, [(at, at ^ mask) for at in range(lax.axis_size(...  7.2 us
    ppermute x8, waiting for transfers between devices, swap_pairs(): return lax.ppermute(value, ('row', 'col'), pairs)  6.45 us
    ppermute x7, waiting for transfers between devices, add_pairs(): lax.ppermute(value, axis, [(at, at ^ mask) for at in range(lax.axis_size(...  4.16 us
    select_n x1, other arithmetic, image_rim(): return rim if flag is None else jnp.where(flag, jnp.zeros_like(rim), rim)  1.06 us
  transfers between devices with their start and end apart: 15, of which 5 were waited for; matrix products, arithmetic and copies ran while one was open for 1% of the time, Pallas kernels for 11%

profile of v11, /device:TPU:0, one launch (start us, length us, event | category | flops | bytes accessed | tf_op | source)
XLA Modules:
  0.0 41.6 jit_solution(1796028794654545059)
XLA Ops:
  0.6 0.0 copy-start
  0.7 1.1 %dynamic-slice_select_fusion = (bf16[32,16,128]{2,1,0:T(8,128)(2,1)S(1)}, bf16[32,16,128]{2,1,0:T(8,128)(2,1)S(1)}) fusion(bf16[32,64,128]{2,1,0:T(8,128)(2,1)} %image_ref.1, s32[]{:T(128)S(6)} %select_n.24, pred[]{:T(512)S(6)} %or.3, s32[]{:T(128)S(6)} %select_n.22), kind=kLoop, calls=%fused_computation | loop fusion | flops 65536 | bytes 524297 | tf_op jit(solution)/shard_map/jit(_where)/select_n | solution.py:323
  1.7 3.0 %collective-permute-start = (bf16[32,16,128]{2,1,0:T(8,128)(2,1)S(1)}, bf16[32,16,128]{2,1,0:T(8,128)(2,1)S(1)}, u32[]{:S(2)}, u32[]{:S(2)}) collective-permute-start(bf16[32,16,128]{2,1,0:T(8,128)(2,1)S(1)} %get-tuple-element.41), channel_id=1, source_target_pairs={{0,4},{1,5},{2,6},{3,7},{4,0},{5,1},{6,2},{7,3},{8,12},{9,13},{10,... | collective-permute-start | bytes 393224 | tf_op jit(solution)/shard_map/ppermute | solution.py:48
  4.8 0.0 copy-start.1
  4.8 0.0 collective-permute-start.1
  4.8 0.0 copy-done
  4.8 0.8 %shard_map.75 = (bf16[64,32,128]{2,1,0:T(8,128)(2,1)S(1)}, bf16[2,8,32,128]{3,2,1,0:T(8,128)(2,1)S(1)}) custom-call(bf16[32,64,128]{2,1,0:T(8,128)(2,1)S(1)} %copy-done), custom_call_target="tpu_custom_call" | custom-call | bytes 1179648 | tf_op jit(solution)/shard_map/pallas_call | solution.py:289
  5.6 4.8 %collective-permute-done.one_ref = bf16[32,16,128]{2,1,0:T(8,128)(2,1)S(1)} collective-permute-done((bf16[32,16,128]{2,1,0:T(8,128)(2,1)S(1)}, bf16[32,16,128]{2,1,0:T(8,128)(2,1)S(1)}, u32[]{:S(2)}, u32[]{:S(2)}) %collective-permute-start) | collective-permute-done | bytes 131104 | tf_op jit(solution)/shard_map/ppermute | solution.py:48
  10.3 0.0 collective-permute-done.1.two_ref
  10.3 0.3 shard_map.76
  10.6 0.1 collective-permute-start.2
  10.7 2.6 %collective-permute-start.3 = (bf16[12,32,128]{2,1,0:T(8,128)(2,1)S(1)}, bf16[12,32,128]{2,1,0:T(8,128)(2,1)S(1)}, u32[]{:S(2)}, u32[]{:S(2)}) collective-permute-start(bf16[12,32,128]{2,1,0:T(8,128)(2,1)S(1)} %get-tuple-element.26), channel_id=1, source_target_pairs={{0,4},{4,0},{8,12},{12,8},{16,20},{20,16},{24,28},{28,24},{1,2},{5... | collective-permute-start | bytes 294920 | tf_op jit(solution)/shard_map/ppermute | solution.py:48
  13.3 0.0 copy-done.2
  13.3 0.1 copy.11
  13.3 0.1 reshape.17.weight_ref
  13.4 0.0 copy-start.3
  13.5 0.6 %copy-done.3 = f32[32]{0:T(128)S(1)} copy-done((f32[32]{0:T(128)S(1)}, f32[32]{0:T(128)}, u32[]{:S(2)}) %copy-start.3) | copy-done | bytes 152
  14.1 0.1 copy.12.bias_ref
  14.2 0.0 collective-permute-done.2.one_ref
  14.2 1.7 %collective-permute-done.3.two_ref = bf16[12,32,128]{2,1,0:T(8,128)(2,1)S(1)} collective-permute-done((bf16[12,32,128]{2,1,0:T(8,128)(2,1)S(1)}, bf16[12,32,128]{2,1,0:T(8,128)(2,1)S(1)}, u32[]{:S(2)}, u32[]{:S(2)}) %collective-permute-start.3) | collective-permute-done | bytes 98336 | tf_op jit(solution)/shard_map/ppermute | solution.py:48
  15.9 0.0 copy-done.1
  15.9 5.1 %shard_map.77 = (bf16[32,64,128]{2,1,0:T(8,128)(2,1)}, bf16[64,32,128]{2,1,0:T(8,128)(2,1)S(1)}, bf16[16,32,128]{2,1,0:T(8,128)(2,1)S(1)}, bf16[16,32,128]{2,1,0...) custom-call(bf16[64,32,128]{2,1,0:T(8,128)(2,1)S(1)} %get-tuple-element.22.own_ref, ...), custom_call_target="tpu_custom_call" | custom-call | flops 301989888 | bytes 3016832 | tf_op jit(solution)/shard_map/pallas_call | solution.py:289
  20.9 0.6 %collective-permute-start.10 = (f32[32,384]{1,0:T(8,128)S(1)}, f32[32,384]{1,0:T(8,128)S(1)}, u32[]{:S(2)}, u32[]{:S(2)}) collective-permute-start(f32[32,384]{1,0:T(8,128)S(1)} %get-tuple-element.36), channel_id=1, source_target_pairs={{0,3},{1,2},{2,1},{3,0},{4,7},{5,6},{6,5},{7,4},{8,11},{9,10},{10,... | collective-permute-start | bytes 147464 | tf_op jit(solution)/shard_map/ppermute | solution.py:62
  21.6 0.0 collective-permute-start.8
  21.6 1.5 %collective-permute-start.9 = (f32[32,384]{1,0:T(8,128)S(1)}, f32[32,384]{1,0:T(8,128)S(1)}, u32[]{:S(2)}, u32[]{:S(2)}) collective-permute-start(f32[32,384]{1,0:T(8,128)S(1)} %get-tuple-element.36), channel_id=1, source_target_pairs={{0,2},{1,3},{2,0},{3,1},{4,6},{5,7},{6,4},{7,5},{8,10},{9,11},{10,... | collective-permute-start | bytes 147464 | tf_op jit(solution)/shard_map/ppermute | solution.py:62
  23.1 2.0 %collective-permute-start.4 = (bf16[16,32,128]{2,1,0:T(8,128)(2,1)S(1)}, bf16[16,32,128]{2,1,0:T(8,128)(2,1)S(1)}, u32[]{:S(2)}, u32[]{:S(2)}) collective-permute-start(bf16[16,32,128]{2,1,0:T(8,128)(2,1)S(1)} %get-tuple-element.29), channel_id=1, source_target_pairs={{0,4},{1,5},{2,6},{3,7},{4,0},{5,1},{6,2},{7,3},{8,12},{9,13},{10,... | collective-permute-start | bytes 393224 | tf_op jit(solution)/shard_map/ppermute | solution.py:48
  25.1 0.0 collective-permute-start.5
  25.1 0.0 collective-permute-done.10
  25.1 0.0 collective-permute-done.8
  25.1 0.8 %collective-permute-done.9 = f32[32,384]{1,0:T(8,128)S(1)} collective-permute-done((f32[32,384]{1,0:T(8,128)S(1)}, f32[32,384]{1,0:T(8,128)S(1)}, u32[]{:S(2)}, u32[]{:S(2)}) %collective-permute-start.9) | collective-permute-done | bytes 49184 | tf_op jit(solution)/shard_map/ppermute | solution.py:62
  25.9 2.3 %collective-permute-start.11 = (f32[32,384]{1,0:T(8,128)S(1)}, f32[32,384]{1,0:T(8,128)S(1)}, u32[]{:S(2)}, u32[]{:S(2)}) collective-permute-start(f32[32,384]{1,0:T(8,128)S(1)} %add_add_fusion.1), channel_id=1, source_target_pairs={{0,8},{4,12},{8,0},{12,4},{16,24},{20,28},{24,16},{28,20},{1,9},{5... | collective-permute-start | bytes 147464 | tf_op jit(solution)/shard_map/ppermute | solution.py:62
  28.2 2.6 %collective-permute-start.12 = (f32[32,384]{1,0:T(8,128)S(1)}, f32[32,384]{1,0:T(8,128)S(1)}, u32[]{:S(2)}, u32[]{:S(2)}) collective-permute-start(f32[32,384]{1,0:T(8,128)S(1)} %add_add_fusion.1), channel_id=1, source_target_pairs={{0,16},{4,20},{8,24},{12,28},{16,0},{20,4},{24,8},{28,12},{1,17},{... | collective-permute-start | bytes 147464 | tf_op jit(solution)/shard_map/ppermute | solution.py:62
  30.8 0.0 collective-permute-start.13
  30.8 0.0 collective-permute-done.4.one_ref
  30.8 0.0 collective-permute-done.5.two_ref
  30.8 0.3 shard_map.78
  31.1 0.1 collective-permute-start.6
  31.1 2.4 %collective-permute-start.7 = (bf16[12,32,128]{2,1,0:T(8,128)(2,1)S(1)}, bf16[12,32,128]{2,1,0:T(8,128)(2,1)S(1)}, u32[]{:S(2)}, u32[]{:S(2)}) collective-permute-start(bf16[12,32,128]{2,1,0:T(8,128)(2,1)S(1)} %get-tuple-element.34), channel_id=1, source_target_pairs={{0,4},{4,0},{8,12},{12,8},{16,20},{20,16},{24,28},{28,24},{1,2},{5... | collective-permute-start | bytes 294920 | tf_op jit(solution)/shard_map/ppermute | solution.py:48
  33.5 0.0 collective-permute-done.11
  33.5 0.0 collective-permute-done.12
  33.5 3.1 %collective-permute-done.13 = f32[32,384]{1,0:T(8,128)S(1)} collective-permute-done((f32[32,384]{1,0:T(8,128)S(1)}, f32[32,384]{1,0:T(8,128)S(1)}, u32[]{:S(2)}, u32[]{:S(2)}) %collective-permute-start.13) | collective-permute-done | bytes 49184 | tf_op jit(solution)/shard_map/ppermute | solution.py:62
  36.7 0.2 collective-permute-start.14
  36.9 0.1 copy.14.weight_ref
  37.0 0.0 collective-permute-done.6.one_ref
  37.0 0.0 collective-permute-done.7.two_ref
  37.0 3.6 %shard_map.79 = (bf16[32,64,128]{2,1,0:T(8,128)(2,1)}, f32[8,128]{1,0:T(8,128)S(1)}) custom-call(bf16[64,32,128]{2,1,0:T(8,128)(2,1)S(1)} %get-tuple-element.28.own_ref, bf16[2,16,32,128]{3,2,1,0:T(8,128)(2,1)S(1)} %get-tuple-element.32.outer_ref, bf16[12,32,128]{2,1,0:T(8,128)(2,1)S(1)} %collective-permute-done.6.one_ref, ...), custom_call_target="tpu_custom_call" | custom-call | flops 150994944 | bytes 1529856 | tf_op jit(solution)/shard_map/pallas_call | solution.py:289
  40.6 0.2 collective-permute-done.14.other_ref
  40.8 0.8 %shard_map.80 = (f32[3,3,32,32]{3,2,1,0:T(8,128)}, f32[1,32]{1,0:T(1,128)}) custom-call(f32[32,384]{1,0:T(8,128)S(1)} %add_add_fusion.one_ref, f32[32,384]{1,0:T(8,128)S(1)} %collective-permute-done.14.other_ref, f32[8,128]{1,0:T(8,128)S(1)} %get-tuple-element.37.after_ref), custom_call_target="tpu_custom_call" | custom-call | bytes 139392 | tf_op jit(solution)/shard_map/pallas_call | solution.py:289
  (4 shorter events, 0.0 us)
Async XLA Ops:
  0.6 4.1 %copy-start = (bf16[32,64,128]{2,1,0:T(8,128)(2,1)S(1)}, bf16[32,64,128]{2,1,0:T(8,128)(2,1)}, u32[]{:S(2)}) copy-start(bf16[32,64,128]{2,1,0:T(8,128)(2,1)} %image_ref.1) | copy-start | bytes 1572868
  1.7 8.6 %collective-permute-start = (bf16[32,16,128]{2,1,0:T(8,128)(2,1)S(1)}, bf16[32,16,128]{2,1,0:T(8,128)(2,1)S(1)}, u32[]{:S(2)}, u32[]{:S(2)}) collective-permute-start(bf16[32,16,128]{2,1,0:T(8,128)(2,1)S(1)} %get-tuple-element.41), channel_id=1, source_target_pairs={{0,4},{1,5},{2,6},{3,7},{4,0},{5,1},{6,2},{7,3},{8,12},{9,13},{10,... | collective-permute-start | bytes 393224 | tf_op jit(solution)/shard_map/ppermute | solution.py:48
  4.8 11.1 %copy-start.1 = (bf16[32,64,128]{2,1,0:T(8,128)(2,1)S(1)}, bf16[32,64,128]{2,1,0:T(8,128)(2,1)}, u32[]{:S(2)}) copy-start(bf16[32,64,128]{2,1,0:T(8,128)(2,1)} %cotangent_ref.1) | copy-start | bytes 1572868
  4.8 5.6 %collective-permute-start.1 = (bf16[32,16,128]{2,1,0:T(8,128)(2,1)S(1)}, bf16[32,16,128]{2,1,0:T(8,128)(2,1)S(1)}, u32[]{:S(2)}, u32[]{:S(2)}) collective-permute-start(bf16[32,16,128]{2,1,0:T(8,128)(2,1)S(1)} %get-tuple-element.40), channel_id=1, source_target_pairs={{0,1},{1,0},{2,3},{3,2},{4,8},{5,9},{6,10},{7,11},{8,4},{9,5},{10,... | collective-permute-start | bytes 393224 | tf_op jit(solution)/shard_map/ppermute | solution.py:48
  10.3 2.9 %copy-start.2 = (bf16[3,3,32,32]{3,2,1,0:T(8,128)(2,1)S(1)}, bf16[3,3,32,32]{3,2,1,0:T(8,128)(2,1)}, u32[]{:S(2)}) copy-start(bf16[3,3,32,32]{3,2,1,0:T(8,128)(2,1)} %param.5) | copy-start | bytes 55300
  10.6 3.6 %collective-permute-start.2 = (bf16[12,32,128]{2,1,0:T(8,128)(2,1)S(1)}, bf16[12,32,128]{2,1,0:T(8,128)(2,1)S(1)}, u32[]{:S(2)}, u32[]{:S(2)}) collective-permute-start(bf16[12,32,128]{2,1,0:T(8,128)(2,1)S(1)} %get-tuple-element.25), channel_id=1, source_target_pairs={{0,1},{4,5},{8,9},{12,13},{16,17},{20,21},{24,25},{28,29},{1,0},{5... | collective-permute-start | bytes 294920 | tf_op jit(solution)/shard_map/ppermute | solution.py:48
  10.7 5.1 %collective-permute-start.3 = (bf16[12,32,128]{2,1,0:T(8,128)(2,1)S(1)}, bf16[12,32,128]{2,1,0:T(8,128)(2,1)S(1)}, u32[]{:S(2)}, u32[]{:S(2)}) collective-permute-start(bf16[12,32,128]{2,1,0:T(8,128)(2,1)S(1)} %get-tuple-element.26), channel_id=1, source_target_pairs={{0,4},{4,0},{8,12},{12,8},{16,20},{20,16},{24,28},{28,24},{1,2},{5... | collective-permute-start | bytes 294920 | tf_op jit(solution)/shard_map/ppermute | solution.py:48
  13.4 0.7 %copy-start.3 = (f32[32]{0:T(128)S(1)}, f32[32]{0:T(128)}, u32[]{:S(2)}) copy-start(f32[32]{0:T(128)} %param.6) | copy-start | bytes 388
  20.9 4.2 %collective-permute-start.10 = (f32[32,384]{1,0:T(8,128)S(1)}, f32[32,384]{1,0:T(8,128)S(1)}, u32[]{:S(2)}, u32[]{:S(2)}) collective-permute-start(f32[32,384]{1,0:T(8,128)S(1)} %get-tuple-element.36), channel_id=1, source_target_pairs={{0,3},{1,2},{2,1},{3,0},{4,7},{5,6},{6,5},{7,4},{8,11},{9,10},{10,... | collective-permute-start | bytes 147464 | tf_op jit(solution)/shard_map/ppermute | solution.py:62
  21.6 3.5 %collective-permute-start.8 = (f32[32,384]{1,0:T(8,128)S(1)}, f32[32,384]{1,0:T(8,128)S(1)}, u32[]{:S(2)}, u32[]{:S(2)}) collective-permute-start(f32[32,384]{1,0:T(8,128)S(1)} %get-tuple-element.36), channel_id=1, source_target_pairs={{0,1},{1,0},{2,3},{3,2},{4,5},{5,4},{6,7},{7,6},{8,9},{9,8},{10,11... | collective-permute-start | bytes 147464 | tf_op jit(solution)/shard_map/ppermute | solution.py:62
  21.6 4.3 %collective-permute-start.9 = (f32[32,384]{1,0:T(8,128)S(1)}, f32[32,384]{1,0:T(8,128)S(1)}, u32[]{:S(2)}, u32[]{:S(2)}) collective-permute-start(f32[32,384]{1,0:T(8,128)S(1)} %get-tuple-element.36), channel_id=1, source_target_pairs={{0,2},{1,3},{2,0},{3,1},{4,6},{5,7},{6,4},{7,5},{8,10},{9,11},{10,... | collective-permute-start | bytes 147464 | tf_op jit(solution)/shard_map/ppermute | solution.py:62
  23.1 7.7 %collective-permute-start.4 = (bf16[16,32,128]{2,1,0:T(8,128)(2,1)S(1)}, bf16[16,32,128]{2,1,0:T(8,128)(2,1)S(1)}, u32[]{:S(2)}, u32[]{:S(2)}) collective-permute-start(bf16[16,32,128]{2,1,0:T(8,128)(2,1)S(1)} %get-tuple-element.29), channel_id=1, source_target_pairs={{0,4},{1,5},{2,6},{3,7},{4,0},{5,1},{6,2},{7,3},{8,12},{9,13},{10,... | collective-permute-start | bytes 393224 | tf_op jit(solution)/shard_map/ppermute | solution.py:48
  25.1 5.7 %collective-permute-start.5 = (bf16[16,32,128]{2,1,0:T(8,128)(2,1)S(1)}, bf16[16,32,128]{2,1,0:T(8,128)(2,1)S(1)}, u32[]{:S(2)}, u32[]{:S(2)}) collective-permute-start(bf16[16,32,128]{2,1,0:T(8,128)(2,1)S(1)} %get-tuple-element.30), channel_id=1, source_target_pairs={{0,1},{1,0},{2,3},{3,2},{4,8},{5,9},{6,10},{7,11},{8,4},{9,5},{10,... | collective-permute-start | bytes 393224 | tf_op jit(solution)/shard_map/ppermute | solution.py:48
  25.9 7.6 %collective-permute-start.11 = (f32[32,384]{1,0:T(8,128)S(1)}, f32[32,384]{1,0:T(8,128)S(1)}, u32[]{:S(2)}, u32[]{:S(2)}) collective-permute-start(f32[32,384]{1,0:T(8,128)S(1)} %add_add_fusion.1), channel_id=1, source_target_pairs={{0,8},{4,12},{8,0},{12,4},{16,24},{20,28},{24,16},{28,20},{1,9},{5... | collective-permute-start | bytes 147464 | tf_op jit(solution)/shard_map/ppermute | solution.py:62
  28.2 5.3 %collective-permute-start.12 = (f32[32,384]{1,0:T(8,128)S(1)}, f32[32,384]{1,0:T(8,128)S(1)}, u32[]{:S(2)}, u32[]{:S(2)}) collective-permute-start(f32[32,384]{1,0:T(8,128)S(1)} %add_add_fusion.1), channel_id=1, source_target_pairs={{0,16},{4,20},{8,24},{12,28},{16,0},{20,4},{24,8},{28,12},{1,17},{... | collective-permute-start | bytes 147464 | tf_op jit(solution)/shard_map/ppermute | solution.py:62
  30.8 5.9 %collective-permute-start.13 = (f32[32,384]{1,0:T(8,128)S(1)}, f32[32,384]{1,0:T(8,128)S(1)}, u32[]{:S(2)}, u32[]{:S(2)}) collective-permute-start(f32[32,384]{1,0:T(8,128)S(1)} %add_add_fusion.1), channel_id=1, source_target_pairs={{0,24},{4,28},{8,16},{12,20},{16,8},{20,12},{24,0},{28,4},{1,25},{... | collective-permute-start | bytes 147464 | tf_op jit(solution)/shard_map/ppermute | solution.py:62
  31.1 5.9 %collective-permute-start.6 = (bf16[12,32,128]{2,1,0:T(8,128)(2,1)S(1)}, bf16[12,32,128]{2,1,0:T(8,128)(2,1)S(1)}, u32[]{:S(2)}, u32[]{:S(2)}) collective-permute-start(bf16[12,32,128]{2,1,0:T(8,128)(2,1)S(1)} %get-tuple-element.33), channel_id=1, source_target_pairs={{0,1},{4,5},{8,9},{12,13},{16,17},{20,21},{24,25},{28,29},{1,0},{5... | collective-permute-start | bytes 294920 | tf_op jit(solution)/shard_map/ppermute | solution.py:48
  31.1 5.9 %collective-permute-start.7 = (bf16[12,32,128]{2,1,0:T(8,128)(2,1)S(1)}, bf16[12,32,128]{2,1,0:T(8,128)(2,1)S(1)}, u32[]{:S(2)}, u32[]{:S(2)}) collective-permute-start(bf16[12,32,128]{2,1,0:T(8,128)(2,1)S(1)} %get-tuple-element.34), channel_id=1, source_target_pairs={{0,4},{4,0},{8,12},{12,8},{16,20},{20,16},{24,28},{28,24},{1,2},{5... | collective-permute-start | bytes 294920 | tf_op jit(solution)/shard_map/ppermute | solution.py:48
  36.7 4.2 %collective-permute-start.14 = (f32[32,384]{1,0:T(8,128)S(1)}, f32[32,384]{1,0:T(8,128)S(1)}, u32[]{:S(2)}, u32[]{:S(2)}) collective-permute-start(f32[32,384]{1,0:T(8,128)S(1)} %add_add_fusion.one_ref), channel_id=1, source_target_pairs={{0,4},{4,0},{8,12},{12,8},{16,20},{20,16},{24,28},{28,24},{1,5},{5... | collective-permute-start | bytes 147464 | tf_op jit(solution)/shard_map/ppermute | solution.py:62

commit v12 on v11

--- a/solution.py
+++ b/solution.py
@@ -53,9 +53,9 @@
     return [(axis, bits[at : at + 2]) for at in range(0, len(bits), 2)]
 
 
-def add_pairs(value, near_axis, far_axis):
+def add_over(value, axis):
     other = jnp.zeros_like(value)
-    for place, (axis, bits) in enumerate(rounds_of(near_axis) + rounds_of(far_axis)):
+    for place, (axis, bits) in enumerate(rounds_of(axis)):
         value = value + other if place else value
         masks = bits[::-1] + [sum(bits)] if len(bits) == 2 else bits
         came = [
@@ -165,6 +165,11 @@
     either("col", pack, send_one_ref, send_two_ref)
     clear_if(alone("col", 0), send_one_ref)
     clear_if(alone("col", 1), send_two_ref)
+
+
+def rim_sum_kernel(one_ref, two_ref, rims_ref, value_ref, other_ref, send_one_ref, send_two_ref, outer_ref, sum_ref):
+    sum_ref[...] = value_ref[...] + other_ref[...]
+    rim_kernel(False, one_ref, two_ref, rims_ref, send_one_ref, send_two_ref, outer_ref)
 
 
 def spread(rows_of, left_ref, right_ref, stack_ref, block, group_start):
@@ -342,8 +347,10 @@
         2 * flops,
     )
     one, two = swap_pairs(one, "row", 0), swap_pairs(two, "row", 1)
-    one, two, grad_outer = call(
-        functools.partial(rim_kernel, False), (packed, packed, outer), (one, two, rims)
+    one, two, grad_outer, terms = call(
+        rim_sum_kernel,
+        (packed, packed, outer, shape(terms.shape, f32)),
+        (one, two, rims, *add_over(terms, "col")),
     )
     two, one = swap_pairs(two, "col", 1), swap_pairs(one, "col", 0)
     grad_image, token = call(
@@ -353,7 +360,7 @@
         (stack,),
         flops,
     )
-    one, other = add_pairs(terms, "col", "row")
+    one, other = add_over(terms, "row")
     grad_weight, grad_bias = call(
         finish_kernel, (shape(weight.shape, f32), shape((1, channels), f32)), (one, other, token)
     )

time: 41.8 us -> 45.2 us (1.081)
  waiting for transfers between devices: 10.6 us -> 14.8 us
  starting transfers between devices: 17.3 us -> 16.7 us
    ppermute x7, waiting for transfers between devices: 4.16 us -> 7.95 us  [add_over(): lax.ppermute(value, axis, [(at, at ^ mask) for at in range(lax.axis_size(...]
    ppermute x8, starting transfers between devices: 10.1 us -> 9.41 us  [swap_pairs(): return lax.ppermute(value, ('row', 'col'), pairs)]
  transfers between devices with their start and end apart: 15 -> 15, of which waited for: 5 -> 8; matrix products, arithmetic and copies ran while one was open for 1% -> 1% of each run, Pallas kernels for 11% -> 10%
where the time goes in v12:
time: 45.2 us; the launch traced here: 45.1 us
  starting transfers between devices  16.7 us (37%)
  waiting for transfers between devices  14.8 us (33%)
  Pallas kernels  10.8 us (24%)
  other arithmetic  1.09 us (2%)
  local copies, waits for them, and re-layouts  1.01 us (2%)
  between operations  0.76 us (2%)
    pallas_call x6, Pallas kernels, call(): pl.pallas_call(kernel, out_shape=out_shapes, in_specs=[whole] * len(opera...  10.8 us
    ppermute x8, starting transfers between devices, swap_pairs(): return lax.ppermute(value, ('row', 'col'), pairs)  9.41 us
    ppermute x7, waiting for transfers between devices, add_over(): lax.ppermute(value, axis, [(at, at ^ mask) for at in range(lax.axis_size(...  7.95 us
    ppermute x7, starting transfers between devices, add_over(): lax.ppermute(value, axis, [(at, at ^ mask) for at in range(lax.axis_size(...  7.25 us
    ppermute x8, waiting for transfers between devices, swap_pairs(): return lax.ppermute(value, ('row', 'col'), pairs)  6.82 us
    select_n x1, other arithmetic, image_rim(): return rim if flag is None else jnp.where(flag, jnp.zeros_like(rim), rim)  1.06 us
  transfers between devices with their start and end apart: 15, of which 8 were waited for; matrix products, arithmetic and copies ran while one was open for 1% of the time, Pallas kernels for 10%

profile of v12, /device:TPU:0, one launch (start us, length us, event | category | flops | bytes accessed | tf_op | source)
XLA Modules:
  0.0 45.1 jit_solution(11142965597272804612)
XLA Ops:
  0.6 0.0 copy-start
  0.7 1.1 %dynamic-slice_select_fusion = (bf16[32,16,128]{2,1,0:T(8,128)(2,1)S(1)}, bf16[32,16,128]{2,1,0:T(8,128)(2,1)S(1)}) fusion(bf16[32,64,128]{2,1,0:T(8,128)(2,1)} %image_ref.1, s32[]{:T(128)S(6)} %select_n.24, pred[]{:T(512)S(6)} %or.3, s32[]{:T(128)S(6)} %select_n.22), kind=kLoop, calls=%fused_computation | loop fusion | flops 65536 | bytes 524297 | tf_op jit(solution)/shard_map/jit(_where)/select_n | solution.py:328
  1.7 3.0 %collective-permute-start = (bf16[32,16,128]{2,1,0:T(8,128)(2,1)S(1)}, bf16[32,16,128]{2,1,0:T(8,128)(2,1)S(1)}, u32[]{:S(2)}, u32[]{:S(2)}) collective-permute-start(bf16[32,16,128]{2,1,0:T(8,128)(2,1)S(1)} %get-tuple-element.43), channel_id=1, source_target_pairs={{0,4},{1,5},{2,6},{3,7},{4,0},{5,1},{6,2},{7,3},{8,12},{9,13},{10,... | collective-permute-start | bytes 393224 | tf_op jit(solution)/shard_map/ppermute | solution.py:48
  4.8 0.0 copy-start.1
  4.8 0.0 collective-permute-start.1
  4.8 0.0 copy-done
  4.8 0.8 %shard_map.75 = (bf16[64,32,128]{2,1,0:T(8,128)(2,1)S(1)}, bf16[2,8,32,128]{3,2,1,0:T(8,128)(2,1)S(1)}) custom-call(bf16[32,64,128]{2,1,0:T(8,128)(2,1)S(1)} %copy-done), custom_call_target="tpu_custom_call" | custom-call | bytes 1179648 | tf_op jit(solution)/shard_map/pallas_call | solution.py:294
  5.6 4.8 %collective-permute-done.one_ref = bf16[32,16,128]{2,1,0:T(8,128)(2,1)S(1)} collective-permute-done((bf16[32,16,128]{2,1,0:T(8,128)(2,1)S(1)}, bf16[32,16,128]{2,1,0:T(8,128)(2,1)S(1)}, u32[]{:S(2)}, u32[]{:S(2)}) %collective-permute-start) | collective-permute-done | bytes 131104 | tf_op jit(solution)/shard_map/ppermute | solution.py:48
  10.3 0.0 collective-permute-done.1.two_ref
  10.3 0.3 shard_map.76
  10.6 0.1 collective-permute-start.2
  10.7 2.6 %collective-permute-start.3 = (bf16[12,32,128]{2,1,0:T(8,128)(2,1)S(1)}, bf16[12,32,128]{2,1,0:T(8,128)(2,1)S(1)}, u32[]{:S(2)}, u32[]{:S(2)}) collective-permute-start(bf16[12,32,128]{2,1,0:T(8,128)(2,1)S(1)} %get-tuple-element.27), channel_id=1, source_target_pairs={{0,4},{4,0},{8,12},{12,8},{16,20},{20,16},{24,28},{28,24},{1,2},{5... | collective-permute-start | bytes 294920 | tf_op jit(solution)/shard_map/ppermute | solution.py:48
  13.3 0.0 copy-done.2
  13.3 0.1 copy.11
  13.3 0.1 reshape.17.weight_ref
  13.4 0.0 copy-start.3
  13.5 0.6 %copy-done.3 = f32[32]{0:T(128)S(1)} copy-done((f32[32]{0:T(128)S(1)}, f32[32]{0:T(128)}, u32[]{:S(2)}) %copy-start.3) | copy-done | bytes 152
  14.1 0.1 copy.12.bias_ref
  14.2 0.0 collective-permute-done.2.one_ref
  14.2 1.7 %collective-permute-done.3.two_ref = bf16[12,32,128]{2,1,0:T(8,128)(2,1)S(1)} collective-permute-done((bf16[12,32,128]{2,1,0:T(8,128)(2,1)S(1)}, bf16[12,32,128]{2,1,0:T(8,128)(2,1)S(1)}, u32[]{:S(2)}, u32[]{:S(2)}) %collective-permute-start.3) | collective-permute-done | bytes 98336 | tf_op jit(solution)/shard_map/ppermute | solution.py:48
  15.9 0.0 copy-done.1
  15.9 5.1 %shard_map.77 = (bf16[32,64,128]{2,1,0:T(8,128)(2,1)}, bf16[64,32,128]{2,1,0:T(8,128)(2,1)S(1)}, bf16[16,32,128]{2,1,0:T(8,128)(2,1)S(1)}, bf16[16,32,128]{2,1,0...) custom-call(bf16[64,32,128]{2,1,0:T(8,128)(2,1)S(1)} %get-tuple-element.23.own_ref, ...), custom_call_target="tpu_custom_call" | custom-call | flops 301989888 | bytes 3016832 | tf_op jit(solution)/shard_map/pallas_call | solution.py:294
  20.9 2.0 %collective-permute-start.4 = (bf16[16,32,128]{2,1,0:T(8,128)(2,1)S(1)}, bf16[16,32,128]{2,1,0:T(8,128)(2,1)S(1)}, u32[]{:S(2)}, u32[]{:S(2)}) collective-permute-start(bf16[16,32,128]{2,1,0:T(8,128)(2,1)S(1)} %get-tuple-element.30), channel_id=1, source_target_pairs={{0,4},{1,5},{2,6},{3,7},{4,0},{5,1},{6,2},{7,3},{8,12},{9,13},{10,... | collective-permute-start | bytes 393224 | tf_op jit(solution)/shard_map/ppermute | solution.py:48
  23.0 0.0 collective-permute-start.5
  23.0 0.5 %collective-permute-start.6 = (f32[32,384]{1,0:T(8,128)S(1)}, f32[32,384]{1,0:T(8,128)S(1)}, u32[]{:S(2)}, u32[]{:S(2)}) collective-permute-start(f32[32,384]{1,0:T(8,128)S(1)} %get-tuple-element.33), channel_id=1, source_target_pairs={{0,1},{1,0},{2,3},{3,2},{4,5},{5,4},{6,7},{7,6},{8,9},{9,8},{10,11... | collective-permute-start | bytes 147464 | tf_op jit(solution)/shard_map/ppermute | solution.py:62
  23.5 0.9 %collective-permute-start.7 = (f32[32,384]{1,0:T(8,128)S(1)}, f32[32,384]{1,0:T(8,128)S(1)}, u32[]{:S(2)}, u32[]{:S(2)}) collective-permute-start(f32[32,384]{1,0:T(8,128)S(1)} %get-tuple-element.33), channel_id=1, source_target_pairs={{0,2},{1,3},{2,0},{3,1},{4,6},{5,7},{6,4},{7,5},{8,10},{9,11},{10,... | collective-permute-start | bytes 147464 | tf_op jit(solution)/shard_map/ppermute | solution.py:62
  24.4 0.5 %collective-permute-start.8 = (f32[32,384]{1,0:T(8,128)S(1)}, f32[32,384]{1,0:T(8,128)S(1)}, u32[]{:S(2)}, u32[]{:S(2)}) collective-permute-start(f32[32,384]{1,0:T(8,128)S(1)} %get-tuple-element.33), channel_id=1, source_target_pairs={{0,3},{1,2},{2,1},{3,0},{4,7},{5,6},{6,5},{7,4},{8,11},{9,10},{10,... | collective-permute-start | bytes 147464 | tf_op jit(solution)/shard_map/ppermute | solution.py:62
  24.8 0.0 collective-permute-done.6
  24.8 2.9 %collective-permute-done.7 = f32[32,384]{1,0:T(8,128)S(1)} collective-permute-done((f32[32,384]{1,0:T(8,128)S(1)}, f32[32,384]{1,0:T(8,128)S(1)}, u32[]{:S(2)}, u32[]{:S(2)}) %collective-permute-start.7) | collective-permute-done | bytes 49184 | tf_op jit(solution)/shard_map/ppermute | solution.py:62
  27.8 0.7 %collective-permute-done.8 = f32[32,384]{1,0:T(8,128)S(1)} collective-permute-done((f32[32,384]{1,0:T(8,128)S(1)}, f32[32,384]{1,0:T(8,128)S(1)}, u32[]{:S(2)}, u32[]{:S(2)}) %collective-permute-start.8) | collective-permute-done | bytes 49184 | tf_op jit(solution)/shard_map/ppermute | solution.py:62
  28.4 0.4 collective-permute-done.4.one_ref
  28.8 0.0 collective-permute-done.5.two_ref
  28.8 0.3 shard_map.78
  29.1 2.6 %collective-permute-start.11 = (f32[32,384]{1,0:T(8,128)S(1)}, f32[32,384]{1,0:T(8,128)S(1)}, u32[]{:S(2)}, u32[]{:S(2)}) collective-permute-start(f32[32,384]{1,0:T(8,128)S(1)} %get-tuple-element.38), channel_id=1, source_target_pairs={{0,8},{4,12},{8,0},{12,4},{16,24},{20,28},{24,16},{28,20},{1,9},{5... | collective-permute-start | bytes 147464 | tf_op jit(solution)/shard_map/ppermute | solution.py:62
  31.7 2.6 %collective-permute-start.12 = (f32[32,384]{1,0:T(8,128)S(1)}, f32[32,384]{1,0:T(8,128)S(1)}, u32[]{:S(2)}, u32[]{:S(2)}) collective-permute-start(f32[32,384]{1,0:T(8,128)S(1)} %get-tuple-element.38), channel_id=1, source_target_pairs={{0,16},{4,20},{8,24},{12,28},{16,0},{20,4},{24,8},{28,12},{1,17},{... | collective-permute-start | bytes 147464 | tf_op jit(solution)/shard_map/ppermute | solution.py:62
  34.3 0.0 collective-permute-start.13
  34.3 1.7 %collective-permute-start.10 = (bf16[12,32,128]{2,1,0:T(8,128)(2,1)S(1)}, bf16[12,32,128]{2,1,0:T(8,128)(2,1)S(1)}, u32[]{:S(2)}, u32[]{:S(2)}) collective-permute-start(bf16[12,32,128]{2,1,0:T(8,128)(2,1)S(1)} %get-tuple-element.36), channel_id=1, source_target_pairs={{0,4},{4,0},{8,12},{12,8},{16,20},{20,16},{24,28},{28,24},{1,2},{5... | collective-permute-start | bytes 294920 | tf_op jit(solution)/shard_map/ppermute | solution.py:48
  36.0 0.0 collective-permute-start.9
  36.0 0.0 collective-permute-done.11
  36.0 1.2 %collective-permute-done.12 = f32[32,384]{1,0:T(8,128)S(1)} collective-permute-done((f32[32,384]{1,0:T(8,128)S(1)}, f32[32,384]{1,0:T(8,128)S(1)}, u32[]{:S(2)}, u32[]{:S(2)}) %collective-permute-start.12) | collective-permute-done | bytes 49184 | tf_op jit(solution)/shard_map/ppermute | solution.py:62
  37.2 3.0 %collective-permute-done.13 = f32[32,384]{1,0:T(8,128)S(1)} collective-permute-done((f32[32,384]{1,0:T(8,128)S(1)}, f32[32,384]{1,0:T(8,128)S(1)}, u32[]{:S(2)}, u32[]{:S(2)}) %collective-permute-start.13) | collective-permute-done | bytes 49184 | tf_op jit(solution)/shard_map/ppermute | solution.py:62
  40.2 0.2 collective-permute-start.14
  40.4 0.1 copy.14.weight_ref
  40.5 0.0 collective-permute-done.10.two_ref
  40.5 0.0 collective-permute-done.9.one_ref
  40.5 3.6 %shard_map.79 = (bf16[32,64,128]{2,1,0:T(8,128)(2,1)}, f32[8,128]{1,0:T(8,128)S(1)}) custom-call(bf16[64,32,128]{2,1,0:T(8,128)(2,1)S(1)} %get-tuple-element.29.own_ref, bf16[2,16,32,128]{3,2,1,0:T(8,128)(2,1)S(1)} %get-tuple-element.34.outer_ref, bf16[12,32,128]{2,1,0:T(8,128)(2,1)S(1)} %collective-permute-done.9.one_ref, ...), custom_call_target="tpu_custom_call" | custom-call | flops 150994944 | bytes 1529856 | tf_op jit(solution)/shard_map/pallas_call | solution.py:294
  44.1 0.2 collective-permute-done.14.other_ref
  44.3 0.8 %shard_map.80 = (f32[3,3,32,32]{3,2,1,0:T(8,128)}, f32[1,32]{1,0:T(1,128)}) custom-call(f32[32,384]{1,0:T(8,128)S(1)} %add_add_fusion.one_ref, f32[32,384]{1,0:T(8,128)S(1)} %collective-permute-done.14.other_ref, f32[8,128]{1,0:T(8,128)S(1)} %get-tuple-element.39.after_ref), custom_call_target="tpu_custom_call" | custom-call | bytes 139392 | tf_op jit(solution)/shard_map/pallas_call | solution.py:294
  (5 shorter events, 0.0 us)
Async XLA Ops:
  0.6 4.1 %copy-start = (bf16[32,64,128]{2,1,0:T(8,128)(2,1)S(1)}, bf16[32,64,128]{2,1,0:T(8,128)(2,1)}, u32[]{:S(2)}) copy-start(bf16[32,64,128]{2,1,0:T(8,128)(2,1)} %image_ref.1) | copy-start | bytes 1572868
  1.7 8.6 %collective-permute-start = (bf16[32,16,128]{2,1,0:T(8,128)(2,1)S(1)}, bf16[32,16,128]{2,1,0:T(8,128)(2,1)S(1)}, u32[]{:S(2)}, u32[]{:S(2)}) collective-permute-start(bf16[32,16,128]{2,1,0:T(8,128)(2,1)S(1)} %get-tuple-element.43), channel_id=1, source_target_pairs={{0,4},{1,5},{2,6},{3,7},{4,0},{5,1},{6,2},{7,3},{8,12},{9,13},{10,... | collective-permute-start | bytes 393224 | tf_op jit(solution)/shard_map/ppermute | solution.py:48
  4.8 11.1 %copy-start.1 = (bf16[32,64,128]{2,1,0:T(8,128)(2,1)S(1)}, bf16[32,64,128]{2,1,0:T(8,128)(2,1)}, u32[]{:S(2)}) copy-start(bf16[32,64,128]{2,1,0:T(8,128)(2,1)} %cotangent_ref.1) | copy-start | bytes 1572868
  4.8 5.6 %collective-permute-start.1 = (bf16[32,16,128]{2,1,0:T(8,128)(2,1)S(1)}, bf16[32,16,128]{2,1,0:T(8,128)(2,1)S(1)}, u32[]{:S(2)}, u32[]{:S(2)}) collective-permute-start(bf16[32,16,128]{2,1,0:T(8,128)(2,1)S(1)} %get-tuple-element.42), channel_id=1, source_target_pairs={{0,1},{1,0},{2,3},{3,2},{4,8},{5,9},{6,10},{7,11},{8,4},{9,5},{10,... | collective-permute-start | bytes 393224 | tf_op jit(solution)/shard_map/ppermute | solution.py:48
  10.3 2.9 %copy-start.2 = (bf16[3,3,32,32]{3,2,1,0:T(8,128)(2,1)S(1)}, bf16[3,3,32,32]{3,2,1,0:T(8,128)(2,1)}, u32[]{:S(2)}) copy-start(bf16[3,3,32,32]{3,2,1,0:T(8,128)(2,1)} %param.5) | copy-start | bytes 55300
  10.6 3.6 %collective-permute-start.2 = (bf16[12,32,128]{2,1,0:T(8,128)(2,1)S(1)}, bf16[12,32,128]{2,1,0:T(8,128)(2,1)S(1)}, u32[]{:S(2)}, u32[]{:S(2)}) collective-permute-start(bf16[12,32,128]{2,1,0:T(8,128)(2,1)S(1)} %get-tuple-element.26), channel_id=1, source_target_pairs={{0,1},{4,5},{8,9},{12,13},{16,17},{20,21},{24,25},{28,29},{1,0},{5... | collective-permute-start | bytes 294920 | tf_op jit(solution)/shard_map/ppermute | solution.py:48
  10.7 5.1 %collective-permute-start.3 = (bf16[12,32,128]{2,1,0:T(8,128)(2,1)S(1)}, bf16[12,32,128]{2,1,0:T(8,128)(2,1)S(1)}, u32[]{:S(2)}, u32[]{:S(2)}) collective-permute-start(bf16[12,32,128]{2,1,0:T(8,128)(2,1)S(1)} %get-tuple-element.27), channel_id=1, source_target_pairs={{0,4},{4,0},{8,12},{12,8},{16,20},{20,16},{24,28},{28,24},{1,2},{5... | collective-permute-start | bytes 294920 | tf_op jit(solution)/shard_map/ppermute | solution.py:48
  13.4 0.7 %copy-start.3 = (f32[32]{0:T(128)S(1)}, f32[32]{0:T(128)}, u32[]{:S(2)}) copy-start(f32[32]{0:T(128)} %param.6) | copy-start | bytes 388
  20.9 7.9 %collective-permute-start.4 = (bf16[16,32,128]{2,1,0:T(8,128)(2,1)S(1)}, bf16[16,32,128]{2,1,0:T(8,128)(2,1)S(1)}, u32[]{:S(2)}, u32[]{:S(2)}) collective-permute-start(bf16[16,32,128]{2,1,0:T(8,128)(2,1)S(1)} %get-tuple-element.30), channel_id=1, source_target_pairs={{0,4},{1,5},{2,6},{3,7},{4,0},{5,1},{6,2},{7,3},{8,12},{9,13},{10,... | collective-permute-start | bytes 393224 | tf_op jit(solution)/shard_map/ppermute | solution.py:48
  23.0 5.8 %collective-permute-start.5 = (bf16[16,32,128]{2,1,0:T(8,128)(2,1)S(1)}, bf16[16,32,128]{2,1,0:T(8,128)(2,1)S(1)}, u32[]{:S(2)}, u32[]{:S(2)}) collective-permute-start(bf16[16,32,128]{2,1,0:T(8,128)(2,1)S(1)} %get-tuple-element.31), channel_id=1, source_target_pairs={{0,1},{1,0},{2,3},{3,2},{4,8},{5,9},{6,10},{7,11},{8,4},{9,5},{10,... | collective-permute-start | bytes 393224 | tf_op jit(solution)/shard_map/ppermute | solution.py:48
  23.0 1.9 %collective-permute-start.6 = (f32[32,384]{1,0:T(8,128)S(1)}, f32[32,384]{1,0:T(8,128)S(1)}, u32[]{:S(2)}, u32[]{:S(2)}) collective-permute-start(f32[32,384]{1,0:T(8,128)S(1)} %get-tuple-element.33), channel_id=1, source_target_pairs={{0,1},{1,0},{2,3},{3,2},{4,5},{5,4},{6,7},{7,6},{8,9},{9,8},{10,11... | collective-permute-start | bytes 147464 | tf_op jit(solution)/shard_map/ppermute | solution.py:62
  23.5 4.3 %collective-permute-start.7 = (f32[32,384]{1,0:T(8,128)S(1)}, f32[32,384]{1,0:T(8,128)S(1)}, u32[]{:S(2)}, u32[]{:S(2)}) collective-permute-start(f32[32,384]{1,0:T(8,128)S(1)} %get-tuple-element.33), channel_id=1, source_target_pairs={{0,2},{1,3},{2,0},{3,1},{4,6},{5,7},{6,4},{7,5},{8,10},{9,11},{10,... | collective-permute-start | bytes 147464 | tf_op jit(solution)/shard_map/ppermute | solution.py:62
  24.4 4.0 %collective-permute-start.8 = (f32[32,384]{1,0:T(8,128)S(1)}, f32[32,384]{1,0:T(8,128)S(1)}, u32[]{:S(2)}, u32[]{:S(2)}) collective-permute-start(f32[32,384]{1,0:T(8,128)S(1)} %get-tuple-element.33), channel_id=1, source_target_pairs={{0,3},{1,2},{2,1},{3,0},{4,7},{5,6},{6,5},{7,4},{8,11},{9,10},{10,... | collective-permute-start | bytes 147464 | tf_op jit(solution)/shard_map/ppermute | solution.py:62
  29.1 6.9 %collective-permute-start.11 = (f32[32,384]{1,0:T(8,128)S(1)}, f32[32,384]{1,0:T(8,128)S(1)}, u32[]{:S(2)}, u32[]{:S(2)}) collective-permute-start(f32[32,384]{1,0:T(8,128)S(1)} %get-tuple-element.38), channel_id=1, source_target_pairs={{0,8},{4,12},{8,0},{12,4},{16,24},{20,28},{24,16},{28,20},{1,9},{5... | collective-permute-start | bytes 147464 | tf_op jit(solution)/shard_map/ppermute | solution.py:62
  31.7 5.5 %collective-permute-start.12 = (f32[32,384]{1,0:T(8,128)S(1)}, f32[32,384]{1,0:T(8,128)S(1)}, u32[]{:S(2)}, u32[]{:S(2)}) collective-permute-start(f32[32,384]{1,0:T(8,128)S(1)} %get-tuple-element.38), channel_id=1, source_target_pairs={{0,16},{4,20},{8,24},{12,28},{16,0},{20,4},{24,8},{28,12},{1,17},{... | collective-permute-start | bytes 147464 | tf_op jit(solution)/shard_map/ppermute | solution.py:62
  34.3 5.9 %collective-permute-start.13 = (f32[32,384]{1,0:T(8,128)S(1)}, f32[32,384]{1,0:T(8,128)S(1)}, u32[]{:S(2)}, u32[]{:S(2)}) collective-permute-start(f32[32,384]{1,0:T(8,128)S(1)} %get-tuple-element.38), channel_id=1, source_target_pairs={{0,24},{4,28},{8,16},{12,20},{16,8},{20,12},{24,0},{28,4},{1,25},{... | collective-permute-start | bytes 147464 | tf_op jit(solution)/shard_map/ppermute | solution.py:62
  34.3 6.2 %collective-permute-start.10 = (bf16[12,32,128]{2,1,0:T(8,128)(2,1)S(1)}, bf16[12,32,128]{2,1,0:T(8,128)(2,1)S(1)}, u32[]{:S(2)}, u32[]{:S(2)}) collective-permute-start(bf16[12,32,128]{2,1,0:T(8,128)(2,1)S(1)} %get-tuple-element.36), channel_id=1, source_target_pairs={{0,4},{4,0},{8,12},{12,8},{16,20},{20,16},{24,28},{28,24},{1,2},{5... | collective-permute-start | bytes 294920 | tf_op jit(solution)/shard_map/ppermute | solution.py:48
  36.0 4.5 %collective-permute-start.9 = (bf16[12,32,128]{2,1,0:T(8,128)(2,1)S(1)}, bf16[12,32,128]{2,1,0:T(8,128)(2,1)S(1)}, u32[]{:S(2)}, u32[]{:S(2)}) collective-permute-start(bf16[12,32,128]{2,1,0:T(8,128)(2,1)S(1)} %get-tuple-element.35), channel_id=1, source_target_pairs={{0,1},{4,5},{8,9},{12,13},{16,17},{20,21},{24,25},{28,29},{1,0},{5... | collective-permute-start | bytes 294920 | tf_op jit(solution)/shard_map/ppermute | solution.py:48
  40.2 4.2 %collective-permute-start.14 = (f32[32,384]{1,0:T(8,128)S(1)}, f32[32,384]{1,0:T(8,128)S(1)}, u32[]{:S(2)}, u32[]{:S(2)}) collective-permute-start(f32[32,384]{1,0:T(8,128)S(1)} %add_add_fusion.one_ref), channel_id=1, source_target_pairs={{0,4},{4,0},{8,12},{12,8},{16,20},{20,16},{24,28},{28,24},{1,5},{5... | collective-permute-start | bytes 147464 | tf_op jit(solution)/shard_map/ppermute | solution.py:62

commit v13 on v11

--- a/solution.py
+++ b/solution.py
@@ -48,14 +48,16 @@
     return lax.ppermute(value, ("row", "col"), pairs)
 
 
-def rounds_of(axis):
-    bits = [2**k for k in reversed(range(lax.axis_size(axis).bit_length() - 1))]
-    return [(axis, bits[at : at + 2]) for at in range(0, len(bits), 2)]
+def rounds_of(near_axis, far_axis):
+    near = [2**k for k in range(lax.axis_size(near_axis).bit_length() - 1)]
+    far = [2**k for k in reversed(range(lax.axis_size(far_axis).bit_length() - 1))]
+    rounds = [(near_axis, [bit]) for bit in near]
+    return rounds + [(far_axis, far[at : at + 2]) for at in range(0, len(far), 2)]
 
 
 def add_pairs(value, near_axis, far_axis):
     other = jnp.zeros_like(value)
-    for place, (axis, bits) in enumerate(rounds_of(near_axis) + rounds_of(far_axis)):
+    for place, (axis, bits) in enumerate(rounds_of(near_axis, far_axis)):
         value = value + other if place else value
         masks = bits[::-1] + [sum(bits)] if len(bits) == 2 else bits
         came = [

time: 41.8 us -> 42.9 us (1.026)
  waiting for transfers between devices: 10.6 us -> 12.3 us
  starting transfers between devices: 17.3 us -> 16.8 us
    ppermute x7 -> x6, waiting for transfers between devices: 4.16 us -> 5.85 us  [add_pairs(): lax.ppermute(value, axis, [(at, at ^ mask) for at in range(lax.axis_size(...]
    ppermute x7 -> x6, starting transfers between devices: 7.2 us -> 5.84 us  [add_pairs(): lax.ppermute(value, axis, [(at, at ^ mask) for at in range(lax.axis_size(...]
    ppermute x8, starting transfers between devices: 10.1 us -> 10.9 us  [swap_pairs(): return lax.ppermute(value, ('row', 'col'), pairs)]
  transfers between devices with their start and end apart: 15 -> 14, of which waited for: 5 -> 4; matrix products, arithmetic and copies ran while one was open for 1% -> 1% of each run, Pallas kernels for 11% -> 11%
where the time goes in v13:
time: 42.9 us; the launch traced here: 42.7 us
  starting transfers between devices  16.8 us (39%)
  waiting for transfers between devices  12.3 us (29%)
  Pallas kernels  10.8 us (25%)
  other arithmetic  1.09 us (3%)
  local copies, waits for them, and re-layouts  1.01 us (2%)
  between operations  0.77 us (2%)
    ppermute x8, starting transfers between devices, swap_pairs(): return lax.ppermute(value, ('row', 'col'), pairs)  10.9 us
    pallas_call x6, Pallas kernels, call(): pl.pallas_call(kernel, out_shape=out_shapes, in_specs=[whole] * len(opera...  10.8 us
    ppermute x8, waiting for transfers between devices, swap_pairs(): return lax.ppermute(value, ('row', 'col'), pairs)  6.45 us
    ppermute x6, waiting for transfers between devices, add_pairs(): lax.ppermute(value, axis, [(at, at ^ mask) for at in range(lax.axis_size(...  5.85 us
    ppermute x6, starting transfers between devices, add_pairs(): lax.ppermute(value, axis, [(at, at ^ mask) for at in range(lax.axis_size(...  5.84 us
    select_n x1, other arithmetic, image_rim(): return rim if flag is None else jnp.where(flag, jnp.zeros_like(rim), rim)  1.06 us
  transfers between devices with their start and end apart: 14, of which 4 were waited for; matrix products, arithmetic and copies ran while one was open for 1% of the time, Pallas kernels for 11%

profile of v13, /device:TPU:0, one launch (start us, length us, event | category | flops | bytes accessed | tf_op | source)
XLA Modules:
  0.0 42.7 jit_solution(5565802440365721284)
XLA Ops:
  0.6 0.0 copy-start
  0.7 1.1 %dynamic-slice_select_fusion = (bf16[32,16,128]{2,1,0:T(8,128)(2,1)S(1)}, bf16[32,16,128]{2,1,0:T(8,128)(2,1)S(1)}) fusion(bf16[32,64,128]{2,1,0:T(8,128)(2,1)} %image_ref.1, s32[]{:T(128)S(6)} %select_n.24, pred[]{:T(512)S(6)} %or.3, s32[]{:T(128)S(6)} %select_n.22), kind=kLoop, calls=%fused_computation | loop fusion | flops 65536 | bytes 524297 | tf_op jit(solution)/shard_map/jit(_where)/select_n | solution.py:325
  1.7 3.0 %collective-permute-start = (bf16[32,16,128]{2,1,0:T(8,128)(2,1)S(1)}, bf16[32,16,128]{2,1,0:T(8,128)(2,1)S(1)}, u32[]{:S(2)}, u32[]{:S(2)}) collective-permute-start(bf16[32,16,128]{2,1,0:T(8,128)(2,1)S(1)} %get-tuple-element.41), channel_id=1, source_target_pairs={{0,4},{1,5},{2,6},{3,7},{4,0},{5,1},{6,2},{7,3},{8,12},{9,13},{10,... | collective-permute-start | bytes 393224 | tf_op jit(solution)/shard_map/ppermute | solution.py:48
  4.8 0.0 copy-start.1
  4.8 0.0 collective-permute-start.1
  4.8 0.0 copy-done
  4.8 0.8 %shard_map.75 = (bf16[64,32,128]{2,1,0:T(8,128)(2,1)S(1)}, bf16[2,8,32,128]{3,2,1,0:T(8,128)(2,1)S(1)}) custom-call(bf16[32,64,128]{2,1,0:T(8,128)(2,1)S(1)} %copy-done), custom_call_target="tpu_custom_call" | custom-call | bytes 1179648 | tf_op jit(solution)/shard_map/pallas_call | solution.py:291
  5.6 4.8 %collective-permute-done.one_ref = bf16[32,16,128]{2,1,0:T(8,128)(2,1)S(1)} collective-permute-done((bf16[32,16,128]{2,1,0:T(8,128)(2,1)S(1)}, bf16[32,16,128]{2,1,0:T(8,128)(2,1)S(1)}, u32[]{:S(2)}, u32[]{:S(2)}) %collective-permute-start) | collective-permute-done | bytes 131104 | tf_op jit(solution)/shard_map/ppermute | solution.py:48
  10.3 0.0 collective-permute-done.1.two_ref
  10.3 0.0 copy-start.2
  10.3 0.3 shard_map.76
  10.6 0.1 collective-permute-start.2
  10.7 2.6 %collective-permute-start.3 = (bf16[12,32,128]{2,1,0:T(8,128)(2,1)S(1)}, bf16[12,32,128]{2,1,0:T(8,128)(2,1)S(1)}, u32[]{:S(2)}, u32[]{:S(2)}) collective-permute-start(bf16[12,32,128]{2,1,0:T(8,128)(2,1)S(1)} %get-tuple-element.26), channel_id=1, source_target_pairs={{0,4},{4,0},{8,12},{12,8},{16,20},{20,16},{24,28},{28,24},{1,2},{5... | collective-permute-start | bytes 294920 | tf_op jit(solution)/shard_map/ppermute | solution.py:48
  13.3 0.0 copy-done.2
  13.3 0.1 copy.11
  13.3 0.1 reshape.17.weight_ref
  13.4 0.0 copy-start.3
  13.5 0.6 %copy-done.3 = f32[32]{0:T(128)S(1)} copy-done((f32[32]{0:T(128)S(1)}, f32[32]{0:T(128)}, u32[]{:S(2)}) %copy-start.3) | copy-done | bytes 152
  14.1 0.1 copy.12.bias_ref
  14.2 0.0 collective-permute-done.2.one_ref
  14.2 1.7 %collective-permute-done.3.two_ref = bf16[12,32,128]{2,1,0:T(8,128)(2,1)S(1)} collective-permute-done((bf16[12,32,128]{2,1,0:T(8,128)(2,1)S(1)}, bf16[12,32,128]{2,1,0:T(8,128)(2,1)S(1)}, u32[]{:S(2)}, u32[]{:S(2)}) %collective-permute-start.3) | collective-permute-done | bytes 98336 | tf_op jit(solution)/shard_map/ppermute | solution.py:48
  15.9 0.0 copy-done.1
  15.9 5.1 %shard_map.77 = (bf16[32,64,128]{2,1,0:T(8,128)(2,1)}, bf16[64,32,128]{2,1,0:T(8,128)(2,1)S(1)}, bf16[16,32,128]{2,1,0:T(8,128)(2,1)S(1)}, bf16[16,32,128]{2,1,0...) custom-call(bf16[64,32,128]{2,1,0:T(8,128)(2,1)S(1)} %get-tuple-element.22.own_ref, ...), custom_call_target="tpu_custom_call" | custom-call | flops 301989888 | bytes 3016832 | tf_op jit(solution)/shard_map/pallas_call | solution.py:291
  20.9 0.0 collective-permute-start.8
  20.9 2.1 %collective-permute-start.4 = (bf16[16,32,128]{2,1,0:T(8,128)(2,1)S(1)}, bf16[16,32,128]{2,1,0:T(8,128)(2,1)S(1)}, u32[]{:S(2)}, u32[]{:S(2)}) collective-permute-start(bf16[16,32,128]{2,1,0:T(8,128)(2,1)S(1)} %get-tuple-element.29), channel_id=1, source_target_pairs={{0,4},{1,5},{2,6},{3,7},{4,0},{5,1},{6,2},{7,3},{8,12},{9,13},{10,... | collective-permute-start | bytes 393224 | tf_op jit(solution)/shard_map/ppermute | solution.py:48
  23.1 0.1 collective-permute-start.5
  23.2 0.0 collective-permute-done.8
  23.2 0.9 %collective-permute-start.9 = (f32[32,384]{1,0:T(8,128)S(1)}, f32[32,384]{1,0:T(8,128)S(1)}, u32[]{:S(2)}, u32[]{:S(2)}) collective-permute-start(f32[32,384]{1,0:T(8,128)S(1)} %add.28), channel_id=1, source_target_pairs={{0,2},{1,3},{2,0},{3,1},{4,6},{5,7},{6,4},{7,5},{8,10},{9,11},{10,... | collective-permute-start | bytes 147464 | tf_op jit(solution)/shard_map/ppermute | solution.py:64
  24.2 3.2 %collective-permute-done.9 = f32[32,384]{1,0:T(8,128)S(1)} collective-permute-done((f32[32,384]{1,0:T(8,128)S(1)}, f32[32,384]{1,0:T(8,128)S(1)}, u32[]{:S(2)}, u32[]{:S(2)}) %collective-permute-start.9) | collective-permute-done | bytes 49184 | tf_op jit(solution)/shard_map/ppermute | solution.py:64
  27.4 1.5 %collective-permute-start.10 = (f32[32,384]{1,0:T(8,128)S(1)}, f32[32,384]{1,0:T(8,128)S(1)}, u32[]{:S(2)}, u32[]{:S(2)}) collective-permute-start(f32[32,384]{1,0:T(8,128)S(1)} %add.29), channel_id=1, source_target_pairs={{0,8},{4,12},{8,0},{12,4},{16,24},{20,28},{24,16},{28,20},{1,9},{5... | collective-permute-start | bytes 147464 | tf_op jit(solution)/shard_map/ppermute | solution.py:64
  28.9 3.0 %collective-permute-start.11 = (f32[32,384]{1,0:T(8,128)S(1)}, f32[32,384]{1,0:T(8,128)S(1)}, u32[]{:S(2)}, u32[]{:S(2)}) collective-permute-start(f32[32,384]{1,0:T(8,128)S(1)} %add.29), channel_id=1, source_target_pairs={{0,16},{4,20},{8,24},{12,28},{16,0},{20,4},{24,8},{28,12},{1,17},{... | collective-permute-start | bytes 147464 | tf_op jit(solution)/shard_map/ppermute | solution.py:64
  31.9 0.0 collective-permute-start.12
  31.9 0.0 collective-permute-done.4.one_ref
  31.9 0.0 collective-permute-done.5.two_ref
  31.9 0.3 shard_map.78
  32.2 0.1 collective-permute-start.6
  32.2 2.9 %collective-permute-start.7 = (bf16[12,32,128]{2,1,0:T(8,128)(2,1)S(1)}, bf16[12,32,128]{2,1,0:T(8,128)(2,1)S(1)}, u32[]{:S(2)}, u32[]{:S(2)}) collective-permute-start(bf16[12,32,128]{2,1,0:T(8,128)(2,1)S(1)} %get-tuple-element.34), channel_id=1, source_target_pairs={{0,4},{4,0},{8,12},{12,8},{16,20},{20,16},{24,28},{28,24},{1,2},{5... | collective-permute-start | bytes 294920 | tf_op jit(solution)/shard_map/ppermute | solution.py:48
  35.1 0.0 collective-permute-done.10
  35.2 0.0 collective-permute-done.11
  35.2 2.6 %collective-permute-done.12 = f32[32,384]{1,0:T(8,128)S(1)} collective-permute-done((f32[32,384]{1,0:T(8,128)S(1)}, f32[32,384]{1,0:T(8,128)S(1)}, u32[]{:S(2)}, u32[]{:S(2)}) %collective-permute-start.12) | collective-permute-done | bytes 49184 | tf_op jit(solution)/shard_map/ppermute | solution.py:64
  37.8 0.4 %collective-permute-start.13 = (f32[32,384]{1,0:T(8,128)S(1)}, f32[32,384]{1,0:T(8,128)S(1)}, u32[]{:S(2)}, u32[]{:S(2)}) collective-permute-start(f32[32,384]{1,0:T(8,128)S(1)} %add_add_fusion.one_ref), channel_id=1, source_target_pairs={{0,4},{4,0},{8,12},{12,8},{16,20},{20,16},{24,28},{28,24},{1,5},{5... | collective-permute-start | bytes 147464 | tf_op jit(solution)/shard_map/ppermute | solution.py:64
  38.2 0.1 copy.14.weight_ref
  38.3 0.0 collective-permute-done.6.one_ref
  38.3 0.0 collective-permute-done.7.two_ref
  38.3 3.6 %shard_map.79 = (bf16[32,64,128]{2,1,0:T(8,128)(2,1)}, f32[8,128]{1,0:T(8,128)S(1)}) custom-call(bf16[64,32,128]{2,1,0:T(8,128)(2,1)S(1)} %get-tuple-element.28.own_ref, bf16[2,16,32,128]{3,2,1,0:T(8,128)(2,1)S(1)} %get-tuple-element.32.outer_ref, bf16[12,32,128]{2,1,0:T(8,128)(2,1)S(1)} %collective-permute-done.6.one_ref, ...), custom_call_target="tpu_custom_call" | custom-call | flops 150994944 | bytes 1529856 | tf_op jit(solution)/shard_map/pallas_call | solution.py:291
  42.0 0.0 collective-permute-done.13.other_ref
  42.0 0.8 %shard_map.80 = (f32[3,3,32,32]{3,2,1,0:T(8,128)}, f32[1,32]{1,0:T(1,128)}) custom-call(f32[32,384]{1,0:T(8,128)S(1)} %add_add_fusion.one_ref, f32[32,384]{1,0:T(8,128)S(1)} %collective-permute-done.13.other_ref, f32[8,128]{1,0:T(8,128)S(1)} %get-tuple-element.37.after_ref), custom_call_target="tpu_custom_call" | custom-call | bytes 139392 | tf_op jit(solution)/shard_map/pallas_call | solution.py:291
  (4 shorter events, 0.0 us)
Async XLA Ops:
  0.6 4.1 %copy-start = (bf16[32,64,128]{2,1,0:T(8,128)(2,1)S(1)}, bf16[32,64,128]{2,1,0:T(8,128)(2,1)}, u32[]{:S(2)}) copy-start(bf16[32,64,128]{2,1,0:T(8,128)(2,1)} %image_ref.1) | copy-start | bytes 1572868
  1.7 8.6 %collective-permute-start = (bf16[32,16,128]{2,1,0:T(8,128)(2,1)S(1)}, bf16[32,16,128]{2,1,0:T(8,128)(2,1)S(1)}, u32[]{:S(2)}, u32[]{:S(2)}) collective-permute-start(bf16[32,16,128]{2,1,0:T(8,128)(2,1)S(1)} %get-tuple-element.41), channel_id=1, source_target_pairs={{0,4},{1,5},{2,6},{3,7},{4,0},{5,1},{6,2},{7,3},{8,12},{9,13},{10,... | collective-permute-start | bytes 393224 | tf_op jit(solution)/shard_map/ppermute | solution.py:48
  4.8 11.1 %copy-start.1 = (bf16[32,64,128]{2,1,0:T(8,128)(2,1)S(1)}, bf16[32,64,128]{2,1,0:T(8,128)(2,1)}, u32[]{:S(2)}) copy-start(bf16[32,64,128]{2,1,0:T(8,128)(2,1)} %cotangent_ref.1) | copy-start | bytes 1572868
  4.8 5.6 %collective-permute-start.1 = (bf16[32,16,128]{2,1,0:T(8,128)(2,1)S(1)}, bf16[32,16,128]{2,1,0:T(8,128)(2,1)S(1)}, u32[]{:S(2)}, u32[]{:S(2)}) collective-permute-start(bf16[32,16,128]{2,1,0:T(8,128)(2,1)S(1)} %get-tuple-element.40), channel_id=1, source_target_pairs={{0,1},{1,0},{2,3},{3,2},{4,8},{5,9},{6,10},{7,11},{8,4},{9,5},{10,... | collective-permute-start | bytes 393224 | tf_op jit(solution)/shard_map/ppermute | solution.py:48
  10.3 2.9 %copy-start.2 = (bf16[3,3,32,32]{3,2,1,0:T(8,128)(2,1)S(1)}, bf16[3,3,32,32]{3,2,1,0:T(8,128)(2,1)}, u32[]{:S(2)}) copy-start(bf16[3,3,32,32]{3,2,1,0:T(8,128)(2,1)} %param.5) | copy-start | bytes 55300
  10.6 3.6 %collective-permute-start.2 = (bf16[12,32,128]{2,1,0:T(8,128)(2,1)S(1)}, bf16[12,32,128]{2,1,0:T(8,128)(2,1)S(1)}, u32[]{:S(2)}, u32[]{:S(2)}) collective-permute-start(bf16[12,32,128]{2,1,0:T(8,128)(2,1)S(1)} %get-tuple-element.25), channel_id=1, source_target_pairs={{0,1},{4,5},{8,9},{12,13},{16,17},{20,21},{24,25},{28,29},{1,0},{5... | collective-permute-start | bytes 294920 | tf_op jit(solution)/shard_map/ppermute | solution.py:48
  10.7 5.1 %collective-permute-start.3 = (bf16[12,32,128]{2,1,0:T(8,128)(2,1)S(1)}, bf16[12,32,128]{2,1,0:T(8,128)(2,1)S(1)}, u32[]{:S(2)}, u32[]{:S(2)}) collective-permute-start(bf16[12,32,128]{2,1,0:T(8,128)(2,1)S(1)} %get-tuple-element.26), channel_id=1, source_target_pairs={{0,4},{4,0},{8,12},{12,8},{16,20},{20,16},{24,28},{28,24},{1,2},{5... | collective-permute-start | bytes 294920 | tf_op jit(solution)/shard_map/ppermute | solution.py:48
  13.4 0.7 %copy-start.3 = (f32[32]{0:T(128)S(1)}, f32[32]{0:T(128)}, u32[]{:S(2)}) copy-start(f32[32]{0:T(128)} %param.6) | copy-start | bytes 388
  20.9 2.3 %collective-permute-start.8 = (f32[32,384]{1,0:T(8,128)S(1)}, f32[32,384]{1,0:T(8,128)S(1)}, u32[]{:S(2)}, u32[]{:S(2)}) collective-permute-start(f32[32,384]{1,0:T(8,128)S(1)} %get-tuple-element.36), channel_id=1, source_target_pairs={{0,1},{1,0},{2,3},{3,2},{4,5},{5,4},{6,7},{7,6},{8,9},{9,8},{10,11... | collective-permute-start | bytes 147464 | tf_op jit(solution)/shard_map/ppermute | solution.py:64
  20.9 10.9 %collective-permute-start.4 = (bf16[16,32,128]{2,1,0:T(8,128)(2,1)S(1)}, bf16[16,32,128]{2,1,0:T(8,128)(2,1)S(1)}, u32[]{:S(2)}, u32[]{:S(2)}) collective-permute-start(bf16[16,32,128]{2,1,0:T(8,128)(2,1)S(1)} %get-tuple-element.29), channel_id=1, source_target_pairs={{0,4},{1,5},{2,6},{3,7},{4,0},{5,1},{6,2},{7,3},{8,12},{9,13},{10,... | collective-permute-start | bytes 393224 | tf_op jit(solution)/shard_map/ppermute | solution.py:48
  23.1 8.8 %collective-permute-start.5 = (bf16[16,32,128]{2,1,0:T(8,128)(2,1)S(1)}, bf16[16,32,128]{2,1,0:T(8,128)(2,1)S(1)}, u32[]{:S(2)}, u32[]{:S(2)}) collective-permute-start(bf16[16,32,128]{2,1,0:T(8,128)(2,1)S(1)} %get-tuple-element.30), channel_id=1, source_target_pairs={{0,1},{1,0},{2,3},{3,2},{4,8},{5,9},{6,10},{7,11},{8,4},{9,5},{10,... | collective-permute-start | bytes 393224 | tf_op jit(solution)/shard_map/ppermute | solution.py:48
  23.2 4.2 %collective-permute-start.9 = (f32[32,384]{1,0:T(8,128)S(1)}, f32[32,384]{1,0:T(8,128)S(1)}, u32[]{:S(2)}, u32[]{:S(2)}) collective-permute-start(f32[32,384]{1,0:T(8,128)S(1)} %add.28), channel_id=1, source_target_pairs={{0,2},{1,3},{2,0},{3,1},{4,6},{5,7},{6,4},{7,5},{8,10},{9,11},{10,... | collective-permute-start | bytes 147464 | tf_op jit(solution)/shard_map/ppermute | solution.py:64
  27.4 7.7 %collective-permute-start.10 = (f32[32,384]{1,0:T(8,128)S(1)}, f32[32,384]{1,0:T(8,128)S(1)}, u32[]{:S(2)}, u32[]{:S(2)}) collective-permute-start(f32[32,384]{1,0:T(8,128)S(1)} %add.29), channel_id=1, source_target_pairs={{0,8},{4,12},{8,0},{12,4},{16,24},{20,28},{24,16},{28,20},{1,9},{5... | collective-permute-start | bytes 147464 | tf_op jit(solution)/shard_map/ppermute | solution.py:64
  28.9 6.3 %collective-permute-start.11 = (f32[32,384]{1,0:T(8,128)S(1)}, f32[32,384]{1,0:T(8,128)S(1)}, u32[]{:S(2)}, u32[]{:S(2)}) collective-permute-start(f32[32,384]{1,0:T(8,128)S(1)} %add.29), channel_id=1, source_target_pairs={{0,16},{4,20},{8,24},{12,28},{16,0},{20,4},{24,8},{28,12},{1,17},{... | collective-permute-start | bytes 147464 | tf_op jit(solution)/shard_map/ppermute | solution.py:64
  31.9 5.9 %collective-permute-start.12 = (f32[32,384]{1,0:T(8,128)S(1)}, f32[32,384]{1,0:T(8,128)S(1)}, u32[]{:S(2)}, u32[]{:S(2)}) collective-permute-start(f32[32,384]{1,0:T(8,128)S(1)} %add.29), channel_id=1, source_target_pairs={{0,24},{4,28},{8,16},{12,20},{16,8},{20,12},{24,0},{28,4},{1,25},{... | collective-permute-start | bytes 147464 | tf_op jit(solution)/shard_map/ppermute | solution.py:64
  32.2 6.2 %collective-permute-start.6 = (bf16[12,32,128]{2,1,0:T(8,128)(2,1)S(1)}, bf16[12,32,128]{2,1,0:T(8,128)(2,1)S(1)}, u32[]{:S(2)}, u32[]{:S(2)}) collective-permute-start(bf16[12,32,128]{2,1,0:T(8,128)(2,1)S(1)} %get-tuple-element.33), channel_id=1, source_target_pairs={{0,1},{4,5},{8,9},{12,13},{16,17},{20,21},{24,25},{28,29},{1,0},{5... | collective-permute-start | bytes 294920 | tf_op jit(solution)/shard_map/ppermute | solution.py:48
  32.2 6.1 %collective-permute-start.7 = (bf16[12,32,128]{2,1,0:T(8,128)(2,1)S(1)}, bf16[12,32,128]{2,1,0:T(8,128)(2,1)S(1)}, u32[]{:S(2)}, u32[]{:S(2)}) collective-permute-start(bf16[12,32,128]{2,1,0:T(8,128)(2,1)S(1)} %get-tuple-element.34), channel_id=1, source_target_pairs={{0,4},{4,0},{8,12},{12,8},{16,20},{20,16},{24,28},{28,24},{1,2},{5... | collective-permute-start | bytes 294920 | tf_op jit(solution)/shard_map/ppermute | solution.py:48
  37.8 4.2 %collective-permute-start.13 = (f32[32,384]{1,0:T(8,128)S(1)}, f32[32,384]{1,0:T(8,128)S(1)}, u32[]{:S(2)}, u32[]{:S(2)}) collective-permute-start(f32[32,384]{1,0:T(8,128)S(1)} %add_add_fusion.one_ref), channel_id=1, source_target_pairs={{0,4},{4,0},{8,12},{12,8},{16,20},{20,16},{24,28},{28,24},{1,5},{5... | collective-permute-start | bytes 147464 | tf_op jit(solution)/shard_map/ppermute | solution.py:64

commit v14 on v11

--- a/solution.py
+++ b/solution.py
@@ -69,11 +69,10 @@
 
 
 def gelu_pair(preact):
-    coef = 0.7978845608
+    coef, cubic = 0.7978845608, 0.7978845608 * 0.044715
     square = preact * preact
-    tval = jnp.tanh(coef * (preact + 0.044715 * (square * preact)))
-    half = 0.5 * (1.0 + tval)
-    slope_val = half + 0.5 * preact * (1.0 - tval * tval) * coef * (1.0 + 3.0 * 0.044715 * square)
+    half = 0.5 + 0.5 * jnp.tanh(preact * (coef + cubic * square))
+    slope_val = half * (1.0 + (1.0 - half) * (preact * (2.0 * coef + 6.0 * cubic * square)))
     return (preact * half, slope_val)
 
 
@@ -119,7 +118,12 @@
         store(first_group + group, first, last)
 
 
-def own_kernel(image_ref, rows_ref, rims_ref):
+def rolled(rows):
+    axis, width = rows.ndim - 1, rows.shape[-1]
+    return pltpu.roll(rows, DILATION, axis), rows, pltpu.roll(rows, width - DILATION, axis)
+
+
+def own_kernel(image_ref, cotangent_ref, rows_ref, cotangent_rows_ref, rims_ref):
     count = image_ref.shape[1] // DILATION
     groups = rims_ref.shape[1] // count
 
@@ -130,7 +134,11 @@
     def body(block, carry):
         start = pl.multiple_of(block * DILATION, DILATION)
         rows = jnp.swapaxes(image_ref[:, pl.ds(start, DILATION), :], 0, 1)
-        rows_ref[pl.ds(start, DILATION)] = rows
+        for index, moved in enumerate(rolled(rows)):
+            rows_ref[index, pl.ds(start, DILATION)] = moved
+        cotangent_rows_ref[pl.ds(start, DILATION)] = jnp.swapaxes(
+            cotangent_ref[:, pl.ds(start, DILATION), :], 0, 1
+        )
         pack_rows(rows, store, block * groups)
         return carry
 
@@ -175,31 +183,31 @@
         rims = unpack_group(left_ref[group_start + group], right_ref[group_start + group], pieces)
         for k in range(pieces):
             row = group * pieces + k
-            value = rows_of(row)
+            before, value, after = rows_of(row)
             columns = slice(row * width, (row + 1) * width)
-            before = jnp.where(lane < DILATION, rims[k], pltpu.roll(value, DILATION, 1))
-            after = jnp.where(lane >= width - DILATION, rims[k], pltpu.roll(value, width - DILATION, 1))
+            before = jnp.where(lane < DILATION, rims[k], before)
+            after = jnp.where(lane >= width - DILATION, rims[k], after)
             stack_ref[block, 0:channels, columns] = before
             stack_ref[block, channels : 2 * channels, columns] = value
             stack_ref[block, 2 * channels : 3 * channels, columns] = after
 
 
-def spread_all(own_ref, outer_ref, one_ref, two_ref, stack_ref):
-    count = own_ref.shape[0] // DILATION
+def spread_all(own_of, outer_ref, one_ref, two_ref, stack_ref):
+    count = stack_ref.shape[0] - 2
     groups = one_ref.shape[0] // (count + 2)
 
     def every(left_ref, right_ref):
-        spread(lambda row: outer_ref[0, row], left_ref, right_ref, stack_ref, 0, 0)
+        spread(lambda row: rolled(outer_ref[0, row]), left_ref, right_ref, stack_ref, 0, 0)
 
         def body(block, carry):
             spread(
-                lambda row: own_ref[block * DILATION + row],
+                lambda row: own_of(block * DILATION + row),
                 left_ref, right_ref, stack_ref, block + 1, (block + 1) * groups,
             )
             return carry
 
         lax.fori_loop(0, count, body, 0)
-        spread(lambda row: outer_ref[1, row], left_ref, right_ref, stack_ref, count + 1, (count + 1) * groups)
+        spread(lambda row: rolled(outer_ref[1, row]), left_ref, right_ref, stack_ref, count + 1, (count + 1) * groups)
 
     either("col", every, one_ref, two_ref)
 
@@ -208,10 +216,10 @@
     scale, own_ref, outer_ref, one_ref, two_ref, cotangent_ref, weight_ref, bias_ref,
     activation_ref, grad_ref, send_one_ref, send_two_ref, rims_ref, terms_ref, stack_ref, sum_ref, taps_ref,
 ):
-    height, channels, width = own_ref.shape
+    height, channels, width = own_ref.shape[1:]
     count = height // DILATION
     groups = rims_ref.shape[1] // count
-    spread_all(own_ref, outer_ref, one_ref, two_ref, stack_ref)
+    spread_all(lambda at: [own_ref[k, at] for k in range(3)], outer_ref, one_ref, two_ref, stack_ref)
     taps_ref[...] = jnp.zeros_like(taps_ref)
     sum_ref[...] = jnp.zeros_like(sum_ref)
     depth = 9 * channels
@@ -224,14 +232,13 @@
         start = pl.multiple_of(block * DILATION, DILATION)
         stacked = stack_ref[pl.ds(block, 3)].reshape(depth, DILATION * width)
         preact = jnp.dot(weight_ref[...], stacked, preferred_element_type=jnp.float32)
-        cotangent = jnp.swapaxes(cotangent_ref[:, pl.ds(start, DILATION), :], 0, 1)
         bias = jnp.broadcast_to(bias_ref[...], (channels, width))
         values, grads = [], []
         total = sum_ref[...]
         for row in range(DILATION):
             value, slope_val = gelu_pair(preact[:, row * width : (row + 1) * width] + bias)
             values.append(value.astype(jnp.bfloat16))
-            grad = (cotangent[row].astype(jnp.float32) * slope_val).astype(jnp.bfloat16)
+            grad = (cotangent_ref[start + row].astype(jnp.float32) * slope_val).astype(jnp.bfloat16)
             grads.append(grad)
             total = total + grad.astype(jnp.float32)
             grad_ref[start + row] = grad
@@ -261,7 +268,7 @@
 ):
     height, channels, width = own_ref.shape
     token_ref[...] = jnp.zeros_like(token_ref)
-    spread_all(own_ref, outer_ref, one_ref, two_ref, stack_ref)
+    spread_all(lambda at: rolled(own_ref[at]), outer_ref, one_ref, two_ref, stack_ref)
 
     def body(block, carry):
         start = pl.multiple_of(block * DILATION, DILATION)
@@ -324,7 +331,9 @@
 
     one = swap_pairs(image_rim((1 - odd) * end, 0), "row", 0)
     two = swap_pairs(image_rim(odd * end, 1), "row", 1)
-    image_rows, rims = call(own_kernel, (rows, own_rims), (image,))
+    image_rows, cotangent_rows, rims = call(
+        own_kernel, (shape((3, *rows.shape), bf16), rows, own_rims), (image, cotangent)
+    )
     forward_weight = jnp.transpose(weight, (2, 0, 1, 3)).reshape(channels, depth)
     backward_weight = jnp.transpose(weight[::-1, ::-1], (3, 0, 1, 2)).reshape(channels, depth)
     one, two, image_outer = call(
@@ -337,7 +346,7 @@
             shape(image.shape, bf16), rows, edge, edge, own_rims,
             shape((channels, -(-(depth + 1) // 128) * 128), f32),
         ),
-        (image_rows, image_outer, one, two, cotangent, forward_weight, bias[:, None]),
+        (image_rows, image_outer, one, two, cotangent_rows, forward_weight, bias[:, None]),
         (stack, pltpu.VMEM((channels, width), f32), pltpu.VMEM((depth, channels), f32)),
         2 * flops,
     )

time: 41.8 us -> 41.6 us (level)
  waiting for transfers between devices: 10.6 us -> 8.89 us
  local copies, waits for them, and re-layouts: 1.01 us -> 2.44 us
    ppermute x8, waiting for transfers between devices: 6.45 us -> 4.72 us  [swap_pairs(): return lax.ppermute(value, ('row', 'col'), pairs)]
    unnamed x8, local copies, waits for them, and re-layouts: 0.66 us -> 2.09 us
  transfers between devices with their start and end apart: 15 -> 15, of which waited for: 5 -> 5; matrix products, arithmetic and copies ran while one was open for 1% -> 1% of each run, Pallas kernels for 11% -> 12%
where the time goes in v14:
time: 41.6 us; the launch traced here: 41.3 us
  starting transfers between devices  17.3 us (42%)
  Pallas kernels  10.8 us (26%)
  waiting for transfers between devices  8.89 us (21%)
  local copies, waits for them, and re-layouts  2.44 us (6%)
  other arithmetic  1.04 us (2%)
  between operations  0.78 us (2%)
    pallas_call x6, Pallas kernels, call(): pl.pallas_call(kernel, out_shape=out_shapes, in_specs=[whole] * len(opera...  10.8 us
    ppermute x8, starting transfers between devices, swap_pairs(): return lax.ppermute(value, ('row', 'col'), pairs)  10.1 us
    ppermute x7, starting transfers between devices, add_pairs(): lax.ppermute(value, axis, [(at, at ^ mask) for at in range(lax.axis_size(...  7.21 us
    ppermute x8, waiting for transfers between devices, swap_pairs(): return lax.ppermute(value, ('row', 'col'), pairs)  4.72 us
    ppermute x7, waiting for transfers between devices, add_pairs(): lax.ppermute(value, axis, [(at, at ^ mask) for at in range(lax.axis_size(...  4.17 us
    unnamed x8, local copies, waits for them, and re-layouts  2.09 us
    select_n x1, other arithmetic, image_rim(): return rim if flag is None else jnp.where(flag, jnp.zeros_like(rim), rim)  1.01 us
  transfers between devices with their start and end apart: 15, of which 5 were waited for; matrix products, arithmetic and copies ran while one was open for 1% of the time, Pallas kernels for 12%

profile of v14, /device:TPU:0, one launch (start us, length us, event | category | flops | bytes accessed | tf_op | source)
XLA Modules:
  0.0 41.3 jit_solution(2195435646909473692)
XLA Ops:
  0.6 0.0 copy-start.2
  0.6 0.0 copy-start.3
  0.7 1.0 %dynamic-slice_select_fusion = (bf16[32,16,128]{2,1,0:T(8,128)(2,1)S(1)}, bf16[32,16,128]{2,1,0:T(8,128)(2,1)S(1)}) fusion(bf16[32,64,128]{2,1,0:T(8,128)(2,1)} %image_ref.1, s32[]{:T(128)S(6)} %select_n.24, pred[]{:T(512)S(6)} %or.3, s32[]{:T(128)S(6)} %select_n.22), kind=kLoop, calls=%fused_computation | loop fusion | flops 65536 | bytes 524297 | tf_op jit(solution)/shard_map/jit(_where)/select_n | solution.py:330
  1.7 3.0 %collective-permute-start = (bf16[32,16,128]{2,1,0:T(8,128)(2,1)S(1)}, bf16[32,16,128]{2,1,0:T(8,128)(2,1)S(1)}, u32[]{:S(2)}, u32[]{:S(2)}) collective-permute-start(bf16[32,16,128]{2,1,0:T(8,128)(2,1)S(1)} %get-tuple-element.43), channel_id=1, source_target_pairs={{0,4},{1,5},{2,6},{3,7},{4,0},{5,1},{6,2},{7,3},{8,12},{9,13},{10,... | collective-permute-start | bytes 393224 | tf_op jit(solution)/shard_map/ppermute | solution.py:48
  4.7 0.0 collective-permute-start.1
  4.7 0.0 copy-start
  4.7 1.0 %copy-done = bf16[32,64,128]{2,1,0:T(8,128)(2,1)S(1)} copy-done((bf16[32,64,128]{2,1,0:T(8,128)(2,1)S(1)}, bf16[32,64,128]{2,1,0:T(8,128)(2,1)}, u32[]{:S(2)}) %copy-start) | copy-done | bytes 524312
  5.8 1.0 %copy-done.1 = bf16[32,64,128]{2,1,0:T(8,128)(2,1)S(1)} copy-done((bf16[32,64,128]{2,1,0:T(8,128)(2,1)S(1)}, bf16[32,64,128]{2,1,0:T(8,128)(2,1)}, u32[]{:S(2)}) %copy-start.1) | copy-done | bytes 524312
  6.8 1.1 %shard_map.75 = (bf16[3,64,32,128]{3,2,1,0:T(8,128)(2,1)S(1)}, bf16[64,32,128]{2,1,0:T(8,128)(2,1)S(1)}, bf16[2,8,32,128]{3,2,1,0:T(8,128)(2,1)S(1)}) custom-call(bf16[32,64,128]{2,1,0:T(8,128)(2,1)S(1)} %copy-done, bf16[32,64,128]{2,1,0:T(8,128)(2,1)S(1)} %copy-done.1), custom_call_target="tpu_custom_call" | custom-call | bytes 3276800 | tf_op jit(solution)/shard_map/pallas_call | solution.py:296
  7.9 2.4 %collective-permute-done.one_ref = bf16[32,16,128]{2,1,0:T(8,128)(2,1)S(1)} collective-permute-done((bf16[32,16,128]{2,1,0:T(8,128)(2,1)S(1)}, bf16[32,16,128]{2,1,0:T(8,128)(2,1)S(1)}, u32[]{:S(2)}, u32[]{:S(2)}) %collective-permute-start) | collective-permute-done | bytes 131104 | tf_op jit(solution)/shard_map/ppermute | solution.py:48
  10.3 0.0 collective-permute-done.1.two_ref
  10.3 0.3 shard_map.76
  10.6 0.1 collective-permute-start.2
  10.7 2.6 %collective-permute-start.3 = (bf16[12,32,128]{2,1,0:T(8,128)(2,1)S(1)}, bf16[12,32,128]{2,1,0:T(8,128)(2,1)S(1)}, u32[]{:S(2)}, u32[]{:S(2)}) collective-permute-start(bf16[12,32,128]{2,1,0:T(8,128)(2,1)S(1)} %get-tuple-element.27), channel_id=1, source_target_pairs={{0,4},{4,0},{8,12},{12,8},{16,20},{20,16},{24,28},{28,24},{1,2},{5... | collective-permute-start | bytes 294920 | tf_op jit(solution)/shard_map/ppermute | solution.py:48
  13.2 0.0 copy-done.2
  13.2 0.1 copy.11
  13.3 0.1 reshape.17.weight_ref
  13.4 0.0 copy-done.3
  13.4 0.1 copy.12.bias_ref
  13.5 0.0 collective-permute-done.2.one_ref
  13.5 2.3 %collective-permute-done.3.two_ref = bf16[12,32,128]{2,1,0:T(8,128)(2,1)S(1)} collective-permute-done((bf16[12,32,128]{2,1,0:T(8,128)(2,1)S(1)}, bf16[12,32,128]{2,1,0:T(8,128)(2,1)S(1)}, u32[]{:S(2)}, u32[]{:S(2)}) %collective-permute-start.3) | collective-permute-done | bytes 98336 | tf_op jit(solution)/shard_map/ppermute | solution.py:48
  15.8 4.8 %shard_map.77 = (bf16[32,64,128]{2,1,0:T(8,128)(2,1)}, bf16[64,32,128]{2,1,0:T(8,128)(2,1)S(1)}, bf16[16,32,128]{2,1,0:T(8,128)(2,1)S(1)}, bf16[16,32,128]{2,1,0...) custom-call(bf16[3,64,32,128]{3,2,1,0:T(8,128)(2,1)S(1)} %get-tuple-element.23.own_ref, ...), custom_call_target="tpu_custom_call" | custom-call | flops 301989888 | bytes 4065408 | tf_op jit(solution)/shard_map/pallas_call | solution.py:296
  20.7 0.6 %collective-permute-start.10 = (f32[32,384]{1,0:T(8,128)S(1)}, f32[32,384]{1,0:T(8,128)S(1)}, u32[]{:S(2)}, u32[]{:S(2)}) collective-permute-start(f32[32,384]{1,0:T(8,128)S(1)} %get-tuple-element.38), channel_id=1, source_target_pairs={{0,3},{1,2},{2,1},{3,0},{4,7},{5,6},{6,5},{7,4},{8,11},{9,10},{10,... | collective-permute-start | bytes 147464 | tf_op jit(solution)/shard_map/ppermute | solution.py:62
  21.3 0.0 collective-permute-start.8
  21.3 1.5 %collective-permute-start.9 = (f32[32,384]{1,0:T(8,128)S(1)}, f32[32,384]{1,0:T(8,128)S(1)}, u32[]{:S(2)}, u32[]{:S(2)}) collective-permute-start(f32[32,384]{1,0:T(8,128)S(1)} %get-tuple-element.38), channel_id=1, source_target_pairs={{0,2},{1,3},{2,0},{3,1},{4,6},{5,7},{6,4},{7,5},{8,10},{9,11},{10,... | collective-permute-start | bytes 147464 | tf_op jit(solution)/shard_map/ppermute | solution.py:62
  22.8 2.0 %collective-permute-start.4 = (bf16[16,32,128]{2,1,0:T(8,128)(2,1)S(1)}, bf16[16,32,128]{2,1,0:T(8,128)(2,1)S(1)}, u32[]{:S(2)}, u32[]{:S(2)}) collective-permute-start(bf16[16,32,128]{2,1,0:T(8,128)(2,1)S(1)} %get-tuple-element.31), channel_id=1, source_target_pairs={{0,4},{1,5},{2,6},{3,7},{4,0},{5,1},{6,2},{7,3},{8,12},{9,13},{10,... | collective-permute-start | bytes 393224 | tf_op jit(solution)/shard_map/ppermute | solution.py:48
  24.8 0.0 collective-permute-start.5
  24.8 0.0 collective-permute-done.10
  24.8 0.0 collective-permute-done.8
  24.8 0.8 %collective-permute-done.9 = f32[32,384]{1,0:T(8,128)S(1)} collective-permute-done((f32[32,384]{1,0:T(8,128)S(1)}, f32[32,384]{1,0:T(8,128)S(1)}, u32[]{:S(2)}, u32[]{:S(2)}) %collective-permute-start.9) | collective-permute-done | bytes 49184 | tf_op jit(solution)/shard_map/ppermute | solution.py:62
  25.6 2.3 %collective-permute-start.11 = (f32[32,384]{1,0:T(8,128)S(1)}, f32[32,384]{1,0:T(8,128)S(1)}, u32[]{:S(2)}, u32[]{:S(2)}) collective-permute-start(f32[32,384]{1,0:T(8,128)S(1)} %add_add_fusion.1), channel_id=1, source_target_pairs={{0,8},{4,12},{8,0},{12,4},{16,24},{20,28},{24,16},{28,20},{1,9},{5... | collective-permute-start | bytes 147464 | tf_op jit(solution)/shard_map/ppermute | solution.py:62
  27.9 2.6 %collective-permute-start.12 = (f32[32,384]{1,0:T(8,128)S(1)}, f32[32,384]{1,0:T(8,128)S(1)}, u32[]{:S(2)}, u32[]{:S(2)}) collective-permute-start(f32[32,384]{1,0:T(8,128)S(1)} %add_add_fusion.1), channel_id=1, source_target_pairs={{0,16},{4,20},{8,24},{12,28},{16,0},{20,4},{24,8},{28,12},{1,17},{... | collective-permute-start | bytes 147464 | tf_op jit(solution)/shard_map/ppermute | solution.py:62
  30.5 0.0 collective-permute-start.13
  30.5 0.0 collective-permute-done.4.one_ref
  30.5 0.0 collective-permute-done.5.two_ref
  30.5 0.3 shard_map.78
  30.8 0.1 collective-permute-start.6
  30.9 2.4 %collective-permute-start.7 = (bf16[12,32,128]{2,1,0:T(8,128)(2,1)S(1)}, bf16[12,32,128]{2,1,0:T(8,128)(2,1)S(1)}, u32[]{:S(2)}, u32[]{:S(2)}) collective-permute-start(bf16[12,32,128]{2,1,0:T(8,128)(2,1)S(1)} %get-tuple-element.36), channel_id=1, source_target_pairs={{0,4},{4,0},{8,12},{12,8},{16,20},{20,16},{24,28},{28,24},{1,2},{5... | collective-permute-start | bytes 294920 | tf_op jit(solution)/shard_map/ppermute | solution.py:48
  33.3 0.0 collective-permute-done.11
  33.3 0.0 collective-permute-done.12
  33.3 3.1 %collective-permute-done.13 = f32[32,384]{1,0:T(8,128)S(1)} collective-permute-done((f32[32,384]{1,0:T(8,128)S(1)}, f32[32,384]{1,0:T(8,128)S(1)}, u32[]{:S(2)}, u32[]{:S(2)}) %collective-permute-start.13) | collective-permute-done | bytes 49184 | tf_op jit(solution)/shard_map/ppermute | solution.py:62
  36.4 0.2 collective-permute-start.14
  36.6 0.1 copy.14.weight_ref
  36.7 0.0 collective-permute-done.6.one_ref
  36.7 0.0 collective-permute-done.7.two_ref
  36.7 3.6 %shard_map.79 = (bf16[32,64,128]{2,1,0:T(8,128)(2,1)}, f32[8,128]{1,0:T(8,128)S(1)}) custom-call(bf16[64,32,128]{2,1,0:T(8,128)(2,1)S(1)} %get-tuple-element.30.own_ref, bf16[2,16,32,128]{3,2,1,0:T(8,128)(2,1)S(1)} %get-tuple-element.34.outer_ref, bf16[12,32,128]{2,1,0:T(8,128)(2,1)S(1)} %collective-permute-done.6.one_ref, ...), custom_call_target="tpu_custom_call" | custom-call | flops 150994944 | bytes 1529856 | tf_op jit(solution)/shard_map/pallas_call | solution.py:296
  40.3 0.2 collective-permute-done.14.other_ref
  40.6 0.8 %shard_map.80 = (f32[3,3,32,32]{3,2,1,0:T(8,128)}, f32[1,32]{1,0:T(1,128)}) custom-call(f32[32,384]{1,0:T(8,128)S(1)} %add_add_fusion.one_ref, f32[32,384]{1,0:T(8,128)S(1)} %collective-permute-done.14.other_ref, f32[8,128]{1,0:T(8,128)S(1)} %get-tuple-element.39.after_ref), custom_call_target="tpu_custom_call" | custom-call | bytes 139392 | tf_op jit(solution)/shard_map/pallas_call | solution.py:296
  (4 shorter events, 0.0 us)
Async XLA Ops:
  0.6 12.6 %copy-start.2 = (bf16[3,3,32,32]{3,2,1,0:T(8,128)(2,1)S(1)}, bf16[3,3,32,32]{3,2,1,0:T(8,128)(2,1)}, u32[]{:S(2)}) copy-start(bf16[3,3,32,32]{3,2,1,0:T(8,128)(2,1)} %param.5) | copy-start | bytes 55300
  0.6 12.8 %copy-start.3 = (f32[32]{0:T(128)S(1)}, f32[32]{0:T(128)}, u32[]{:S(2)}) copy-start(f32[32]{0:T(128)} %param.6) | copy-start | bytes 388
  1.7 8.6 %collective-permute-start = (bf16[32,16,128]{2,1,0:T(8,128)(2,1)S(1)}, bf16[32,16,128]{2,1,0:T(8,128)(2,1)S(1)}, u32[]{:S(2)}, u32[]{:S(2)}) collective-permute-start(bf16[32,16,128]{2,1,0:T(8,128)(2,1)S(1)} %get-tuple-element.43), channel_id=1, source_target_pairs={{0,4},{1,5},{2,6},{3,7},{4,0},{5,1},{6,2},{7,3},{8,12},{9,13},{10,... | collective-permute-start | bytes 393224 | tf_op jit(solution)/shard_map/ppermute | solution.py:48
  4.7 5.6 %collective-permute-start.1 = (bf16[32,16,128]{2,1,0:T(8,128)(2,1)S(1)}, bf16[32,16,128]{2,1,0:T(8,128)(2,1)S(1)}, u32[]{:S(2)}, u32[]{:S(2)}) collective-permute-start(bf16[32,16,128]{2,1,0:T(8,128)(2,1)S(1)} %get-tuple-element.42), channel_id=1, source_target_pairs={{0,1},{1,0},{2,3},{3,2},{4,8},{5,9},{6,10},{7,11},{8,4},{9,5},{10,... | collective-permute-start | bytes 393224 | tf_op jit(solution)/shard_map/ppermute | solution.py:48
  4.7 1.0 %copy-start = (bf16[32,64,128]{2,1,0:T(8,128)(2,1)S(1)}, bf16[32,64,128]{2,1,0:T(8,128)(2,1)}, u32[]{:S(2)}) copy-start(bf16[32,64,128]{2,1,0:T(8,128)(2,1)} %image_ref.1) | copy-start | bytes 1572868
  5.8 1.0 %copy-start.1 = (bf16[32,64,128]{2,1,0:T(8,128)(2,1)S(1)}, bf16[32,64,128]{2,1,0:T(8,128)(2,1)}, u32[]{:S(2)}) copy-start(bf16[32,64,128]{2,1,0:T(8,128)(2,1)} %cotangent_ref.1) | copy-start | bytes 1572868
  10.6 2.9 %collective-permute-start.2 = (bf16[12,32,128]{2,1,0:T(8,128)(2,1)S(1)}, bf16[12,32,128]{2,1,0:T(8,128)(2,1)S(1)}, u32[]{:S(2)}, u32[]{:S(2)}) collective-permute-start(bf16[12,32,128]{2,1,0:T(8,128)(2,1)S(1)} %get-tuple-element.26), channel_id=1, source_target_pairs={{0,1},{4,5},{8,9},{12,13},{16,17},{20,21},{24,25},{28,29},{1,0},{5... | collective-permute-start | bytes 294920 | tf_op jit(solution)/shard_map/ppermute | solution.py:48
  10.7 5.1 %collective-permute-start.3 = (bf16[12,32,128]{2,1,0:T(8,128)(2,1)S(1)}, bf16[12,32,128]{2,1,0:T(8,128)(2,1)S(1)}, u32[]{:S(2)}, u32[]{:S(2)}) collective-permute-start(bf16[12,32,128]{2,1,0:T(8,128)(2,1)S(1)} %get-tuple-element.27), channel_id=1, source_target_pairs={{0,4},{4,0},{8,12},{12,8},{16,20},{20,16},{24,28},{28,24},{1,2},{5... | collective-permute-start | bytes 294920 | tf_op jit(solution)/shard_map/ppermute | solution.py:48
  20.7 4.2 %collective-permute-start.10 = (f32[32,384]{1,0:T(8,128)S(1)}, f32[32,384]{1,0:T(8,128)S(1)}, u32[]{:S(2)}, u32[]{:S(2)}) collective-permute-start(f32[32,384]{1,0:T(8,128)S(1)} %get-tuple-element.38), channel_id=1, source_target_pairs={{0,3},{1,2},{2,1},{3,0},{4,7},{5,6},{6,5},{7,4},{8,11},{9,10},{10,... | collective-permute-start | bytes 147464 | tf_op jit(solution)/shard_map/ppermute | solution.py:62
  21.3 3.5 %collective-permute-start.8 = (f32[32,384]{1,0:T(8,128)S(1)}, f32[32,384]{1,0:T(8,128)S(1)}, u32[]{:S(2)}, u32[]{:S(2)}) collective-permute-start(f32[32,384]{1,0:T(8,128)S(1)} %get-tuple-element.38), channel_id=1, source_target_pairs={{0,1},{1,0},{2,3},{3,2},{4,5},{5,4},{6,7},{7,6},{8,9},{9,8},{10,11... | collective-permute-start | bytes 147464 | tf_op jit(solution)/shard_map/ppermute | solution.py:62
  21.3 4.3 %collective-permute-start.9 = (f32[32,384]{1,0:T(8,128)S(1)}, f32[32,384]{1,0:T(8,128)S(1)}, u32[]{:S(2)}, u32[]{:S(2)}) collective-permute-start(f32[32,384]{1,0:T(8,128)S(1)} %get-tuple-element.38), channel_id=1, source_target_pairs={{0,2},{1,3},{2,0},{3,1},{4,6},{5,7},{6,4},{7,5},{8,10},{9,11},{10,... | collective-permute-start | bytes 147464 | tf_op jit(solution)/shard_map/ppermute | solution.py:62
  22.8 7.7 %collective-permute-start.4 = (bf16[16,32,128]{2,1,0:T(8,128)(2,1)S(1)}, bf16[16,32,128]{2,1,0:T(8,128)(2,1)S(1)}, u32[]{:S(2)}, u32[]{:S(2)}) collective-permute-start(bf16[16,32,128]{2,1,0:T(8,128)(2,1)S(1)} %get-tuple-element.31), channel_id=1, source_target_pairs={{0,4},{1,5},{2,6},{3,7},{4,0},{5,1},{6,2},{7,3},{8,12},{9,13},{10,... | collective-permute-start | bytes 393224 | tf_op jit(solution)/shard_map/ppermute | solution.py:48
  24.8 5.7 %collective-permute-start.5 = (bf16[16,32,128]{2,1,0:T(8,128)(2,1)S(1)}, bf16[16,32,128]{2,1,0:T(8,128)(2,1)S(1)}, u32[]{:S(2)}, u32[]{:S(2)}) collective-permute-start(bf16[16,32,128]{2,1,0:T(8,128)(2,1)S(1)} %get-tuple-element.32), channel_id=1, source_target_pairs={{0,1},{1,0},{2,3},{3,2},{4,8},{5,9},{6,10},{7,11},{8,4},{9,5},{10,... | collective-permute-start | bytes 393224 | tf_op jit(solution)/shard_map/ppermute | solution.py:48
  25.6 7.6 %collective-permute-start.11 = (f32[32,384]{1,0:T(8,128)S(1)}, f32[32,384]{1,0:T(8,128)S(1)}, u32[]{:S(2)}, u32[]{:S(2)}) collective-permute-start(f32[32,384]{1,0:T(8,128)S(1)} %add_add_fusion.1), channel_id=1, source_target_pairs={{0,8},{4,12},{8,0},{12,4},{16,24},{20,28},{24,16},{28,20},{1,9},{5... | collective-permute-start | bytes 147464 | tf_op jit(solution)/shard_map/ppermute | solution.py:62
  27.9 5.3 %collective-permute-start.12 = (f32[32,384]{1,0:T(8,128)S(1)}, f32[32,384]{1,0:T(8,128)S(1)}, u32[]{:S(2)}, u32[]{:S(2)}) collective-permute-start(f32[32,384]{1,0:T(8,128)S(1)} %add_add_fusion.1), channel_id=1, source_target_pairs={{0,16},{4,20},{8,24},{12,28},{16,0},{20,4},{24,8},{28,12},{1,17},{... | collective-permute-start | bytes 147464 | tf_op jit(solution)/shard_map/ppermute | solution.py:62
  30.5 5.9 %collective-permute-start.13 = (f32[32,384]{1,0:T(8,128)S(1)}, f32[32,384]{1,0:T(8,128)S(1)}, u32[]{:S(2)}, u32[]{:S(2)}) collective-permute-start(f32[32,384]{1,0:T(8,128)S(1)} %add_add_fusion.1), channel_id=1, source_target_pairs={{0,24},{4,28},{8,16},{12,20},{16,8},{20,12},{24,0},{28,4},{1,25},{... | collective-permute-start | bytes 147464 | tf_op jit(solution)/shard_map/ppermute | solution.py:62
  30.8 5.9 %collective-permute-start.6 = (bf16[12,32,128]{2,1,0:T(8,128)(2,1)S(1)}, bf16[12,32,128]{2,1,0:T(8,128)(2,1)S(1)}, u32[]{:S(2)}, u32[]{:S(2)}) collective-permute-start(bf16[12,32,128]{2,1,0:T(8,128)(2,1)S(1)} %get-tuple-element.35), channel_id=1, source_target_pairs={{0,1},{4,5},{8,9},{12,13},{16,17},{20,21},{24,25},{28,29},{1,0},{5... | collective-permute-start | bytes 294920 | tf_op jit(solution)/shard_map/ppermute | solution.py:48
  30.9 5.9 %collective-permute-start.7 = (bf16[12,32,128]{2,1,0:T(8,128)(2,1)S(1)}, bf16[12,32,128]{2,1,0:T(8,128)(2,1)S(1)}, u32[]{:S(2)}, u32[]{:S(2)}) collective-permute-start(bf16[12,32,128]{2,1,0:T(8,128)(2,1)S(1)} %get-tuple-element.36), channel_id=1, source_target_pairs={{0,4},{4,0},{8,12},{12,8},{16,20},{20,16},{24,28},{28,24},{1,2},{5... | collective-permute-start | bytes 294920 | tf_op jit(solution)/shard_map/ppermute | solution.py:48
  36.4 4.2 %collective-permute-start.14 = (f32[32,384]{1,0:T(8,128)S(1)}, f32[32,384]{1,0:T(8,128)S(1)}, u32[]{:S(2)}, u32[]{:S(2)}) collective-permute-start(f32[32,384]{1,0:T(8,128)S(1)} %add_add_fusion.one_ref), channel_id=1, source_target_pairs={{0,4},{4,0},{8,12},{12,8},{16,20},{20,16},{24,28},{28,24},{1,5},{5... | collective-permute-start | bytes 147464 | tf_op jit(solution)/shard_map/ppermute | solution.py:62

commit v15 on v14

--- a/solution.py
+++ b/solution.py
@@ -123,7 +123,7 @@
     return pltpu.roll(rows, DILATION, axis), rows, pltpu.roll(rows, width - DILATION, axis)
 
 
-def own_kernel(image_ref, cotangent_ref, rows_ref, cotangent_rows_ref, rims_ref):
+def own_kernel(image_ref, cotangent_ref, rows_ref, cotangent_rows_ref, one_ref, two_ref, rims_ref):
     count = image_ref.shape[1] // DILATION
     groups = rims_ref.shape[1] // count
 
@@ -144,6 +144,14 @@
 
     lax.fori_loop(0, count, body, 0)
 
+    def send(first_ref, last_ref):
+        first_ref[...] = rims_ref[0]
+        last_ref[...] = rims_ref[1]
+
+    either("col", send, one_ref, two_ref)
+    clear_if(alone("col", 0), one_ref)
+    clear_if(alone("col", 1), two_ref)
+
 
 def either(axis, body, one, two):
     odd = lax.axis_index(axis) % 2 == 1
@@ -168,6 +176,27 @@
         send_last_ref[groups : groups + own] = rims_ref[1]
         for index in range(2):
             pack_rows(outer_ref[index], store, index * (groups + own))
+
+    either("row", order, one_ref, two_ref)
+    either("col", pack, send_one_ref, send_two_ref)
+    clear_if(alone("col", 0), send_one_ref)
+    clear_if(alone("col", 1), send_two_ref)
+
+
+def outer_kernel(one_ref, two_ref, got_one_ref, got_two_ref, send_one_ref, send_two_ref, outer_ref):
+    groups = send_one_ref.shape[0] // 2
+
+    def order(upper_ref, lower_ref):
+        for index, ref in enumerate((upper_ref, lower_ref)):
+            outer_ref[index] = jnp.swapaxes(ref[...], 0, 1)
+
+    def pack(send_first_ref, send_last_ref):
+        def store(place, first, last):
+            send_first_ref[place] = first
+            send_last_ref[place] = last
+
+        for index in range(2):
+            pack_rows(outer_ref[index], store, index * groups)
 
     either("row", order, one_ref, two_ref)
     either("col", pack, send_one_ref, send_two_ref)
@@ -192,34 +221,36 @@
             stack_ref[block, 2 * channels : 3 * channels, columns] = after
 
 
-def spread_all(own_of, outer_ref, one_ref, two_ref, stack_ref):
+def spread_all(own_of, outer_ref, one, two, stack_ref):
     count = stack_ref.shape[0] - 2
-    groups = one_ref.shape[0] // (count + 2)
-
-    def every(left_ref, right_ref):
+
+    def every(left, right):
+        (left_ref, own_left_ref, own_start), (right_ref, own_right_ref, _) = left, right
+        groups = DILATION // (stack_ref.shape[2] // DILATION // DILATION)
+        end = left_ref.shape[0] - groups
         spread(lambda row: rolled(outer_ref[0, row]), left_ref, right_ref, stack_ref, 0, 0)
 
         def body(block, carry):
             spread(
                 lambda row: own_of(block * DILATION + row),
-                left_ref, right_ref, stack_ref, block + 1, (block + 1) * groups,
+                own_left_ref, own_right_ref, stack_ref, block + 1, own_start + block * groups,
             )
             return carry
 
         lax.fori_loop(0, count, body, 0)
-        spread(lambda row: rolled(outer_ref[1, row]), left_ref, right_ref, stack_ref, count + 1, (count + 1) * groups)
-
-    either("col", every, one_ref, two_ref)
+        spread(lambda row: rolled(outer_ref[1, row]), left_ref, right_ref, stack_ref, count + 1, end)
+
+    either("col", every, one, two)
 
 
 def forward_kernel(
-    scale, own_ref, outer_ref, one_ref, two_ref, cotangent_ref, weight_ref, bias_ref,
+    scale, own_ref, outer_ref, one_ref, two_ref, own_one_ref, own_two_ref, cotangent_ref, weight_ref, bias_ref,
     activation_ref, grad_ref, send_one_ref, send_two_ref, rims_ref, terms_ref, stack_ref, sum_ref, taps_ref,
 ):
     height, channels, width = own_ref.shape[1:]
     count = height // DILATION
     groups = rims_ref.shape[1] // count
-    spread_all(lambda at: [own_ref[k, at] for k in range(3)], outer_ref, one_ref, two_ref, stack_ref)
+    spread_all(lambda at: [own_ref[k, at] for k in range(3)], outer_ref, (one_ref, own_one_ref, 0), (two_ref, own_two_ref, 0), stack_ref)
     taps_ref[...] = jnp.zeros_like(taps_ref)
     sum_ref[...] = jnp.zeros_like(sum_ref)
     depth = 9 * channels
@@ -268,7 +299,8 @@
 ):
     height, channels, width = own_ref.shape
     token_ref[...] = jnp.zeros_like(token_ref)
-    spread_all(lambda at: rolled(own_ref[at]), outer_ref, one_ref, two_ref, stack_ref)
+    start = one_ref.shape[0] // (height // DILATION + 2)
+    spread_all(lambda at: rolled(own_ref[at]), outer_ref, (one_ref, one_ref, start), (two_ref, two_ref, start), stack_ref)
 
     def body(block, carry):
         start = pl.multiple_of(block * DILATION, DILATION)
@@ -331,13 +363,17 @@
 
     one = swap_pairs(image_rim((1 - odd) * end, 0), "row", 0)
     two = swap_pairs(image_rim(odd * end, 1), "row", 1)
-    image_rows, cotangent_rows, rims = call(
-        own_kernel, (shape((3, *rows.shape), bf16), rows, own_rims), (image, cotangent)
-    )
+    own_packed = shape((own_groups, channels, width), bf16)
+    outer_packed = shape((all_groups - own_groups, channels, width), bf16)
+    image_rows, cotangent_rows, own_one, own_two = call(
+        own_kernel, (shape((3, *rows.shape), bf16), rows, own_packed, own_packed), (image, cotangent),
+        (pltpu.VMEM(own_rims.shape, bf16),),
+    )
+    own_one, own_two = swap_pairs(own_one, "col", 0), swap_pairs(own_two, "col", 1)
     forward_weight = jnp.transpose(weight, (2, 0, 1, 3)).reshape(channels, depth)
     backward_weight = jnp.transpose(weight[::-1, ::-1], (3, 0, 1, 2)).reshape(channels, depth)
     one, two, image_outer = call(
-        functools.partial(rim_kernel, True), (packed, packed, outer), (one, two, rims)
+        outer_kernel, (outer_packed, outer_packed, outer), (one, two, own_one, own_two)
     )
     two, one = swap_pairs(two, "col", 1), swap_pairs(one, "col", 0)
     activation, grads, one, two, rims, terms = call(
@@ -346,7 +382,7 @@
             shape(image.shape, bf16), rows, edge, edge, own_rims,
             shape((channels, -(-(depth + 1) // 128) * 128), f32),
         ),
-        (image_rows, image_outer, one, two, cotangent_rows, forward_weight, bias[:, None]),
+        (image_rows, image_outer, one, two, own_one, own_two, cotangent_rows, forward_weight, bias[:, None]),
         (stack, pltpu.VMEM((channels, width), f32), pltpu.VMEM((depth, channels), f32)),
         2 * flops,
     )

time: 41.6 us -> 43.1 us (1.036)
  starting transfers between devices: 17.3 us -> 20.8 us
  waiting for transfers between devices: 8.89 us -> 6.98 us
    ppermute x8 -> x10, starting transfers between devices: 10.1 us -> 13.1 us  [swap_pairs(): return lax.ppermute(value, ('row', 'col'), pairs)]
    ppermute x7, waiting for transfers between devices: 4.17 us -> 2.35 us  [add_pairs(): lax.ppermute(value, axis, [(at, at ^ mask) for at in range(lax.axis_size(...]
    ppermute x7, starting transfers between devices: 7.21 us -> 7.71 us  [add_pairs(): lax.ppermute(value, axis, [(at, at ^ mask) for at in range(lax.axis_size(...]
    ppermute x8 -> x10, waiting for transfers between devices: 4.72 us -> 4.64 us  [swap_pairs(): return lax.ppermute(value, ('row', 'col'), pairs)]
  transfers between devices with their start and end apart: 15 -> 17, of which waited for: 5 -> 6; matrix products, arithmetic and copies ran while one was open for 1% -> 1% of each run, Pallas kernels for 12% -> 12%
where the time goes in v15:
time: 43.1 us; the launch traced here: 42.9 us
  starting transfers between devices  20.8 us (48%)
  Pallas kernels  10.8 us (25%)
  waiting for transfers between devices  6.98 us (16%)
  local copies, waits for them, and re-layouts  2.44 us (6%)
  other arithmetic  1.04 us (2%)
  between operations  0.77 us (2%)
    ppermute x10, starting transfers between devices, swap_pairs(): return lax.ppermute(value, ('row', 'col'), pairs)  13.1 us
    pallas_call x6, Pallas kernels, call(): pl.pallas_call(kernel, out_shape=out_shapes, in_specs=[whole] * len(opera...  10.8 us
    ppermute x7, starting transfers between devices, add_pairs(): lax.ppermute(value, axis, [(at, at ^ mask) for at in range(lax.axis_size(...  7.71 us
    ppermute x10, waiting for transfers between devices, swap_pairs(): return lax.ppermute(value, ('row', 'col'), pairs)  4.64 us
    ppermute x7, waiting for transfers between devices, add_pairs(): lax.ppermute(value, axis, [(at, at ^ mask) for at in range(lax.axis_size(...  2.35 us
    unnamed x8, local copies, waits for them, and re-layouts  2.09 us
    select_n x1, other arithmetic, image_rim(): return rim if flag is None else jnp.where(flag, jnp.zeros_like(rim), rim)  1.01 us
  transfers between devices with their start and end apart: 17, of which 6 were waited for; matrix products, arithmetic and copies ran while one was open for 1% of the time, Pallas kernels for 12%

profile of v15, /device:TPU:0, one launch (start us, length us, event | category | flops | bytes accessed | tf_op | source)
XLA Modules:
  0.0 42.9 jit_solution(2926197206806258087)
XLA Ops:
  0.6 0.0 copy-start.2
  0.7 1.0 %dynamic-slice_select_fusion = (bf16[32,16,128]{2,1,0:T(8,128)(2,1)S(1)}, bf16[32,16,128]{2,1,0:T(8,128)(2,1)S(1)}) fusion(bf16[32,64,128]{2,1,0:T(8,128)(2,1)} %image_ref.1, s32[]{:T(128)S(6)} %select_n.24, pred[]{:T(512)S(6)} %or.3, s32[]{:T(128)S(6)} %select_n.22), kind=kLoop, calls=%fused_computation | loop fusion | flops 65536 | bytes 524297 | tf_op jit(solution)/shard_map/jit(_where)/select_n | solution.py:362
  1.7 3.0 %collective-permute-start = (bf16[32,16,128]{2,1,0:T(8,128)(2,1)S(1)}, bf16[32,16,128]{2,1,0:T(8,128)(2,1)S(1)}, u32[]{:S(2)}, u32[]{:S(2)}) collective-permute-start(bf16[32,16,128]{2,1,0:T(8,128)(2,1)S(1)} %get-tuple-element.45), channel_id=1, source_target_pairs={{0,4},{1,5},{2,6},{3,7},{4,0},{5,1},{6,2},{7,3},{8,12},{9,13},{10,... | collective-permute-start | bytes 393224 | tf_op jit(solution)/shard_map/ppermute | solution.py:48
  4.7 0.0 collective-permute-start.1
  4.7 1.0 %copy-done = bf16[32,64,128]{2,1,0:T(8,128)(2,1)S(1)} copy-done((bf16[32,64,128]{2,1,0:T(8,128)(2,1)S(1)}, bf16[32,64,128]{2,1,0:T(8,128)(2,1)}, u32[]{:S(2)}) %copy-start) | copy-done | bytes 524312
  5.8 1.0 %copy-done.1 = bf16[32,64,128]{2,1,0:T(8,128)(2,1)S(1)} copy-done((bf16[32,64,128]{2,1,0:T(8,128)(2,1)S(1)}, bf16[32,64,128]{2,1,0:T(8,128)(2,1)}, u32[]{:S(2)}) %copy-start.1) | copy-done | bytes 524312
  6.8 1.1 %shard_map.75 = (bf16[3,64,32,128]{3,2,1,0:T(8,128)(2,1)S(1)}, bf16[64,32,128]{2,1,0:T(8,128)(2,1)S(1)}, bf16[8,32,128]{2,1,0:T(8,128)(2,1)S(1)}, bf16[8,32,128]{2,1,0:T(8,128)(2,1)S(1)}) custom-call(bf16[32,64,128]{2,1,0:T(8,128)(2,1)S(1)} %copy-done, bf16[32,64,128]{2,1,0:T(8,128)(2,1)S(1)} %copy-done.1), custom_call_target="tpu_custom_call" | custom-call | bytes 3276800 | tf_op jit(solution)/shard_map/pallas_call | solution.py:328
  7.9 0.6 %collective-permute-start.2 = (bf16[8,32,128]{2,1,0:T(8,128)(2,1)S(1)}, bf16[8,32,128]{2,1,0:T(8,128)(2,1)S(1)}, u32[]{:S(2)}, u32[]{:S(2)}) collective-permute-start(bf16[8,32,128]{2,1,0:T(8,128)(2,1)S(1)} %get-tuple-element.25), channel_id=1, source_target_pairs={{0,1},{4,5},{8,9},{12,13},{16,17},{20,21},{24,25},{28,29},{1,0},{5... | collective-permute-start | bytes 196616 | tf_op jit(solution)/shard_map/ppermute | solution.py:48
  8.5 2.6 %collective-permute-start.3 = (bf16[8,32,128]{2,1,0:T(8,128)(2,1)S(1)}, bf16[8,32,128]{2,1,0:T(8,128)(2,1)S(1)}, u32[]{:S(2)}, u32[]{:S(2)}) collective-permute-start(bf16[8,32,128]{2,1,0:T(8,128)(2,1)S(1)} %get-tuple-element.26), channel_id=1, source_target_pairs={{0,4},{4,0},{8,12},{12,8},{16,20},{20,16},{24,28},{28,24},{1,2},{5... | collective-permute-start | bytes 196616 | tf_op jit(solution)/shard_map/ppermute | solution.py:48
  11.1 0.0 collective-permute-done.2.got_one_ref.own_one_ref
  11.1 2.2 %collective-permute-done.3.got_two_ref.own_two_ref = bf16[8,32,128]{2,1,0:T(8,128)(2,1)S(1)} collective-permute-done((bf16[8,32,128]{2,1,0:T(8,128)(2,1)S(1)}, bf16[8,32,128]{2,1,0:T(8,128)(2,1)S(1)}, u32[]{:S(2)}, u32[]{:S(2)}) %collective-permute-start.3) | collective-permute-done | bytes 65568 | tf_op jit(solution)/shard_map/ppermute | solution.py:48
  13.4 0.0 collective-permute-done.one_ref
  13.4 0.0 collective-permute-done.1.two_ref
  13.4 0.3 shard_map.76
  13.7 0.1 collective-permute-start.4
  13.8 2.1 %collective-permute-start.5 = (bf16[4,32,128]{2,1,0:T(8,128)(2,1)S(1)}, bf16[4,32,128]{2,1,0:T(8,128)(2,1)S(1)}, u32[]{:S(2)}, u32[]{:S(2)}) collective-permute-start(bf16[4,32,128]{2,1,0:T(8,128)(2,1)S(1)} %get-tuple-element.29), channel_id=1, source_target_pairs={{0,4},{4,0},{8,12},{12,8},{16,20},{20,16},{24,28},{28,24},{1,2},{5... | collective-permute-start | bytes 98312 | tf_op jit(solution)/shard_map/ppermute | solution.py:48
  15.9 0.1 copy.11
  15.9 0.1 reshape.17.weight_ref
  16.1 0.1 copy.12.bias_ref
  16.1 0.0 collective-permute-done.4.one_ref
  16.2 1.6 %collective-permute-done.5.two_ref = bf16[4,32,128]{2,1,0:T(8,128)(2,1)S(1)} collective-permute-done((bf16[4,32,128]{2,1,0:T(8,128)(2,1)S(1)}, bf16[4,32,128]{2,1,0:T(8,128)(2,1)S(1)}, u32[]{:S(2)}, u32[]{:S(2)}) %collective-permute-start.5) | collective-permute-done | bytes 32800 | tf_op jit(solution)/shard_map/ppermute | solution.py:48
  17.8 4.8 %shard_map.77 = (bf16[32,64,128]{2,1,0:T(8,128)(2,1)}, bf16[64,32,128]{2,1,0:T(8,128)(2,1)S(1)}, bf16[16,32,128]{2,1,0:T(8,128)(2,1)S(1)}, bf16[16,32,128]{2,1,0...) custom-call(bf16[3,64,32,128]{3,2,1,0:T(8,128)(2,1)S(1)} %get-tuple-element.24.own_ref, ...), custom_call_target="tpu_custom_call" | custom-call | flops 301989888 | bytes 4065408 | tf_op jit(solution)/shard_map/pallas_call | solution.py:328
  22.6 0.1 collective-permute-start.10
  22.7 0.4 collective-permute-start.11
  23.1 1.4 %collective-permute-start.12 = (f32[32,384]{1,0:T(8,128)S(1)}, f32[32,384]{1,0:T(8,128)S(1)}, u32[]{:S(2)}, u32[]{:S(2)}) collective-permute-start(f32[32,384]{1,0:T(8,128)S(1)} %get-tuple-element.40), channel_id=1, source_target_pairs={{0,3},{1,2},{2,1},{3,0},{4,7},{5,6},{6,5},{7,4},{8,11},{9,10},{10,... | collective-permute-start | bytes 147464 | tf_op jit(solution)/shard_map/ppermute | solution.py:62
  24.5 2.0 %collective-permute-start.6 = (bf16[16,32,128]{2,1,0:T(8,128)(2,1)S(1)}, bf16[16,32,128]{2,1,0:T(8,128)(2,1)S(1)}, u32[]{:S(2)}, u32[]{:S(2)}) collective-permute-start(bf16[16,32,128]{2,1,0:T(8,128)(2,1)S(1)} %get-tuple-element.33), channel_id=1, source_target_pairs={{0,4},{1,5},{2,6},{3,7},{4,0},{5,1},{6,2},{7,3},{8,12},{9,13},{10,... | collective-permute-start | bytes 393224 | tf_op jit(solution)/shard_map/ppermute | solution.py:48
  26.5 0.1 collective-permute-start.7
  26.6 0.0 collective-permute-done.10
  26.6 0.7 %collective-permute-done.11 = f32[32,384]{1,0:T(8,128)S(1)} collective-permute-done((f32[32,384]{1,0:T(8,128)S(1)}, f32[32,384]{1,0:T(8,128)S(1)}, u32[]{:S(2)}, u32[]{:S(2)}) %collective-permute-start.11) | collective-permute-done | bytes 49184 | tf_op jit(solution)/shard_map/ppermute | solution.py:62
  27.3 0.1 collective-permute-done.12
  27.4 1.6 %collective-permute-start.13 = (f32[32,384]{1,0:T(8,128)S(1)}, f32[32,384]{1,0:T(8,128)S(1)}, u32[]{:S(2)}, u32[]{:S(2)}) collective-permute-start(f32[32,384]{1,0:T(8,128)S(1)} %add_add_fusion.1), channel_id=1, source_target_pairs={{0,8},{4,12},{8,0},{12,4},{16,24},{20,28},{24,16},{28,20},{1,9},{5... | collective-permute-start | bytes 147464 | tf_op jit(solution)/shard_map/ppermute | solution.py:62
  29.0 2.0 %collective-permute-start.14 = (f32[32,384]{1,0:T(8,128)S(1)}, f32[32,384]{1,0:T(8,128)S(1)}, u32[]{:S(2)}, u32[]{:S(2)}) collective-permute-start(f32[32,384]{1,0:T(8,128)S(1)} %add_add_fusion.1), channel_id=1, source_target_pairs={{0,16},{4,20},{8,24},{12,28},{16,0},{20,4},{24,8},{28,12},{1,17},{... | collective-permute-start | bytes 147464 | tf_op jit(solution)/shard_map/ppermute | solution.py:62
  31.0 0.9 %collective-permute-start.15 = (f32[32,384]{1,0:T(8,128)S(1)}, f32[32,384]{1,0:T(8,128)S(1)}, u32[]{:S(2)}, u32[]{:S(2)}) collective-permute-start(f32[32,384]{1,0:T(8,128)S(1)} %add_add_fusion.1), channel_id=1, source_target_pairs={{0,24},{4,28},{8,16},{12,20},{16,8},{20,12},{24,0},{28,4},{1,25},{... | collective-permute-start | bytes 147464 | tf_op jit(solution)/shard_map/ppermute | solution.py:62
  31.8 0.8 %collective-permute-done.6.one_ref = bf16[16,32,128]{2,1,0:T(8,128)(2,1)S(1)} collective-permute-done((bf16[16,32,128]{2,1,0:T(8,128)(2,1)S(1)}, bf16[16,32,128]{2,1,0:T(8,128)(2,1)S(1)}, u32[]{:S(2)}, u32[]{:S(2)}) %collective-permute-start.6) | collective-permute-done | bytes 131104 | tf_op jit(solution)/shard_map/ppermute | solution.py:48
  32.6 0.0 collective-permute-done.7.two_ref
  32.6 0.2 shard_map.78
  32.8 0.1 collective-permute-start.8
  32.9 2.6 %collective-permute-start.9 = (bf16[12,32,128]{2,1,0:T(8,128)(2,1)S(1)}, bf16[12,32,128]{2,1,0:T(8,128)(2,1)S(1)}, u32[]{:S(2)}, u32[]{:S(2)}) collective-permute-start(bf16[12,32,128]{2,1,0:T(8,128)(2,1)S(1)} %get-tuple-element.38), channel_id=1, source_target_pairs={{0,4},{4,0},{8,12},{12,8},{16,20},{20,16},{24,28},{28,24},{1,2},{5... | collective-permute-start | bytes 294920 | tf_op jit(solution)/shard_map/ppermute | solution.py:48
  35.5 0.0 collective-permute-done.13
  35.5 0.0 collective-permute-done.14
  35.5 1.6 %collective-permute-done.15 = f32[32,384]{1,0:T(8,128)S(1)} collective-permute-done((f32[32,384]{1,0:T(8,128)S(1)}, f32[32,384]{1,0:T(8,128)S(1)}, u32[]{:S(2)}, u32[]{:S(2)}) %collective-permute-start.15) | collective-permute-done | bytes 49184 | tf_op jit(solution)/shard_map/ppermute | solution.py:62
  37.1 1.4 %collective-permute-start.16 = (f32[32,384]{1,0:T(8,128)S(1)}, f32[32,384]{1,0:T(8,128)S(1)}, u32[]{:S(2)}, u32[]{:S(2)}) collective-permute-start(f32[32,384]{1,0:T(8,128)S(1)} %add_add_fusion.one_ref), channel_id=1, source_target_pairs={{0,4},{4,0},{8,12},{12,8},{16,20},{20,16},{24,28},{28,24},{1,5},{5... | collective-permute-start | bytes 147464 | tf_op jit(solution)/shard_map/ppermute | solution.py:62
  38.4 0.1 copy.14.weight_ref
  38.5 0.0 collective-permute-done.8.one_ref
  38.5 0.0 collective-permute-done.9.two_ref
  38.5 3.6 %shard_map.79 = (bf16[32,64,128]{2,1,0:T(8,128)(2,1)}, f32[8,128]{1,0:T(8,128)S(1)}) custom-call(bf16[64,32,128]{2,1,0:T(8,128)(2,1)S(1)} %get-tuple-element.32.own_ref, bf16[2,16,32,128]{3,2,1,0:T(8,128)(2,1)S(1)} %get-tuple-element.36.outer_ref, bf16[12,32,128]{2,1,0:T(8,128)(2,1)S(1)} %collective-permute-done.8.one_ref, ...), custom_call_target="tpu_custom_call" | custom-call | flops 150994944 | bytes 1529856 | tf_op jit(solution)/shard_map/pallas_call | solution.py:328
  42.1 0.0 collective-permute-done.16.other_ref
  42.1 0.8 %shard_map.80 = (f32[3,3,32,32]{3,2,1,0:T(8,128)}, f32[1,32]{1,0:T(1,128)}) custom-call(f32[32,384]{1,0:T(8,128)S(1)} %add_add_fusion.one_ref, f32[32,384]{1,0:T(8,128)S(1)} %collective-permute-done.16.other_ref, f32[8,128]{1,0:T(8,128)S(1)} %get-tuple-element.41.after_ref), custom_call_target="tpu_custom_call" | custom-call | bytes 139392 | tf_op jit(solution)/shard_map/pallas_call | solution.py:328
  (8 shorter events, 0.0 us)
Async XLA Ops:
  0.6 15.2 %copy-start.2 = (bf16[3,3,32,32]{3,2,1,0:T(8,128)(2,1)S(1)}, bf16[3,3,32,32]{3,2,1,0:T(8,128)(2,1)}, u32[]{:S(2)}) copy-start(bf16[3,3,32,32]{3,2,1,0:T(8,128)(2,1)} %param.5) | copy-start | bytes 55300
  0.6 15.4 %copy-start.3 = (f32[32]{0:T(128)S(1)}, f32[32]{0:T(128)}, u32[]{:S(2)}) copy-start(f32[32]{0:T(128)} %param.6) | copy-start | bytes 388
  1.7 11.7 %collective-permute-start = (bf16[32,16,128]{2,1,0:T(8,128)(2,1)S(1)}, bf16[32,16,128]{2,1,0:T(8,128)(2,1)S(1)}, u32[]{:S(2)}, u32[]{:S(2)}) collective-permute-start(bf16[32,16,128]{2,1,0:T(8,128)(2,1)S(1)} %get-tuple-element.45), channel_id=1, source_target_pairs={{0,4},{1,5},{2,6},{3,7},{4,0},{5,1},{6,2},{7,3},{8,12},{9,13},{10,... | collective-permute-start | bytes 393224 | tf_op jit(solution)/shard_map/ppermute | solution.py:48
  4.7 8.6 %collective-permute-start.1 = (bf16[32,16,128]{2,1,0:T(8,128)(2,1)S(1)}, bf16[32,16,128]{2,1,0:T(8,128)(2,1)S(1)}, u32[]{:S(2)}, u32[]{:S(2)}) collective-permute-start(bf16[32,16,128]{2,1,0:T(8,128)(2,1)S(1)} %get-tuple-element.44), channel_id=1, source_target_pairs={{0,1},{1,0},{2,3},{3,2},{4,8},{5,9},{6,10},{7,11},{8,4},{9,5},{10,... | collective-permute-start | bytes 393224 | tf_op jit(solution)/shard_map/ppermute | solution.py:48
  4.7 1.0 %copy-start = (bf16[32,64,128]{2,1,0:T(8,128)(2,1)S(1)}, bf16[32,64,128]{2,1,0:T(8,128)(2,1)}, u32[]{:S(2)}) copy-start(bf16[32,64,128]{2,1,0:T(8,128)(2,1)} %image_ref.1) | copy-start | bytes 1572868
  5.8 1.0 %copy-start.1 = (bf16[32,64,128]{2,1,0:T(8,128)(2,1)S(1)}, bf16[32,64,128]{2,1,0:T(8,128)(2,1)}, u32[]{:S(2)}) copy-start(bf16[32,64,128]{2,1,0:T(8,128)(2,1)} %cotangent_ref.1) | copy-start | bytes 1572868
  7.9 3.2 %collective-permute-start.2 = (bf16[8,32,128]{2,1,0:T(8,128)(2,1)S(1)}, bf16[8,32,128]{2,1,0:T(8,128)(2,1)S(1)}, u32[]{:S(2)}, u32[]{:S(2)}) collective-permute-start(bf16[8,32,128]{2,1,0:T(8,128)(2,1)S(1)} %get-tuple-element.25), channel_id=1, source_target_pairs={{0,1},{4,5},{8,9},{12,13},{16,17},{20,21},{24,25},{28,29},{1,0},{5... | collective-permute-start | bytes 196616 | tf_op jit(solution)/shard_map/ppermute | solution.py:48
  8.5 4.9 %collective-permute-start.3 = (bf16[8,32,128]{2,1,0:T(8,128)(2,1)S(1)}, bf16[8,32,128]{2,1,0:T(8,128)(2,1)S(1)}, u32[]{:S(2)}, u32[]{:S(2)}) collective-permute-start(bf16[8,32,128]{2,1,0:T(8,128)(2,1)S(1)} %get-tuple-element.26), channel_id=1, source_target_pairs={{0,4},{4,0},{8,12},{12,8},{16,20},{20,16},{24,28},{28,24},{1,2},{5... | collective-permute-start | bytes 196616 | tf_op jit(solution)/shard_map/ppermute | solution.py:48
  13.7 2.5 %collective-permute-start.4 = (bf16[4,32,128]{2,1,0:T(8,128)(2,1)S(1)}, bf16[4,32,128]{2,1,0:T(8,128)(2,1)S(1)}, u32[]{:S(2)}, u32[]{:S(2)}) collective-permute-start(bf16[4,32,128]{2,1,0:T(8,128)(2,1)S(1)} %get-tuple-element.28), channel_id=1, source_target_pairs={{0,1},{4,5},{8,9},{12,13},{16,17},{20,21},{24,25},{28,29},{1,0},{5... | collective-permute-start | bytes 98312 | tf_op jit(solution)/shard_map/ppermute | solution.py:48
  13.8 4.0 %collective-permute-start.5 = (bf16[4,32,128]{2,1,0:T(8,128)(2,1)S(1)}, bf16[4,32,128]{2,1,0:T(8,128)(2,1)S(1)}, u32[]{:S(2)}, u32[]{:S(2)}) collective-permute-start(bf16[4,32,128]{2,1,0:T(8,128)(2,1)S(1)} %get-tuple-element.29), channel_id=1, source_target_pairs={{0,4},{4,0},{8,12},{12,8},{16,20},{20,16},{24,28},{28,24},{1,2},{5... | collective-permute-start | bytes 98312 | tf_op jit(solution)/shard_map/ppermute | solution.py:48
  22.6 4.0 %collective-permute-start.10 = (f32[32,384]{1,0:T(8,128)S(1)}, f32[32,384]{1,0:T(8,128)S(1)}, u32[]{:S(2)}, u32[]{:S(2)}) collective-permute-start(f32[32,384]{1,0:T(8,128)S(1)} %get-tuple-element.40), channel_id=1, source_target_pairs={{0,1},{1,0},{2,3},{3,2},{4,5},{5,4},{6,7},{7,6},{8,9},{9,8},{10,11... | collective-permute-start | bytes 147464 | tf_op jit(solution)/shard_map/ppermute | solution.py:62
  22.7 4.5 %collective-permute-start.11 = (f32[32,384]{1,0:T(8,128)S(1)}, f32[32,384]{1,0:T(8,128)S(1)}, u32[]{:S(2)}, u32[]{:S(2)}) collective-permute-start(f32[32,384]{1,0:T(8,128)S(1)} %get-tuple-element.40), channel_id=1, source_target_pairs={{0,2},{1,3},{2,0},{3,1},{4,6},{5,7},{6,4},{7,5},{8,10},{9,11},{10,... | collective-permute-start | bytes 147464 | tf_op jit(solution)/shard_map/ppermute | solution.py:62
  23.1 4.3 %collective-permute-start.12 = (f32[32,384]{1,0:T(8,128)S(1)}, f32[32,384]{1,0:T(8,128)S(1)}, u32[]{:S(2)}, u32[]{:S(2)}) collective-permute-start(f32[32,384]{1,0:T(8,128)S(1)} %get-tuple-element.40), channel_id=1, source_target_pairs={{0,3},{1,2},{2,1},{3,0},{4,7},{5,6},{6,5},{7,4},{8,11},{9,10},{10,... | collective-permute-start | bytes 147464 | tf_op jit(solution)/shard_map/ppermute | solution.py:62
  24.5 8.1 %collective-permute-start.6 = (bf16[16,32,128]{2,1,0:T(8,128)(2,1)S(1)}, bf16[16,32,128]{2,1,0:T(8,128)(2,1)S(1)}, u32[]{:S(2)}, u32[]{:S(2)}) collective-permute-start(bf16[16,32,128]{2,1,0:T(8,128)(2,1)S(1)} %get-tuple-element.33), channel_id=1, source_target_pairs={{0,4},{1,5},{2,6},{3,7},{4,0},{5,1},{6,2},{7,3},{8,12},{9,13},{10,... | collective-permute-start | bytes 393224 | tf_op jit(solution)/shard_map/ppermute | solution.py:48
  26.5 6.1 %collective-permute-start.7 = (bf16[16,32,128]{2,1,0:T(8,128)(2,1)S(1)}, bf16[16,32,128]{2,1,0:T(8,128)(2,1)S(1)}, u32[]{:S(2)}, u32[]{:S(2)}) collective-permute-start(bf16[16,32,128]{2,1,0:T(8,128)(2,1)S(1)} %get-tuple-element.34), channel_id=1, source_target_pairs={{0,1},{1,0},{2,3},{3,2},{4,8},{5,9},{6,10},{7,11},{8,4},{9,5},{10,... | collective-permute-start | bytes 393224 | tf_op jit(solution)/shard_map/ppermute | solution.py:48
  27.4 8.1 %collective-permute-start.13 = (f32[32,384]{1,0:T(8,128)S(1)}, f32[32,384]{1,0:T(8,128)S(1)}, u32[]{:S(2)}, u32[]{:S(2)}) collective-permute-start(f32[32,384]{1,0:T(8,128)S(1)} %add_add_fusion.1), channel_id=1, source_target_pairs={{0,8},{4,12},{8,0},{12,4},{16,24},{20,28},{24,16},{28,20},{1,9},{5... | collective-permute-start | bytes 147464 | tf_op jit(solution)/shard_map/ppermute | solution.py:62
  29.0 6.5 %collective-permute-start.14 = (f32[32,384]{1,0:T(8,128)S(1)}, f32[32,384]{1,0:T(8,128)S(1)}, u32[]{:S(2)}, u32[]{:S(2)}) collective-permute-start(f32[32,384]{1,0:T(8,128)S(1)} %add_add_fusion.1), channel_id=1, source_target_pairs={{0,16},{4,20},{8,24},{12,28},{16,0},{20,4},{24,8},{28,12},{1,17},{... | collective-permute-start | bytes 147464 | tf_op jit(solution)/shard_map/ppermute | solution.py:62
  31.0 6.1 %collective-permute-start.15 = (f32[32,384]{1,0:T(8,128)S(1)}, f32[32,384]{1,0:T(8,128)S(1)}, u32[]{:S(2)}, u32[]{:S(2)}) collective-permute-start(f32[32,384]{1,0:T(8,128)S(1)} %add_add_fusion.1), channel_id=1, source_target_pairs={{0,24},{4,28},{8,16},{12,20},{16,8},{20,12},{24,0},{28,4},{1,25},{... | collective-permute-start | bytes 147464 | tf_op jit(solution)/shard_map/ppermute | solution.py:62
  32.8 5.7 %collective-permute-start.8 = (bf16[12,32,128]{2,1,0:T(8,128)(2,1)S(1)}, bf16[12,32,128]{2,1,0:T(8,128)(2,1)S(1)}, u32[]{:S(2)}, u32[]{:S(2)}) collective-permute-start(bf16[12,32,128]{2,1,0:T(8,128)(2,1)S(1)} %get-tuple-element.37), channel_id=1, source_target_pairs={{0,1},{4,5},{8,9},{12,13},{16,17},{20,21},{24,25},{28,29},{1,0},{5... | collective-permute-start | bytes 294920 | tf_op jit(solution)/shard_map/ppermute | solution.py:48
  32.9 5.6 %collective-permute-start.9 = (bf16[12,32,128]{2,1,0:T(8,128)(2,1)S(1)}, bf16[12,32,128]{2,1,0:T(8,128)(2,1)S(1)}, u32[]{:S(2)}, u32[]{:S(2)}) collective-permute-start(bf16[12,32,128]{2,1,0:T(8,128)(2,1)S(1)} %get-tuple-element.38), channel_id=1, source_target_pairs={{0,4},{4,0},{8,12},{12,8},{16,20},{20,16},{24,28},{28,24},{1,2},{5... | collective-permute-start | bytes 294920 | tf_op jit(solution)/shard_map/ppermute | solution.py:48
  37.1 5.1 %collective-permute-start.16 = (f32[32,384]{1,0:T(8,128)S(1)}, f32[32,384]{1,0:T(8,128)S(1)}, u32[]{:S(2)}, u32[]{:S(2)}) collective-permute-start(f32[32,384]{1,0:T(8,128)S(1)} %add_add_fusion.one_ref), channel_id=1, source_target_pairs={{0,4},{4,0},{8,12},{12,8},{16,20},{20,16},{24,28},{28,24},{1,5},{5... | collective-permute-start | bytes 147464 | tf_op jit(solution)/shard_map/ppermute | solution.py:62

commit v16 on v14

--- a/solution.py
+++ b/solution.py
@@ -213,8 +213,8 @@
 
 
 def forward_kernel(
-    scale, own_ref, outer_ref, one_ref, two_ref, cotangent_ref, weight_ref, bias_ref,
-    activation_ref, grad_ref, send_one_ref, send_two_ref, rims_ref, terms_ref, stack_ref, sum_ref, taps_ref,
+    own_ref, outer_ref, one_ref, two_ref, cotangent_ref, weight_ref, bias_ref,
+    activation_ref, grad_ref, send_one_ref, send_two_ref, rims_ref, taps_ref, sum_ref, stack_ref,
 ):
     height, channels, width = own_ref.shape[1:]
     count = height // DILATION
@@ -258,6 +258,10 @@
     send_two_ref[...] = grad_ref[pl.ds(odd * end, DILATION)]
     clear_if(alone("row", 0), send_one_ref)
     clear_if(alone("row", 1), send_two_ref)
+
+
+def terms_kernel(scale, taps_ref, sum_ref, terms_ref):
+    channels, depth = sum_ref.shape[0], taps_ref.shape[0]
     terms_ref[:, :depth] = jnp.transpose(taps_ref[...]) * scale
     sums = jnp.sum(sum_ref[...], axis=1, keepdims=True) * scale
     terms_ref[:, depth:] = jnp.broadcast_to(sums, (channels, terms_ref.shape[1] - depth))
@@ -340,15 +344,20 @@
         functools.partial(rim_kernel, True), (packed, packed, outer), (one, two, rims)
     )
     two, one = swap_pairs(two, "col", 1), swap_pairs(one, "col", 0)
-    activation, grads, one, two, rims, terms = call(
-        functools.partial(forward_kernel, scale),
+    activation, grads, one, two, rims, taps, sums = call(
+        forward_kernel,
         (
             shape(image.shape, bf16), rows, edge, edge, own_rims,
-            shape((channels, -(-(depth + 1) // 128) * 128), f32),
+            shape((depth, channels), f32), shape((channels, width), f32),
         ),
         (image_rows, image_outer, one, two, cotangent_rows, forward_weight, bias[:, None]),
-        (stack, pltpu.VMEM((channels, width), f32), pltpu.VMEM((depth, channels), f32)),
+        (stack,),
         2 * flops,
+    )
+    (terms,) = call(
+        functools.partial(terms_kernel, scale),
+        (shape((channels, -(-(depth + 1) // 128) * 128), f32),),
+        (taps, sums),
     )
     one, two = swap_pairs(one, "row", 0), swap_pairs(two, "row", 1)
     one, two, grad_outer = call(

time: 41.6 us -> 41.7 us (level)
    pallas_call x6 -> x7, Pallas kernels: 10.8 us -> 10.9 us  [call(): pl.pallas_call(kernel, out_shape=out_shapes, in_specs=[whole] * len(opera...]
where the time goes in v16:
time: 41.7 us; the launch traced here: 41.5 us
  starting transfers between devices  17.4 us (42%)
  Pallas kernels  10.9 us (26%)
  waiting for transfers between devices  8.89 us (21%)
  local copies, waits for them, and re-layouts  2.44 us (6%)
  other arithmetic  1.04 us (2%)
  between operations  0.78 us (2%)
    pallas_call x7, Pallas kernels, call(): pl.pallas_call(kernel, out_shape=out_shapes, in_specs=[whole] * len(opera...  10.9 us
    ppermute x8, starting transfers between devices, swap_pairs(): return lax.ppermute(value, ('row', 'col'), pairs)  10.1 us
    ppermute x7, starting transfers between devices, add_pairs(): lax.ppermute(value, axis, [(at, at ^ mask) for at in range(lax.axis_size(...  7.27 us
    ppermute x8, waiting for transfers between devices, swap_pairs(): return lax.ppermute(value, ('row', 'col'), pairs)  4.72 us
    ppermute x7, waiting for transfers between devices, add_pairs(): lax.ppermute(value, axis, [(at, at ^ mask) for at in range(lax.axis_size(...  4.17 us
    unnamed x8, local copies, waits for them, and re-layouts  2.09 us
    select_n x1, other arithmetic, image_rim(): return rim if flag is None else jnp.where(flag, jnp.zeros_like(rim), rim)  1.01 us
  transfers between devices with their start and end apart: 15, of which 5 were waited for; matrix products, arithmetic and copies ran while one was open for 1% of the time, Pallas kernels for 12%

profile of v16, /device:TPU:0, one launch (start us, length us, event | category | flops | bytes accessed | tf_op | source)
XLA Modules:
  0.0 41.5 jit_solution(15481730030096622487)
XLA Ops:
  0.6 0.0 copy-start.2
  0.6 0.0 copy-start.3
  0.7 1.0 %dynamic-slice_select_fusion = (bf16[32,16,128]{2,1,0:T(8,128)(2,1)S(1)}, bf16[32,16,128]{2,1,0:T(8,128)(2,1)S(1)}) fusion(bf16[32,64,128]{2,1,0:T(8,128)(2,1)} %image_ref.1, s32[]{:T(128)S(6)} %select_n.24, pred[]{:T(512)S(6)} %or.3, s32[]{:T(128)S(6)} %select_n.22), kind=kLoop, calls=%fused_computation | loop fusion | flops 65536 | bytes 524297 | tf_op jit(solution)/shard_map/jit(_where)/select_n | solution.py:334
  1.7 3.0 %collective-permute-start = (bf16[32,16,128]{2,1,0:T(8,128)(2,1)S(1)}, bf16[32,16,128]{2,1,0:T(8,128)(2,1)S(1)}, u32[]{:S(2)}, u32[]{:S(2)}) collective-permute-start(bf16[32,16,128]{2,1,0:T(8,128)(2,1)S(1)} %get-tuple-element.45), channel_id=1, source_target_pairs={{0,4},{1,5},{2,6},{3,7},{4,0},{5,1},{6,2},{7,3},{8,12},{9,13},{10,... | collective-permute-start | bytes 393224 | tf_op jit(solution)/shard_map/ppermute | solution.py:48
  4.7 0.0 collective-permute-start.1
  4.7 1.0 %copy-done = bf16[32,64,128]{2,1,0:T(8,128)(2,1)S(1)} copy-done((bf16[32,64,128]{2,1,0:T(8,128)(2,1)S(1)}, bf16[32,64,128]{2,1,0:T(8,128)(2,1)}, u32[]{:S(2)}) %copy-start) | copy-done | bytes 524312
  5.8 1.0 %copy-done.1 = bf16[32,64,128]{2,1,0:T(8,128)(2,1)S(1)} copy-done((bf16[32,64,128]{2,1,0:T(8,128)(2,1)S(1)}, bf16[32,64,128]{2,1,0:T(8,128)(2,1)}, u32[]{:S(2)}) %copy-start.1) | copy-done | bytes 524312
  6.8 1.1 %shard_map.75 = (bf16[3,64,32,128]{3,2,1,0:T(8,128)(2,1)S(1)}, bf16[64,32,128]{2,1,0:T(8,128)(2,1)S(1)}, bf16[2,8,32,128]{3,2,1,0:T(8,128)(2,1)S(1)}) custom-call(bf16[32,64,128]{2,1,0:T(8,128)(2,1)S(1)} %copy-done, bf16[32,64,128]{2,1,0:T(8,128)(2,1)S(1)} %copy-done.1), custom_call_target="tpu_custom_call" | custom-call | bytes 3276800 | tf_op jit(solution)/shard_map/pallas_call | solution.py:300
  7.9 2.4 %collective-permute-done.one_ref = bf16[32,16,128]{2,1,0:T(8,128)(2,1)S(1)} collective-permute-done((bf16[32,16,128]{2,1,0:T(8,128)(2,1)S(1)}, bf16[32,16,128]{2,1,0:T(8,128)(2,1)S(1)}, u32[]{:S(2)}, u32[]{:S(2)}) %collective-permute-start) | collective-permute-done | bytes 131104 | tf_op jit(solution)/shard_map/ppermute | solution.py:48
  10.3 0.0 collective-permute-done.1.two_ref
  10.3 0.3 shard_map.76
  10.6 0.1 collective-permute-start.2
  10.7 2.6 %collective-permute-start.3 = (bf16[12,32,128]{2,1,0:T(8,128)(2,1)S(1)}, bf16[12,32,128]{2,1,0:T(8,128)(2,1)S(1)}, u32[]{:S(2)}, u32[]{:S(2)}) collective-permute-start(bf16[12,32,128]{2,1,0:T(8,128)(2,1)S(1)} %get-tuple-element.28), channel_id=1, source_target_pairs={{0,4},{4,0},{8,12},{12,8},{16,20},{20,16},{24,28},{28,24},{1,2},{5... | collective-permute-start | bytes 294920 | tf_op jit(solution)/shard_map/ppermute | solution.py:48
  13.2 0.0 copy-done.2
  13.2 0.1 copy.11
  13.3 0.1 reshape.17.weight_ref
  13.4 0.0 copy-done.3
  13.4 0.1 copy.12.bias_ref
  13.5 0.0 collective-permute-done.2.one_ref
  13.5 2.3 %collective-permute-done.3.two_ref = bf16[12,32,128]{2,1,0:T(8,128)(2,1)S(1)} collective-permute-done((bf16[12,32,128]{2,1,0:T(8,128)(2,1)S(1)}, bf16[12,32,128]{2,1,0:T(8,128)(2,1)S(1)}, u32[]{:S(2)}, u32[]{:S(2)}) %collective-permute-start.3) | collective-permute-done | bytes 98336 | tf_op jit(solution)/shard_map/ppermute | solution.py:48
  15.8 4.8 %shard_map.77 = (bf16[32,64,128]{2,1,0:T(8,128)(2,1)}, bf16[64,32,128]{2,1,0:T(8,128)(2,1)S(1)}, bf16[16,32,128]{2,1,0:T(8,128)(2,1)S(1)}, bf16[16,32,128]{2,1,0...) custom-call(bf16[3,64,32,128]{3,2,1,0:T(8,128)(2,1)S(1)} %get-tuple-element.24, ...), custom_call_target="tpu_custom_call" | custom-call | flops 301989888 | bytes 4069504 | tf_op jit(solution)/shard_map/pallas_call | solution.py:300
  20.7 0.1 shard_map.80
  20.8 0.7 %collective-permute-start.10 = (f32[32,384]{1,0:T(8,128)S(1)}, f32[32,384]{1,0:T(8,128)S(1)}, u32[]{:S(2)}, u32[]{:S(2)}) collective-permute-start(f32[32,384]{1,0:T(8,128)S(1)} %shard_map.80), channel_id=1, source_target_pairs={{0,3},{1,2},{2,1},{3,0},{4,7},{5,6},{6,5},{7,4},{8,11},{9,10},{10,... | collective-permute-start | bytes 147464 | tf_op jit(solution)/shard_map/ppermute | solution.py:62
  21.5 0.0 collective-permute-start.8
  21.5 1.5 %collective-permute-start.9 = (f32[32,384]{1,0:T(8,128)S(1)}, f32[32,384]{1,0:T(8,128)S(1)}, u32[]{:S(2)}, u32[]{:S(2)}) collective-permute-start(f32[32,384]{1,0:T(8,128)S(1)} %shard_map.80), channel_id=1, source_target_pairs={{0,2},{1,3},{2,0},{3,1},{4,6},{5,7},{6,4},{7,5},{8,10},{9,11},{10,... | collective-permute-start | bytes 147464 | tf_op jit(solution)/shard_map/ppermute | solution.py:62
  23.0 2.0 %collective-permute-start.4 = (bf16[16,32,128]{2,1,0:T(8,128)(2,1)S(1)}, bf16[16,32,128]{2,1,0:T(8,128)(2,1)S(1)}, u32[]{:S(2)}, u32[]{:S(2)}) collective-permute-start(bf16[16,32,128]{2,1,0:T(8,128)(2,1)S(1)} %get-tuple-element.32), channel_id=1, source_target_pairs={{0,4},{1,5},{2,6},{3,7},{4,0},{5,1},{6,2},{7,3},{8,12},{9,13},{10,... | collective-permute-start | bytes 393224 | tf_op jit(solution)/shard_map/ppermute | solution.py:48
  25.0 0.0 collective-permute-start.5
  25.0 0.0 collective-permute-done.10
  25.0 0.0 collective-permute-done.8
  25.0 0.8 %collective-permute-done.9 = f32[32,384]{1,0:T(8,128)S(1)} collective-permute-done((f32[32,384]{1,0:T(8,128)S(1)}, f32[32,384]{1,0:T(8,128)S(1)}, u32[]{:S(2)}, u32[]{:S(2)}) %collective-permute-start.9) | collective-permute-done | bytes 49184 | tf_op jit(solution)/shard_map/ppermute | solution.py:62
  25.8 2.3 %collective-permute-start.11 = (f32[32,384]{1,0:T(8,128)S(1)}, f32[32,384]{1,0:T(8,128)S(1)}, u32[]{:S(2)}, u32[]{:S(2)}) collective-permute-start(f32[32,384]{1,0:T(8,128)S(1)} %add_add_fusion.1), channel_id=1, source_target_pairs={{0,8},{4,12},{8,0},{12,4},{16,24},{20,28},{24,16},{28,20},{1,9},{5... | collective-permute-start | bytes 147464 | tf_op jit(solution)/shard_map/ppermute | solution.py:62
  28.1 2.6 %collective-permute-start.12 = (f32[32,384]{1,0:T(8,128)S(1)}, f32[32,384]{1,0:T(8,128)S(1)}, u32[]{:S(2)}, u32[]{:S(2)}) collective-permute-start(f32[32,384]{1,0:T(8,128)S(1)} %add_add_fusion.1), channel_id=1, source_target_pairs={{0,16},{4,20},{8,24},{12,28},{16,0},{20,4},{24,8},{28,12},{1,17},{... | collective-permute-start | bytes 147464 | tf_op jit(solution)/shard_map/ppermute | solution.py:62
  30.7 0.0 collective-permute-start.13
  30.7 0.0 collective-permute-done.4.one_ref
  30.7 0.0 collective-permute-done.5.two_ref
  30.7 0.3 shard_map.78
  31.0 0.1 collective-permute-start.6
  31.0 2.4 %collective-permute-start.7 = (bf16[12,32,128]{2,1,0:T(8,128)(2,1)S(1)}, bf16[12,32,128]{2,1,0:T(8,128)(2,1)S(1)}, u32[]{:S(2)}, u32[]{:S(2)}) collective-permute-start(bf16[12,32,128]{2,1,0:T(8,128)(2,1)S(1)} %get-tuple-element.37), channel_id=1, source_target_pairs={{0,4},{4,0},{8,12},{12,8},{16,20},{20,16},{24,28},{28,24},{1,2},{5... | collective-permute-start | bytes 294920 | tf_op jit(solution)/shard_map/ppermute | solution.py:48
  33.4 0.0 collective-permute-done.11
  33.4 0.0 collective-permute-done.12
  33.4 3.1 %collective-permute-done.13 = f32[32,384]{1,0:T(8,128)S(1)} collective-permute-done((f32[32,384]{1,0:T(8,128)S(1)}, f32[32,384]{1,0:T(8,128)S(1)}, u32[]{:S(2)}, u32[]{:S(2)}) %collective-permute-start.13) | collective-permute-done | bytes 49184 | tf_op jit(solution)/shard_map/ppermute | solution.py:62
  36.6 0.2 collective-permute-start.14
  36.8 0.1 copy.14.weight_ref
  36.9 0.0 collective-permute-done.6.one_ref
  36.9 0.0 collective-permute-done.7.two_ref
  36.9 3.6 %shard_map.79 = (bf16[32,64,128]{2,1,0:T(8,128)(2,1)}, f32[8,128]{1,0:T(8,128)S(1)}) custom-call(bf16[64,32,128]{2,1,0:T(8,128)(2,1)S(1)} %get-tuple-element.31.own_ref, bf16[2,16,32,128]{3,2,1,0:T(8,128)(2,1)S(1)} %get-tuple-element.35.outer_ref, bf16[12,32,128]{2,1,0:T(8,128)(2,1)S(1)} %collective-permute-done.6.one_ref, ...), custom_call_target="tpu_custom_call" | custom-call | flops 150994944 | bytes 1529856 | tf_op jit(solution)/shard_map/pallas_call | solution.py:300
  40.5 0.2 collective-permute-done.14.other_ref
  40.7 0.8 %shard_map.81 = (f32[3,3,32,32]{3,2,1,0:T(8,128)}, f32[1,32]{1,0:T(1,128)}) custom-call(f32[32,384]{1,0:T(8,128)S(1)} %add_add_fusion.one_ref, f32[32,384]{1,0:T(8,128)S(1)} %collective-permute-done.14.other_ref, f32[8,128]{1,0:T(8,128)S(1)} %get-tuple-element.41.after_ref), custom_call_target="tpu_custom_call" | custom-call | bytes 139392 | tf_op jit(solution)/shard_map/pallas_call | solution.py:300
  (5 shorter events, 0.0 us)
Async XLA Ops:
  0.6 12.6 %copy-start.2 = (bf16[3,3,32,32]{3,2,1,0:T(8,128)(2,1)S(1)}, bf16[3,3,32,32]{3,2,1,0:T(8,128)(2,1)}, u32[]{:S(2)}) copy-start(bf16[3,3,32,32]{3,2,1,0:T(8,128)(2,1)} %param.5) | copy-start | bytes 55300
  0.6 12.8 %copy-start.3 = (f32[32]{0:T(128)S(1)}, f32[32]{0:T(128)}, u32[]{:S(2)}) copy-start(f32[32]{0:T(128)} %param.6) | copy-start | bytes 388
  1.7 8.6 %collective-permute-start = (bf16[32,16,128]{2,1,0:T(8,128)(2,1)S(1)}, bf16[32,16,128]{2,1,0:T(8,128)(2,1)S(1)}, u32[]{:S(2)}, u32[]{:S(2)}) collective-permute-start(bf16[32,16,128]{2,1,0:T(8,128)(2,1)S(1)} %get-tuple-element.45), channel_id=1, source_target_pairs={{0,4},{1,5},{2,6},{3,7},{4,0},{5,1},{6,2},{7,3},{8,12},{9,13},{10,... | collective-permute-start | bytes 393224 | tf_op jit(solution)/shard_map/ppermute | solution.py:48
  4.7 5.6 %collective-permute-start.1 = (bf16[32,16,128]{2,1,0:T(8,128)(2,1)S(1)}, bf16[32,16,128]{2,1,0:T(8,128)(2,1)S(1)}, u32[]{:S(2)}, u32[]{:S(2)}) collective-permute-start(bf16[32,16,128]{2,1,0:T(8,128)(2,1)S(1)} %get-tuple-element.44), channel_id=1, source_target_pairs={{0,1},{1,0},{2,3},{3,2},{4,8},{5,9},{6,10},{7,11},{8,4},{9,5},{10,... | collective-permute-start | bytes 393224 | tf_op jit(solution)/shard_map/ppermute | solution.py:48
  4.7 1.0 %copy-start = (bf16[32,64,128]{2,1,0:T(8,128)(2,1)S(1)}, bf16[32,64,128]{2,1,0:T(8,128)(2,1)}, u32[]{:S(2)}) copy-start(bf16[32,64,128]{2,1,0:T(8,128)(2,1)} %image_ref.1) | copy-start | bytes 1572868
  5.8 1.0 %copy-start.1 = (bf16[32,64,128]{2,1,0:T(8,128)(2,1)S(1)}, bf16[32,64,128]{2,1,0:T(8,128)(2,1)}, u32[]{:S(2)}) copy-start(bf16[32,64,128]{2,1,0:T(8,128)(2,1)} %cotangent_ref.1) | copy-start | bytes 1572868
  10.6 2.9 %collective-permute-start.2 = (bf16[12,32,128]{2,1,0:T(8,128)(2,1)S(1)}, bf16[12,32,128]{2,1,0:T(8,128)(2,1)S(1)}, u32[]{:S(2)}, u32[]{:S(2)}) collective-permute-start(bf16[12,32,128]{2,1,0:T(8,128)(2,1)S(1)} %get-tuple-element.27), channel_id=1, source_target_pairs={{0,1},{4,5},{8,9},{12,13},{16,17},{20,21},{24,25},{28,29},{1,0},{5... | collective-permute-start | bytes 294920 | tf_op jit(solution)/shard_map/ppermute | solution.py:48
  10.7 5.1 %collective-permute-start.3 = (bf16[12,32,128]{2,1,0:T(8,128)(2,1)S(1)}, bf16[12,32,128]{2,1,0:T(8,128)(2,1)S(1)}, u32[]{:S(2)}, u32[]{:S(2)}) collective-permute-start(bf16[12,32,128]{2,1,0:T(8,128)(2,1)S(1)} %get-tuple-element.28), channel_id=1, source_target_pairs={{0,4},{4,0},{8,12},{12,8},{16,20},{20,16},{24,28},{28,24},{1,2},{5... | collective-permute-start | bytes 294920 | tf_op jit(solution)/shard_map/ppermute | solution.py:48
  20.8 4.2 %collective-permute-start.10 = (f32[32,384]{1,0:T(8,128)S(1)}, f32[32,384]{1,0:T(8,128)S(1)}, u32[]{:S(2)}, u32[]{:S(2)}) collective-permute-start(f32[32,384]{1,0:T(8,128)S(1)} %shard_map.80), channel_id=1, source_target_pairs={{0,3},{1,2},{2,1},{3,0},{4,7},{5,6},{6,5},{7,4},{8,11},{9,10},{10,... | collective-permute-start | bytes 147464 | tf_op jit(solution)/shard_map/ppermute | solution.py:62
  21.5 3.5 %collective-permute-start.8 = (f32[32,384]{1,0:T(8,128)S(1)}, f32[32,384]{1,0:T(8,128)S(1)}, u32[]{:S(2)}, u32[]{:S(2)}) collective-permute-start(f32[32,384]{1,0:T(8,128)S(1)} %shard_map.80), channel_id=1, source_target_pairs={{0,1},{1,0},{2,3},{3,2},{4,5},{5,4},{6,7},{7,6},{8,9},{9,8},{10,11... | collective-permute-start | bytes 147464 | tf_op jit(solution)/shard_map/ppermute | solution.py:62
  21.5 4.3 %collective-permute-start.9 = (f32[32,384]{1,0:T(8,128)S(1)}, f32[32,384]{1,0:T(8,128)S(1)}, u32[]{:S(2)}, u32[]{:S(2)}) collective-permute-start(f32[32,384]{1,0:T(8,128)S(1)} %shard_map.80), channel_id=1, source_target_pairs={{0,2},{1,3},{2,0},{3,1},{4,6},{5,7},{6,4},{7,5},{8,10},{9,11},{10,... | collective-permute-start | bytes 147464 | tf_op jit(solution)/shard_map/ppermute | solution.py:62
  23.0 7.7 %collective-permute-start.4 = (bf16[16,32,128]{2,1,0:T(8,128)(2,1)S(1)}, bf16[16,32,128]{2,1,0:T(8,128)(2,1)S(1)}, u32[]{:S(2)}, u32[]{:S(2)}) collective-permute-start(bf16[16,32,128]{2,1,0:T(8,128)(2,1)S(1)} %get-tuple-element.32), channel_id=1, source_target_pairs={{0,4},{1,5},{2,6},{3,7},{4,0},{5,1},{6,2},{7,3},{8,12},{9,13},{10,... | collective-permute-start | bytes 393224 | tf_op jit(solution)/shard_map/ppermute | solution.py:48
  25.0 5.7 %collective-permute-start.5 = (bf16[16,32,128]{2,1,0:T(8,128)(2,1)S(1)}, bf16[16,32,128]{2,1,0:T(8,128)(2,1)S(1)}, u32[]{:S(2)}, u32[]{:S(2)}) collective-permute-start(bf16[16,32,128]{2,1,0:T(8,128)(2,1)S(1)} %get-tuple-element.33), channel_id=1, source_target_pairs={{0,1},{1,0},{2,3},{3,2},{4,8},{5,9},{6,10},{7,11},{8,4},{9,5},{10,... | collective-permute-start | bytes 393224 | tf_op jit(solution)/shard_map/ppermute | solution.py:48
  25.8 7.6 %collective-permute-start.11 = (f32[32,384]{1,0:T(8,128)S(1)}, f32[32,384]{1,0:T(8,128)S(1)}, u32[]{:S(2)}, u32[]{:S(2)}) collective-permute-start(f32[32,384]{1,0:T(8,128)S(1)} %add_add_fusion.1), channel_id=1, source_target_pairs={{0,8},{4,12},{8,0},{12,4},{16,24},{20,28},{24,16},{28,20},{1,9},{5... | collective-permute-start | bytes 147464 | tf_op jit(solution)/shard_map/ppermute | solution.py:62
  28.1 5.4 %collective-permute-start.12 = (f32[32,384]{1,0:T(8,128)S(1)}, f32[32,384]{1,0:T(8,128)S(1)}, u32[]{:S(2)}, u32[]{:S(2)}) collective-permute-start(f32[32,384]{1,0:T(8,128)S(1)} %add_add_fusion.1), channel_id=1, source_target_pairs={{0,16},{4,20},{8,24},{12,28},{16,0},{20,4},{24,8},{28,12},{1,17},{... | collective-permute-start | bytes 147464 | tf_op jit(solution)/shard_map/ppermute | solution.py:62
  30.7 5.9 %collective-permute-start.13 = (f32[32,384]{1,0:T(8,128)S(1)}, f32[32,384]{1,0:T(8,128)S(1)}, u32[]{:S(2)}, u32[]{:S(2)}) collective-permute-start(f32[32,384]{1,0:T(8,128)S(1)} %add_add_fusion.1), channel_id=1, source_target_pairs={{0,24},{4,28},{8,16},{12,20},{16,8},{20,12},{24,0},{28,4},{1,25},{... | collective-permute-start | bytes 147464 | tf_op jit(solution)/shard_map/ppermute | solution.py:62
  31.0 5.9 %collective-permute-start.6 = (bf16[12,32,128]{2,1,0:T(8,128)(2,1)S(1)}, bf16[12,32,128]{2,1,0:T(8,128)(2,1)S(1)}, u32[]{:S(2)}, u32[]{:S(2)}) collective-permute-start(bf16[12,32,128]{2,1,0:T(8,128)(2,1)S(1)} %get-tuple-element.36), channel_id=1, source_target_pairs={{0,1},{4,5},{8,9},{12,13},{16,17},{20,21},{24,25},{28,29},{1,0},{5... | collective-permute-start | bytes 294920 | tf_op jit(solution)/shard_map/ppermute | solution.py:48
  31.0 5.9 %collective-permute-start.7 = (bf16[12,32,128]{2,1,0:T(8,128)(2,1)S(1)}, bf16[12,32,128]{2,1,0:T(8,128)(2,1)S(1)}, u32[]{:S(2)}, u32[]{:S(2)}) collective-permute-start(bf16[12,32,128]{2,1,0:T(8,128)(2,1)S(1)} %get-tuple-element.37), channel_id=1, source_target_pairs={{0,4},{4,0},{8,12},{12,8},{16,20},{20,16},{24,28},{28,24},{1,2},{5... | collective-permute-start | bytes 294920 | tf_op jit(solution)/shard_map/ppermute | solution.py:48
  36.6 4.2 %collective-permute-start.14 = (f32[32,384]{1,0:T(8,128)S(1)}, f32[32,384]{1,0:T(8,128)S(1)}, u32[]{:S(2)}, u32[]{:S(2)}) collective-permute-start(f32[32,384]{1,0:T(8,128)S(1)} %add_add_fusion.one_ref), channel_id=1, source_target_pairs={{0,4},{4,0},{8,12},{12,8},{16,20},{20,16},{24,28},{28,24},{1,5},{5... | collective-permute-start | bytes 147464 | tf_op jit(solution)/shard_map/ppermute | solution.py:62

commit v17 on v11

--- a/solution.py
+++ b/solution.py
@@ -165,6 +165,10 @@
     either("col", pack, send_one_ref, send_two_ref)
     clear_if(alone("col", 0), send_one_ref)
     clear_if(alone("col", 1), send_two_ref)
+
+
+def rim_after_kernel(one_ref, two_ref, rims_ref, after_ref, send_one_ref, send_two_ref, outer_ref):
+    rim_kernel(False, one_ref, two_ref, rims_ref, send_one_ref, send_two_ref, outer_ref)
 
 
 def spread(rows_of, left_ref, right_ref, stack_ref, block, group_start):
@@ -283,18 +287,18 @@
     bias_ref[...] = flipped[127:128, :channels]
 
 
-def call(kernel, out_shapes, operands, scratch=(), flops=0):
+def call(kernel, out_shapes, operands, scratch=(), flops=0, after=()):
     whole = pl.BlockSpec(memory_space=pltpu.VMEM)
     size = sum(math.prod(x.shape) * jnp.dtype(x.dtype).itemsize for x in (*operands, *out_shapes))
     return pl.pallas_call(
         kernel,
         out_shape=out_shapes,
-        in_specs=[whole] * len(operands),
+        in_specs=[whole] * len(operands) + [pl.BlockSpec(memory_space=pl.ANY)] * len(after),
         out_specs=[whole] * len(out_shapes),
         scratch_shapes=list(scratch),
         compiler_params=pltpu.CompilerParams(vmem_limit_bytes=VMEM_BYTES),
         cost_estimate=pl.CostEstimate(flops=flops, bytes_accessed=size, transcendentals=0),
-    )(*operands)
+    )(*operands, *after)
 
 
 def shards(image, weight, bias, cotangent):
@@ -343,7 +347,7 @@
     )
     one, two = swap_pairs(one, "row", 0), swap_pairs(two, "row", 1)
     one, two, grad_outer = call(
-        functools.partial(rim_kernel, False), (packed, packed, outer), (one, two, rims)
+        rim_after_kernel, (packed, packed, outer), (one, two, rims), after=(activation,)
     )
     two, one = swap_pairs(two, "col", 1), swap_pairs(one, "col", 0)
     grad_image, token = call(

time: 41.8 us -> 41.9 us (level)
  local copies, waits for them, and re-layouts: 1.01 us -> 2.04 us
  waiting for transfers between devices: 10.6 us -> 9.59 us
    ppermute x7, waiting for transfers between devices: 4.16 us -> 2.9 us  [add_pairs(): lax.ppermute(value, axis, [(at, at ^ mask) for at in range(lax.axis_size(...]
    unnamed x8 -> x10, local copies, waits for them, and re-layouts: 0.66 us -> 1.7 us
where the time goes in v17:
time: 41.9 us; the launch traced here: 41.6 us
  starting transfers between devices  17.4 us (42%)
  Pallas kernels  10.7 us (26%)
  waiting for transfers between devices  9.59 us (23%)
  local copies, waits for them, and re-layouts  2.04 us (5%)
  other arithmetic  1.09 us (3%)
  between operations  0.77 us (2%)
    pallas_call x6, Pallas kernels, call(): pl.pallas_call(kernel, out_shape=out_shapes, in_specs=[whole] * len(opera...  10.7 us
    ppermute x8, starting transfers between devices, swap_pairs(): return lax.ppermute(value, ('row', 'col'), pairs)  10.2 us
    ppermute x7, starting transfers between devices, add_pairs(): lax.ppermute(value, axis, [(at, at ^ mask) for at in range(lax.axis_size(...  7.2 us
    ppermute x8, waiting for transfers between devices, swap_pairs(): return lax.ppermute(value, ('row', 'col'), pairs)  6.69 us
    ppermute x7, waiting for transfers between devices, add_pairs(): lax.ppermute(value, axis, [(at, at ^ mask) for at in range(lax.axis_size(...  2.9 us
    unnamed x10, local copies, waits for them, and re-layouts  1.7 us
    select_n x1, other arithmetic, image_rim(): return rim if flag is None else jnp.where(flag, jnp.zeros_like(rim), rim)  1.06 us
  transfers between devices with their start and end apart: 15, of which 5 were waited for; matrix products, arithmetic and copies ran while one was open for 1% of the time, Pallas kernels for 11%

profile of v17, /device:TPU:0, one launch (start us, length us, event | category | flops | bytes accessed | tf_op | source)
XLA Modules:
  0.0 41.6 jit_solution(11332955914067101779)
XLA Ops:
  0.6 0.0 copy-start
  0.7 1.1 %dynamic-slice_select_fusion = (bf16[32,16,128]{2,1,0:T(8,128)(2,1)S(1)}, bf16[32,16,128]{2,1,0:T(8,128)(2,1)S(1)}) fusion(bf16[32,64,128]{2,1,0:T(8,128)(2,1)} %image_ref.1, s32[]{:T(128)S(6)} %select_n.24, pred[]{:T(512)S(6)} %or.3, s32[]{:T(128)S(6)} %select_n.22), kind=kLoop, calls=%fused_computation | loop fusion | flops 65536 | bytes 524297 | tf_op jit(solution)/shard_map/jit(_where)/select_n | solution.py:327
  1.7 3.0 %collective-permute-start = (bf16[32,16,128]{2,1,0:T(8,128)(2,1)S(1)}, bf16[32,16,128]{2,1,0:T(8,128)(2,1)S(1)}, u32[]{:S(2)}, u32[]{:S(2)}) collective-permute-start(bf16[32,16,128]{2,1,0:T(8,128)(2,1)S(1)} %get-tuple-element.41), channel_id=1, source_target_pairs={{0,4},{1,5},{2,6},{3,7},{4,0},{5,1},{6,2},{7,3},{8,12},{9,13},{10,... | collective-permute-start | bytes 393224 | tf_op jit(solution)/shard_map/ppermute | solution.py:48
  4.8 0.0 collective-permute-start.1
  4.8 0.0 copy-done
  4.8 0.8 %shard_map.75 = (bf16[64,32,128]{2,1,0:T(8,128)(2,1)S(1)}, bf16[2,8,32,128]{3,2,1,0:T(8,128)(2,1)S(1)}) custom-call(bf16[32,64,128]{2,1,0:T(8,128)(2,1)S(1)} %copy-done), custom_call_target="tpu_custom_call" | custom-call | bytes 1179648 | tf_op jit(solution)/shard_map/pallas_call | solution.py:293
  5.6 4.8 %collective-permute-done.one_ref = bf16[32,16,128]{2,1,0:T(8,128)(2,1)S(1)} collective-permute-done((bf16[32,16,128]{2,1,0:T(8,128)(2,1)S(1)}, bf16[32,16,128]{2,1,0:T(8,128)(2,1)S(1)}, u32[]{:S(2)}, u32[]{:S(2)}) %collective-permute-start) | collective-permute-done | bytes 131104 | tf_op jit(solution)/shard_map/ppermute | solution.py:48
  10.3 0.0 collective-permute-done.1.two_ref
  10.3 0.3 shard_map.76
  10.6 0.1 collective-permute-start.2
  10.7 2.6 %collective-permute-start.3 = (bf16[12,32,128]{2,1,0:T(8,128)(2,1)S(1)}, bf16[12,32,128]{2,1,0:T(8,128)(2,1)S(1)}, u32[]{:S(2)}, u32[]{:S(2)}) collective-permute-start(bf16[12,32,128]{2,1,0:T(8,128)(2,1)S(1)} %get-tuple-element.26), channel_id=1, source_target_pairs={{0,4},{4,0},{8,12},{12,8},{16,20},{20,16},{24,28},{28,24},{1,2},{5... | collective-permute-start | bytes 294920 | tf_op jit(solution)/shard_map/ppermute | solution.py:48
  13.3 0.0 copy-done.3
  13.3 0.1 copy.11
  13.3 0.1 reshape.17.weight_ref
  13.4 0.0 copy-start.4
  13.5 0.6 %copy-done.4 = f32[32]{0:T(128)S(1)} copy-done((f32[32]{0:T(128)S(1)}, f32[32]{0:T(128)}, u32[]{:S(2)}) %copy-start.4) | copy-done | bytes 152
  14.1 0.1 copy.12.bias_ref
  14.2 0.0 collective-permute-done.2.one_ref
  14.2 1.7 %collective-permute-done.3.two_ref = bf16[12,32,128]{2,1,0:T(8,128)(2,1)S(1)} collective-permute-done((bf16[12,32,128]{2,1,0:T(8,128)(2,1)S(1)}, bf16[12,32,128]{2,1,0:T(8,128)(2,1)S(1)}, u32[]{:S(2)}, u32[]{:S(2)}) %collective-permute-start.3) | collective-permute-done | bytes 98336 | tf_op jit(solution)/shard_map/ppermute | solution.py:48
  15.9 5.1 %shard_map.77 = (bf16[32,64,128]{2,1,0:T(8,128)(2,1)}, bf16[64,32,128]{2,1,0:T(8,128)(2,1)S(1)}, bf16[16,32,128]{2,1,0:T(8,128)(2,1)S(1)}, bf16[16,32,128]{2,1,0...) custom-call(bf16[64,32,128]{2,1,0:T(8,128)(2,1)S(1)} %get-tuple-element.22.own_ref, ...), custom_call_target="tpu_custom_call" | custom-call | flops 301989888 | bytes 3016832 | tf_op jit(solution)/shard_map/pallas_call | solution.py:293
  20.9 0.6 %collective-permute-start.10 = (f32[32,384]{1,0:T(8,128)S(1)}, f32[32,384]{1,0:T(8,128)S(1)}, u32[]{:S(2)}, u32[]{:S(2)}) collective-permute-start(f32[32,384]{1,0:T(8,128)S(1)} %get-tuple-element.36), channel_id=1, source_target_pairs={{0,3},{1,2},{2,1},{3,0},{4,7},{5,6},{6,5},{7,4},{8,11},{9,10},{10,... | collective-permute-start | bytes 147464 | tf_op jit(solution)/shard_map/ppermute | solution.py:62
  21.6 0.0 collective-permute-start.8
  21.6 1.5 %collective-permute-start.9 = (f32[32,384]{1,0:T(8,128)S(1)}, f32[32,384]{1,0:T(8,128)S(1)}, u32[]{:S(2)}, u32[]{:S(2)}) collective-permute-start(f32[32,384]{1,0:T(8,128)S(1)} %get-tuple-element.36), channel_id=1, source_target_pairs={{0,2},{1,3},{2,0},{3,1},{4,6},{5,7},{6,4},{7,5},{8,10},{9,11},{10,... | collective-permute-start | bytes 147464 | tf_op jit(solution)/shard_map/ppermute | solution.py:62
  23.1 2.0 %collective-permute-start.4 = (bf16[16,32,128]{2,1,0:T(8,128)(2,1)S(1)}, bf16[16,32,128]{2,1,0:T(8,128)(2,1)S(1)}, u32[]{:S(2)}, u32[]{:S(2)}) collective-permute-start(bf16[16,32,128]{2,1,0:T(8,128)(2,1)S(1)} %get-tuple-element.29), channel_id=1, source_target_pairs={{0,4},{1,5},{2,6},{3,7},{4,0},{5,1},{6,2},{7,3},{8,12},{9,13},{10,... | collective-permute-start | bytes 393224 | tf_op jit(solution)/shard_map/ppermute | solution.py:48
  25.1 0.0 collective-permute-start.5
  25.1 0.0 collective-permute-done.10
  25.1 0.0 collective-permute-done.8
  25.1 0.8 %collective-permute-done.9 = f32[32,384]{1,0:T(8,128)S(1)} collective-permute-done((f32[32,384]{1,0:T(8,128)S(1)}, f32[32,384]{1,0:T(8,128)S(1)}, u32[]{:S(2)}, u32[]{:S(2)}) %collective-permute-start.9) | collective-permute-done | bytes 49184 | tf_op jit(solution)/shard_map/ppermute | solution.py:62
  25.9 2.3 %collective-permute-start.11 = (f32[32,384]{1,0:T(8,128)S(1)}, f32[32,384]{1,0:T(8,128)S(1)}, u32[]{:S(2)}, u32[]{:S(2)}) collective-permute-start(f32[32,384]{1,0:T(8,128)S(1)} %add_add_fusion.1), channel_id=1, source_target_pairs={{0,8},{4,12},{8,0},{12,4},{16,24},{20,28},{24,16},{28,20},{1,9},{5... | collective-permute-start | bytes 147464 | tf_op jit(solution)/shard_map/ppermute | solution.py:62
  28.2 2.6 %collective-permute-start.12 = (f32[32,384]{1,0:T(8,128)S(1)}, f32[32,384]{1,0:T(8,128)S(1)}, u32[]{:S(2)}, u32[]{:S(2)}) collective-permute-start(f32[32,384]{1,0:T(8,128)S(1)} %add_add_fusion.1), channel_id=1, source_target_pairs={{0,16},{4,20},{8,24},{12,28},{16,0},{20,4},{24,8},{28,12},{1,17},{... | collective-permute-start | bytes 147464 | tf_op jit(solution)/shard_map/ppermute | solution.py:62
  30.8 0.0 collective-permute-start.13
  30.8 0.0 collective-permute-done.4.one_ref
  30.8 0.0 collective-permute-done.5.two_ref
  30.8 0.0 copy-start.2
  30.8 1.0 %copy-done.2 = bf16[32,64,128]{2,1,0:T(8,128)(2,1)S(1)} copy-done((bf16[32,64,128]{2,1,0:T(8,128)(2,1)S(1)}, bf16[32,64,128]{2,1,0:T(8,128)(2,1)}, u32[]{:S(2)}) %copy-start.2) | copy-done | bytes 524312
  31.8 0.2 shard_map.78
  32.1 0.1 collective-permute-start.6
  32.2 2.4 %collective-permute-start.7 = (bf16[12,32,128]{2,1,0:T(8,128)(2,1)S(1)}, bf16[12,32,128]{2,1,0:T(8,128)(2,1)S(1)}, u32[]{:S(2)}, u32[]{:S(2)}) collective-permute-start(bf16[12,32,128]{2,1,0:T(8,128)(2,1)S(1)} %get-tuple-element.34), channel_id=1, source_target_pairs={{0,4},{4,0},{8,12},{12,8},{16,20},{20,16},{24,28},{28,24},{1,2},{5... | collective-permute-start | bytes 294920 | tf_op jit(solution)/shard_map/ppermute | solution.py:48
  34.6 0.0 collective-permute-done.11
  34.6 0.0 collective-permute-done.12
  34.6 2.1 %collective-permute-done.13 = f32[32,384]{1,0:T(8,128)S(1)} collective-permute-done((f32[32,384]{1,0:T(8,128)S(1)}, f32[32,384]{1,0:T(8,128)S(1)}, u32[]{:S(2)}, u32[]{:S(2)}) %collective-permute-start.13) | collective-permute-done | bytes 49184 | tf_op jit(solution)/shard_map/ppermute | solution.py:62
  36.7 0.2 collective-permute-start.14
  36.9 0.1 copy.14.weight_ref
  37.0 0.0 collective-permute-done.6.one_ref
  37.0 0.2 collective-permute-done.7.two_ref
  37.2 3.6 %shard_map.79 = (bf16[32,64,128]{2,1,0:T(8,128)(2,1)}, f32[8,128]{1,0:T(8,128)S(1)}) custom-call(bf16[64,32,128]{2,1,0:T(8,128)(2,1)S(1)} %get-tuple-element.28.own_ref, bf16[2,16,32,128]{3,2,1,0:T(8,128)(2,1)S(1)} %get-tuple-element.32.outer_ref, bf16[12,32,128]{2,1,0:T(8,128)(2,1)S(1)} %collective-permute-done.6.one_ref, ...), custom_call_target="tpu_custom_call" | custom-call | flops 150994944 | bytes 1529856 | tf_op jit(solution)/shard_map/pallas_call | solution.py:293
  40.8 0.0 collective-permute-done.14.other_ref
  40.8 0.8 %shard_map.80 = (f32[3,3,32,32]{3,2,1,0:T(8,128)}, f32[1,32]{1,0:T(1,128)}) custom-call(f32[32,384]{1,0:T(8,128)S(1)} %add_add_fusion.one_ref, f32[32,384]{1,0:T(8,128)S(1)} %collective-permute-done.14.other_ref, f32[8,128]{1,0:T(8,128)S(1)} %get-tuple-element.37.after_ref), custom_call_target="tpu_custom_call" | custom-call | bytes 139392 | tf_op jit(solution)/shard_map/pallas_call | solution.py:293
  (6 shorter events, 0.0 us)
Async XLA Ops:
  0.6 4.1 %copy-start = (bf16[32,64,128]{2,1,0:T(8,128)(2,1)S(1)}, bf16[32,64,128]{2,1,0:T(8,128)(2,1)}, u32[]{:S(2)}) copy-start(bf16[32,64,128]{2,1,0:T(8,128)(2,1)} %image_ref.1) | copy-start | bytes 1572868
  1.7 8.6 %collective-permute-start = (bf16[32,16,128]{2,1,0:T(8,128)(2,1)S(1)}, bf16[32,16,128]{2,1,0:T(8,128)(2,1)S(1)}, u32[]{:S(2)}, u32[]{:S(2)}) collective-permute-start(bf16[32,16,128]{2,1,0:T(8,128)(2,1)S(1)} %get-tuple-element.41), channel_id=1, source_target_pairs={{0,4},{1,5},{2,6},{3,7},{4,0},{5,1},{6,2},{7,3},{8,12},{9,13},{10,... | collective-permute-start | bytes 393224 | tf_op jit(solution)/shard_map/ppermute | solution.py:48
  4.8 11.1 %copy-start.1 = (bf16[32,64,128]{2,1,0:T(8,128)(2,1)S(1)}, bf16[32,64,128]{2,1,0:T(8,128)(2,1)}, u32[]{:S(2)}) copy-start(bf16[32,64,128]{2,1,0:T(8,128)(2,1)} %cotangent_ref.1) | copy-start | bytes 1572868
  4.8 5.6 %collective-permute-start.1 = (bf16[32,16,128]{2,1,0:T(8,128)(2,1)S(1)}, bf16[32,16,128]{2,1,0:T(8,128)(2,1)S(1)}, u32[]{:S(2)}, u32[]{:S(2)}) collective-permute-start(bf16[32,16,128]{2,1,0:T(8,128)(2,1)S(1)} %get-tuple-element.40), channel_id=1, source_target_pairs={{0,1},{1,0},{2,3},{3,2},{4,8},{5,9},{6,10},{7,11},{8,4},{9,5},{10,... | collective-permute-start | bytes 393224 | tf_op jit(solution)/shard_map/ppermute | solution.py:48
  10.3 2.9 %copy-start.3 = (bf16[3,3,32,32]{3,2,1,0:T(8,128)(2,1)S(1)}, bf16[3,3,32,32]{3,2,1,0:T(8,128)(2,1)}, u32[]{:S(2)}) copy-start(bf16[3,3,32,32]{3,2,1,0:T(8,128)(2,1)} %param.5) | copy-start | bytes 55300
  10.6 3.6 %collective-permute-start.2 = (bf16[12,32,128]{2,1,0:T(8,128)(2,1)S(1)}, bf16[12,32,128]{2,1,0:T(8,128)(2,1)S(1)}, u32[]{:S(2)}, u32[]{:S(2)}) collective-permute-start(bf16[12,32,128]{2,1,0:T(8,128)(2,1)S(1)} %get-tuple-element.25), channel_id=1, source_target_pairs={{0,1},{4,5},{8,9},{12,13},{16,17},{20,21},{24,25},{28,29},{1,0},{5... | collective-permute-start | bytes 294920 | tf_op jit(solution)/shard_map/ppermute | solution.py:48
  10.7 5.1 %collective-permute-start.3 = (bf16[12,32,128]{2,1,0:T(8,128)(2,1)S(1)}, bf16[12,32,128]{2,1,0:T(8,128)(2,1)S(1)}, u32[]{:S(2)}, u32[]{:S(2)}) collective-permute-start(bf16[12,32,128]{2,1,0:T(8,128)(2,1)S(1)} %get-tuple-element.26), channel_id=1, source_target_pairs={{0,4},{4,0},{8,12},{12,8},{16,20},{20,16},{24,28},{28,24},{1,2},{5... | collective-permute-start | bytes 294920 | tf_op jit(solution)/shard_map/ppermute | solution.py:48
  13.4 0.7 %copy-start.4 = (f32[32]{0:T(128)S(1)}, f32[32]{0:T(128)}, u32[]{:S(2)}) copy-start(f32[32]{0:T(128)} %param.6) | copy-start | bytes 388
  20.9 4.2 %collective-permute-start.10 = (f32[32,384]{1,0:T(8,128)S(1)}, f32[32,384]{1,0:T(8,128)S(1)}, u32[]{:S(2)}, u32[]{:S(2)}) collective-permute-start(f32[32,384]{1,0:T(8,128)S(1)} %get-tuple-element.36), channel_id=1, source_target_pairs={{0,3},{1,2},{2,1},{3,0},{4,7},{5,6},{6,5},{7,4},{8,11},{9,10},{10,... | collective-permute-start | bytes 147464 | tf_op jit(solution)/shard_map/ppermute | solution.py:62
  21.6 3.5 %collective-permute-start.8 = (f32[32,384]{1,0:T(8,128)S(1)}, f32[32,384]{1,0:T(8,128)S(1)}, u32[]{:S(2)}, u32[]{:S(2)}) collective-permute-start(f32[32,384]{1,0:T(8,128)S(1)} %get-tuple-element.36), channel_id=1, source_target_pairs={{0,1},{1,0},{2,3},{3,2},{4,5},{5,4},{6,7},{7,6},{8,9},{9,8},{10,11... | collective-permute-start | bytes 147464 | tf_op jit(solution)/shard_map/ppermute | solution.py:62
  21.6 4.3 %collective-permute-start.9 = (f32[32,384]{1,0:T(8,128)S(1)}, f32[32,384]{1,0:T(8,128)S(1)}, u32[]{:S(2)}, u32[]{:S(2)}) collective-permute-start(f32[32,384]{1,0:T(8,128)S(1)} %get-tuple-element.36), channel_id=1, source_target_pairs={{0,2},{1,3},{2,0},{3,1},{4,6},{5,7},{6,4},{7,5},{8,10},{9,11},{10,... | collective-permute-start | bytes 147464 | tf_op jit(solution)/shard_map/ppermute | solution.py:62
  23.1 7.7 %collective-permute-start.4 = (bf16[16,32,128]{2,1,0:T(8,128)(2,1)S(1)}, bf16[16,32,128]{2,1,0:T(8,128)(2,1)S(1)}, u32[]{:S(2)}, u32[]{:S(2)}) collective-permute-start(bf16[16,32,128]{2,1,0:T(8,128)(2,1)S(1)} %get-tuple-element.29), channel_id=1, source_target_pairs={{0,4},{1,5},{2,6},{3,7},{4,0},{5,1},{6,2},{7,3},{8,12},{9,13},{10,... | collective-permute-start | bytes 393224 | tf_op jit(solution)/shard_map/ppermute | solution.py:48
  25.1 5.7 %collective-permute-start.5 = (bf16[16,32,128]{2,1,0:T(8,128)(2,1)S(1)}, bf16[16,32,128]{2,1,0:T(8,128)(2,1)S(1)}, u32[]{:S(2)}, u32[]{:S(2)}) collective-permute-start(bf16[16,32,128]{2,1,0:T(8,128)(2,1)S(1)} %get-tuple-element.30), channel_id=1, source_target_pairs={{0,1},{1,0},{2,3},{3,2},{4,8},{5,9},{6,10},{7,11},{8,4},{9,5},{10,... | collective-permute-start | bytes 393224 | tf_op jit(solution)/shard_map/ppermute | solution.py:48
  25.9 8.7 %collective-permute-start.11 = (f32[32,384]{1,0:T(8,128)S(1)}, f32[32,384]{1,0:T(8,128)S(1)}, u32[]{:S(2)}, u32[]{:S(2)}) collective-permute-start(f32[32,384]{1,0:T(8,128)S(1)} %add_add_fusion.1), channel_id=1, source_target_pairs={{0,8},{4,12},{8,0},{12,4},{16,24},{20,28},{24,16},{28,20},{1,9},{5... | collective-permute-start | bytes 147464 | tf_op jit(solution)/shard_map/ppermute | solution.py:62
  28.2 6.4 %collective-permute-start.12 = (f32[32,384]{1,0:T(8,128)S(1)}, f32[32,384]{1,0:T(8,128)S(1)}, u32[]{:S(2)}, u32[]{:S(2)}) collective-permute-start(f32[32,384]{1,0:T(8,128)S(1)} %add_add_fusion.1), channel_id=1, source_target_pairs={{0,16},{4,20},{8,24},{12,28},{16,0},{20,4},{24,8},{28,12},{1,17},{... | collective-permute-start | bytes 147464 | tf_op jit(solution)/shard_map/ppermute | solution.py:62
  30.8 5.9 %collective-permute-start.13 = (f32[32,384]{1,0:T(8,128)S(1)}, f32[32,384]{1,0:T(8,128)S(1)}, u32[]{:S(2)}, u32[]{:S(2)}) collective-permute-start(f32[32,384]{1,0:T(8,128)S(1)} %add_add_fusion.1), channel_id=1, source_target_pairs={{0,24},{4,28},{8,16},{12,20},{16,8},{20,12},{24,0},{28,4},{1,25},{... | collective-permute-start | bytes 147464 | tf_op jit(solution)/shard_map/ppermute | solution.py:62
  30.8 1.0 %copy-start.2 = (bf16[32,64,128]{2,1,0:T(8,128)(2,1)S(1)}, bf16[32,64,128]{2,1,0:T(8,128)(2,1)}, u32[]{:S(2)}) copy-start(bf16[32,64,128]{2,1,0:T(8,128)(2,1)} %get-tuple-element.18.after_ref) | copy-start | bytes 1572868
  32.1 4.9 %collective-permute-start.6 = (bf16[12,32,128]{2,1,0:T(8,128)(2,1)S(1)}, bf16[12,32,128]{2,1,0:T(8,128)(2,1)S(1)}, u32[]{:S(2)}, u32[]{:S(2)}) collective-permute-start(bf16[12,32,128]{2,1,0:T(8,128)(2,1)S(1)} %get-tuple-element.33), channel_id=1, source_target_pairs={{0,1},{4,5},{8,9},{12,13},{16,17},{20,21},{24,25},{28,29},{1,0},{5... | collective-permute-start | bytes 294920 | tf_op jit(solution)/shard_map/ppermute | solution.py:48
  32.2 5.1 %collective-permute-start.7 = (bf16[12,32,128]{2,1,0:T(8,128)(2,1)S(1)}, bf16[12,32,128]{2,1,0:T(8,128)(2,1)S(1)}, u32[]{:S(2)}, u32[]{:S(2)}) collective-permute-start(bf16[12,32,128]{2,1,0:T(8,128)(2,1)S(1)} %get-tuple-element.34), channel_id=1, source_target_pairs={{0,4},{4,0},{8,12},{12,8},{16,20},{20,16},{24,28},{28,24},{1,2},{5... | collective-permute-start | bytes 294920 | tf_op jit(solution)/shard_map/ppermute | solution.py:48
  36.7 4.2 %collective-permute-start.14 = (f32[32,384]{1,0:T(8,128)S(1)}, f32[32,384]{1,0:T(8,128)S(1)}, u32[]{:S(2)}, u32[]{:S(2)}) collective-permute-start(f32[32,384]{1,0:T(8,128)S(1)} %add_add_fusion.one_ref), channel_id=1, source_target_pairs={{0,4},{4,0},{8,12},{12,8},{16,20},{20,16},{24,28},{28,24},{1,5},{5... | collective-permute-start | bytes 147464 | tf_op jit(solution)/shard_map/ppermute | solution.py:62
